TPU v7x, 32 devices: a whole 2x2x4 slice. The times are simulated.
32 devices in a mesh: groups: 2 (over y), tensor: 4 (over z), context: 4 (over x, core).
Axes of the slice: x: 2, y: 2, z: 4, core: 2. Of those that a mesh axis runs over, the one named last changes fastest.
Arguments:
- queries: bfloat16 [4096, 1024], P(('groups', 'context'), 'tensor'), parts along dimension 0, may hold values from -200 to 200
- span_kv: bfloat16 [4096, 1, 256], P(('groups', 'context')), parts along dimension 0, may hold values from -6 to 6
- cache: bfloat16 [2, 4096, 256], P('groups', 'context'), parts along dimension 0, may hold values from -6 to 6
- lengths: int32 [8], P(('groups', 'context')), parts along dimension 0, may hold values from 1 to 1024, 3072 in all
- offset: int32 [2], P('groups'), parts along dimension 0, may hold values from 4096 to 20479
- out_weight: bfloat16 [1024, 8192], P('tensor'), may hold values from -0.25 to 0.25
- residual: bfloat16 [4096, 8192], P(('groups', 'context'), 'tensor'), parts along dimension 0, may hold values from -40 to 40
- gain: float32 [8192], replicated, may hold values from 0.1 to 1.9
Outputs:
- hidden: bfloat16 [4096, 8192], P(('groups', 'context'), 'tensor'), parts along dimension 0
- normed: bfloat16 [4096, 8192], P(('groups', 'context')), parts along dimension 0
There are 2 independent parts, one for each index of `groups`. A program takes and returns all parts, laid end to end along the dimension named above; an argument that names none is the same for every part. Nothing has to cross between parts.
All inputs are finite; a program needn't handle non-finite values. Where the computation divides by a largest or mean magnitude, that divisor is 1e-20 or more. No bound on the sum of `lengths` on one device may be relied on, other than what follows from the above.
Results may differ from a plain program's by a relative error of at most 0.0095.
Values may be sent and summed in bfloat16 or wider, within the bound.
No kernel may reach another device: no remote copies, remote signals or barrier semaphores. Data moves between devices by JAX's collectives and lax.ppermute only.
A program may use at most 128 MiB of HBM per device.

v0:
```python
import math

import jax
import jax.numpy as jnp
from jax import lax
from jax.sharding import PartitionSpec as P

GROUP = 8
HB = 128


NEG = -1e30
EPS_NORM = 1e-05
EPS_SCALE = 1e-06


def frequencies(head_width):
    counter = jnp.arange(head_width // 2, dtype=jnp.float32)
    base_freq = jnp.exp(-(2.0 * counter / head_width) * math.log(500000.0))
    wavelength = 2.0 * math.pi / base_freq
    smoothing = (8192.0 / wavelength - 1.0) / 3.0
    blended = (1.0 - smoothing) * base_freq / 8.0 + smoothing * base_freq
    return jnp.where(
        wavelength < 2048.0, base_freq, jnp.where(wavelength > 8192.0, base_freq / 8.0, blended)
    )


def rotate(vectors, positions):
    head_width = vectors.shape[-1]
    angles = positions.astype(jnp.float32)[:, None] * frequencies(head_width)[None, :]
    cosine = jnp.cos(angles)[:, None, :]
    sine = jnp.sin(angles)[:, None, :]
    lower = vectors[..., : head_width // 2]
    upper = vectors[..., head_width // 2 :]
    return jnp.concatenate([lower * cosine - upper * sine, upper * cosine + lower * sine], axis=-1)


def hadamard(length):
    counter = jnp.arange(length, dtype=jnp.int32)
    parity = jnp.zeros((length, length), jnp.int32)
    for shift_by in range(length.bit_length() - 1):
        digits = jnp.bitwise_and(jnp.right_shift(counter, shift_by), 1)
        parity = parity + digits[:, None] * digits[None, :]
    return (1 - 2 * jnp.bitwise_and(parity, 1)).astype(jnp.float32) / math.sqrt(length)


def absorb(carry, query_rows, key_rows, value_rows, allowed):
    running_max, running_sum, running_out = carry
    scores = lax.dot_general(
        query_rows, key_rows, (((1,), (1,)), ((), ())), preferred_element_type=jnp.float32
    )
    scores = scores * (1.0 / math.sqrt(query_rows.shape[1]))
    scores = jnp.where(allowed, scores, NEG)
    new_max = jnp.maximum(running_max, jnp.max(scores, axis=1))
    weights = jnp.where(allowed, jnp.exp(scores - new_max[:, None]), 0.0)
    fading = jnp.exp(running_max - new_max)
    new_sum = running_sum * fading + jnp.sum(weights, axis=1)
    new_out = running_out * fading[:, None] + jnp.dot(
        weights.astype(jnp.bfloat16), value_rows, preferred_element_type=jnp.float32
    )
    return (new_max, new_sum, new_out)


def pick_block(count):
    for candidate in (2048, 1024, 512, 256, 128):
        return candidate
    return count


def empty_state(count, head_width):
    return (
        jnp.full((count,), NEG, jnp.float32),
        jnp.zeros((count,), jnp.float32),
        jnp.zeros((count, head_width), jnp.float32),
    )


def per_device(queries, span_kv, cache, lengths, offset, out_weight, residual, gain):
    rows_here = queries.shape[0]
    head_width = span_kv.shape[2] // 2
    heads_here = queries.shape[1] // head_width
    query_count = rows_here * heads_here
    context_index = lax.axis_index("context")
    context_count = lax.axis_size("context")
    kv_index = lax.axis_index("tensor") * heads_here // GROUP
    positions = offset[0] + context_index * rows_here + jnp.arange(rows_here, dtype=jnp.int32)
    query_rows = rotate(
        queries.astype(jnp.float32).reshape(rows_here, heads_here, head_width), positions
    )
    query_rows = query_rows.astype(jnp.bfloat16).reshape(query_count, head_width)
    span_head = lax.dynamic_index_in_dim(span_kv, kv_index, 1, keepdims=True)
    key_turned = rotate(span_head[:, :, :head_width].astype(jnp.float32), positions).astype(
        jnp.bfloat16
    )
    span_pairs = jnp.concatenate([key_turned[:, 0, :], span_head[:, 0, head_width:]], axis=1)
    query_order = context_index * rows_here + jnp.arange(query_count, dtype=jnp.int32) // heads_here
    piece = lax.all_gather(span_pairs, "context", axis=0, tiled=True)
    key_order = jnp.arange(piece.shape[0], dtype=jnp.int32)
    allowed = key_order[None, :] <= query_order[:, None]
    state = absorb(
        empty_state(query_count, head_width),
        query_rows,
        piece[:, :head_width],
        piece[:, head_width:],
        allowed,
    )
    cache_local = lax.dynamic_index_in_dim(cache, kv_index, 0, keepdims=False)
    slot_count = cache_local.shape[0]
    length_list = lax.all_gather(lengths, "context", axis=0, tiled=True)
    owner_ids = jnp.arange(context_count, dtype=jnp.int32)
    carry = state
    piece = lax.all_gather(cache_local, "context", axis=0, tiled=True)
    start = jnp.int32(0)
    piece_rows = piece.shape[0]
    step_rows = pick_block(piece_rows)
    for block_start in range(0, piece_rows, step_rows):
        slot_order = start + block_start + jnp.arange(step_rows, dtype=jnp.int32)
        owner_match = (slot_order // slot_count)[:, None] == owner_ids[None, :]
        owner_length = jnp.sum(jnp.where(owner_match, length_list[None, :], 0), axis=1)
        live = slot_order % slot_count < owner_length
        key_block = piece[block_start : block_start + step_rows]
        carry = absorb(
            carry, query_rows, key_block[:, :head_width], key_block[:, head_width:], live[None, :]
        )
    state = carry
    running_max, running_sum, running_out = state
    attention = (
        (running_out / running_sum[:, None])
        .astype(jnp.bfloat16)
        .reshape(rows_here, heads_here * head_width)
    )
    partial_value = jnp.dot(attention, out_weight, preferred_element_type=jnp.float32)
    model_width = partial_value.shape[1]
    group_count = lax.axis_size("tensor")
    slab = model_width // group_count
    table = hadamard(HB)
    turned = jnp.einsum(
        "tbk,kj->tbj",
        partial_value.reshape(rows_here, model_width // HB, HB),
        table,
        precision=lax.Precision.HIGHEST,
    )
    block_scale = (jnp.max(jnp.abs(turned), axis=-1) + EPS_SCALE).astype(jnp.bfloat16)
    coded = (turned / block_scale.astype(jnp.float32)[..., None]).astype(jnp.bfloat16)
    send_codes = coded.reshape(rows_here, group_count, slab)
    send_scales = block_scale.reshape(rows_here, group_count, slab // HB)
    got_codes = lax.all_to_all(send_codes, "tensor", split_axis=1, concat_axis=1, tiled=True)
    got_scales = lax.all_to_all(send_scales, "tensor", split_axis=1, concat_axis=1, tiled=True)
    item_count = got_codes.shape[0]
    restored = (
        got_codes.astype(jnp.float32).reshape(item_count, group_count, slab // HB, HB)
        * got_scales.astype(jnp.float32)[..., None]
    )
    summed = jnp.sum(restored, axis=1)
    attention_slab = jnp.einsum(
        "tbk,kj->tbj", summed, table, precision=lax.Precision.HIGHEST
    ).reshape(item_count, slab)
    hidden = (residual.astype(jnp.float32) + attention_slab).astype(jnp.bfloat16)
    hidden_f = hidden.astype(jnp.float32)
    local_squares = jnp.sum(hidden_f * hidden_f, axis=1)
    all_squares = lax.psum(local_squares, "tensor")
    inverse = lax.rsqrt(all_squares / model_width + EPS_NORM)
    gain_slab = lax.dynamic_slice_in_dim(gain, lax.axis_index("tensor") * slab, slab, 0)
    normed_slab = (hidden_f * inverse[:, None] * gain_slab[None, :]).astype(jnp.bfloat16)
    normed = lax.all_gather(normed_slab, "tensor", axis=1, tiled=True)
    return (hidden, normed)


def solution(mesh):
    in_specs = (
        P(("groups", "context"), "tensor"),
        P(("groups", "context"), None, None),
        P("groups", "context", None),
        P(("groups", "context")),
        P("groups"),
        P("tensor", None),
        P(("groups", "context"), "tensor"),
        P(),
    )
    out_specs = (P(("groups", "context"), "tensor"), P(("groups", "context"), None))
    return jax.shard_map(
        per_device, mesh=mesh, in_specs=in_specs, out_specs=out_specs, check_vma=False
    )
```

profile of v0, /device:TPU:0, one launch (start us, length us, event | category | flops | bytes accessed | tf_op | source)
XLA Modules:
  0.0 503.6 jit_solution(6273844511556532736)
XLA Ops:
  14.4 6.3 %all-reduce = s32[4]{0:T(128)S(1)} all-reduce(s32[4]{0:T(128)S(1)} %dynamic-update-slice), channel_id=1, replica_groups=mesh['groups'=2,'tensor'=4,'context'=4] {'context'}, use_global_device_ids=true, to_apply=%add | all-reduce | flops 4 | bytes 32
  22.1 6.4 %copy.17 = bf16[8192,256]{1,0:T(8,128)(2,1)} copy(bf16[8192,256]{0,1:T(8,128)(2,1)} %bitcast.39) | data formatting | bytes 8388608 | tf_op jit(solution)/shard_map/dot_general | solution.py:132
  30.6 5.4 %fusion.3 = (f32[1024]{0:T(1024)S(1)}, f32[1024,2048]{1,0:T(8,128)}) fusion(s32[1024]{0:T(1024)S(1)} %fusion.77, bf16[2048,256]{1,0:T(8,128)(2,1)} %all-gather.5.cloned.1.call-done, bf16[1024,64]{1,0:T(8,128)(2,1)S(1)} %bitcast.43, bf16[1024,64]{1,0:T(8,128)(2,1)S(1)} %bitcast.40), kind=kOutput, calls=%fused_computation.13 | convolution fusion | flops 545782784 | bytes 9183232 | tf_op jit(solution)/shard_map/dot_general | solution.py:49
  36.0 18.7 %all-gather.9.cloned.1.call-done = bf16[1,4096,256]{2,1,0:T(8,128)(2,1)} async-done(((bf16[1,1024,256]{2,1,0:T(8,128)(2,1)}), bf16[1,4096,256]{2,1,0:T(8,128)(2,1)}) %all-gather.9.cloned.1.call-update) | async-done | bytes 2097168 | tf_op jit(solution)/shard_map/all_gather | solution.py:112
  54.8 2.7 fusion.2
  59.7 3.0 fusion.8
  62.8 2.5 fusion.4
  65.3 2.7 fusion.6
  68.1 2.4 fusion.33
  70.5 1.9 fusion.27
  72.4 1.9 fusion.39
  74.4 9.2 %fusion.100 = f32[512,64,128]{2,0,1:T(8,128)} fusion(bf16[512,256,1]{1,0,2:T(8,128)(2,1)S(1)} %reshape.386, bf16[64,128,256]{2,1,0:T(8,128)(2,1)} %bitcast.34), kind=kOutput, calls=%fused_computation.143 | convolution fusion | flops 2147483648 | bytes 21233664 | tf_op jit(solution)/shard_map/dot_general | solution.py:132
  83.6 22.7 %abs_reduce_fusion = (f32[512,64]{0,1:T(8,128)S(1)}, f32[512,64,128]{0,2,1:T(8,128)}) fusion(f32[512,64,128]{2,0,1:T(8,128)} %fusion.100, s32[128]{0:T(128)S(1)} %get-tuple-element.33, s32[128]{0:T(128)S(1)} %get-tuple-element.34, s32[128]{0:T(128)S(1)} %get-tuple-element.35, s32[128]{0:T(128)S(1)} %get-tuple-element.36, s32[128]{0:T(128)S(1)} %get-tuple-element.37, ...), kind=kOutput, calls=%fused_computation.3 | convolution fusion | flops 6451101696 | bytes 33689088 | tf_op jit(solution)/shard_map/tbk,kj->tbj/dot_general | solution.py:137
  107.0 4.4 all-to-all-start.1
  111.4 9.7 %divide_convert_fusion = bf16[512,64,128]{0,2,1:T(8,128)(2,1)} fusion(f32[512,64,128]{0,2,1:T(8,128)} %get-tuple-element.30, f32[512,64]{0,1:T(8,128)S(1)} %get-tuple-element.6), kind=kLoop, calls=%fused_computation.2 | loop fusion | flops 8388608 | bytes 25296896 | tf_op jit(solution)/shard_map/convert_element_type | solution.py:144
  121.1 5.7 %all-to-all-start = ((bf16[512,4,2048]{0,2,1:T(8,128)(2,1)}), bf16[512,4,2048]{0,2,1:T(8,128)(2,1)}, u32[]{:S(2)}, u32[]{:S(2)}) async-start(bf16[512,4,2048]{0,2,1:T(8,128)(2,1)} %bitcast.33), calls=%async_computation | async-start | bytes 16777216 | tf_op jit(solution)/shard_map/all_to_all | solution.py:147
  126.8 183.4 %all-to-all-done = bf16[512,4,2048]{0,2,1:T(8,128)(2,1)} async-done(((bf16[512,4,2048]{0,2,1:T(8,128)(2,1)}), bf16[512,4,2048]{0,2,1:T(8,128)(2,1)}, u32[]{:S(2)}, u32[]{:S(2)}) %all-to-all-start) | async-done | bytes 8388640 | tf_op jit(solution)/shard_map/all_to_all | solution.py:147
  310.2 5.5 %fusion = f32[512,2048]{0,1:T(8,128)S(1)} fusion(bf16[512,4,2048]{0,2,1:T(8,128)(2,1)} %all-to-all-done, f32[512,4,16]{0,2,1:T(8,128)S(1)} %convert_element_type.87), kind=kLoop, calls=%fused_computation.1 | loop fusion | flops 11534336 | bytes 12713984 | tf_op jit(solution)/shard_map/reduce_sum | solution.py:154
  315.7 5.8 %fusion.61 = f32[512,16,128]{0,2,1:T(8,128)} fusion(f32[512,16,128]{0,2,1:T(8,128)S(1)} %bitcast.35, s32[128]{0:T(128)S(1)} %get-tuple-element.33, s32[128]{0:T(128)S(1)} %get-tuple-element.34, s32[128]{0:T(128)S(1)} %get-tuple-element.35, s32[128]{0:T(128)S(1)} %get-tuple-element.36, s32[128]{0:T(128)S(1)} %get-tuple-element.37, ...), kind=kOutput, calls=%fused_computation.68 | convolution fusion | flops 1610907648 | bytes 8392192 | tf_op jit(solution)/shard_map/tbk,kj->tbj/dot_general | solution.py:155
  321.5 5.4 %copy.15 = f32[512,2048]{1,0:T(8,128)} copy(f32[512,2048]{0,1:T(8,128)} %bitcast.36) | data formatting | bytes 8388608 | tf_op jit(solution)/shard_map/reshape | solution.py:157
  326.9 3.6 fusion.10
  330.5 9.8 %psum.7 = f32[512]{0:T(512)S(1)} all-reduce(f32[512]{0:T(512)S(1)} %get-tuple-element.4), channel_id=1, replica_groups=mesh['groups'=2,'tensor'=4,'context'=4] {'tensor'}, use_global_device_ids=true, to_apply=%region_11.12 | all-reduce | flops 512 | bytes 4096 | tf_op jit(solution)/shard_map/psum | solution.py:161
  342.2 147.0 %all-gather.7.cloned.1.call-done = bf16[512,8192]{1,0:T(8,128)(2,1)} async-done(((bf16[512,2048]{1,0:T(8,128)(2,1)}), bf16[512,8192]{1,0:T(8,128)(2,1)}) %all-gather.7.cloned.1.call-update) | async-done | bytes 8388624 | tf_op jit(solution)/shard_map/all_gather | solution.py:165
  489.2 7.8 %copy.22 = bf16[512,8192]{1,0:T(8,128)(2,1)} copy(bf16[512,8192]{1,0:T(8,128)(2,1)} %all-gather.7.cloned.1.call-done) | data formatting | bytes 16777216
  (49 shorter events, 14.2 us)
Async XLA Ops:
  7.2 23.4 %all-gather.5.cloned.1.call-start = ((), (), s32[]{:S(2)}) async-start(), calls=%async_computation.2 | async-start | bytes 1310720 | tf_op jit(solution)/shard_map/all_gather | solution.py:97
  11.0 43.8 %all-gather.9.cloned.1.call-start = ((), (), s32[]{:S(2)}) async-start(), calls=%async_computation.4 | async-start | bytes 2621440 | tf_op jit(solution)/shard_map/all_gather | solution.py:112
  54.8 2.7 copy-start.1
  54.8 4.3 slice-start
  57.5 2.3 slice-start.1
  62.8 5.3 %copy-start.2 = (bf16[2048,256]{1,0:T(8,128)(2,1)S(1)}, bf16[2048,256]{1,0:T(8,128)(2,1)}, u32[]{:S(2)}) copy-start(bf16[2048,256]{1,0:T(8,128)(2,1)} %all-gather.5.cloned.1.call-done) | copy-start | bytes 3145732
  107.0 14.1 %all-to-all-start.1 = ((bf16[512,4,16]{0,2,1:T(8,128)(2,1)}), bf16[512,4,16]{0,2,1:T(8,128)(2,1)S(1)}, u32[]{:S(2)}, u32[]{:S(2)}) async-start(bf16[512,4,16]{0,2,1:T(8,128)(2,1)} %bitcast.12), calls=%async_computation.1 | async-start | bytes 131072 | tf_op jit(solution)/shard_map/all_to_all | solution.py:148
  121.1 189.1 %all-to-all-start = ((bf16[512,4,2048]{0,2,1:T(8,128)(2,1)}), bf16[512,4,2048]{0,2,1:T(8,128)(2,1)}, u32[]{:S(2)}, u32[]{:S(2)}) async-start(bf16[512,4,2048]{0,2,1:T(8,128)(2,1)} %bitcast.33), calls=%async_computation | async-start | bytes 16777216 | tf_op jit(solution)/shard_map/all_to_all | solution.py:147
  126.7 362.5 %all-gather.7.cloned.1.call-start = ((), (), s32[]{:S(2)}) async-start(), calls=%async_computation.3 | async-start | bytes 10485760 | tf_op jit(solution)/shard_map/all_gather | solution.py:165
  321.5 18.8 %dynamic-slice-start = ((f32[8192]{0:T(1024)}, s32[]{:T(128)}), f32[2048]{0:T(1024)S(1)}, s32[]{:S(2)}) async-start(f32[8192]{0:T(1024)} %param.15, s32[]{:T(128)} %select_n.116), calls=%async_computation.7 | async-start | bytes 16896 | tf_op jit(solution)/shard_map/dynamic_slice | solution.py:163
  330.5 166.5 %copy-start = (bf16[512,2048]{1,0:T(8,128)(2,1)}, bf16[512,2048]{1,0:T(8,128)(2,1)S(1)}, u32[]{:S(2)}) copy-start(bf16[512,2048]{1,0:T(8,128)(2,1)S(1)} %get-tuple-element.41) | copy-start | bytes 6291460
Sparse Core Ops, SparseCore 0:
  11.1 19.4 all-gather.4
  32.1 22.5 all-gather.8
  342.3 146.8 all-gather.6
where the time goes:
time: 504 us
  waiting for transfers between devices  350 us (69%)
  matrix products  53.6 us (11%)
  other arithmetic  34.7 us (7%)
  local copies, waits for them, and re-layouts  23.7 us (5%)
  blocking collectives  16.2 us (3%)
  between operations  15.3 us (3%)
  starting transfers between devices  10.2 us (2%)
    all_to_all x1, waiting for transfers between devices, per_device(): lax.all_to_all(send_codes, 'tensor', split_axis=1, concat_axis=1, tiled=T...  183 us
    all_gather x1, waiting for transfers between devices, per_device(): normed = lax.all_gather(normed_slab, 'tensor', axis=1, tiled=True)  147 us
    dot_general x1, matrix products, per_device(): jnp.einsum('tbk,kj->tbj', partial_value.reshape(rows_here, model_width //...  22.7 us
    all_gather x1, waiting for transfers between devices, per_device(): piece = lax.all_gather(cache_local, 'context', axis=0, tiled=True)  18.7 us
    unnamed x14, local copies, waits for them, and re-layouts  10.5 us
  transfers between devices with their start and end apart: 5, of which 4 were waited for; matrix products, arithmetic and copies ran while one was open for 5% of the time, Pallas kernels for 0%

commit v1 on v0

v1 whole, which is shorter than its diff:
```python
import functools
import math

import jax
import jax.numpy as jnp
from jax import lax
from jax.experimental import pallas as pl
from jax.experimental.pallas import tpu as pltpu
from jax.sharding import PartitionSpec as P

GROUP = 8
HD = 128
NEG = -1e30
EPS_NORM = 1e-05
VMEM_BYTES = 48 * 1024 * 1024
CHUNK = 128
KEY_BLOCK = 512


def frequencies(head_width):
    counter = jnp.arange(head_width // 2, dtype=jnp.float32)
    base_freq = jnp.exp(-(2.0 * counter / head_width) * math.log(500000.0))
    wavelength = 2.0 * math.pi / base_freq
    smoothing = (8192.0 / wavelength - 1.0) / 3.0
    blended = (1.0 - smoothing) * base_freq / 8.0 + smoothing * base_freq
    return jnp.where(
        wavelength < 2048.0, base_freq, jnp.where(wavelength > 8192.0, base_freq / 8.0, blended)
    )


def pieces_of(value, axis, count, me):
    if count & (count - 1) == 0:
        held = {0: value}
        bit = count // 2
        while bit:
            pairs = [(i, i ^ bit) for i in range(count)]
            for mask in sorted(held):
                held[mask | bit] = lax.ppermute(held[mask], axis, pairs)
            bit //= 2
        return [held[mask] for mask in range(count)], [me ^ mask for mask in range(count)]
    blocks, owners = [value], [me]
    for shift in range(1, count):
        pairs = [(i, (i + shift) % count) for i in range(count)]
        blocks.append(lax.ppermute(value, axis, pairs))
        owners.append((me + count - shift) % count)
    return blocks, owners


def rotate_kernel(q_ref, kv_ref, cos_ref, sin_ref, q_out, kv_out):
    cosine, sine = cos_ref[...], sin_ref[...]

    def turn(block):
        block = block.astype(jnp.float32)
        return (block * cosine + pltpu.roll(block, HD // 2, 1) * sine).astype(jnp.bfloat16)

    for head in range(q_ref.shape[1] // HD):
        cols = slice(head * HD, (head + 1) * HD)
        q_out[:, cols] = turn(q_ref[:, cols])
    kv_out[:, :HD] = turn(kv_ref[:, :HD])
    kv_out[:, HD:] = kv_ref[:, HD:]


def rotate_all(queries, span_pairs, cosine, sine):
    rows = queries.shape[0]
    block = min(rows, 256)
    spec = lambda width: pl.BlockSpec((block, width), lambda i: (i, 0))
    return pl.pallas_call(
        rotate_kernel,
        grid=(rows // block,),
        out_shape=(
            jax.ShapeDtypeStruct(queries.shape, jnp.bfloat16),
            jax.ShapeDtypeStruct(span_pairs.shape, jnp.bfloat16),
        ),
        in_specs=[spec(queries.shape[1]), spec(2 * HD), spec(HD), spec(HD)],
        out_specs=(spec(queries.shape[1]), spec(2 * HD)),
        name="rotate",
    )(queries, span_pairs, cosine, sine)


def attend_kernel(count, first, info, q_ref, *refs):
    caches, spans = refs[:count], refs[count : 2 * count]
    out_ref, s_ref = refs[2 * count], refs[2 * count + 1]
    rows = q_ref.shape[0]
    heads = q_ref.shape[1] // HD
    chunk = pl.program_id(0) + first
    mine = info[0]
    q = jnp.concatenate([q_ref[:, h * HD : (h + 1) * HD] for h in range(heads)], axis=0)
    exponent = math.log2(math.e) / math.sqrt(HD)

    blocks = []
    peak = jnp.full((heads * rows, HD), NEG, jnp.float32)
    column = 0
    for kind, group in (("cache", caches), ("span", spans)):
        for number, ref in enumerate(group):
            width = min(KEY_BLOCK, ref.shape[0])
            for begin in range(0, ref.shape[0], width):
                scores = lax.dot_general(
                    q,
                    ref[begin : begin + width, :HD],
                    (((1,), (1,)), ((), ())),
                    preferred_element_type=jnp.float32,
                )
                if kind == "cache":
                    slot = lax.broadcasted_iota(jnp.int32, (1, width), 1) + begin
                    live = slot < info[1 + count + number]
                    scores = scores + jnp.where(live, 0.0, NEG)
                elif number == 0:
                    key = lax.broadcasted_iota(jnp.int32, (rows, width), 1) + begin
                    row = lax.broadcasted_iota(jnp.int32, (rows, width), 0) + chunk * rows
                    bias = jnp.where(key <= row, 0.0, NEG)
                    scores = scores + jnp.concatenate([bias] * heads, axis=0)
                else:
                    scores = scores + jnp.where(info[1 + number] < mine, 0.0, NEG)
                s_ref[:, column : column + width] = scores
                for lane in range(0, width, HD):
                    peak = jnp.maximum(peak, scores[:, lane : lane + HD])
                blocks.append((ref, begin, column, width))
                column += width
    top = jnp.max(peak, axis=1, keepdims=True)
    total = jnp.zeros((heads * rows, HD), jnp.float32)
    mixed = jnp.zeros((heads * rows, HD), jnp.float32)
    for ref, begin, column, width in blocks:
        weights = jnp.exp2((s_ref[:, column : column + width] - top) * exponent)
        for lane in range(0, width, HD):
            total = total + weights[:, lane : lane + HD]
        mixed = mixed + jnp.dot(
            weights.astype(jnp.bfloat16),
            ref[begin : begin + width, HD:],
            preferred_element_type=jnp.float32,
        )
    result = (mixed / jnp.sum(total, axis=1, keepdims=True)).astype(jnp.bfloat16)
    for h in range(heads):
        out_ref[:, h * HD : (h + 1) * HD] = result[h * rows : (h + 1) * rows]


def attend(info, queries, caches, spans, first, chunks, rows):
    count = len(caches)
    width = queries.shape[1]
    heads = width // HD
    keys = sum(a.shape[0] for a in caches) + sum(a.shape[0] for a in spans)
    whole = lambda a: pl.BlockSpec(a.shape, lambda i, info: (0, 0))
    return pl.pallas_call(
        functools.partial(attend_kernel, count, first),
        grid_spec=pltpu.PrefetchScalarGridSpec(
            num_scalar_prefetch=1,
            grid=(chunks,),
            in_specs=[pl.BlockSpec((rows, width), lambda i, info: (i + first, 0))]
            + [whole(a) for a in caches]
            + [whole(a) for a in spans],
            out_specs=pl.BlockSpec((rows, width), lambda i, info: (i, 0)),
            scratch_shapes=[pltpu.VMEM((heads * rows, keys), jnp.float32)],
        ),
        out_shape=jax.ShapeDtypeStruct((chunks * rows, width), jnp.bfloat16),
        compiler_params=pltpu.CompilerParams(vmem_limit_bytes=VMEM_BYTES),
        cost_estimate=pl.CostEstimate(
            flops=4 * chunks * rows * heads * keys * HD,
            bytes_accessed=keys * 4 * HD,
            transcendentals=chunks * rows * heads * keys,
        ),
        name="attend",
    )(info, queries, *caches, *spans)


def cut_kernel(count, info, w_ref, *refs):
    outs, sems = refs[:count], refs[count]
    part, slab = outs[0].shape
    copies = []
    for number, out in enumerate(outs):
        start = pl.multiple_of(info[1 + number] * slab, slab)
        copies.append(
            pltpu.make_async_copy(
                w_ref.at[pl.ds(pl.multiple_of(info[0] * part, part), part), pl.ds(start, slab)],
                out,
                sems.at[number],
            )
        )
    for copy in copies:
        copy.start()
    for copy in copies:
        copy.wait()


def cut(info, out_weight, part, slab, count):
    anywhere = pl.BlockSpec(memory_space=pl.ANY)
    return pl.pallas_call(
        functools.partial(cut_kernel, count),
        grid_spec=pltpu.PrefetchScalarGridSpec(
            num_scalar_prefetch=1,
            grid=(),
            in_specs=[anywhere],
            out_specs=[anywhere] * count,
            scratch_shapes=[pltpu.SemaphoreType.DMA((count,))],
        ),
        out_shape=[jax.ShapeDtypeStruct((part, slab), out_weight.dtype)] * count,
        name="cut",
    )(info, out_weight)


def project_kernel(count, info, a_ref, w_ref, r_ref, h_ref):
    total = r_ref[...].astype(jnp.float32)
    depth = a_ref.shape[2]
    for number in range(count):
        weight = w_ref[:, number].reshape(depth, w_ref.shape[3])
        total = total + jnp.dot(
            a_ref[info[number]], weight, preferred_element_type=jnp.float32
        )
    h_ref[...] = total.astype(jnp.bfloat16)


def project(order, attention, weights, residual, place, chunk, rows):
    count, depth = attention.shape[0], attention.shape[2]
    slab = residual.shape[1]
    tile = min(slab, 512)
    shares, part = weights.shape[0], weights.shape[2]
    return pl.pallas_call(
        functools.partial(project_kernel, count),
        grid_spec=pltpu.PrefetchScalarGridSpec(
            num_scalar_prefetch=1,
            grid=(slab // tile,),
            in_specs=[
                pl.BlockSpec((count, rows, depth), lambda j, info: (0, place, 0)),
                pl.BlockSpec((shares, count, part, tile), lambda j, info: (0, 0, 0, j)),
                pl.BlockSpec((rows, tile), lambda j, info: (chunk, j)),
            ],
            out_specs=pl.BlockSpec((rows, tile), lambda j, info: (0, j)),
        ),
        out_shape=jax.ShapeDtypeStruct((rows, slab), jnp.bfloat16),
        compiler_params=pltpu.CompilerParams(vmem_limit_bytes=VMEM_BYTES),
        cost_estimate=pl.CostEstimate(
            flops=2 * rows * count * depth * slab,
            bytes_accessed=2 * count * depth * slab,
            transcendentals=0,
        ),
        name="project",
    )(order, attention, weights, residual)


def norm_kernel(h_ref, g_ref, *refs):
    out_ref = refs[-1]
    count, rows, slab = h_ref.shape
    squares = jnp.zeros((rows, 1), jnp.float32)
    for number in range(count):
        block = h_ref[number].astype(jnp.float32)
        squares = squares + jnp.sum(block * block, axis=1, keepdims=True)
    inverse = lax.rsqrt(squares / (count * slab) + EPS_NORM)
    for number in range(count):
        cols = slice(number * slab, (number + 1) * slab)
        block = h_ref[number].astype(jnp.float32)
        out_ref[:, cols] = (block * inverse * g_ref[:, cols]).astype(jnp.bfloat16)


def norm_into(buffer, gathered, gain, chunk, total_rows):
    count, rows, slab = gathered.shape
    width = count * slab
    step = min(rows, 32)
    steps = rows // step
    in_specs = [
        pl.BlockSpec((count, step, slab), lambda i: (0, i, 0)),
        pl.BlockSpec((1, width), lambda i: (0, 0)),
    ]
    args = [gathered, gain.reshape(1, width)]
    aliases = {}
    if buffer is not None:
        in_specs.append(pl.BlockSpec(memory_space=pl.ANY))
        args.append(buffer)
        aliases = {2: 0}
    return pl.pallas_call(
        norm_kernel,
        grid=(steps,),
        in_specs=in_specs,
        out_specs=pl.BlockSpec((step, width), lambda i: (chunk * steps + i, 0)),
        out_shape=jax.ShapeDtypeStruct((total_rows, width), jnp.bfloat16),
        input_output_aliases=aliases,
        compiler_params=pltpu.CompilerParams(vmem_limit_bytes=VMEM_BYTES),
        cost_estimate=pl.CostEstimate(
            flops=6 * rows * width, bytes_accessed=4 * rows * width, transcendentals=0
        ),
        name="norm",
    )(*args)


def per_device(queries, span_kv, cache, lengths, offset, out_weight, residual, gain):
    rows = queries.shape[0]
    heads = queries.shape[1] // HD
    depth, model_width = out_weight.shape
    slab = residual.shape[1]
    context_count = lax.axis_size("context")
    tensor_count = lax.axis_size("tensor")
    context_index = lax.axis_index("context")
    tensor_index = lax.axis_index("tensor")
    kv_index = tensor_index * heads // GROUP
    shares = lax.axis_size("groups") * context_count
    share = lax.axis_index("groups") * context_count + context_index

    part = depth // shares
    targets = [(tensor_index + d) % tensor_count for d in range(tensor_count)]
    cuts = cut(
        jnp.stack([share] + targets).astype(jnp.int32), out_weight, part, slab, tensor_count
    )
    mine = [cuts[0]]
    for shift in range(1, tensor_count):
        pairs = [(i, (i + shift) % tensor_count) for i in range(tensor_count)]
        mine.append(lax.ppermute(cuts[shift], "tensor", pairs))
    order = jnp.stack(
        [(tensor_index + tensor_count - d) % tensor_count for d in range(tensor_count)]
    ).astype(jnp.int32)
    weights = lax.all_gather(jnp.stack(mine), ("groups", "context"), axis=0, tiled=False)

    cache_local = lax.dynamic_index_in_dim(cache, kv_index, 0, keepdims=False)
    caches, owners = pieces_of(cache_local, "context", context_count, context_index)
    length_pieces, _ = pieces_of(lengths, "context", context_count, context_index)
    span_local = lax.dynamic_index_in_dim(span_kv, kv_index, 1, keepdims=False)
    positions = offset[0] + context_index * rows + jnp.arange(rows, dtype=jnp.int32)
    angles = positions.astype(jnp.float32)[:, None] * frequencies(HD)[None, :]
    cosine, sine = jnp.cos(angles), jnp.sin(angles)
    q_turned, span_turned = rotate_all(
        queries,
        span_local,
        jnp.concatenate([cosine, cosine], axis=1),
        jnp.concatenate([-sine, sine], axis=1),
    )
    spans, _ = pieces_of(span_turned, "context", context_count, context_index)
    info = jnp.concatenate(
        [jnp.stack([context_index] + owners).astype(jnp.int32)] + length_pieces
    )

    chunk = min(CHUNK, rows)
    chunks = rows // chunk
    gathered = [
        lax.all_gather(
            attend(info, q_turned, caches, spans, 0, 1, chunk), "tensor", axis=0, tiled=False
        )
    ]
    if chunks > 1:
        gathered.append(
            lax.all_gather(
                attend(info, q_turned, caches, spans, 1, chunks - 1, chunk),
                "tensor",
                axis=0,
                tiled=False,
            )
        )

    hidden_parts = []
    normed = None
    for number in range(chunks):
        source = gathered[0] if number == 0 else gathered[1]
        place = 0 if number == 0 else number - 1
        part_hidden = project(order, source, weights, residual, place, number, chunk)
        hidden_parts.append(part_hidden)
    for number in range(chunks):
        whole = lax.all_gather(hidden_parts[number], "tensor", axis=0, tiled=False)
        normed = norm_into(normed, whole, gain, number, rows)
    return (jnp.concatenate(hidden_parts, axis=0), normed)


def solution(mesh):
    in_specs = (
        P(("groups", "context"), "tensor"),
        P(("groups", "context"), None, None),
        P("groups", "context", None),
        P(("groups", "context")),
        P("groups"),
        P("tensor", None),
        P(("groups", "context"), "tensor"),
        P(),
    )
    out_specs = (P(("groups", "context"), "tensor"), P(("groups", "context"), None))
    return jax.shard_map(
        per_device, mesh=mesh, in_specs=in_specs, out_specs=out_specs, check_vma=False
    )
```

time: 504 us -> 312 us (0.62)
  waiting for transfers between devices: 350 us -> 153 us
  Pallas kernels: 0 us -> 65.7 us
  matrix products: 53.6 us -> 0 us
  other arithmetic: 34.7 us -> 7.08 us
  blocking collectives: 16.2 us -> 43.6 us
  local copies, waits for them, and re-layouts: 23.7 us -> 14.5 us
    all_to_all x2 -> x0, waiting for transfers between devices: 183 us -> none  [the longest x1 183 us: per_device(): lax.all_to_all(send_codes, 'tensor', split_axis=1, concat_axis=1, tiled=T...]
    pallas_call x0 -> x12, Pallas kernels: none -> 65.7 us  [the longest x4 20.1 us: project(): pl.pallas_call(functools.partial(project_kernel, count), grid_spec=pltpu....]
    dot_general x9 -> x0, matrix products: 53.6 us -> none  [the longest x1 22.7 us: per_device(): jnp.einsum('tbk,kj->tbj', partial_value.reshape(rows_here, model_width //...]
    all_gather x0 -> x2, blocking collectives: none -> 43.6 us  [the longest x1 29.7 us: per_device(): lax.all_gather(attend(info, q_turned, caches, spans, 1, chunks - 1, chunk...]
    all_gather x3 -> x5, waiting for transfers between devices: 166 us -> 124 us  [the longest x4 124 us: per_device(): whole = lax.all_gather(hidden_parts[number], 'tensor', axis=0, tiled=False)]
    ppermute x0 -> x12, waiting for transfers between devices: none -> 29 us  [the longest x9 21.5 us: pieces_of(): held[mask | bit] = lax.ppermute(held[mask], axis, pairs)]
    reduce_sum x6 -> x0, other arithmetic: 17.5 us -> none  [the longest x3 8.27 us: absorb(): new_sum = running_sum * fading + jnp.sum(weights, axis=1)]
    convert_element_type x6 -> x1, other arithmetic: 13.2 us -> 0.01 us  [per_device(): angles = positions.astype(jnp.float32)[:, None] * frequencies(HD)[None, :]]
  transfers between devices with their start and end apart: 5 -> 17, of which waited for: 4 -> 10; matrix products, arithmetic and copies ran while one was open for 5% -> 2% of each run, Pallas kernels for 0% -> 13%
where the time goes in v1:
time: 312 us; the launch traced here: 311 us
  waiting for transfers between devices  153 us (49%)
  Pallas kernels  65.7 us (21%)
  blocking collectives  43.6 us (14%)
  between operations  15.3 us (5%)
  local copies, waits for them, and re-layouts  14.5 us (5%)
  starting transfers between devices  11.8 us (4%)
  other arithmetic  7.08 us (2%)
    all_gather x4, waiting for transfers between devices, per_device(): whole = lax.all_gather(hidden_parts[number], 'tensor', axis=0, tiled=False)  124 us
    all_gather x1, blocking collectives, per_device(): lax.all_gather(attend(info, q_turned, caches, spans, 1, chunks - 1, chunk...  29.7 us
    ppermute x9, waiting for transfers between devices, pieces_of(): held[mask | bit] = lax.ppermute(held[mask], axis, pairs)  21.5 us
    pallas_call x4, Pallas kernels, project(): pl.pallas_call(functools.partial(project_kernel, count), grid_spec=pltpu....  20.1 us
    pallas_call x1, Pallas kernels, cut(): pl.pallas_call(functools.partial(cut_kernel, count), grid_spec=pltpu.Pref...  17.7 us
    pallas_call x2, Pallas kernels, attend(): pl.pallas_call(functools.partial(attend_kernel, count, first), grid_spec=...  15.2 us
    all_gather x1, blocking collectives, per_device(): lax.all_gather(attend(info, q_turned, caches, spans, 0, 1, chunk), 'tenso...  14 us
    unnamed x26, local copies, waits for them, and re-layouts  11.8 us
  transfers between devices with their start and end apart: 17, of which 10 were waited for; matrix products, arithmetic and copies ran while one was open for 2% of the time, Pallas kernels for 13%

profile of v1, /device:TPU:0, one launch (start us, length us, event | category | flops | bytes accessed | tf_op | source)
XLA Modules:
  0.0 311.4 jit_solution(17968969214604452229)
XLA Ops:
  7.9 17.7 %cut.1 = (bf16[32,2048]{1,0:T(8,128)(2,1)}, bf16[32,2048]{1,0:T(8,128)(2,1)}, bf16[32,2048]{1,0:T(8,128)(2,1)}, bf16[32,2048]{1,0:T(8,128)(2,1)}) custom-call(s32[5]{0:T(128)} %stack.66.info, bf16[256,8192]{1,0:T(8,128)(2,1)} %w_ref.1), custom_call_target="tpu_custom_call" | custom-call | tf_op jit(solution)/shard_map/cut/pallas_call | solution.py:185
  25.6 3.1 collective-permute-start.9
  28.7 2.6 collective-permute-start.10
  32.6 2.7 collective-permute-done.9
  35.4 4.8 %collective-permute-done.10 = bf16[32,2048]{1,0:T(8,128)(2,1)S(1)} collective-permute-done((bf16[32,2048]{1,0:T(8,128)(2,1)}, bf16[32,2048]{1,0:T(8,128)(2,1)S(1)}, u32[]{:S(2)}, u32[]{:S(2)}) %collective-permute-start.10) | collective-permute-done | bytes 131104 | tf_op jit(solution)/shard_map/ppermute | solution.py:303
  49.0 10.6 %collective-permute-done.4.refs_2_ = bf16[1024,256]{1,0:T(8,128)(2,1)S(1)} collective-permute-done((bf16[1024,256]{1,0:T(8,128)(2,1)S(1)}, bf16[1024,256]{1,0:T(8,128)(2,1)S(1)}, u32[]{:S(2)}, u32[]{:S(2)}) %collective-permute-start.4) | collective-permute-done | bytes 524320 | tf_op jit(solution)/shard_map/ppermute | solution.py:38
  60.2 7.0 %collective-permute-done.7.refs_6_ = bf16[512,256]{1,0:T(8,128)(2,1)S(1)} collective-permute-done((bf16[512,256]{1,0:T(8,128)(2,1)}, bf16[512,256]{1,0:T(8,128)(2,1)S(1)}, u32[]{:S(2)}, u32[]{:S(2)}) %collective-permute-start.7) | collective-permute-done | bytes 262176 | tf_op jit(solution)/shard_map/ppermute | solution.py:38
  70.3 2.1 collective-permute-done.1
  77.6 4.8 %attend.2 = bf16[128,256]{1,0:T(8,128)(2,1)S(1)} custom-call(s32[9]{0:T(128)S(1)} %concatenate.12.info, bf16[512,256]{1,0:T(8,128)(2,1)S(1)} %copy-done.7, bf16[1024,256]{1,0:T(8,128)(2,1)S(1)} %bitcast.40, bf16[1024,256]{1,0:T(8,128)(2,1)} %collective-permute-done.3.refs_1_, bf16[1024,256]{1,0:T(8,128)(2,1)S(1)} %collective-permute-done.4.refs_2_, ...), custom_call_target="tpu_custom_call" | custom-call | flops 805306368 | bytes 3145728 | tf_op jit(solution)/shard_map/attend/pallas_call | solution.py:142
  83.1 14.0 %all-gather = bf16[512,256]{1,0:T(8,128)(2,1)S(1)} all-gather(bf16[128,256]{1,0:T(8,128)(2,1)S(1)} %attend.2), channel_id=2, replica_groups=mesh['groups'=2,'tensor'=4,'context'=4] {'tensor'}, dimensions={0}, use_global_device_ids=true | all-gather | bytes 327680 | tf_op jit(solution)/shard_map/all_gather | solution.py:330
  97.1 5.0 %project.4 = bf16[128,2048]{1,0:T(8,128)(2,1)} custom-call(s32[4]{0:T(128)S(1)} %pad_add_fusion.info, bf16[4,128,256]{2,1,0:T(8,128)(2,1)S(1)} %bitcast.33, bf16[8,4,32,2048]{3,2,1,0:T(8,128)(2,1)} %bitcast.42, bf16[512,2048]{1,0:T(8,128)(2,1)S(1)} %copy-done), custom_call_target="tpu_custom_call" | custom-call | flops 536870912 | bytes 4194304 | tf_op jit(solution)/shard_map/project/pallas_call | solution.py:215
  105.0 10.5 %attend.3 = bf16[384,256]{1,0:T(8,128)(2,1)S(1)} custom-call(s32[9]{0:T(128)S(1)} %concatenate.12.info, bf16[512,256]{1,0:T(8,128)(2,1)S(1)} %copy-done.8, bf16[1024,256]{1,0:T(8,128)(2,1)S(1)} %bitcast.41, bf16[1024,256]{1,0:T(8,128)(2,1)} %collective-permute-done.3.refs_1_, bf16[1024,256]{1,0:T(8,128)(2,1)S(1)} %collective-permute-done.4.refs_2_, ...), custom_call_target="tpu_custom_call" | custom-call | flops 2415919104 | bytes 3145728 | tf_op jit(solution)/shard_map/attend/pallas_call | solution.py:142
  115.5 29.7 %all-gather.2 = bf16[1536,256]{1,0:T(8,128)(2,1)S(1)} all-gather(bf16[384,256]{1,0:T(8,128)(2,1)S(1)} %attend.3), channel_id=4, replica_groups=mesh['groups'=2,'tensor'=4,'context'=4] {'tensor'}, dimensions={0}, use_global_device_ids=true | all-gather | bytes 983040 | tf_op jit(solution)/shard_map/all_gather | solution.py:336
  145.2 5.1 %project.5 = bf16[128,2048]{1,0:T(8,128)(2,1)} custom-call(s32[4]{0:T(128)S(1)} %pad_add_fusion.info, bf16[4,384,256]{2,1,0:T(8,128)(2,1)S(1)} %bitcast.26, bf16[8,4,32,2048]{3,2,1,0:T(8,128)(2,1)} %bitcast.43, bf16[512,2048]{1,0:T(8,128)(2,1)S(1)} %copy-done), custom_call_target="tpu_custom_call" | custom-call | flops 536870912 | bytes 4194304 | tf_op jit(solution)/shard_map/project/pallas_call | solution.py:215
  150.3 5.0 %project.6 = bf16[128,2048]{1,0:T(8,128)(2,1)} custom-call(s32[4]{0:T(128)S(1)} %pad_add_fusion.info, bf16[4,384,256]{2,1,0:T(8,128)(2,1)S(1)} %bitcast.27, bf16[8,4,32,2048]{3,2,1,0:T(8,128)(2,1)} %bitcast.44, bf16[512,2048]{1,0:T(8,128)(2,1)S(1)} %copy-done), custom_call_target="tpu_custom_call" | custom-call | flops 536870912 | bytes 4194304 | tf_op jit(solution)/shard_map/project/pallas_call | solution.py:215
  155.4 5.0 %project.7 = bf16[128,2048]{1,0:T(8,128)(2,1)} custom-call(s32[4]{0:T(128)S(1)} %pad_add_fusion.info, bf16[4,384,256]{2,1,0:T(8,128)(2,1)S(1)} %bitcast.28, bf16[8,4,32,2048]{3,2,1,0:T(8,128)(2,1)} %bitcast.45, bf16[512,2048]{1,0:T(8,128)(2,1)S(1)} %copy-done), custom_call_target="tpu_custom_call" | custom-call | flops 536870912 | bytes 4194304 | tf_op jit(solution)/shard_map/project/pallas_call | solution.py:215
  160.5 3.1 pad_maximum_fusion
  165.2 2.6 norm.4.refs_0_
  167.8 40.7 %all-gather.19.cloned.1.call-done = bf16[512,2048]{1,0:T(8,128)(2,1)} async-done(((bf16[128,2048]{1,0:T(8,128)(2,1)}), bf16[512,2048]{1,0:T(8,128)(2,1)}) %all-gather.19.cloned.1.call-update) | async-done | bytes 2097168 | tf_op jit(solution)/shard_map/all_gather | solution.py:352
  210.0 2.6 norm.5.refs_0_
  212.7 41.9 %all-gather.17.cloned.1.call-done = bf16[512,2048]{1,0:T(8,128)(2,1)} async-done(((bf16[128,2048]{1,0:T(8,128)(2,1)}), bf16[512,2048]{1,0:T(8,128)(2,1)}) %all-gather.17.cloned.1.call-update) | async-done | bytes 2097168 | tf_op jit(solution)/shard_map/all_gather | solution.py:352
  256.2 2.6 norm.6.refs_0_
  258.8 41.9 %all-gather.15.cloned.1.call-done = bf16[512,2048]{1,0:T(8,128)(2,1)} async-done(((bf16[128,2048]{1,0:T(8,128)(2,1)}), bf16[512,2048]{1,0:T(8,128)(2,1)}) %all-gather.15.cloned.1.call-update) | async-done | bytes 2097168 | tf_op jit(solution)/shard_map/all_gather | solution.py:352
  302.3 2.6 norm.7
  (64 shorter events, 28.5 us)
Async XLA Ops:
  7.2 35.0 %copy-start.6 = (bf16[1,1024,256]{2,1,0:T(8,128)(2,1)S(1)}, bf16[1,1024,256]{2,1,0:T(8,128)(2,1)}, u32[]{:S(2)}) copy-start(bf16[1,1024,256]{2,1,0:T(8,128)(2,1)} %param.10) | copy-start | bytes 1572868
  7.2 89.9 %all-gather.13.cloned.1.call-start = ((), (), s32[]{:S(2)}) async-start(), calls=%async_computation | async-start | bytes 4718592 | tf_op jit(solution)/shard_map/all_gather | solution.py:307
  25.6 9.7 %collective-permute-start.9 = (bf16[32,2048]{1,0:T(8,128)(2,1)}, bf16[32,2048]{1,0:T(8,128)(2,1)S(1)}, u32[]{:S(2)}, u32[]{:S(2)}) collective-permute-start(bf16[32,2048]{1,0:T(8,128)(2,1)} %get-tuple-element.11), channel_id=1, source_target_pairs={{0,4},{4,8},{8,12},{12,0},{1,5},{5,9},{9,13},{13,1},{2,6},{6,10},{... | collective-permute-start | bytes 393224 | tf_op jit(solution)/shard_map/ppermute | solution.py:303
  28.7 11.4 %collective-permute-start.10 = (bf16[32,2048]{1,0:T(8,128)(2,1)}, bf16[32,2048]{1,0:T(8,128)(2,1)S(1)}, u32[]{:S(2)}, u32[]{:S(2)}) collective-permute-start(bf16[32,2048]{1,0:T(8,128)(2,1)} %get-tuple-element.12), channel_id=1, source_target_pairs={{0,8},{4,12},{8,0},{12,4},{1,9},{5,13},{9,1},{13,5},{2,10},{6,14},... | collective-permute-start | bytes 393224 | tf_op jit(solution)/shard_map/ppermute | solution.py:303
  31.3 8.9 %collective-permute-start.11 = (bf16[32,2048]{1,0:T(8,128)(2,1)}, bf16[32,2048]{1,0:T(8,128)(2,1)S(1)}, u32[]{:S(2)}, u32[]{:S(2)}) collective-permute-start(bf16[32,2048]{1,0:T(8,128)(2,1)} %get-tuple-element.13), channel_id=1, source_target_pairs={{0,12},{4,0},{8,4},{12,8},{1,13},{5,1},{9,5},{13,9},{2,14},{6,2},{... | collective-permute-start | bytes 393224 | tf_op jit(solution)/shard_map/ppermute | solution.py:303
  40.1 57.0 %copy-start = (bf16[512,2048]{1,0:T(8,128)(2,1)S(1)}, bf16[512,2048]{1,0:T(8,128)(2,1)}, u32[]{:S(2)}) copy-start(bf16[512,2048]{1,0:T(8,128)(2,1)} %r_ref.7) | copy-start | bytes 6291460
  42.1 121.5 %all-gather.21.cloned.1.call-start = ((), (), s32[]{:S(2)}) async-start(), calls=%async_computation.4 | async-start | bytes 2621440 | tf_op jit(solution)/shard_map/all_gather | solution.py:352
  42.1 17.5 %collective-permute-start.4 = (bf16[1024,256]{1,0:T(8,128)(2,1)S(1)}, bf16[1024,256]{1,0:T(8,128)(2,1)S(1)}, u32[]{:S(2)}, u32[]{:S(2)}) collective-permute-start(bf16[1024,256]{1,0:T(8,128)(2,1)S(1)} %bitcast.38), channel_id=1, source_target_pairs={{0,2},{1,3},{2,0},{3,1},{4,6},{5,7},{6,4},{7,5},{8,10},{9,11},{10,... | collective-permute-start | bytes 1572872 | tf_op jit(solution)/shard_map/ppermute | solution.py:38
  43.7 32.0 %collective-permute-start.3 = (bf16[1024,256]{1,0:T(8,128)(2,1)S(1)}, bf16[1024,256]{1,0:T(8,128)(2,1)}, u32[]{:S(2)}, u32[]{:S(2)}) collective-permute-start(bf16[1024,256]{1,0:T(8,128)(2,1)S(1)} %bitcast.39), channel_id=1, source_target_pairs={{0,1},{1,0},{2,3},{3,2},{4,5},{5,4},{6,7},{7,6},{8,9},{9,8},{10,11... | collective-permute-start | bytes 1572872 | tf_op jit(solution)/shard_map/ppermute | solution.py:38
  48.5 18.7 %collective-permute-start.7 = (bf16[512,256]{1,0:T(8,128)(2,1)}, bf16[512,256]{1,0:T(8,128)(2,1)S(1)}, u32[]{:S(2)}, u32[]{:S(2)}) collective-permute-start(bf16[512,256]{1,0:T(8,128)(2,1)} %get-tuple-element.9.refs_4_), channel_id=1, source_target_pairs={{0,2},{1,3},{2,0},{3,1},{4,6},{5,7},{6,4},{7,5},{8,10},{9,11},{10,... | collective-permute-start | bytes 786440 | tf_op jit(solution)/shard_map/ppermute | solution.py:38
  59.6 16.1 %collective-permute-start.5 = (bf16[1024,256]{1,0:T(8,128)(2,1)S(1)}, bf16[1024,256]{1,0:T(8,128)(2,1)}, u32[]{:S(2)}, u32[]{:S(2)}) collective-permute-start(bf16[1024,256]{1,0:T(8,128)(2,1)S(1)} %collective-permute-done.4.refs_2_), channel_id=1, source_target_pairs={{0,1},{1,0},{2,3},{3,2},{4,5},{5,4},{6,7},{7,6},{8,9},{9,8},{10,11... | collective-permute-start | bytes 1572872 | tf_op jit(solution)/shard_map/ppermute | solution.py:38
  59.6 16.1 %collective-permute-start.6 = (bf16[512,256]{1,0:T(8,128)(2,1)}, bf16[512,256]{1,0:T(8,128)(2,1)}, u32[]{:S(2)}, u32[]{:S(2)}) collective-permute-start(bf16[512,256]{1,0:T(8,128)(2,1)} %get-tuple-element.9.refs_4_), channel_id=1, source_target_pairs={{0,1},{1,0},{2,3},{3,2},{4,5},{5,4},{6,7},{7,6},{8,9},{9,8},{10,11... | collective-permute-start | bytes 786440 | tf_op jit(solution)/shard_map/ppermute | solution.py:38
  67.2 8.5 %collective-permute-start.8 = (bf16[512,256]{1,0:T(8,128)(2,1)S(1)}, bf16[512,256]{1,0:T(8,128)(2,1)}, u32[]{:S(2)}, u32[]{:S(2)}) collective-permute-start(bf16[512,256]{1,0:T(8,128)(2,1)S(1)} %collective-permute-done.7.refs_6_), channel_id=1, source_target_pairs={{0,1},{1,0},{2,3},{3,2},{4,5},{5,4},{6,7},{7,6},{8,9},{9,8},{10,11... | collective-permute-start | bytes 786440 | tf_op jit(solution)/shard_map/ppermute | solution.py:38
  67.2 1.6 collective-permute-start
  68.8 3.6 %collective-permute-start.1 = (s32[1]{0:T(128)}, s32[1]{0:T(128)}, u32[]{:S(2)}, u32[]{:S(2)}) collective-permute-start(s32[1]{0:T(128)} %param.11), channel_id=1, source_target_pairs={{0,2},{1,3},{2,0},{3,1},{4,6},{5,7},{6,4},{7,5},{8,10},{9,11},{10,... | collective-permute-start | bytes 20 | tf_op jit(solution)/shard_map/ppermute | solution.py:38
  72.4 1.3 collective-permute-start.2
  102.1 106.3 %all-gather.19.cloned.1.call-start = ((), (), s32[]{:S(2)}) async-start(), calls=%async_computation.3 | async-start | bytes 2621440 | tf_op jit(solution)/shard_map/all_gather | solution.py:352
  150.3 104.3 %all-gather.17.cloned.1.call-start = ((), (), s32[]{:S(2)}) async-start(), calls=%async_computation.2 | async-start | bytes 2621440 | tf_op jit(solution)/shard_map/all_gather | solution.py:352
  155.4 145.3 %all-gather.15.cloned.1.call-start = ((), (), s32[]{:S(2)}) async-start(), calls=%async_computation.1 | async-start | bytes 2621440 | tf_op jit(solution)/shard_map/all_gather | solution.py:352
  160.5 3.1 %copy-start.5 = (f32[8192]{0:T(1024)S(1)}, f32[8192]{0:T(1024)}, u32[]{:S(2)}) copy-start(f32[8192]{0:T(1024)} %param.15) | copy-start | bytes 98308
  163.6 1.6 copy-start.1
  208.5 1.6 copy-start.2
  254.6 1.6 copy-start.3
  300.7 1.6 copy-start.4
  (6 other events, 5.5 us)
Sparse Core Ops, SparseCore 0:
  42.2 44.1 all-gather.12
  102.3 59.8 all-gather.20
  163.8 44.6 all-gather.18
  209.9 44.6 all-gather.16
  256.0 44.6 all-gather.14

commit v2 on v1

v2 whole, which is shorter than its diff:
```python
import functools
import math

import jax
import jax.numpy as jnp
from jax import lax
from jax.experimental import pallas as pl
from jax.experimental.pallas import tpu as pltpu
from jax.sharding import PartitionSpec as P

GROUP = 8
HD = 128
NEG = -1e30
EPS_NORM = 1e-05
VMEM_BYTES = 48 * 1024 * 1024
CHUNK = 128
KEY_BLOCK = 512
TAIL = 16
DIGIT = 32
PARAMS = pltpu.CompilerParams(vmem_limit_bytes=VMEM_BYTES)
ANYWHERE = pl.BlockSpec(memory_space=pl.ANY)


def frequencies(head_width):
    counter = jnp.arange(head_width // 2, dtype=jnp.float32)
    base_freq = jnp.exp(-(2.0 * counter / head_width) * math.log(500000.0))
    wavelength = 2.0 * math.pi / base_freq
    smoothing = (8192.0 / wavelength - 1.0) / 3.0
    blended = (1.0 - smoothing) * base_freq / 8.0 + smoothing * base_freq
    return jnp.where(
        wavelength < 2048.0, base_freq, jnp.where(wavelength > 8192.0, base_freq / 8.0, blended)
    )


def pieces_of(value, axis, count):
    if count & (count - 1) == 0:
        held = {0: value}
        bit = count // 2
        while bit:
            pairs = [(i, i ^ bit) for i in range(count)]
            for mask in sorted(held):
                held[mask | bit] = lax.ppermute(held[mask], axis, pairs)
            bit //= 2
        return [held[mask] for mask in range(count)]
    blocks = [value]
    for shift in range(1, count):
        pairs = [(i, (i + shift) % count) for i in range(count)]
        blocks.append(lax.ppermute(value, axis, pairs))
    return blocks


def owners_of(count, me):
    if count & (count - 1) == 0:
        return [me ^ mask for mask in range(count)]
    return [(me + count - shift) % count for shift in range(count)]


def line_gather(value, count):
    if count != 4:
        return [lax.all_gather(value, "tensor", axis=0, tiled=False)]
    up = lax.ppermute(value, "tensor", [(0, 1), (1, 2), (2, 3)])
    down = lax.ppermute(value, "tensor", [(1, 0), (2, 1), (3, 2)])
    far = lax.ppermute(value, "tensor", [(0, 2), (1, 3), (2, 0), (3, 1)])
    last = lax.ppermute(far, "tensor", [(1, 0), (2, 3)])
    return [value, up, down, far, last]


class Table:
    def __init__(self, contexts, count):
        self.contexts, self.count = contexts, count
        self.owner = 1
        self.place = 1 + contexts
        self.low = self.place + count
        self.high = self.low + 1
        self.share = self.low + 2


def line_read(table, info, refs, d, cols=slice(None)):
    if len(refs) == 1:
        return refs[0][info[table.place + d], :, cols].astype(jnp.float32)
    if d == 0:
        return refs[0][:, cols].astype(jnp.float32)
    if d == 2:
        return refs[3][:, cols].astype(jnp.float32)
    near = refs[1 if d == 1 else 2][:, cols].astype(jnp.float32)
    other = refs[4][:, cols].astype(jnp.float32)
    at_end = info[table.low if d == 1 else table.high]
    return jnp.where(at_end == 1, other, near)


def line_spec(blocks, rows, index):
    if len(blocks) == 1:
        count, _, width = blocks[0].shape
        return [pl.BlockSpec((count, rows, width), lambda i, info: (0, index(i), 0))]
    width = blocks[0].shape[1]
    return [pl.BlockSpec((rows, width), lambda i, info: (index(i), 0)) for _ in blocks]


def call(kernel, name, info, args, in_specs, out_specs, out_shape, grid=(1,), aliases=None,
         scratch=(), flops=0, transcendentals=0):
    size = sum(math.prod(a.shape) * a.dtype.itemsize for a in args)
    return pl.pallas_call(
        kernel,
        grid_spec=pltpu.PrefetchScalarGridSpec(
            num_scalar_prefetch=1,
            grid=grid,
            in_specs=in_specs,
            out_specs=out_specs,
            scratch_shapes=list(scratch),
        ),
        out_shape=out_shape,
        input_output_aliases=aliases or {},
        compiler_params=PARAMS,
        cost_estimate=pl.CostEstimate(
            flops=flops, bytes_accessed=size, transcendentals=transcendentals
        ),
        name=name,
    )(info, *args)


def whole(a):
    zeros = (0,) * len(a.shape)
    return pl.BlockSpec(tuple(a.shape), lambda i, info: zeros)


def cut_kernel(table, slab, keep, info, w_ref, *outs):
    for d, out in enumerate(outs):
        target = lax.rem(info[table.place] + d, table.count)
        start = pl.multiple_of(target * slab, slab)
        out[:, :keep] = w_ref[:, pl.ds(start, keep)]
        for j in range(table.count if keep < slab else 0):
            raw = slab - keep
            out[:, keep + j * raw : keep + (j + 1) * raw] = w_ref[
                :, j * slab + keep : (j + 1) * slab
            ]


def cut(table, info, out_weight, part, slab, keep):
    width = keep + table.count * (slab - keep)
    shape = jax.ShapeDtypeStruct((part, width), out_weight.dtype)
    return call(
        functools.partial(cut_kernel, table, slab, keep),
        "cut",
        info,
        [out_weight],
        [pl.BlockSpec((part, out_weight.shape[1]), lambda i, info: (info[table.share], 0))],
        [whole(shape)] * table.count,
        [shape] * table.count,
    )


def stack_kernel(count, begin, info, *refs):
    parts, outs = refs[:count], refs[-1]
    for number, part in enumerate(parts):
        outs[number] = part[:, begin : begin + outs.shape[2]]


def stack_raw_kernel(count, begin, raw, info, *refs):
    stack_kernel(count, begin, info, *refs[:count], refs[-2])
    refs[-1][...] = refs[count][...]


def stack(info, parts, begin, width, after=None, residual=None, raw=0):
    count, part = len(parts), parts[0].shape[0]
    shape = jax.ShapeDtypeStruct((count, part, width), parts[0].dtype)
    specs = [whole(p) for p in parts]
    if residual is not None:
        rows, slab = residual.shape
        out = jax.ShapeDtypeStruct((rows, raw), residual.dtype)
        return call(
            functools.partial(stack_raw_kernel, count, begin, raw),
            "stack",
            info,
            [*parts, residual],
            specs + [pl.BlockSpec((rows, raw), lambda i, info: (0, slab // raw - 1))],
            [whole(shape), whole(out)],
            [shape, out],
        )
    extra = [] if after is None else [after]
    return call(
        functools.partial(stack_kernel, count, begin),
        "stack",
        info,
        [*parts, *extra],
        specs + [ANYWHERE] * len(extra),
        whole(shape),
        shape,
    )


def rotate_kernel(info, q_ref, kv_ref, cos_ref, sin_ref, length_ref, q_out, kv_out):
    cosine, sine = cos_ref[...], sin_ref[...]
    rows = q_ref.shape[0]

    def turn(block):
        block = block.astype(jnp.float32)
        return (block * cosine + pltpu.roll(block, HD // 2, 1) * sine).astype(jnp.bfloat16)

    kv_out[:rows, :HD] = turn(kv_ref[:, :HD])
    kv_out[:rows, HD:] = kv_ref[:, HD:]
    length = length_ref[0]
    upper = lax.div(length, DIGIT)
    lower = length - upper * DIGIT
    kv_out[rows:, :HD] = jnp.full((TAIL, HD), upper.astype(jnp.float32)).astype(jnp.bfloat16)
    kv_out[rows:, HD:] = jnp.full((TAIL, HD), lower.astype(jnp.float32)).astype(jnp.bfloat16)
    for head in range(q_ref.shape[1] // HD):
        cols = slice(head * HD, (head + 1) * HD)
        q_out[:, cols] = turn(q_ref[:, cols])


def rotate_all(info, queries, span_pairs, cosine, sine, lengths):
    rows = queries.shape[0]
    pairs = jax.ShapeDtypeStruct((rows + TAIL, 2 * HD), jnp.bfloat16)
    turned = jax.ShapeDtypeStruct(queries.shape, jnp.bfloat16)
    return call(
        rotate_kernel,
        "rotate",
        info,
        [queries, span_pairs, cosine, sine, lengths],
        [whole(a) for a in (queries, span_pairs, cosine, sine)]
        + [pl.BlockSpec(memory_space=pltpu.SMEM)],
        [whole(turned), whole(pairs)],
        [turned, pairs],
    )


def attend_kernel(table, info, q_ref, *refs):
    count = table.contexts
    caches, spans = refs[:count], refs[count : 2 * count]
    out_ref, s_ref = refs[2 * count], refs[2 * count + 1]
    rows = q_ref.shape[0]
    heads = q_ref.shape[1] // HD
    chunk = pl.program_id(0)
    mine = info[0]
    q = jnp.concatenate([q_ref[:, h * HD : (h + 1) * HD] for h in range(heads)], axis=0)
    exponent = math.log2(math.e) / math.sqrt(HD)

    blocks = []
    peak = jnp.full((heads * rows, HD), NEG, jnp.float32)
    column = 0
    for kind, group in (("cache", caches), ("span", spans)):
        for number, ref in enumerate(group):
            keys = ref.shape[0] if kind == "cache" else ref.shape[0] - TAIL
            width = min(KEY_BLOCK, keys)
            tail = spans[number]
            tail_row = tail.shape[0] - TAIL
            length = tail[tail_row : tail_row + 1, :HD].astype(jnp.float32) * DIGIT + tail[
                tail_row : tail_row + 1, HD:
            ].astype(jnp.float32)
            length = jnp.concatenate([length] * (width // HD), axis=1)
            for begin in range(0, keys, width):
                scores = lax.dot_general(
                    q,
                    ref[begin : begin + width, :HD],
                    (((1,), (1,)), ((), ())),
                    preferred_element_type=jnp.float32,
                )
                if kind == "cache":
                    slot = lax.broadcasted_iota(jnp.int32, (1, width), 1) + begin
                    live = slot.astype(jnp.float32) < length
                    scores = scores + jnp.where(live, 0.0, NEG)
                elif number == 0:
                    key = lax.broadcasted_iota(jnp.int32, (rows, width), 1) + begin
                    row = lax.broadcasted_iota(jnp.int32, (rows, width), 0) + chunk * rows
                    bias = jnp.where(key <= row, 0.0, NEG)
                    scores = scores + jnp.concatenate([bias] * heads, axis=0)
                else:
                    scores = scores + jnp.where(info[table.owner + number] < mine, 0.0, NEG)
                s_ref[:, column : column + width] = scores
                for lane in range(0, width, HD):
                    peak = jnp.maximum(peak, scores[:, lane : lane + HD])
                blocks.append((ref, begin, column, width))
                column += width
    top = jnp.max(peak, axis=1, keepdims=True)
    total = jnp.zeros((heads * rows, HD), jnp.float32)
    mixed = jnp.zeros((heads * rows, HD), jnp.float32)
    for ref, begin, column, width in blocks:
        weights = jnp.exp2((s_ref[:, column : column + width] - top) * exponent)
        for lane in range(0, width, HD):
            total = total + weights[:, lane : lane + HD]
        mixed = mixed + jnp.dot(
            weights.astype(jnp.bfloat16),
            ref[begin : begin + width, HD:],
            preferred_element_type=jnp.float32,
        )
    result = (mixed / jnp.sum(total, axis=1, keepdims=True)).astype(jnp.bfloat16)
    for h in range(heads):
        out_ref[:, h * HD : (h + 1) * HD] = result[h * rows : (h + 1) * rows]


def attend(table, info, queries, caches, spans, rows):
    all_rows, width = queries.shape
    heads = width // HD
    keys = sum(a.shape[0] for a in caches) + sum(a.shape[0] - TAIL for a in spans)
    chunk_spec = pl.BlockSpec((rows, width), lambda i, info: (i, 0))
    return call(
        functools.partial(attend_kernel, table),
        "attend",
        info,
        [queries, *caches, *spans],
        [chunk_spec] + [whole(a) for a in caches] + [whole(a) for a in spans],
        chunk_spec,
        jax.ShapeDtypeStruct((all_rows, width), jnp.bfloat16),
        grid=(all_rows // rows,),
        scratch=[pltpu.VMEM((heads * rows, keys), jnp.float32)],
        flops=4 * all_rows * heads * keys * HD,
        transcendentals=all_rows * heads * keys,
    )


def project_kernel(table, lines, keep, info, *refs):
    count = table.count
    attention = refs[:lines]
    w_ref, r_ref = refs[lines], refs[lines + 1]
    parts, h_ref = refs[lines + 2 : -1], refs[-1]
    total = r_ref[:, :keep].astype(jnp.float32)
    for d in range(count):
        block = line_read(table, info, attention, d).astype(jnp.bfloat16)
        weight = w_ref[:, d].reshape(block.shape[1], keep)
        total = total + jnp.dot(block, weight, preferred_element_type=jnp.float32)
    result = total.astype(jnp.bfloat16)
    h_ref[:, :keep] = result
    for number, part in enumerate(parts):

        @pl.when(pl.program_id(0) == number)
        def _():
            part[...] = result


def project(table, info, attention, weights, residual, rows):
    all_rows, slab = residual.shape
    keep = weights.shape[3]
    chunks = all_rows // rows
    part = jax.ShapeDtypeStruct((rows, keep), jnp.bfloat16)
    hidden = jax.ShapeDtypeStruct(residual.shape, jnp.bfloat16)
    row_spec = pl.BlockSpec((rows, slab), lambda i, info: (i, 0))
    return call(
        functools.partial(project_kernel, table, len(attention), keep),
        "project",
        info,
        [*attention, weights, residual],
        line_spec(attention, rows, lambda i: i) + [whole(weights), row_spec],
        [whole(part)] * chunks + [row_spec],
        [part] * chunks + [hidden],
        grid=(chunks,),
        flops=2 * all_rows * math.prod(weights.shape),
    )


def project_raw_kernel(table, lines, raw_lines, info, *refs):
    count = table.count
    attention, residuals = refs[:lines], refs[lines : lines + raw_lines]
    w_ref = refs[lines + raw_lines]
    raw_ref, h_ref = refs[-2:]
    raw = h_ref.shape[1]
    blocks = [
        line_read(table, info, attention, d).astype(jnp.bfloat16) for d in range(count)
    ]
    for slab in range(count):
        start = pl.multiple_of(info[table.place + slab] * raw, raw)
        total = line_read(table, info, residuals, slab)
        for d in range(count):
            weight = w_ref[:, d, :, pl.ds(start, raw)].reshape(blocks[d].shape[1], raw)
            total = total + jnp.dot(blocks[d], weight, preferred_element_type=jnp.float32)
        result = total.astype(jnp.bfloat16)
        raw_ref[:, slab * raw : (slab + 1) * raw] = result
        if slab == 0:
            h_ref[...] = result


def project_raw(table, info, attention, residuals, weights, hidden, raw, rows):
    all_rows, slab = hidden.shape
    args = [*attention, *residuals, weights, hidden]
    out = jax.ShapeDtypeStruct((all_rows, table.count * raw), jnp.bfloat16)
    return call(
        functools.partial(project_raw_kernel, table, len(attention), len(residuals)),
        "project_raw",
        info,
        args,
        line_spec(attention, rows, lambda i: i)
        + line_spec(residuals, rows, lambda i: i)
        + [whole(weights), ANYWHERE],
        [
            pl.BlockSpec((rows, table.count * raw), lambda i, info: (i, 0)),
            pl.BlockSpec((rows, raw), lambda i, info: (i, slab // raw - 1)),
        ],
        [out, jax.ShapeDtypeStruct(hidden.shape, jnp.bfloat16)],
        grid=(all_rows // rows,),
        aliases={len(args): 1},
        flops=2 * all_rows * math.prod(weights.shape),
    )


def norm_kernel(table, lines, keep, slab, info, g_ref, *refs):
    count = table.count
    blocks, out_ref = refs[:lines], refs[-1]
    raw = slab - keep
    values = []
    squares = jnp.zeros((out_ref.shape[0], 1), jnp.float32)

    def read(d):
        found = [(0, keep, line_read(table, info, blocks, d))]
        if raw:
            cols = slice(d * raw, (d + 1) * raw)
            found.append((keep, raw, refs[lines][:, cols].astype(jnp.float32)))
        return found

    for d in range(count):
        for _, _, value in read(d):
            squares = squares + jnp.sum(value * value, axis=1, keepdims=True)
    inverse = lax.rsqrt(squares / (count * slab) + EPS_NORM)
    for d in range(count):
        for offset, width, value in read(d):
            start = pl.multiple_of(info[table.place + d] * slab + offset, HD)
            cols = pl.ds(start, width)
            out_ref[:, cols] = (value * inverse * g_ref[:, cols]).astype(jnp.bfloat16)


def norm_into(table, info, buffer, blocks, raw_hidden, gain, chunk, rows, keep, slab, total_rows):
    width = table.count * slab
    step = min(rows, 32)
    steps = rows // step
    args = [gain.reshape(1, width), *blocks]
    in_specs = [pl.BlockSpec((1, width), lambda i, info: (0, 0))]
    in_specs += line_spec(blocks, step, lambda i: i)
    if raw_hidden is not None:
        args.append(raw_hidden)
        in_specs.append(
            pl.BlockSpec((step, raw_hidden.shape[1]), lambda i, info: (chunk * steps + i, 0))
        )
    aliases = {}
    if buffer is not None:
        args.append(buffer)
        in_specs.append(ANYWHERE)
        aliases = {len(args): 0}
    return call(
        functools.partial(norm_kernel, table, len(blocks), keep, slab),
        "norm",
        info,
        args,
        in_specs,
        pl.BlockSpec((step, width), lambda i, info: (chunk * steps + i, 0)),
        jax.ShapeDtypeStruct((total_rows, width), jnp.bfloat16),
        grid=(steps,),
        aliases=aliases,
        flops=6 * rows * width,
    )


def per_device(queries, span_kv, cache, lengths, offset, out_weight, residual, gain):
    rows = queries.shape[0]
    heads = queries.shape[1] // HD
    depth = out_weight.shape[0]
    slab = residual.shape[1]
    contexts = lax.axis_size("context")
    count = lax.axis_size("tensor")
    context_index = lax.axis_index("context")
    tensor_index = lax.axis_index("tensor")
    kv_index = tensor_index * heads // GROUP
    shares = lax.axis_size("groups") * contexts
    share = lax.axis_index("groups") * contexts + context_index
    raw = slab // 4 if slab % 512 == 0 else 0
    keep = slab - raw
    chunk = min(CHUNK, rows)
    chunks = rows // chunk

    table = Table(contexts, count)
    steering = [context_index, *owners_of(contexts, context_index)]
    steering += [lax.rem(tensor_index + (count - d), count) for d in range(count)]
    steering += [tensor_index == 0, tensor_index == count - 1, share]
    info = jnp.stack([jnp.asarray(v).astype(jnp.int32) for v in steering])

    cache_local = lax.dynamic_index_in_dim(cache, kv_index, 0, keepdims=False)
    caches = pieces_of(cache_local, "context", contexts)
    span_local = lax.dynamic_index_in_dim(span_kv, kv_index, 1, keepdims=False)
    positions = offset[0] + context_index * rows + jnp.arange(rows, dtype=jnp.int32)
    both = jnp.concatenate([frequencies(HD)] * 2)
    angles = positions.astype(jnp.float32)[:, None] * both[None, :]
    sign = jnp.where(jnp.arange(HD) < HD // 2, -1.0, 1.0)
    q_turned, span_turned = rotate_all(
        info, queries, span_local, jnp.cos(angles), jnp.sin(angles) * sign[None, :], lengths
    )
    spans = pieces_of(span_turned, "context", contexts)

    cuts = cut(table, info, out_weight, depth // shares, slab, keep)
    parts = [cuts[0]]
    for shift in range(1, count):
        pairs = [(i, (i + shift) % count) for i in range(count)]
        parts.append(lax.ppermute(cuts[shift], "tensor", pairs))
    plane = ("groups", "context")
    if raw:
        own_weights, residual_raw = stack(info, parts, 0, keep, residual=residual, raw=raw)
        residuals = line_gather(residual_raw, count)
    else:
        own_weights = stack(info, parts, 0, keep)
    own_weights = lax.all_gather(own_weights, plane, axis=0, tiled=False)

    mixed = attend(table, info, q_turned, caches, spans, chunk)
    attention = line_gather(mixed, count)

    *hidden_parts, hidden = project(table, info, attention, own_weights, residual, chunk)
    raw_hidden = None
    if raw:
        raw_weights = stack(info, parts, keep, count * raw, after=mixed)
        raw_weights = lax.all_gather(raw_weights, plane, axis=0, tiled=False)
        raw_hidden, hidden = project_raw(
            table, info, attention, residuals, raw_weights, hidden, raw, chunk
        )
    normed = None
    for number in range(chunks):
        blocks = line_gather(hidden_parts[number], count)
        normed = norm_into(
            table, info, normed, blocks, raw_hidden, gain, number, chunk, keep, slab, rows
        )
    return (hidden, normed)


def solution(mesh):
    in_specs = (
        P(("groups", "context"), "tensor"),
        P(("groups", "context"), None, None),
        P("groups", "context", None),
        P(("groups", "context")),
        P("groups"),
        P("tensor", None),
        P(("groups", "context"), "tensor"),
        P(),
    )
    out_specs = (P(("groups", "context"), "tensor"), P(("groups", "context"), None))
    return jax.shard_map(
        per_device, mesh=mesh, in_specs=in_specs, out_specs=out_specs, check_vma=False
    )
```

time: 312 us -> 280 us (0.90)
  starting transfers between devices: 11.8 us -> 75.4 us
  blocking collectives: 43.6 us -> 0 us
  waiting for transfers between devices: 153 us -> 125 us
  Pallas kernels: 65.7 us -> 47 us
  other arithmetic: 7.08 us -> 1.1 us
    all_gather x5 -> x2, waiting for transfers between devices: 124 us -> 0.04 us  [the longest x1 0.02 us: per_device(): raw_weights = lax.all_gather(raw_weights, plane, axis=0, tiled=False)]
    ppermute x3 -> x27, waiting for transfers between devices: 7.51 us -> 105 us  [the longest x6 68.5 us: line_gather(): far = lax.ppermute(value, 'tensor', [(0, 2), (1, 3), (2, 0), (3, 1)])]
    ppermute x3 -> x27, starting transfers between devices: 7.01 us -> 72.7 us  [the longest x6 26.1 us: line_gather(): up = lax.ppermute(value, 'tensor', [(0, 1), (1, 2), (2, 3)])]
    all_gather x2 -> x0, blocking collectives: 43.6 us -> none  [the longest x1 29.7 us: per_device(): lax.all_gather(attend(info, q_turned, caches, spans, 1, chunks - 1, chunk...]
    pallas_call x12 -> x11, Pallas kernels: 65.7 us -> 47 us  [call(): pl.pallas_call(kernel, grid_spec=pltpu.PrefetchScalarGridSpec(num_scalar_...]
    concatenate x2 -> x0, other arithmetic: 4.07 us -> none  [the longest x1 3.09 us: per_device(): return (jnp.concatenate(hidden_parts, axis=0), normed)]
    unnamed x26 -> x62, local copies, waits for them, and re-layouts: 11.8 us -> 14.3 us
    ppermute x9 -> x6, waiting for transfers between devices: 21.5 us -> 19.7 us  [pieces_of(): held[mask | bit] = lax.ppermute(held[mask], axis, pairs)]
  transfers between devices with their start and end apart: 17 -> 35, of which waited for: 10 -> 14; matrix products, arithmetic and copies ran while one was open for 2% -> 0% of each run, Pallas kernels for 13% -> 15%
where the time goes in v2:
time: 280 us; the launch traced here: 279 us
  waiting for transfers between devices  125 us (45%)
  starting transfers between devices  75.4 us (27%)
  Pallas kernels  47 us (17%)
  between operations  15.8 us (6%)
  local copies, waits for them, and re-layouts  14.4 us (5%)
    ppermute x6, waiting for transfers between devices, line_gather(): far = lax.ppermute(value, 'tensor', [(0, 2), (1, 3), (2, 0), (3, 1)])  68.5 us
    pallas_call x11, Pallas kernels, call(): pl.pallas_call(kernel, grid_spec=pltpu.PrefetchScalarGridSpec(num_scalar_...  47 us
    ppermute x6, starting transfers between devices, line_gather(): up = lax.ppermute(value, 'tensor', [(0, 1), (1, 2), (2, 3)])  26.1 us
    ppermute x6, starting transfers between devices, line_gather(): far = lax.ppermute(value, 'tensor', [(0, 2), (1, 3), (2, 0), (3, 1)])  24.2 us
    ppermute x6, waiting for transfers between devices, line_gather(): last = lax.ppermute(far, 'tensor', [(1, 0), (2, 3)])  20.1 us
    ppermute x6, waiting for transfers between devices, pieces_of(): held[mask | bit] = lax.ppermute(held[mask], axis, pairs)  19.7 us
    unnamed x62, local copies, waits for them, and re-layouts  14.3 us
    ppermute x3, waiting for transfers between devices, per_device(): parts.append(lax.ppermute(cuts[shift], 'tensor', pairs))  13.7 us
  transfers between devices with their start and end apart: 35, of which 14 were waited for; matrix products, arithmetic and copies ran while one was open for 0% of the time, Pallas kernels for 15%

profile of v2, /device:TPU:0, one launch (start us, length us, event | category | flops | bytes accessed | tf_op | source)
XLA Modules:
  0.0 278.9 jit_solution(6590254174335322058)
XLA Ops:
  17.3 4.7 %collective-permute-done.10.refs_1_ = bf16[32,3584]{1,0:T(8,128)(2,1)S(1)} collective-permute-done((bf16[32,3584]{1,0:T(8,128)(2,1)S(1)}, bf16[32,3584]{1,0:T(8,128)(2,1)S(1)}, u32[]{:S(2)}, u32[]{:S(2)}) %collective-permute-start.10) | collective-permute-done | bytes 229408 | tf_op jit(solution)/shard_map/ppermute | solution.py:489
  21.9 9.0 %collective-permute-done.11.refs_2_ = bf16[32,3584]{1,0:T(8,128)(2,1)S(1)} collective-permute-done((bf16[32,3584]{1,0:T(8,128)(2,1)S(1)}, bf16[32,3584]{1,0:T(8,128)(2,1)S(1)}, u32[]{:S(2)}, u32[]{:S(2)}) %collective-permute-start.11) | collective-permute-done | bytes 229408 | tf_op jit(solution)/shard_map/ppermute | solution.py:489
  38.6 10.6 %collective-permute-done.1.refs_2_ = bf16[1024,256]{1,0:T(8,128)(2,1)} collective-permute-done((bf16[1024,256]{1,0:T(8,128)(2,1)}, bf16[1024,256]{1,0:T(8,128)(2,1)}, u32[]{:S(2)}, u32[]{:S(2)}) %collective-permute-start.1) | collective-permute-done | bytes 524320 | tf_op jit(solution)/shard_map/ppermute | solution.py:42
  49.7 7.5 %collective-permute-done.4.refs_6_ = bf16[528,256]{1,0:T(8,128)(2,1)S(1)} collective-permute-done((bf16[528,256]{1,0:T(8,128)(2,1)S(1)}, bf16[528,256]{1,0:T(8,128)(2,1)S(1)}, u32[]{:S(2)}, u32[]{:S(2)}) %collective-permute-start.4) | collective-permute-done | bytes 270368 | tf_op jit(solution)/shard_map/ppermute | solution.py:42
  59.8 13.3 %attend.1.refs_4_.refs_0_ = bf16[512,256]{1,0:T(8,128)(2,1)S(1)} custom-call(s32[12]{0:T(128)S(1)} %stack.58.info, bf16[512,256]{1,0:T(8,128)(2,1)S(1)} %get-tuple-element.17.q_ref, bf16[1024,256]{1,0:T(8,128)(2,1)S(1)} %bitcast.25, bf16[1024,256]{1,0:T(8,128)(2,1)S(1)} %collective-permute-done.refs_1_, bf16[1024,256]{1,0:T(8,128)(2,1)} %collective-permute-done.1.refs_2_, ...), custom_call_target="tpu_custom_call" | custom-call | flops 3221225472 | bytes 3440640 | tf_op jit(solution)/shard_map/attend/pallas_call | solution.py:102
  79.1 6.2 %collective-permute-start.6 = (bf16[512,256]{1,0:T(8,128)(2,1)S(1)}, bf16[512,256]{1,0:T(8,128)(2,1)S(1)}, u32[]{:S(2)}, u32[]{:S(2)}) collective-permute-start(bf16[512,256]{1,0:T(8,128)(2,1)S(1)} %attend.1.refs_4_.refs_0_), channel_id=1, source_target_pairs={{0,4},{4,8},{8,12},{1,5},{5,9},{9,13},{2,6},{6,10},{10,14},{3,7},{... | collective-permute-start | bytes 786440 | tf_op jit(solution)/shard_map/ppermute | solution.py:61
  86.5 27.8 %collective-permute-done.8.refs_3_ = bf16[512,256]{1,0:T(8,128)(2,1)S(1)} collective-permute-done((bf16[512,256]{1,0:T(8,128)(2,1)S(1)}, bf16[512,256]{1,0:T(8,128)(2,1)S(1)}, u32[]{:S(2)}, u32[]{:S(2)}) %collective-permute-start.8) | collective-permute-done | bytes 262176 | tf_op jit(solution)/shard_map/ppermute | solution.py:63
  115.7 5.4 %collective-permute-start.13 = (bf16[512,512]{1,0:T(8,128)(2,1)}, bf16[512,512]{1,0:T(8,128)(2,1)}, u32[]{:S(2)}, u32[]{:S(2)}) collective-permute-start(bf16[512,512]{1,0:T(8,128)(2,1)} %copy-done.3), channel_id=1, source_target_pairs={{0,4},{4,8},{8,12},{1,5},{5,9},{9,13},{2,6},{6,10},{10,14},{3,7},{... | collective-permute-start | bytes 1572872 | tf_op jit(solution)/shard_map/ppermute | solution.py:61
  123.7 6.2 %project.1 = (bf16[128,1536]{1,0:T(8,128)(2,1)S(1)}, bf16[128,1536]{1,0:T(8,128)(2,1)S(1)}, bf16[128,1536]{1,0:T(8,128)(2,1)}, bf16[128,1536]{1,0:T(8,128)(2,1)}, bf16[512,2048]{1,0:T(8,128)(2,1)}) custom-call(s32[12]{0:T(128)S(1)} %stack.58.info, bf16[512,256]{1,0:T(8,128)(2,1)S(1)} %attend.1.refs_4_.refs_0_, ...), custom_call_target="tpu_custom_call" | custom-call | flops 1610612736 | bytes 6553600 | tf_op jit(solution)/shard_map/project/pallas_call | solution.py:102
  129.9 5.7 %collective-permute-start.31 = (bf16[128,1536]{1,0:T(8,128)(2,1)S(1)}, bf16[128,1536]{1,0:T(8,128)(2,1)S(1)}, u32[]{:S(2)}, u32[]{:S(2)}) collective-permute-start(bf16[128,1536]{1,0:T(8,128)(2,1)S(1)} %get-tuple-element.31.refs_0_), channel_id=1, source_target_pairs={{0,8},{4,12},{8,0},{12,4},{1,9},{5,13},{9,1},{13,5},{2,10},{6,14},... | collective-permute-start | bytes 1179656 | tf_op jit(solution)/shard_map/ppermute | solution.py:63
  139.3 7.5 %collective-permute-start.27 = (bf16[128,1536]{1,0:T(8,128)(2,1)S(1)}, bf16[128,1536]{1,0:T(8,128)(2,1)S(1)}, u32[]{:S(2)}, u32[]{:S(2)}) collective-permute-start(bf16[128,1536]{1,0:T(8,128)(2,1)S(1)} %get-tuple-element.30.refs_0_), channel_id=1, source_target_pairs={{0,8},{4,12},{8,0},{12,4},{1,9},{5,13},{9,1},{13,5},{2,10},{6,14},... | collective-permute-start | bytes 1179656 | tf_op jit(solution)/shard_map/ppermute | solution.py:63
  146.8 10.1 %collective-permute-done.16.refs_9_ = bf16[512,512]{1,0:T(8,128)(2,1)} collective-permute-done((bf16[512,512]{1,0:T(8,128)(2,1)}, bf16[512,512]{1,0:T(8,128)(2,1)}, u32[]{:S(2)}, u32[]{:S(2)}) %collective-permute-start.16) | collective-permute-done | bytes 524320 | tf_op jit(solution)/shard_map/ppermute | solution.py:64
  158.4 5.8 %collective-permute-done.31.refs_3_ = bf16[128,1536]{1,0:T(8,128)(2,1)S(1)} collective-permute-done((bf16[128,1536]{1,0:T(8,128)(2,1)S(1)}, bf16[128,1536]{1,0:T(8,128)(2,1)S(1)}, u32[]{:S(2)}, u32[]{:S(2)}) %collective-permute-start.31) | collective-permute-done | bytes 393248 | tf_op jit(solution)/shard_map/ppermute | solution.py:63
  167.0 6.3 %collective-permute-start.23 = (bf16[128,1536]{1,0:T(8,128)(2,1)}, bf16[128,1536]{1,0:T(8,128)(2,1)}, u32[]{:S(2)}, u32[]{:S(2)}) collective-permute-start(bf16[128,1536]{1,0:T(8,128)(2,1)} %get-tuple-element.29.refs_0_), channel_id=1, source_target_pairs={{0,8},{4,12},{8,0},{12,4},{1,9},{5,13},{9,1},{13,5},{2,10},{6,14},... | collective-permute-start | bytes 1179656 | tf_op jit(solution)/shard_map/ppermute | solution.py:63
  174.1 5.4 %collective-permute-start.21 = (bf16[128,1536]{1,0:T(8,128)(2,1)}, bf16[128,1536]{1,0:T(8,128)(2,1)S(1)}, u32[]{:S(2)}, u32[]{:S(2)}) collective-permute-start(bf16[128,1536]{1,0:T(8,128)(2,1)} %get-tuple-element.29.refs_0_), channel_id=1, source_target_pairs={{0,4},{4,8},{8,12},{1,5},{5,9},{9,13},{2,6},{6,10},{10,14},{3,7},{... | collective-permute-start | bytes 1179656 | tf_op jit(solution)/shard_map/ppermute | solution.py:61
  179.5 18.4 %collective-permute-done.27.refs_3_ = bf16[128,1536]{1,0:T(8,128)(2,1)S(1)} collective-permute-done((bf16[128,1536]{1,0:T(8,128)(2,1)S(1)}, bf16[128,1536]{1,0:T(8,128)(2,1)S(1)}, u32[]{:S(2)}, u32[]{:S(2)}) %collective-permute-start.27) | collective-permute-done | bytes 393248 | tf_op jit(solution)/shard_map/ppermute | solution.py:63
  203.5 11.5 %collective-permute-done.23.refs_3_ = bf16[128,1536]{1,0:T(8,128)(2,1)} collective-permute-done((bf16[128,1536]{1,0:T(8,128)(2,1)}, bf16[128,1536]{1,0:T(8,128)(2,1)}, u32[]{:S(2)}, u32[]{:S(2)}) %collective-permute-start.23) | collective-permute-done | bytes 393248 | tf_op jit(solution)/shard_map/ppermute | solution.py:63
  218.3 5.0 %collective-permute-done.19.refs_3_ = bf16[128,1536]{1,0:T(8,128)(2,1)} collective-permute-done((bf16[128,1536]{1,0:T(8,128)(2,1)}, bf16[128,1536]{1,0:T(8,128)(2,1)}, u32[]{:S(2)}, u32[]{:S(2)}) %collective-permute-start.19) | collective-permute-done | bytes 393248 | tf_op jit(solution)/shard_map/ppermute | solution.py:63
  223.3 6.1 %collective-permute-start.17 = (bf16[128,1536]{1,0:T(8,128)(2,1)}, bf16[128,1536]{1,0:T(8,128)(2,1)}, u32[]{:S(2)}, u32[]{:S(2)}) collective-permute-start(bf16[128,1536]{1,0:T(8,128)(2,1)} %get-tuple-element.27.refs_0_), channel_id=1, source_target_pairs={{0,4},{4,8},{8,12},{1,5},{5,9},{9,13},{2,6},{6,10},{10,14},{3,7},{... | collective-permute-start | bytes 1179656 | tf_op jit(solution)/shard_map/ppermute | solution.py:61
  231.5 4.5 %collective-permute-done.28.refs_4_ = bf16[128,1536]{1,0:T(8,128)(2,1)S(1)} collective-permute-done((bf16[128,1536]{1,0:T(8,128)(2,1)S(1)}, bf16[128,1536]{1,0:T(8,128)(2,1)S(1)}, u32[]{:S(2)}, u32[]{:S(2)}) %collective-permute-start.28) | collective-permute-done | bytes 393248 | tf_op jit(solution)/shard_map/ppermute | solution.py:64
  239.2 7.1 %project_raw.1 = (bf16[512,2048]{1,0:T(8,128)(2,1)S(1)}, bf16[512,2048]{1,0:T(8,128)(2,1)}) custom-call(s32[12]{0:T(128)S(1)} %stack.58.info, bf16[512,256]{1,0:T(8,128)(2,1)S(1)} %attend.1.refs_4_.refs_0_, bf16[512,256]{1,0:T(8,128)(2,1)S(1)} %collective-permute-done.6.refs_1_, ...), custom_call_target="tpu_custom_call", output_to_operand_aliasing={{1}: (12, {})} | custom-call | flops 2147483648 | bytes 10223616 | tf_op jit(solution)/shard_map/project_raw/pallas_call | solution.py:102
  253.3 5.1 %norm.6.refs_6_ = bf16[512,8192]{1,0:T(8,128)(2,1)} custom-call(s32[12]{0:T(128)S(1)} %stack.58.info, f32[1,8192]{1,0:T(1,128)S(1)} %bitcast.20, bf16[128,1536]{1,0:T(8,128)(2,1)} %get-tuple-element.29.refs_0_, bf16[128,1536]{1,0:T(8,128)(2,1)S(1)} %copy-done.25, bf16[128,1536]{1,0:T(8,128)(2,1)} %collective-permute-done.22.refs_2_, ...), custom_call_target="tpu_custom_call", output_to_operand_aliasing={{}: (8, {})} | custom-call | flops 6291456 | bytes 12484608 | tf_op jit(solution)/shard_map/norm/pallas_call | solution.py:102
  261.4 5.5 %collective-permute-done.20.refs_4_ = bf16[128,1536]{1,0:T(8,128)(2,1)} collective-permute-done((bf16[128,1536]{1,0:T(8,128)(2,1)}, bf16[128,1536]{1,0:T(8,128)(2,1)}, u32[]{:S(2)}, u32[]{:S(2)}) %collective-permute-start.20) | collective-permute-done | bytes 393248 | tf_op jit(solution)/shard_map/ppermute | solution.py:64
  266.9 5.1 %norm.7 = bf16[512,8192]{1,0:T(8,128)(2,1)} custom-call(s32[12]{0:T(128)S(1)} %stack.58.info, f32[1,8192]{1,0:T(1,128)S(1)} %bitcast.21, bf16[128,1536]{1,0:T(8,128)(2,1)} %get-tuple-element.27.refs_0_, bf16[128,1536]{1,0:T(8,128)(2,1)} %collective-permute-done.17.refs_1_, ...), custom_call_target="tpu_custom_call", output_to_operand_aliasing={{}: (8, {})} | custom-call | flops 6291456 | bytes 12484608 | tf_op jit(solution)/shard_map/norm/pallas_call | solution.py:102
  (126 shorter events, 63.3 us)
Async XLA Ops:
  7.2 116.5 %all-gather.7.cloned.1.call-start = ((), (), s32[]{:S(2)}) async-start(), calls=%async_computation.1 | async-start | bytes 3538944 | tf_op jit(solution)/shard_map/all_gather | solution.py:496
  33.1 205.0 %all-gather.5.cloned.1.call-start = ((), (), s32[]{:S(2)}) async-start(), calls=%async_computation | async-start | bytes 4718592 | tf_op jit(solution)/shard_map/all_gather | solution.py:505
  74.5 46.6 %collective-permute-start.15 = (bf16[512,512]{1,0:T(8,128)(2,1)}, bf16[512,512]{1,0:T(8,128)(2,1)}, u32[]{:S(2)}, u32[]{:S(2)}) collective-permute-start(bf16[512,512]{1,0:T(8,128)(2,1)} %copy-done.3), channel_id=1, source_target_pairs={{0,8},{4,12},{8,0},{12,4},{1,9},{5,13},{9,1},{13,5},{2,10},{6,14},... | collective-permute-start | bytes 1572872 | tf_op jit(solution)/shard_map/ppermute | solution.py:63
  79.0 35.4 %collective-permute-start.8 = (bf16[512,256]{1,0:T(8,128)(2,1)S(1)}, bf16[512,256]{1,0:T(8,128)(2,1)S(1)}, u32[]{:S(2)}, u32[]{:S(2)}) collective-permute-start(bf16[512,256]{1,0:T(8,128)(2,1)S(1)} %attend.1.refs_4_.refs_0_), channel_id=1, source_target_pairs={{0,8},{4,12},{8,0},{12,4},{1,9},{5,13},{9,1},{13,5},{2,10},{6,14},... | collective-permute-start | bytes 786440 | tf_op jit(solution)/shard_map/ppermute | solution.py:63
  79.1 43.3 %collective-permute-start.6 = (bf16[512,256]{1,0:T(8,128)(2,1)S(1)}, bf16[512,256]{1,0:T(8,128)(2,1)S(1)}, u32[]{:S(2)}, u32[]{:S(2)}) collective-permute-start(bf16[512,256]{1,0:T(8,128)(2,1)S(1)} %attend.1.refs_4_.refs_0_), channel_id=1, source_target_pairs={{0,4},{4,8},{8,12},{1,5},{5,9},{9,13},{2,6},{6,10},{10,14},{3,7},{... | collective-permute-start | bytes 786440 | tf_op jit(solution)/shard_map/ppermute | solution.py:61
  85.2 38.4 %collective-permute-start.7 = (bf16[512,256]{1,0:T(8,128)(2,1)S(1)}, bf16[512,256]{1,0:T(8,128)(2,1)S(1)}, u32[]{:S(2)}, u32[]{:S(2)}) collective-permute-start(bf16[512,256]{1,0:T(8,128)(2,1)S(1)} %attend.1.refs_4_.refs_0_), channel_id=1, source_target_pairs={{4,0},{8,4},{12,8},{5,1},{9,5},{13,9},{6,2},{10,6},{14,10},{7,3},{... | collective-permute-start | bytes 786440 | tf_op jit(solution)/shard_map/ppermute | solution.py:62
  115.7 21.5 %collective-permute-start.13 = (bf16[512,512]{1,0:T(8,128)(2,1)}, bf16[512,512]{1,0:T(8,128)(2,1)}, u32[]{:S(2)}, u32[]{:S(2)}) collective-permute-start(bf16[512,512]{1,0:T(8,128)(2,1)} %copy-done.3), channel_id=1, source_target_pairs={{0,4},{4,8},{8,12},{1,5},{5,9},{9,13},{2,6},{6,10},{10,14},{3,7},{... | collective-permute-start | bytes 1572872 | tf_op jit(solution)/shard_map/ppermute | solution.py:61
  122.4 34.5 %collective-permute-start.16 = (bf16[512,512]{1,0:T(8,128)(2,1)}, bf16[512,512]{1,0:T(8,128)(2,1)}, u32[]{:S(2)}, u32[]{:S(2)}) collective-permute-start(bf16[512,512]{1,0:T(8,128)(2,1)} %collective-permute-done.15.refs_8_), channel_id=1, source_target_pairs={{4,0},{8,12},{5,1},{9,13},{6,2},{10,14},{7,3},{11,15},{20,16},{24,... | collective-permute-start | bytes 1572872 | tf_op jit(solution)/shard_map/ppermute | solution.py:64
  129.9 34.3 %collective-permute-start.31 = (bf16[128,1536]{1,0:T(8,128)(2,1)S(1)}, bf16[128,1536]{1,0:T(8,128)(2,1)S(1)}, u32[]{:S(2)}, u32[]{:S(2)}) collective-permute-start(bf16[128,1536]{1,0:T(8,128)(2,1)S(1)} %get-tuple-element.31.refs_0_), channel_id=1, source_target_pairs={{0,8},{4,12},{8,0},{12,4},{1,9},{5,13},{9,1},{13,5},{2,10},{6,14},... | collective-permute-start | bytes 1179656 | tf_op jit(solution)/shard_map/ppermute | solution.py:63
  135.5 30.7 %collective-permute-start.29 = (bf16[128,1536]{1,0:T(8,128)(2,1)S(1)}, bf16[128,1536]{1,0:T(8,128)(2,1)S(1)}, u32[]{:S(2)}, u32[]{:S(2)}) collective-permute-start(bf16[128,1536]{1,0:T(8,128)(2,1)S(1)} %get-tuple-element.31.refs_0_), channel_id=1, source_target_pairs={{0,4},{4,8},{8,12},{1,5},{5,9},{9,13},{2,6},{6,10},{10,14},{3,7},{... | collective-permute-start | bytes 1179656 | tf_op jit(solution)/shard_map/ppermute | solution.py:61
  137.2 36.2 %collective-permute-start.30 = (bf16[128,1536]{1,0:T(8,128)(2,1)S(1)}, bf16[128,1536]{1,0:T(8,128)(2,1)S(1)}, u32[]{:S(2)}, u32[]{:S(2)}) collective-permute-start(bf16[128,1536]{1,0:T(8,128)(2,1)S(1)} %get-tuple-element.31.refs_0_), channel_id=1, source_target_pairs={{4,0},{8,4},{12,8},{5,1},{9,5},{13,9},{6,2},{10,6},{14,10},{7,3},{... | collective-permute-start | bytes 1179656 | tf_op jit(solution)/shard_map/ppermute | solution.py:62
  139.3 58.6 %collective-permute-start.27 = (bf16[128,1536]{1,0:T(8,128)(2,1)S(1)}, bf16[128,1536]{1,0:T(8,128)(2,1)S(1)}, u32[]{:S(2)}, u32[]{:S(2)}) collective-permute-start(bf16[128,1536]{1,0:T(8,128)(2,1)S(1)} %get-tuple-element.30.refs_0_), channel_id=1, source_target_pairs={{0,8},{4,12},{8,0},{12,4},{1,9},{5,13},{9,1},{13,5},{2,10},{6,14},... | collective-permute-start | bytes 1179656 | tf_op jit(solution)/shard_map/ppermute | solution.py:63
  156.9 41.0 %collective-permute-start.25 = (bf16[128,1536]{1,0:T(8,128)(2,1)S(1)}, bf16[128,1536]{1,0:T(8,128)(2,1)S(1)}, u32[]{:S(2)}, u32[]{:S(2)}) collective-permute-start(bf16[128,1536]{1,0:T(8,128)(2,1)S(1)} %get-tuple-element.30.refs_0_), channel_id=1, source_target_pairs={{0,4},{4,8},{8,12},{1,5},{5,9},{9,13},{2,6},{6,10},{10,14},{3,7},{... | collective-permute-start | bytes 1179656 | tf_op jit(solution)/shard_map/ppermute | solution.py:61
  164.2 36.5 %collective-permute-start.26 = (bf16[128,1536]{1,0:T(8,128)(2,1)S(1)}, bf16[128,1536]{1,0:T(8,128)(2,1)S(1)}, u32[]{:S(2)}, u32[]{:S(2)}) collective-permute-start(bf16[128,1536]{1,0:T(8,128)(2,1)S(1)} %get-tuple-element.30.refs_0_), channel_id=1, source_target_pairs={{4,0},{8,4},{12,8},{5,1},{9,5},{13,9},{6,2},{10,6},{14,10},{7,3},{... | collective-permute-start | bytes 1179656 | tf_op jit(solution)/shard_map/ppermute | solution.py:62
  167.0 47.9 %collective-permute-start.23 = (bf16[128,1536]{1,0:T(8,128)(2,1)}, bf16[128,1536]{1,0:T(8,128)(2,1)}, u32[]{:S(2)}, u32[]{:S(2)}) collective-permute-start(bf16[128,1536]{1,0:T(8,128)(2,1)} %get-tuple-element.29.refs_0_), channel_id=1, source_target_pairs={{0,8},{4,12},{8,0},{12,4},{1,9},{5,13},{9,1},{13,5},{2,10},{6,14},... | collective-permute-start | bytes 1179656 | tf_op jit(solution)/shard_map/ppermute | solution.py:63
  174.1 42.1 %collective-permute-start.21 = (bf16[128,1536]{1,0:T(8,128)(2,1)}, bf16[128,1536]{1,0:T(8,128)(2,1)S(1)}, u32[]{:S(2)}, u32[]{:S(2)}) collective-permute-start(bf16[128,1536]{1,0:T(8,128)(2,1)} %get-tuple-element.29.refs_0_), channel_id=1, source_target_pairs={{0,4},{4,8},{8,12},{1,5},{5,9},{9,13},{2,6},{6,10},{10,14},{3,7},{... | collective-permute-start | bytes 1179656 | tf_op jit(solution)/shard_map/ppermute | solution.py:61
  197.9 25.4 %collective-permute-start.19 = (bf16[128,1536]{1,0:T(8,128)(2,1)}, bf16[128,1536]{1,0:T(8,128)(2,1)}, u32[]{:S(2)}, u32[]{:S(2)}) collective-permute-start(bf16[128,1536]{1,0:T(8,128)(2,1)} %get-tuple-element.27.refs_0_), channel_id=1, source_target_pairs={{0,8},{4,12},{8,0},{12,4},{1,9},{5,13},{9,1},{13,5},{2,10},{6,14},... | collective-permute-start | bytes 1179656 | tf_op jit(solution)/shard_map/ppermute | solution.py:63
  198.6 30.8 %collective-permute-start.32 = (bf16[128,1536]{1,0:T(8,128)(2,1)S(1)}, bf16[128,1536]{1,0:T(8,128)(2,1)S(1)}, u32[]{:S(2)}, u32[]{:S(2)}) collective-permute-start(bf16[128,1536]{1,0:T(8,128)(2,1)S(1)} %collective-permute-done.31.refs_3_), channel_id=1, source_target_pairs={{4,0},{8,12},{5,1},{9,13},{6,2},{10,14},{7,3},{11,15},{20,16},{24,... | collective-permute-start | bytes 1179656 | tf_op jit(solution)/shard_map/ppermute | solution.py:64
  201.4 34.6 %collective-permute-start.28 = (bf16[128,1536]{1,0:T(8,128)(2,1)S(1)}, bf16[128,1536]{1,0:T(8,128)(2,1)S(1)}, u32[]{:S(2)}, u32[]{:S(2)}) collective-permute-start(bf16[128,1536]{1,0:T(8,128)(2,1)S(1)} %collective-permute-done.27.refs_3_), channel_id=1, source_target_pairs={{4,0},{8,12},{5,1},{9,13},{6,2},{10,14},{7,3},{11,15},{20,16},{24,... | collective-permute-start | bytes 1179656 | tf_op jit(solution)/shard_map/ppermute | solution.py:64
  214.9 38.3 %collective-permute-start.22 = (bf16[128,1536]{1,0:T(8,128)(2,1)}, bf16[128,1536]{1,0:T(8,128)(2,1)}, u32[]{:S(2)}, u32[]{:S(2)}) collective-permute-start(bf16[128,1536]{1,0:T(8,128)(2,1)} %get-tuple-element.29.refs_0_), channel_id=1, source_target_pairs={{4,0},{8,4},{12,8},{5,1},{9,5},{13,9},{6,2},{10,6},{14,10},{7,3},{... | collective-permute-start | bytes 1179656 | tf_op jit(solution)/shard_map/ppermute | solution.py:62
  217.0 36.3 %collective-permute-start.24 = (bf16[128,1536]{1,0:T(8,128)(2,1)}, bf16[128,1536]{1,0:T(8,128)(2,1)}, u32[]{:S(2)}, u32[]{:S(2)}) collective-permute-start(bf16[128,1536]{1,0:T(8,128)(2,1)} %collective-permute-done.23.refs_3_), channel_id=1, source_target_pairs={{4,0},{8,12},{5,1},{9,13},{6,2},{10,14},{7,3},{11,15},{20,16},{24,... | collective-permute-start | bytes 1179656 | tf_op jit(solution)/shard_map/ppermute | solution.py:64
  223.3 35.0 %collective-permute-start.17 = (bf16[128,1536]{1,0:T(8,128)(2,1)}, bf16[128,1536]{1,0:T(8,128)(2,1)}, u32[]{:S(2)}, u32[]{:S(2)}) collective-permute-start(bf16[128,1536]{1,0:T(8,128)(2,1)} %get-tuple-element.27.refs_0_), channel_id=1, source_target_pairs={{0,4},{4,8},{8,12},{1,5},{5,9},{9,13},{2,6},{6,10},{10,14},{3,7},{... | collective-permute-start | bytes 1179656 | tf_op jit(solution)/shard_map/ppermute | solution.py:61
  230.2 31.2 %collective-permute-start.18 = (bf16[128,1536]{1,0:T(8,128)(2,1)}, bf16[128,1536]{1,0:T(8,128)(2,1)}, u32[]{:S(2)}, u32[]{:S(2)}) collective-permute-start(bf16[128,1536]{1,0:T(8,128)(2,1)} %get-tuple-element.27.refs_0_), channel_id=1, source_target_pairs={{4,0},{8,4},{12,8},{5,1},{9,5},{13,9},{6,2},{10,6},{14,10},{7,3},{... | collective-permute-start | bytes 1179656 | tf_op jit(solution)/shard_map/ppermute | solution.py:62
  236.8 30.1 %collective-permute-start.20 = (bf16[128,1536]{1,0:T(8,128)(2,1)}, bf16[128,1536]{1,0:T(8,128)(2,1)}, u32[]{:S(2)}, u32[]{:S(2)}) collective-permute-start(bf16[128,1536]{1,0:T(8,128)(2,1)} %collective-permute-done.19.refs_3_), channel_id=1, source_target_pairs={{4,0},{8,12},{5,1},{9,13},{6,2},{10,14},{7,3},{11,15},{20,16},{24,... | collective-permute-start | bytes 1179656 | tf_op jit(solution)/shard_map/ppermute | solution.py:64
  (42 other events, 301.5 us)
Sparse Core Ops, SparseCore 0:
  33.2 40.5 all-gather.6
  75.7 39.1 all-gather.4

commit v3 on v2

v3 whole, which is shorter than its diff:
```python
import functools
import math

import jax
import jax.numpy as jnp
from jax import lax
from jax.experimental import pallas as pl
from jax.experimental.pallas import tpu as pltpu
from jax.sharding import PartitionSpec as P

GROUP = 8
HD = 128
NEG = -1e30
EPS_NORM = 1e-05
MIB = 1024 * 1024
CHUNK = 128
KEY_BLOCK = 512
ATTEND_FLOPS = 16
TAIL = 16
DIGIT = 32
ANYWHERE = pl.BlockSpec(memory_space=pl.ANY)


def frequencies(head_width):
    counter = jnp.arange(head_width // 2, dtype=jnp.float32)
    base_freq = jnp.exp(-(2.0 * counter / head_width) * math.log(500000.0))
    wavelength = 2.0 * math.pi / base_freq
    smoothing = (8192.0 / wavelength - 1.0) / 3.0
    blended = (1.0 - smoothing) * base_freq / 8.0 + smoothing * base_freq
    return jnp.where(
        wavelength < 2048.0, base_freq, jnp.where(wavelength > 8192.0, base_freq / 8.0, blended)
    )


def pieces_of(value, axis, count, between=lambda block: block):
    if count & (count - 1) == 0:
        held = {0: value}
        bit = count // 2
        while bit:
            pairs = [(i, i ^ bit) for i in range(count)]
            for mask in sorted(held):
                held[mask | bit] = lax.ppermute(held[mask], axis, pairs)
            if bit == count // 2:
                held[bit] = between(held[bit])
            bit //= 2
        return [held[mask] for mask in range(count)]
    blocks = [value]
    for shift in range(1, count):
        pairs = [(i, (i + shift) % count) for i in range(count)]
        blocks.append(lax.ppermute(value, axis, pairs))
    return blocks


def owners_of(count, me):
    if count & (count - 1) == 0:
        return [me ^ mask for mask in range(count)]
    return [(me + count - shift) % count for shift in range(count)]


def plane_gather(value, groups, contexts):
    count = groups * contexts
    if count & (count - 1):
        gathered = lax.all_gather(value, ("groups", "context"), axis=0, tiled=False)
        return [gathered[number] for number in range(count)]
    held = {0: value}
    bits = [1 << b for b in range(contexts.bit_length() - 2, 0, -1)]
    bits += [contexts << b for b in range(groups.bit_length() - 1)]
    bits += [1] if contexts > 1 else []
    for bit in bits:
        axis, flip, size = ("context", bit, contexts)
        if bit >= contexts:
            axis, flip, size = ("groups", bit // contexts, groups)
        pairs = [(i, i ^ flip) for i in range(size)]
        for mask in sorted(held):
            held[mask | bit] = lax.ppermute(held[mask], axis, pairs)
    return [held[mask] for mask in range(count)]


def plane_owners(count, me):
    if count & (count - 1):
        return list(range(count))
    return [me ^ mask for mask in range(count)]


def line_gather(value, count):
    if count != 4:
        return [lax.all_gather(value, "tensor", axis=0, tiled=False)]
    up = lax.ppermute(value, "tensor", [(0, 1), (1, 2), (2, 3)])
    down = lax.ppermute(value, "tensor", [(1, 0), (2, 1), (3, 2)])
    far = lax.ppermute(value, "tensor", [(0, 2), (1, 3), (2, 0), (3, 1)])
    last = lax.ppermute(far, "tensor", [(1, 0), (2, 3)])
    return [value, up, down, far, last]


class Table:
    def __init__(self, contexts, count):
        self.contexts, self.count = contexts, count
        self.owner = 1
        self.place = 1 + contexts
        self.low = self.place + count
        self.high = self.low + 1
        self.share = self.low + 2
        self.rows = self.low + 3


def line_read(table, info, refs, d, cols=slice(None)):
    if len(refs) == 1:
        return refs[0][info[table.place + d], :, cols].astype(jnp.float32)
    if d == 0:
        return refs[0][:, cols].astype(jnp.float32)
    if d == 2:
        return refs[3][:, cols].astype(jnp.float32)
    near = refs[1 if d == 1 else 2][:, cols].astype(jnp.float32)
    other = refs[4][:, cols].astype(jnp.float32)
    at_end = info[table.low if d == 1 else table.high]
    return jnp.where(at_end == 1, other, near)


def line_spec(blocks, rows, index):
    if len(blocks) == 1:
        count, _, width = blocks[0].shape
        return [pl.BlockSpec((count, rows, width), lambda i, info: (0, index(i), 0))]
    width = blocks[0].shape[1]
    return [pl.BlockSpec((rows, width), lambda i, info: (index(i), 0)) for _ in blocks]


def call(kernel, name, info, args, in_specs, out_specs, out_shape, grid=(1,), aliases=None,
         scratch=(), flops=1, vmem=16):
    return pl.pallas_call(
        kernel,
        grid_spec=pltpu.PrefetchScalarGridSpec(
            num_scalar_prefetch=1,
            grid=grid,
            in_specs=in_specs,
            out_specs=out_specs,
            scratch_shapes=list(scratch),
        ),
        out_shape=out_shape,
        input_output_aliases=aliases or {},
        compiler_params=pltpu.CompilerParams(vmem_limit_bytes=vmem * MIB),
        cost_estimate=pl.CostEstimate(flops=flops, bytes_accessed=1, transcendentals=0),
        name=name,
    )(info, *args)


def whole(a):
    zeros = (0,) * len(a.shape)
    return pl.BlockSpec(tuple(a.shape), lambda i, info: zeros)


def prepare_kernel(info, q_ref, kv_ref, cache_ref, cos_ref, sin_ref, length_ref, *refs):
    q_out, kv_out = refs[1:3] if len(refs) > 2 else refs
    if len(refs) > 2:
        rows_early = refs[3].shape[0]
        refs[3][...] = refs[0][:rows_early]
        refs[4][...] = refs[0][rows_early:]
    cosine, sine = cos_ref[...], sin_ref[...]
    slots, rows = cache_ref.shape[0], q_ref.shape[0]
    span, tail = slice(slots, slots + rows), slice(slots + rows, slots + rows + TAIL)

    def turn(block):
        block = block.astype(jnp.float32)
        return (block * cosine + pltpu.roll(block, HD // 2, 1) * sine).astype(jnp.bfloat16)

    kv_out[:slots] = cache_ref[...]
    kv_out[span, :HD] = turn(kv_ref[:, :HD])
    kv_out[span, HD:] = kv_ref[:, HD:]
    length = length_ref[0]
    upper = lax.div(length, DIGIT)
    lower = length - upper * DIGIT
    kv_out[tail, :HD] = jnp.full((TAIL, HD), upper.astype(jnp.float32)).astype(jnp.bfloat16)
    kv_out[tail, HD:] = jnp.full((TAIL, HD), lower.astype(jnp.float32)).astype(jnp.bfloat16)
    for head in range(q_ref.shape[1] // HD):
        cols = slice(head * HD, (head + 1) * HD)
        q_out[:, cols] = turn(q_ref[:, cols])


def cut_kernel(table, slab, keep, info, w_ref, *outs):
    raw = slab - keep
    for d in range(table.count):
        target = lax.rem(info[table.place] + d, table.count)
        outs[d][...] = w_ref[:, pl.ds(pl.multiple_of(target * slab, slab), keep)]
    for j in range(table.count if raw else 0):
        outs[-1][:, j * raw : (j + 1) * raw] = w_ref[:, j * slab + keep : (j + 1) * slab]


def cut(table, info, out_weight, part, slab, keep):
    shapes = [jax.ShapeDtypeStruct((part, keep), out_weight.dtype)] * table.count
    if keep < slab:
        shapes.append(
            jax.ShapeDtypeStruct((part, table.count * (slab - keep)), out_weight.dtype)
        )
    return call(
        functools.partial(cut_kernel, table, slab, keep),
        "cut",
        info,
        [out_weight],
        [pl.BlockSpec((part, out_weight.shape[1]), lambda i, info: (info[table.share], 0))],
        [whole(shape) for shape in shapes],
        shapes,
    )


def prepare(info, queries, span_pairs, cache, cosine, sine, lengths, residual, raw, rows_early):
    rows, slab = residual.shape
    shapes = [
        jax.ShapeDtypeStruct(queries.shape, jnp.bfloat16),
        jax.ShapeDtypeStruct((cache.shape[0] + rows + TAIL, 2 * HD), jnp.bfloat16),
    ]
    args = [queries, span_pairs, cache, cosine, sine, lengths]
    in_specs = [whole(a) for a in args[:-1]] + [pl.BlockSpec(memory_space=pltpu.SMEM)]
    if raw:
        shapes.append(jax.ShapeDtypeStruct((rows_early, raw), residual.dtype))
        shapes.append(jax.ShapeDtypeStruct((rows - rows_early, raw), residual.dtype))
        args.append(residual)
        in_specs.append(pl.BlockSpec((rows, raw), lambda i, info: (0, slab // raw - 1)))
    return call(
        prepare_kernel,
        "prepare",
        info,
        args,
        in_specs,
        [whole(shape) for shape in shapes],
        shapes,
        vmem=58,
    )


def stack_kernel(count, info, *refs):
    for number, part in enumerate(refs[:count]):
        refs[-1][number] = part[...]


def stack(info, parts, after):
    shape = jax.ShapeDtypeStruct((len(parts), *parts[0].shape), parts[0].dtype)
    return call(
        functools.partial(stack_kernel, len(parts)),
        "stack",
        info,
        [*parts, *after],
        [whole(p) for p in parts] + [ANYWHERE] * len(after),
        whole(shape),
        shape,
    )


def gate_kernel(info, *refs):
    pass


def gate(info, value, after):
    return call(
        gate_kernel,
        "gate",
        info,
        [value, *after],
        [ANYWHERE] * (1 + len(after)),
        ANYWHERE,
        jax.ShapeDtypeStruct(value.shape, value.dtype),
        aliases={1: 0},
    )


def attend_kernel(table, slots, info, q_ref, *refs):
    count = table.contexts
    pieces, out_ref, s_ref = refs[:count], refs[-2], refs[-1]
    rows = q_ref.shape[0]
    heads = q_ref.shape[1] // HD
    chunk = pl.program_id(0)
    mine = info[0]
    q = jnp.concatenate([q_ref[:, h * HD : (h + 1) * HD] for h in range(heads)], axis=0)
    exponent = math.log2(math.e) / math.sqrt(HD)

    blocks = []
    peak = jnp.full((heads * rows, HD), NEG, jnp.float32)
    column = 0
    for kind in ("cache", "span"):
        for number, ref in enumerate(pieces):
            tail = ref.shape[0] - TAIL
            first, last = (0, slots) if kind == "cache" else (slots, tail)
            width = min(KEY_BLOCK, last - first)
            length = ref[tail : tail + 1, :HD].astype(jnp.float32) * DIGIT + ref[
                tail : tail + 1, HD:
            ].astype(jnp.float32)
            length = jnp.concatenate([length] * (width // HD), axis=1)
            for begin in range(first, last, width):
                scores = lax.dot_general(
                    q,
                    ref[begin : begin + width, :HD],
                    (((1,), (1,)), ((), ())),
                    preferred_element_type=jnp.float32,
                )
                if kind == "cache":
                    slot = lax.broadcasted_iota(jnp.int32, (1, width), 1) + begin
                    live = slot.astype(jnp.float32) < length
                    scores = scores + jnp.where(live, 0.0, NEG)
                elif number == 0:
                    key = lax.broadcasted_iota(jnp.int32, (rows, width), 1) + (begin - first)
                    row = lax.broadcasted_iota(jnp.int32, (rows, width), 0) + chunk * rows
                    bias = jnp.where(key <= row, 0.0, NEG)
                    scores = scores + jnp.concatenate([bias] * heads, axis=0)
                else:
                    scores = scores + jnp.where(info[table.owner + number] < mine, 0.0, NEG)
                s_ref[:, column : column + width] = scores
                for lane in range(0, width, HD):
                    peak = jnp.maximum(peak, scores[:, lane : lane + HD])
                blocks.append((ref, begin, column, width))
                column += width
    top = jnp.max(peak, axis=1, keepdims=True)
    total = jnp.zeros((heads * rows, HD), jnp.float32)
    mixed = jnp.zeros((heads * rows, HD), jnp.float32)
    for ref, begin, column, width in blocks:
        weights = jnp.exp2((s_ref[:, column : column + width] - top) * exponent)
        for lane in range(0, width, HD):
            total = total + weights[:, lane : lane + HD]
        mixed = mixed + jnp.dot(
            weights.astype(jnp.bfloat16),
            ref[begin : begin + width, HD:],
            preferred_element_type=jnp.float32,
        )
    result = (mixed / jnp.sum(total, axis=1, keepdims=True)).astype(jnp.bfloat16)
    for h in range(heads):
        out_ref[:, h * HD : (h + 1) * HD] = result[h * rows : (h + 1) * rows]


def attend(table, info, queries, pieces, slots, rows):
    all_rows, width = queries.shape
    heads = width // HD
    keys = sum(a.shape[0] - TAIL for a in pieces)
    chunk_spec = pl.BlockSpec((rows, width), lambda i, info: (i, 0))
    return call(
        functools.partial(attend_kernel, table, slots),
        "attend",
        info,
        [queries, *pieces],
        [chunk_spec] + [whole(a) for a in pieces],
        chunk_spec,
        jax.ShapeDtypeStruct((all_rows, width), jnp.bfloat16),
        grid=(all_rows // rows,),
        scratch=[pltpu.VMEM((heads * rows, keys), jnp.float32)],
        flops=ATTEND_FLOPS * all_rows * heads * keys * HD,
        vmem=28,
    )


def project_kernel(table, lines, shares, keep, info, *refs):
    count = table.count
    attention, pieces = refs[:lines], refs[lines : lines + shares]
    r_ref = refs[lines + shares]
    parts, h_ref, w_ref = refs[lines + shares + 1 : -2], refs[-2], refs[-1]
    part_rows = pieces[0].shape[1]

    @pl.when(pl.program_id(0) == 0)
    def _():
        for number, piece in enumerate(pieces):
            start = pl.multiple_of(info[table.rows + number] * part_rows, part_rows)
            for d in range(count):
                w_ref[d, pl.ds(start, part_rows)] = piece[d]

    total = r_ref[:, :keep].astype(jnp.float32)
    for d in range(count):
        block = line_read(table, info, attention, d).astype(jnp.bfloat16)
        total = total + jnp.dot(block, w_ref[d], preferred_element_type=jnp.float32)
    result = total.astype(jnp.bfloat16)
    h_ref[:, :keep] = result
    for number, part in enumerate(parts):

        @pl.when(pl.program_id(0) == number)
        def _():
            part[...] = result


def project(table, info, attention, pieces, residual, rows):
    all_rows, slab = residual.shape
    count, part_rows, keep = pieces[0].shape
    depth = len(pieces) * part_rows
    chunks = all_rows // rows
    part = jax.ShapeDtypeStruct((rows, keep), jnp.bfloat16)
    hidden = jax.ShapeDtypeStruct(residual.shape, jnp.bfloat16)
    row_spec = pl.BlockSpec((rows, slab), lambda i, info: (i, 0))
    return call(
        functools.partial(project_kernel, table, len(attention), len(pieces), keep),
        "project",
        info,
        [*attention, *pieces, residual],
        line_spec(attention, rows, lambda i: i) + [whole(p) for p in pieces] + [row_spec],
        [whole(part)] * chunks + [row_spec],
        [part] * chunks + [hidden],
        grid=(chunks,),
        scratch=[pltpu.VMEM((count, depth, keep), jnp.bfloat16)],
        vmem=28,
    )


def project_raw_kernel(table, lines, info, *refs):
    count = table.count
    attention, (early, late) = refs[:lines], refs[lines : lines + 2]
    w_ref = refs[lines + 2]
    raw_ref, h_ref = refs[-2:]
    raw = h_ref.shape[1]
    blocks = [
        line_read(table, info, attention, d).astype(jnp.bfloat16) for d in range(count)
    ]
    for slab in range(count):
        place = info[table.place + slab]
        start = pl.multiple_of(place * raw, raw)
        total = jnp.where(
            pl.program_id(0) == 0,
            early[place].astype(jnp.float32),
            late[place].astype(jnp.float32),
        )
        for d in range(count):
            weight = w_ref[info[table.place + d], :, :, pl.ds(start, raw)]
            weight = weight.reshape(blocks[d].shape[1], raw)
            total = total + jnp.dot(blocks[d], weight, preferred_element_type=jnp.float32)
        result = total.astype(jnp.bfloat16)
        raw_ref[:, slab * raw : (slab + 1) * raw] = result
        if slab == 0:
            h_ref[...] = result


def project_raw(table, info, attention, residuals, weights, hidden, raw, rows):
    all_rows, slab = hidden.shape
    count = table.count
    args = [*attention, *residuals, weights, hidden]
    out = jax.ShapeDtypeStruct((all_rows, count * raw), jnp.bfloat16)
    return call(
        functools.partial(project_raw_kernel, table, len(attention)),
        "project_raw",
        info,
        args,
        line_spec(attention, rows, lambda i: i)
        + [
            pl.BlockSpec((count, rows, raw), lambda i, info: (0, 0, 0)),
            pl.BlockSpec((count, rows, raw), lambda i, info: (0, jnp.maximum(i - 1, 0), 0)),
            whole(weights),
            ANYWHERE,
        ],
        [
            pl.BlockSpec((rows, count * raw), lambda i, info: (i, 0)),
            pl.BlockSpec((rows, raw), lambda i, info: (i, slab // raw - 1)),
        ],
        [out, jax.ShapeDtypeStruct(hidden.shape, jnp.bfloat16)],
        grid=(all_rows // rows,),
        aliases={len(args): 1},
        vmem=28,
    )


def norm_kernel(table, lines, keep, slab, info, g_ref, *refs):
    count = table.count
    blocks, out_ref = refs[:lines], refs[-1]
    raw = slab - keep
    values = []
    squares = jnp.zeros((out_ref.shape[0], 1), jnp.float32)

    def read(d):
        found = [(0, keep, line_read(table, info, blocks, d))]
        if raw:
            cols = slice(d * raw, (d + 1) * raw)
            found.append((keep, raw, refs[lines][:, cols].astype(jnp.float32)))
        return found

    for d in range(count):
        for _, _, value in read(d):
            squares = squares + jnp.sum(value * value, axis=1, keepdims=True)
    inverse = lax.rsqrt(squares / (count * slab) + EPS_NORM)
    for d in range(count):
        for offset, width, value in read(d):
            start = pl.multiple_of(info[table.place + d] * slab + offset, HD)
            cols = pl.ds(start, width)
            out_ref[:, cols] = (value * inverse * g_ref[:, cols]).astype(jnp.bfloat16)


def norm_into(table, info, buffer, blocks, raw_hidden, gain, chunk, rows, keep, slab, total_rows):
    width = table.count * slab
    step = min(rows, 32)
    steps = rows // step
    args = [gain.reshape(1, width), *blocks]
    in_specs = [pl.BlockSpec((1, width), lambda i, info: (0, 0))]
    in_specs += line_spec(blocks, step, lambda i: i)
    if raw_hidden is not None:
        args.append(raw_hidden)
        in_specs.append(
            pl.BlockSpec((step, raw_hidden.shape[1]), lambda i, info: (chunk * steps + i, 0))
        )
    aliases = {}
    if buffer is not None:
        args.append(buffer)
        in_specs.append(ANYWHERE)
        aliases = {len(args): 0}
    return call(
        functools.partial(norm_kernel, table, len(blocks), keep, slab),
        "norm",
        info,
        args,
        in_specs,
        pl.BlockSpec((step, width), lambda i, info: (chunk * steps + i, 0)),
        jax.ShapeDtypeStruct((total_rows, width), jnp.bfloat16),
        grid=(steps,),
        aliases=aliases,
    )


def per_device(queries, span_kv, cache, lengths, offset, out_weight, residual, gain):
    rows = queries.shape[0]
    heads = queries.shape[1] // HD
    depth = out_weight.shape[0]
    slab = residual.shape[1]
    contexts = lax.axis_size("context")
    count = lax.axis_size("tensor")
    context_index = lax.axis_index("context")
    tensor_index = lax.axis_index("tensor")
    kv_index = tensor_index * heads // GROUP
    groups = lax.axis_size("groups")
    shares = groups * contexts
    share = lax.axis_index("groups") * contexts + context_index
    raw = slab // 4 if slab % 512 == 0 and rows > CHUNK else 0
    keep = slab - raw
    chunk = min(CHUNK, rows)
    chunks = rows // chunk

    table = Table(contexts, count)
    steering = [context_index, *owners_of(contexts, context_index)]
    steering += [lax.rem(tensor_index + (count - d), count) for d in range(count)]
    steering += [tensor_index == 0, tensor_index == count - 1, share]
    steering += plane_owners(shares, share)
    info = jnp.stack([jnp.asarray(v).astype(jnp.int32) for v in steering])

    cache_local = lax.dynamic_index_in_dim(cache, kv_index, 0, keepdims=False)
    span_local = lax.dynamic_index_in_dim(span_kv, kv_index, 1, keepdims=False)
    positions = offset[0] + context_index * rows + jnp.arange(rows, dtype=jnp.int32)
    both = jnp.concatenate([frequencies(HD)] * 2)
    angles = positions.astype(jnp.float32)[:, None] * both[None, :]
    sign = jnp.where(jnp.arange(HD) < HD // 2, -1.0, 1.0)
    q_turned, payload, *residual_raw = prepare(
        info, queries, span_local, cache_local, jnp.cos(angles),
        jnp.sin(angles) * sign[None, :], lengths, residual, raw, chunk,
    )
    cuts = cut(table, info, out_weight, depth // shares, slab, keep)
    parts = [cuts[0]]
    for shift in range(1, count):
        pairs = [(i, (i + shift) % count) for i in range(count)]
        parts.append(lax.ppermute(cuts[shift], "tensor", pairs))
    own_weights = stack(info, parts, [])
    early, late = [], []
    if raw:
        early = [lax.all_gather(residual_raw[0], "tensor", axis=0, tiled=False)]
        late = [lax.all_gather(residual_raw[1], "tensor", axis=0, tiled=False)]
    pieces = pieces_of(
        payload, "context", contexts, lambda block: gate(info, block, [own_weights, *early])
    )

    mixed = attend(table, info, q_turned, pieces, cache_local.shape[0], chunk)
    weight_pieces = plane_gather(own_weights, groups, contexts)
    attention = line_gather(mixed, count)

    *hidden_parts, hidden = project(table, info, attention, weight_pieces, residual, chunk)
    lines = []
    for number in range(chunks):
        value = hidden_parts[number]
        if number > 1:
            value = gate(info, value, lines[number - 2][1:])
        lines.append(line_gather(value, count))
    raw_hidden = None
    if raw:
        raw_weights = gate(info, cuts[-1], [*late, hidden_parts[0]])
        raw_weights = lax.all_gather(
            raw_weights, ("tensor", "groups", "context"), axis=0, tiled=False
        )
        raw_weights = raw_weights.reshape(count, shares, *cuts[-1].shape)
        raw_hidden, hidden = project_raw(
            table, info, attention, [*early, *late], raw_weights, hidden, raw, chunk
        )
    normed = None
    for number in range(chunks):
        normed = norm_into(
            table, info, normed, lines[number], raw_hidden, gain, number, chunk, keep, slab, rows
        )
    return (hidden, normed)


def solution(mesh):
    in_specs = (
        P(("groups", "context"), "tensor"),
        P(("groups", "context"), None, None),
        P("groups", "context", None),
        P(("groups", "context")),
        P("groups"),
        P("tensor", None),
        P(("groups", "context"), "tensor"),
        P(),
    )
    out_specs = (P(("groups", "context"), "tensor"), P(("groups", "context"), None))
    return jax.shard_map(
        per_device, mesh=mesh, in_specs=in_specs, out_specs=out_specs, check_vma=False
    )
```

time: 280 us -> 264 us (0.943)
  the two profiles are of different devices: /device:TPU:0 before, /device:TPU:18 now
where the time goes in v3:
time: 264 us; the launch traced here: 263 us
  waiting for transfers between devices  90.5 us (34%)
  starting transfers between devices  74.6 us (28%)
  Pallas kernels  47 us (18%)
  blocking collectives  18 us (7%)
  between operations  15.8 us (6%)
  local copies, waits for them, and re-layouts  14.9 us (6%)
    pallas_call x14, Pallas kernels, call(): pl.pallas_call(kernel, grid_spec=pltpu.PrefetchScalarGridSpec(num_scalar_...  47 us
    ppermute x5, waiting for transfers between devices, line_gather(): far = lax.ppermute(value, 'tensor', [(0, 2), (1, 3), (2, 0), (3, 1)])  32.7 us
    ppermute x5, starting transfers between devices, line_gather(): last = lax.ppermute(far, 'tensor', [(1, 0), (2, 3)])  32.3 us
    ppermute x5, waiting for transfers between devices, line_gather(): up = lax.ppermute(value, 'tensor', [(0, 1), (1, 2), (2, 3)])  21.6 us
    ppermute x5, waiting for transfers between devices, line_gather(): last = lax.ppermute(far, 'tensor', [(1, 0), (2, 3)])  20.3 us
    all_gather x1, blocking collectives, per_device(): early = [lax.all_gather(residual_raw[0], 'tensor', axis=0, tiled=False)]  18 us
    ppermute x5, starting transfers between devices, line_gather(): down = lax.ppermute(value, 'tensor', [(1, 0), (2, 1), (3, 2)])  15.1 us
    unnamed x70, local copies, waits for them, and re-layouts  14.2 us
  transfers between devices with their start and end apart: 35, of which 10 were waited for; matrix products, arithmetic and copies ran while one was open for 0% of the time, Pallas kernels for 14%

profile of v3, /device:TPU:18, one launch (start us, length us, event | category | flops | bytes accessed | tf_op | source)
XLA Modules:
  0.0 262.8 jit_solution(9604792637807355606)
XLA Ops:
  11.2 3.6 %prepare.1 = (bf16[512,256]{1,0:T(8,128)(2,1)}, bf16[1552,256]{1,0:T(8,128)(2,1)}, bf16[128,512]{1,0:T(8,128)(2,1)}, bf16[384,512]{1,0:T(8,128)(2,1)}) custom-call(s32[20]{0:T(128)} %stack.86.info, bf16[512,256]{1,0:T(8,128)(2,1)} %q_ref.1, bf16[512,256]{1,0:T(8,128)(2,1)} %bitcast.36, bf16[1024,256]{1,0:T(8,128)(2,1)} %bitcast.35, ...), custom_call_target="tpu_custom_call" | custom-call | flops 1 | bytes 1 | tf_op jit(solution)/shard_map/prepare/pallas_call | solution.py:129
  22.5 18.0 %all-gather = bf16[512,512]{1,0:T(8,128)(2,1)S(1)} all-gather(bf16[128,512]{1,0:T(8,128)(2,1)S(1)} %copy-done.34), channel_id=2, replica_groups=mesh['groups'=2,'tensor'=4,'context'=4] {'tensor'}, dimensions={0}, use_global_device_ids=true | all-gather | bytes 655360 | tf_op jit(solution)/shard_map/all_gather | solution.py:548
  44.9 8.5 %collective-permute-done.11.refs_7_ = bf16[4,32,1536]{2,1,0:T(8,128)(2,1)S(1)} collective-permute-done((bf16[4,32,1536]{2,1,0:T(8,128)(2,1)S(1)}, bf16[4,32,1536]{2,1,0:T(8,128)(2,1)S(1)}, u32[]{:S(2)}, u32[]{:S(2)}) %collective-permute-start.11) | collective-permute-done | bytes 393248 | tf_op jit(solution)/shard_map/ppermute | solution.py:75
  55.0 13.5 %attend.1.refs_0_ = bf16[512,256]{1,0:T(8,128)(2,1)S(1)} custom-call(s32[20]{0:T(128)S(1)} %copy-done.31, bf16[512,256]{1,0:T(8,128)(2,1)S(1)} %copy-done.33, bf16[1552,256]{1,0:T(8,128)(2,1)S(1)} %copy-done.32, bf16[1552,256]{1,0:T(8,128)(2,1)} %collective-permute-done.refs_1_, bf16[1552,256]{1,0:T(8,128)(2,1)S(1)} %gate.4.refs_2_, ...), custom_call_target="tpu_custom_call" | custom-call | flops 12884901888 | bytes 1 | tf_op jit(solution)/shard_map/attend/pallas_call | solution.py:129
  74.2 3.0 %collective-permute-start.7 = (bf16[512,256]{1,0:T(8,128)(2,1)S(1)}, bf16[512,256]{1,0:T(8,128)(2,1)S(1)}, u32[]{:S(2)}, u32[]{:S(2)}) collective-permute-start(bf16[512,256]{1,0:T(8,128)(2,1)S(1)} %attend.1.refs_0_), channel_id=1, source_target_pairs={{4,0},{8,4},{12,8},{5,1},{9,5},{13,9},{6,2},{10,6},{14,10},{7,3},{... | collective-permute-start | bytes 786440 | tf_op jit(solution)/shard_map/ppermute | solution.py:89
  77.2 12.3 %collective-permute-done.8.refs_3_ = bf16[512,256]{1,0:T(8,128)(2,1)S(1)} collective-permute-done((bf16[512,256]{1,0:T(8,128)(2,1)S(1)}, bf16[512,256]{1,0:T(8,128)(2,1)S(1)}, u32[]{:S(2)}, u32[]{:S(2)}) %collective-permute-start.8) | collective-permute-done | bytes 262176 | tf_op jit(solution)/shard_map/ppermute | solution.py:90
  89.5 4.1 %collective-permute-start.9 = (bf16[512,256]{1,0:T(8,128)(2,1)S(1)}, bf16[512,256]{1,0:T(8,128)(2,1)S(1)}, u32[]{:S(2)}, u32[]{:S(2)}) collective-permute-start(bf16[512,256]{1,0:T(8,128)(2,1)S(1)} %collective-permute-done.8.refs_3_), channel_id=1, source_target_pairs={{4,0},{8,12},{5,1},{9,13},{6,2},{10,14},{7,3},{11,15},{20,16},{24,... | collective-permute-start | bytes 786440 | tf_op jit(solution)/shard_map/ppermute | solution.py:91
  95.8 3.6 %collective-permute-done.9.refs_4_ = bf16[512,256]{1,0:T(8,128)(2,1)S(1)} collective-permute-done((bf16[512,256]{1,0:T(8,128)(2,1)S(1)}, bf16[512,256]{1,0:T(8,128)(2,1)S(1)}, u32[]{:S(2)}, u32[]{:S(2)}) %collective-permute-start.9) | collective-permute-done | bytes 262176 | tf_op jit(solution)/shard_map/ppermute | solution.py:91
  99.4 4.5 %project.1 = (bf16[128,1536]{1,0:T(8,128)(2,1)S(1)}, bf16[128,1536]{1,0:T(8,128)(2,1)S(1)}, bf16[128,1536]{1,0:T(8,128)(2,1)}, bf16[128,1536]{1,0:T(8,128)(2,1)}, bf16[512,2048]{1,0:T(8,128)(2,1)}) custom-call(s32[20]{0:T(128)S(1)} %copy-done.31, bf16[512,256]{1,0:T(8,128)(2,1)S(1)} %attend.1.refs_0_, bf16[512,256]{1,0:T(8,128)(2,1)S(1)} %collective-permute-done.6.refs_1_, ...), custom_call_target="tpu_custom_call" | custom-call | flops 1 | bytes 1 | tf_op jit(solution)/shard_map/project/pallas_call | solution.py:129
  108.0 3.6 %collective-permute-start.27 = (bf16[128,1536]{1,0:T(8,128)(2,1)S(1)}, bf16[128,1536]{1,0:T(8,128)(2,1)S(1)}, u32[]{:S(2)}, u32[]{:S(2)}) collective-permute-start(bf16[128,1536]{1,0:T(8,128)(2,1)S(1)} %get-tuple-element.27.refs_2_.refs_0_), channel_id=1, source_target_pairs={{0,8},{4,12},{8,0},{12,4},{1,9},{5,13},{9,1},{13,5},{2,10},{6,14},... | collective-permute-start | bytes 1179656 | tf_op jit(solution)/shard_map/ppermute | solution.py:90
  117.6 20.4 %collective-permute-done.27.refs_3_ = bf16[128,1536]{1,0:T(8,128)(2,1)S(1)} collective-permute-done((bf16[128,1536]{1,0:T(8,128)(2,1)S(1)}, bf16[128,1536]{1,0:T(8,128)(2,1)S(1)}, u32[]{:S(2)}, u32[]{:S(2)}) %collective-permute-start.27) | collective-permute-done | bytes 393248 | tf_op jit(solution)/shard_map/ppermute | solution.py:90
  141.2 7.7 %collective-permute-done.25.refs_1_ = bf16[128,1536]{1,0:T(8,128)(2,1)S(1)} collective-permute-done((bf16[128,1536]{1,0:T(8,128)(2,1)S(1)}, bf16[128,1536]{1,0:T(8,128)(2,1)S(1)}, u32[]{:S(2)}, u32[]{:S(2)}) %collective-permute-start.25) | collective-permute-done | bytes 393248 | tf_op jit(solution)/shard_map/ppermute | solution.py:88
  150.9 14.8 %collective-permute-start.20 = (bf16[128,1536]{1,0:T(8,128)(2,1)S(1)}, bf16[128,1536]{1,0:T(8,128)(2,1)S(1)}, u32[]{:S(2)}, u32[]{:S(2)}) collective-permute-start(bf16[128,1536]{1,0:T(8,128)(2,1)S(1)} %collective-permute-done.19.refs_3_), channel_id=1, source_target_pairs={{4,0},{8,12},{5,1},{9,13},{6,2},{10,14},{7,3},{11,15},{20,16},{24,... | collective-permute-start | bytes 1179656 | tf_op jit(solution)/shard_map/ppermute | solution.py:91
  169.1 5.9 %collective-permute-done.17.refs_1_ = bf16[128,1536]{1,0:T(8,128)(2,1)S(1)} collective-permute-done((bf16[128,1536]{1,0:T(8,128)(2,1)}, bf16[128,1536]{1,0:T(8,128)(2,1)S(1)}, u32[]{:S(2)}, u32[]{:S(2)}) %collective-permute-start.17) | collective-permute-done | bytes 393248 | tf_op jit(solution)/shard_map/ppermute | solution.py:88
  175.1 7.3 %collective-permute-done.18.refs_2_ = bf16[128,1536]{1,0:T(8,128)(2,1)S(1)} collective-permute-done((bf16[128,1536]{1,0:T(8,128)(2,1)}, bf16[128,1536]{1,0:T(8,128)(2,1)S(1)}, u32[]{:S(2)}, u32[]{:S(2)}) %collective-permute-start.18) | collective-permute-done | bytes 393248 | tf_op jit(solution)/shard_map/ppermute | solution.py:89
  182.3 16.8 %collective-permute-done.20.refs_4_ = bf16[128,1536]{1,0:T(8,128)(2,1)S(1)} collective-permute-done((bf16[128,1536]{1,0:T(8,128)(2,1)S(1)}, bf16[128,1536]{1,0:T(8,128)(2,1)S(1)}, u32[]{:S(2)}, u32[]{:S(2)}) %collective-permute-start.20) | collective-permute-done | bytes 393248 | tf_op jit(solution)/shard_map/ppermute | solution.py:91
  199.7 6.1 %collective-permute-start.30 = (bf16[128,1536]{1,0:T(8,128)(2,1)}, bf16[128,1536]{1,0:T(8,128)(2,1)}, u32[]{:S(2)}, u32[]{:S(2)}) collective-permute-start(bf16[128,1536]{1,0:T(8,128)(2,1)} %gate.7.refs_0_), channel_id=1, source_target_pairs={{4,0},{8,4},{12,8},{5,1},{9,5},{13,9},{6,2},{10,6},{14,10},{7,3},{... | collective-permute-start | bytes 1179656 | tf_op jit(solution)/shard_map/ppermute | solution.py:89
  209.9 5.9 %collective-permute-done.29.refs_1_ = bf16[128,1536]{1,0:T(8,128)(2,1)S(1)} collective-permute-done((bf16[128,1536]{1,0:T(8,128)(2,1)}, bf16[128,1536]{1,0:T(8,128)(2,1)S(1)}, u32[]{:S(2)}, u32[]{:S(2)}) %collective-permute-start.29) | collective-permute-done | bytes 393248 | tf_op jit(solution)/shard_map/ppermute | solution.py:88
  218.4 10.0 %collective-permute-start.24 = (bf16[128,1536]{1,0:T(8,128)(2,1)}, bf16[128,1536]{1,0:T(8,128)(2,1)}, u32[]{:S(2)}, u32[]{:S(2)}) collective-permute-start(bf16[128,1536]{1,0:T(8,128)(2,1)} %collective-permute-done.23.refs_3_), channel_id=1, source_target_pairs={{4,0},{8,12},{5,1},{9,13},{6,2},{10,14},{7,3},{11,15},{20,16},{24,... | collective-permute-start | bytes 1179656 | tf_op jit(solution)/shard_map/ppermute | solution.py:91
  234.4 4.4 %project_raw.1 = (bf16[512,2048]{1,0:T(8,128)(2,1)S(1)}, bf16[512,2048]{1,0:T(8,128)(2,1)}) custom-call(s32[20]{0:T(128)S(1)} %copy-done.31, bf16[512,256]{1,0:T(8,128)(2,1)S(1)} %attend.1.refs_0_, bf16[512,256]{1,0:T(8,128)(2,1)S(1)} %copy-done.20, bf16[512,256]{1,0:T(8,128)(2,1)S(1)} %copy-done.22, ...), custom_call_target="tpu_custom_call", output_to_operand_aliasing={{1}: (9, {})} | custom-call | flops 1 | bytes 1 | tf_op jit(solution)/shard_map/project_raw/pallas_call | solution.py:129
  238.9 3.4 %norm.4.refs_6_ = bf16[512,8192]{1,0:T(8,128)(2,1)} custom-call(s32[20]{0:T(128)S(1)} %copy-done.31, f32[1,8192]{1,0:T(1,128)S(1)} %bitcast.31, bf16[128,1536]{1,0:T(8,128)(2,1)S(1)} %get-tuple-element.27.refs_2_.refs_0_, bf16[128,1536]{1,0:T(8,128)(2,1)S(1)} %collective-permute-done.25.refs_1_, bf16[128,1536]{1,0:T(8,128)(2,1)S(1)} %copy-done.6, ...), custom_call_target="tpu_custom_call" | custom-call | flops 1 | bytes 1 | tf_op jit(solution)/shard_map/norm/pallas_call | solution.py:129
  242.3 3.4 %norm.5.refs_6_ = bf16[512,8192]{1,0:T(8,128)(2,1)} custom-call(s32[20]{0:T(128)S(1)} %copy-done.31, f32[1,8192]{1,0:T(1,128)S(1)} %bitcast.32, bf16[128,1536]{1,0:T(8,128)(2,1)S(1)} %copy-done.27, bf16[128,1536]{1,0:T(8,128)(2,1)S(1)} %copy-done.12, bf16[128,1536]{1,0:T(8,128)(2,1)S(1)} %copy-done.14, ...), custom_call_target="tpu_custom_call", output_to_operand_aliasing={{}: (8, {})} | custom-call | flops 1 | bytes 1 | tf_op jit(solution)/shard_map/norm/pallas_call | solution.py:129
  245.8 5.1 %norm.6.refs_6_ = bf16[512,8192]{1,0:T(8,128)(2,1)} custom-call(s32[20]{0:T(128)S(1)} %copy-done.31, f32[1,8192]{1,0:T(1,128)S(1)} %bitcast.33, bf16[128,1536]{1,0:T(8,128)(2,1)} %gate.7.refs_0_, bf16[128,1536]{1,0:T(8,128)(2,1)S(1)} %copy-done.29, bf16[128,1536]{1,0:T(8,128)(2,1)} %collective-permute-done.30.refs_2_, ...), custom_call_target="tpu_custom_call", output_to_operand_aliasing={{}: (8, {})} | custom-call | flops 1 | bytes 1 | tf_op jit(solution)/shard_map/norm/pallas_call | solution.py:129
  250.8 5.1 %norm.7 = bf16[512,8192]{1,0:T(8,128)(2,1)} custom-call(s32[20]{0:T(128)S(1)} %copy-done.31, f32[1,8192]{1,0:T(1,128)S(1)} %bitcast.34, bf16[128,1536]{1,0:T(8,128)(2,1)} %gate.6.refs_0_, bf16[128,1536]{1,0:T(8,128)(2,1)} %collective-permute-done.21.refs_1_, bf16[128,1536]{1,0:T(8,128)(2,1)} %collective-permute-done.22.refs_2_, ...), custom_call_target="tpu_custom_call", output_to_operand_aliasing={{}: (8, {})} | custom-call | flops 1 | bytes 1 | tf_op jit(solution)/shard_map/norm/pallas_call | solution.py:129
  (138 shorter events, 56.0 us)
Async XLA Ops:
  7.2 98.9 %all-gather.6.cloned.1.call-start = ((), (), s32[]{:S(2)}) async-start(), calls=%async_computation | async-start | bytes 1966080 | tf_op jit(solution)/shard_map/all_gather | solution.py:549
  14.8 26.3 %collective-permute-start.1 = (bf16[1552,256]{1,0:T(8,128)(2,1)}, bf16[1552,256]{1,0:T(8,128)(2,1)S(1)}, u32[]{:S(2)}, u32[]{:S(2)}) collective-permute-start(bf16[1552,256]{1,0:T(8,128)(2,1)} %get-tuple-element.19.refs_0_), channel_id=1, source_target_pairs={{0,2},{1,3},{2,0},{3,1},{4,6},{5,7},{6,4},{7,5},{8,10},{9,11},{10,... | collective-permute-start | bytes 2383880 | tf_op jit(solution)/shard_map/ppermute | solution.py:42
  15.3 39.6 %collective-permute-start = (bf16[1552,256]{1,0:T(8,128)(2,1)}, bf16[1552,256]{1,0:T(8,128)(2,1)}, u32[]{:S(2)}, u32[]{:S(2)}) collective-permute-start(bf16[1552,256]{1,0:T(8,128)(2,1)} %get-tuple-element.19.refs_0_), channel_id=1, source_target_pairs={{0,1},{1,0},{2,3},{3,2},{4,5},{5,4},{6,7},{7,6},{8,9},{9,8},{10,11... | collective-permute-start | bytes 2383880 | tf_op jit(solution)/shard_map/ppermute | solution.py:42
  41.8 186.7 %all-gather.8.cloned.1.call-start = ((), (), s32[]{:S(2)}) async-start(), calls=%async_computation.1 | async-start | bytes 4325376 | tf_op jit(solution)/shard_map/all_gather | solution.py:568
  43.4 27.4 %collective-permute-start.13 = (bf16[4,32,1536]{2,1,0:T(8,128)(2,1)S(1)}, bf16[4,32,1536]{2,1,0:T(8,128)(2,1)S(1)}, u32[]{:S(2)}, u32[]{:S(2)}) collective-permute-start(bf16[4,32,1536]{2,1,0:T(8,128)(2,1)S(1)} %stack.89.refs_1_.refs_5_), channel_id=1, source_target_pairs={{0,16},{16,0},{1,17},{17,1},{2,18},{18,2},{3,19},{19,3},{4,20},{20... | collective-permute-start | bytes 1179656 | tf_op jit(solution)/shard_map/ppermute | solution.py:75
  44.9 26.4 %collective-permute-start.10 = (bf16[4,32,1536]{2,1,0:T(8,128)(2,1)S(1)}, bf16[4,32,1536]{2,1,0:T(8,128)(2,1)S(1)}, u32[]{:S(2)}, u32[]{:S(2)}) collective-permute-start(bf16[4,32,1536]{2,1,0:T(8,128)(2,1)S(1)} %stack.89.refs_1_.refs_5_), channel_id=1, source_target_pairs={{0,1},{1,0},{2,3},{3,2},{4,5},{5,4},{6,7},{7,6},{8,9},{9,8},{10,11... | collective-permute-start | bytes 1179656 | tf_op jit(solution)/shard_map/ppermute | solution.py:75
  70.8 22.8 %collective-permute-start.14 = (bf16[4,32,1536]{2,1,0:T(8,128)(2,1)S(1)}, bf16[4,32,1536]{2,1,0:T(8,128)(2,1)S(1)}, u32[]{:S(2)}, u32[]{:S(2)}) collective-permute-start(bf16[4,32,1536]{2,1,0:T(8,128)(2,1)S(1)} %collective-permute-done.13.refs_9_), channel_id=1, source_target_pairs={{0,1},{1,0},{2,3},{3,2},{4,5},{5,4},{6,7},{7,6},{8,9},{9,8},{10,11... | collective-permute-start | bytes 1179656 | tf_op jit(solution)/shard_map/ppermute | solution.py:75
  71.0 22.6 %collective-permute-start.16 = (bf16[4,32,1536]{2,1,0:T(8,128)(2,1)S(1)}, bf16[4,32,1536]{2,1,0:T(8,128)(2,1)S(1)}, u32[]{:S(2)}, u32[]{:S(2)}) collective-permute-start(bf16[4,32,1536]{2,1,0:T(8,128)(2,1)S(1)} %collective-permute-done.15.refs_11_), channel_id=1, source_target_pairs={{0,1},{1,0},{2,3},{3,2},{4,5},{5,4},{6,7},{7,6},{8,9},{9,8},{10,11... | collective-permute-start | bytes 1179656 | tf_op jit(solution)/shard_map/ppermute | solution.py:75
  71.3 24.5 %collective-permute-start.6 = (bf16[512,256]{1,0:T(8,128)(2,1)S(1)}, bf16[512,256]{1,0:T(8,128)(2,1)S(1)}, u32[]{:S(2)}, u32[]{:S(2)}) collective-permute-start(bf16[512,256]{1,0:T(8,128)(2,1)S(1)} %attend.1.refs_0_), channel_id=1, source_target_pairs={{0,4},{4,8},{8,12},{1,5},{5,9},{9,13},{2,6},{6,10},{10,14},{3,7},{... | collective-permute-start | bytes 786440 | tf_op jit(solution)/shard_map/ppermute | solution.py:88
  108.0 30.0 %collective-permute-start.27 = (bf16[128,1536]{1,0:T(8,128)(2,1)S(1)}, bf16[128,1536]{1,0:T(8,128)(2,1)S(1)}, u32[]{:S(2)}, u32[]{:S(2)}) collective-permute-start(bf16[128,1536]{1,0:T(8,128)(2,1)S(1)} %get-tuple-element.27.refs_2_.refs_0_), channel_id=1, source_target_pairs={{0,8},{4,12},{8,0},{12,4},{1,9},{5,13},{9,1},{13,5},{2,10},{6,14},... | collective-permute-start | bytes 1179656 | tf_op jit(solution)/shard_map/ppermute | solution.py:90
  111.7 37.3 %collective-permute-start.25 = (bf16[128,1536]{1,0:T(8,128)(2,1)S(1)}, bf16[128,1536]{1,0:T(8,128)(2,1)S(1)}, u32[]{:S(2)}, u32[]{:S(2)}) collective-permute-start(bf16[128,1536]{1,0:T(8,128)(2,1)S(1)} %get-tuple-element.27.refs_2_.refs_0_), channel_id=1, source_target_pairs={{0,4},{4,8},{8,12},{1,5},{5,9},{9,13},{2,6},{6,10},{10,14},{3,7},{... | collective-permute-start | bytes 1179656 | tf_op jit(solution)/shard_map/ppermute | solution.py:88
  113.6 37.3 %collective-permute-start.19 = (bf16[128,1536]{1,0:T(8,128)(2,1)}, bf16[128,1536]{1,0:T(8,128)(2,1)S(1)}, u32[]{:S(2)}, u32[]{:S(2)}) collective-permute-start(bf16[128,1536]{1,0:T(8,128)(2,1)} %copy-done.26), channel_id=1, source_target_pairs={{0,8},{4,12},{8,0},{12,4},{1,9},{5,13},{9,1},{13,5},{2,10},{6,14},... | collective-permute-start | bytes 1179656 | tf_op jit(solution)/shard_map/ppermute | solution.py:90
  115.5 50.2 %collective-permute-start.26 = (bf16[128,1536]{1,0:T(8,128)(2,1)S(1)}, bf16[128,1536]{1,0:T(8,128)(2,1)S(1)}, u32[]{:S(2)}, u32[]{:S(2)}) collective-permute-start(bf16[128,1536]{1,0:T(8,128)(2,1)S(1)} %get-tuple-element.27.refs_2_.refs_0_), channel_id=1, source_target_pairs={{4,0},{8,4},{12,8},{5,1},{9,5},{13,9},{6,2},{10,6},{14,10},{7,3},{... | collective-permute-start | bytes 1179656 | tf_op jit(solution)/shard_map/ppermute | solution.py:89
  138.0 27.7 %collective-permute-start.28 = (bf16[128,1536]{1,0:T(8,128)(2,1)S(1)}, bf16[128,1536]{1,0:T(8,128)(2,1)S(1)}, u32[]{:S(2)}, u32[]{:S(2)}) collective-permute-start(bf16[128,1536]{1,0:T(8,128)(2,1)S(1)} %collective-permute-done.27.refs_3_), channel_id=1, source_target_pairs={{4,0},{8,12},{5,1},{9,13},{6,2},{10,14},{7,3},{11,15},{20,16},{24,... | collective-permute-start | bytes 1179656 | tf_op jit(solution)/shard_map/ppermute | solution.py:91
  139.3 35.7 %collective-permute-start.17 = (bf16[128,1536]{1,0:T(8,128)(2,1)}, bf16[128,1536]{1,0:T(8,128)(2,1)S(1)}, u32[]{:S(2)}, u32[]{:S(2)}) collective-permute-start(bf16[128,1536]{1,0:T(8,128)(2,1)} %copy-done.26), channel_id=1, source_target_pairs={{0,4},{4,8},{8,12},{1,5},{5,9},{9,13},{2,6},{6,10},{10,14},{3,7},{... | collective-permute-start | bytes 1179656 | tf_op jit(solution)/shard_map/ppermute | solution.py:88
  148.9 33.4 %collective-permute-start.18 = (bf16[128,1536]{1,0:T(8,128)(2,1)}, bf16[128,1536]{1,0:T(8,128)(2,1)S(1)}, u32[]{:S(2)}, u32[]{:S(2)}) collective-permute-start(bf16[128,1536]{1,0:T(8,128)(2,1)} %copy-done.26), channel_id=1, source_target_pairs={{4,0},{8,4},{12,8},{5,1},{9,5},{13,9},{6,2},{10,6},{14,10},{7,3},{... | collective-permute-start | bytes 1179656 | tf_op jit(solution)/shard_map/ppermute | solution.py:89
  150.9 48.2 %collective-permute-start.20 = (bf16[128,1536]{1,0:T(8,128)(2,1)S(1)}, bf16[128,1536]{1,0:T(8,128)(2,1)S(1)}, u32[]{:S(2)}, u32[]{:S(2)}) collective-permute-start(bf16[128,1536]{1,0:T(8,128)(2,1)S(1)} %collective-permute-done.19.refs_3_), channel_id=1, source_target_pairs={{4,0},{8,12},{5,1},{9,13},{6,2},{10,14},{7,3},{11,15},{20,16},{24,... | collective-permute-start | bytes 1179656 | tf_op jit(solution)/shard_map/ppermute | solution.py:91
  167.2 40.6 %collective-permute-start.31 = (bf16[128,1536]{1,0:T(8,128)(2,1)}, bf16[128,1536]{1,0:T(8,128)(2,1)}, u32[]{:S(2)}, u32[]{:S(2)}) collective-permute-start(bf16[128,1536]{1,0:T(8,128)(2,1)} %gate.7.refs_0_), channel_id=1, source_target_pairs={{0,8},{4,12},{8,0},{12,4},{1,9},{5,13},{9,1},{13,5},{2,10},{6,14},... | collective-permute-start | bytes 1179656 | tf_op jit(solution)/shard_map/ppermute | solution.py:90
  167.2 48.5 %collective-permute-start.29 = (bf16[128,1536]{1,0:T(8,128)(2,1)}, bf16[128,1536]{1,0:T(8,128)(2,1)S(1)}, u32[]{:S(2)}, u32[]{:S(2)}) collective-permute-start(bf16[128,1536]{1,0:T(8,128)(2,1)} %gate.7.refs_0_), channel_id=1, source_target_pairs={{0,4},{4,8},{8,12},{1,5},{5,9},{9,13},{2,6},{6,10},{10,14},{3,7},{... | collective-permute-start | bytes 1179656 | tf_op jit(solution)/shard_map/ppermute | solution.py:88
  199.7 46.0 %collective-permute-start.30 = (bf16[128,1536]{1,0:T(8,128)(2,1)}, bf16[128,1536]{1,0:T(8,128)(2,1)}, u32[]{:S(2)}, u32[]{:S(2)}) collective-permute-start(bf16[128,1536]{1,0:T(8,128)(2,1)} %gate.7.refs_0_), channel_id=1, source_target_pairs={{4,0},{8,4},{12,8},{5,1},{9,5},{13,9},{6,2},{10,6},{14,10},{7,3},{... | collective-permute-start | bytes 1179656 | tf_op jit(solution)/shard_map/ppermute | solution.py:89
  205.9 45.0 %collective-permute-start.21 = (bf16[128,1536]{1,0:T(8,128)(2,1)}, bf16[128,1536]{1,0:T(8,128)(2,1)}, u32[]{:S(2)}, u32[]{:S(2)}) collective-permute-start(bf16[128,1536]{1,0:T(8,128)(2,1)} %gate.6.refs_0_), channel_id=1, source_target_pairs={{0,4},{4,8},{8,12},{1,5},{5,9},{9,13},{2,6},{6,10},{10,14},{3,7},{... | collective-permute-start | bytes 1179656 | tf_op jit(solution)/shard_map/ppermute | solution.py:88
  207.8 37.9 %collective-permute-start.32 = (bf16[128,1536]{1,0:T(8,128)(2,1)}, bf16[128,1536]{1,0:T(8,128)(2,1)}, u32[]{:S(2)}, u32[]{:S(2)}) collective-permute-start(bf16[128,1536]{1,0:T(8,128)(2,1)} %collective-permute-done.31.refs_3_), channel_id=1, source_target_pairs={{4,0},{8,12},{5,1},{9,13},{6,2},{10,14},{7,3},{11,15},{20,16},{24,... | collective-permute-start | bytes 1179656 | tf_op jit(solution)/shard_map/ppermute | solution.py:91
  216.5 34.3 %collective-permute-start.22 = (bf16[128,1536]{1,0:T(8,128)(2,1)}, bf16[128,1536]{1,0:T(8,128)(2,1)}, u32[]{:S(2)}, u32[]{:S(2)}) collective-permute-start(bf16[128,1536]{1,0:T(8,128)(2,1)} %gate.6.refs_0_), channel_id=1, source_target_pairs={{4,0},{8,4},{12,8},{5,1},{9,5},{13,9},{6,2},{10,6},{14,10},{7,3},{... | collective-permute-start | bytes 1179656 | tf_op jit(solution)/shard_map/ppermute | solution.py:89
  218.4 32.4 %collective-permute-start.24 = (bf16[128,1536]{1,0:T(8,128)(2,1)}, bf16[128,1536]{1,0:T(8,128)(2,1)}, u32[]{:S(2)}, u32[]{:S(2)}) collective-permute-start(bf16[128,1536]{1,0:T(8,128)(2,1)} %collective-permute-done.23.refs_3_), channel_id=1, source_target_pairs={{4,0},{8,12},{5,1},{9,13},{6,2},{10,14},{7,3},{11,15},{20,16},{24,... | collective-permute-start | bytes 1179656 | tf_op jit(solution)/shard_map/ppermute | solution.py:91
  (46 other events, 642.4 us)
Sparse Core Ops, SparseCore 0:
  41.9 45.5 all-gather.5
  108.1 89.6 all-gather.7

commit v4 on v3

--- a/solution.py
+++ b/solution.py
@@ -57,7 +57,7 @@
     return [(me + count - shift) % count for shift in range(count)]
 
 
-def plane_gather(value, groups, contexts):
+def plane_gather(value, groups, contexts, between=lambda block: block):
     count = groups * contexts
     if count & (count - 1):
         gathered = lax.all_gather(value, ("groups", "context"), axis=0, tiled=False)
@@ -73,6 +73,8 @@
         pairs = [(i, i ^ flip) for i in range(size)]
         for mask in sorted(held):
             held[mask | bit] = lax.ppermute(held[mask], axis, pairs)
+        if bit == bits[0]:
+            held[bit] = between(held[bit])
     return [held[mask] for mask in range(count)]
 
 
@@ -137,7 +139,7 @@
         ),
         out_shape=out_shape,
         input_output_aliases=aliases or {},
-        compiler_params=pltpu.CompilerParams(vmem_limit_bytes=vmem * MIB),
+        compiler_params=pltpu.CompilerParams(vmem_limit_bytes=vmem * MIB or None),
         cost_estimate=pl.CostEstimate(flops=flops, bytes_accessed=1, transcendentals=0),
         name=name,
     )(info, *args)
@@ -149,11 +151,7 @@
 
 
 def prepare_kernel(info, q_ref, kv_ref, cache_ref, cos_ref, sin_ref, length_ref, *refs):
-    q_out, kv_out = refs[1:3] if len(refs) > 2 else refs
-    if len(refs) > 2:
-        rows_early = refs[3].shape[0]
-        refs[3][...] = refs[0][:rows_early]
-        refs[4][...] = refs[0][rows_early:]
+    q_out, kv_out = refs[-2:]
     cosine, sine = cos_ref[...], sin_ref[...]
     slots, rows = cache_ref.shape[0], q_ref.shape[0]
     span, tail = slice(slots, slots + rows), slice(slots + rows, slots + rows + TAIL)
@@ -175,66 +173,83 @@
         q_out[:, cols] = turn(q_ref[:, cols])
 
 
-def cut_kernel(table, slab, keep, info, w_ref, *outs):
+def cut_kernel(table, slab, keep, info, w_ref, r_ref, *refs):
+    count, raw = table.count, slab - keep
+    outs, rows_ref, sems = refs[:count], refs[-2], refs[-1]
+    part = rows_ref.shape[0]
+    start = pl.multiple_of(info[table.share] * part, part)
+    copies = [pltpu.make_async_copy(w_ref.at[pl.ds(start, part)], rows_ref, sems.at[0])]
+    if raw:
+        source = r_ref.at[:, pl.ds(keep, raw)]
+        copies.append(pltpu.make_async_copy(source, refs[count], sems.at[1]))
+    for copy in copies:
+        copy.start()
+    copies[0].wait()
+    for d, out in enumerate(outs):
+        target = lax.rem(info[table.place] + d, count)
+        out[:, :keep] = rows_ref[:, pl.ds(pl.multiple_of(target * slab, slab), keep)]
+        for j in range(count if raw else 0):
+            out[:, keep + j * raw : keep + (j + 1) * raw] = rows_ref[
+                :, j * slab + keep : (j + 1) * slab
+            ]
+    if raw:
+        copies[1].wait()
+
+
+def cut(table, info, out_weight, residual, part, keep):
+    rows, slab = residual.shape
     raw = slab - keep
-    for d in range(table.count):
-        target = lax.rem(info[table.place] + d, table.count)
-        outs[d][...] = w_ref[:, pl.ds(pl.multiple_of(target * slab, slab), keep)]
-    for j in range(table.count if raw else 0):
-        outs[-1][:, j * raw : (j + 1) * raw] = w_ref[:, j * slab + keep : (j + 1) * slab]
-
-
-def cut(table, info, out_weight, part, slab, keep):
-    shapes = [jax.ShapeDtypeStruct((part, keep), out_weight.dtype)] * table.count
-    if keep < slab:
-        shapes.append(
-            jax.ShapeDtypeStruct((part, table.count * (slab - keep)), out_weight.dtype)
-        )
+    width = keep + table.count * raw
+    shapes = [jax.ShapeDtypeStruct((part, width), out_weight.dtype)] * table.count
+    if raw:
+        shapes.append(jax.ShapeDtypeStruct((rows, raw), residual.dtype))
     return call(
         functools.partial(cut_kernel, table, slab, keep),
         "cut",
         info,
-        [out_weight],
-        [pl.BlockSpec((part, out_weight.shape[1]), lambda i, info: (info[table.share], 0))],
+        [out_weight, residual],
+        [pl.BlockSpec(memory_space=pltpu.HBM)] * 2,
         [whole(shape) for shape in shapes],
         shapes,
-    )
-
-
-def prepare(info, queries, span_pairs, cache, cosine, sine, lengths, residual, raw, rows_early):
-    rows, slab = residual.shape
+        scratch=[
+            pltpu.VMEM((part, out_weight.shape[1]), out_weight.dtype),
+            pltpu.SemaphoreType.DMA((2,)),
+        ],
+        vmem=0,
+    )
+
+
+def prepare(info, queries, span_pairs, cache, cosine, sine, lengths, after):
+    rows = queries.shape[0]
     shapes = [
         jax.ShapeDtypeStruct(queries.shape, jnp.bfloat16),
         jax.ShapeDtypeStruct((cache.shape[0] + rows + TAIL, 2 * HD), jnp.bfloat16),
     ]
     args = [queries, span_pairs, cache, cosine, sine, lengths]
-    in_specs = [whole(a) for a in args[:-1]] + [pl.BlockSpec(memory_space=pltpu.SMEM)]
-    if raw:
-        shapes.append(jax.ShapeDtypeStruct((rows_early, raw), residual.dtype))
-        shapes.append(jax.ShapeDtypeStruct((rows - rows_early, raw), residual.dtype))
-        args.append(residual)
-        in_specs.append(pl.BlockSpec((rows, raw), lambda i, info: (0, slab // raw - 1)))
     return call(
         prepare_kernel,
         "prepare",
         info,
-        args,
-        in_specs,
+        [*args, *after],
+        [whole(a) for a in args[:-1]]
+        + [pl.BlockSpec(memory_space=pltpu.SMEM)]
+        + [ANYWHERE] * len(after),
         [whole(shape) for shape in shapes],
         shapes,
-        vmem=58,
-    )
-
-
-def stack_kernel(count, info, *refs):
+        vmem=32,
+    )
+
+
+def stack_kernel(count, begin, info, *refs):
+    width = refs[-1].shape[2]
     for number, part in enumerate(refs[:count]):
-        refs[-1][number] = part[...]
-
-
-def stack(info, parts, after):
-    shape = jax.ShapeDtypeStruct((len(parts), *parts[0].shape), parts[0].dtype)
-    return call(
-        functools.partial(stack_kernel, len(parts)),
+        refs[-1][number] = part[:, begin : begin + width]
+
+
+def stack(info, parts, begin, width, after=()):
+    shape = jax.ShapeDtypeStruct((len(parts), parts[0].shape[0], width), parts[0].dtype)
+    return call(
+        functools.partial(stack_kernel, len(parts), begin),
         "stack",
         info,
         [*parts, *after],
@@ -343,11 +358,11 @@
     )
 
 
-def project_kernel(table, lines, shares, keep, info, *refs):
+def project_kernel(table, lines, shares, keep, chunks, info, *refs):
     count = table.count
     attention, pieces = refs[:lines], refs[lines : lines + shares]
     r_ref = refs[lines + shares]
-    parts, h_ref, w_ref = refs[lines + shares + 1 : -2], refs[-2], refs[-1]
+    parts, h_ref, w_ref = refs[-2 - chunks : -2], refs[-2], refs[-1]
     part_rows = pieces[0].shape[1]
 
     @pl.when(pl.program_id(0) == 0)
@@ -370,7 +385,7 @@
             part[...] = result
 
 
-def project(table, info, attention, pieces, residual, rows):
+def project(table, info, attention, pieces, residual, rows, after):
     all_rows, slab = residual.shape
     count, part_rows, keep = pieces[0].shape
     depth = len(pieces) * part_rows
@@ -379,11 +394,14 @@
     hidden = jax.ShapeDtypeStruct(residual.shape, jnp.bfloat16)
     row_spec = pl.BlockSpec((rows, slab), lambda i, info: (i, 0))
     return call(
-        functools.partial(project_kernel, table, len(attention), len(pieces), keep),
+        functools.partial(project_kernel, table, len(attention), len(pieces), keep, chunks),
         "project",
         info,
-        [*attention, *pieces, residual],
-        line_spec(attention, rows, lambda i: i) + [whole(p) for p in pieces] + [row_spec],
+        [*attention, *pieces, residual, *after],
+        line_spec(attention, rows, lambda i: i)
+        + [whole(p) for p in pieces]
+        + [row_spec]
+        + [ANYWHERE] * len(after),
         [whole(part)] * chunks + [row_spec],
         [part] * chunks + [hidden],
         grid=(chunks,),
@@ -394,8 +412,7 @@
 
 def project_raw_kernel(table, lines, info, *refs):
     count = table.count
-    attention, (early, late) = refs[:lines], refs[lines : lines + 2]
-    w_ref = refs[lines + 2]
+    attention, r_ref, w_ref = refs[:lines], refs[lines], refs[lines + 1]
     raw_ref, h_ref = refs[-2:]
     raw = h_ref.shape[1]
     blocks = [
@@ -404,13 +421,9 @@
     for slab in range(count):
         place = info[table.place + slab]
         start = pl.multiple_of(place * raw, raw)
-        total = jnp.where(
-            pl.program_id(0) == 0,
-            early[place].astype(jnp.float32),
-            late[place].astype(jnp.float32),
-        )
+        total = r_ref[place].astype(jnp.float32)
         for d in range(count):
-            weight = w_ref[info[table.place + d], :, :, pl.ds(start, raw)]
+            weight = w_ref[:, d, :, pl.ds(start, raw)]
             weight = weight.reshape(blocks[d].shape[1], raw)
             total = total + jnp.dot(blocks[d], weight, preferred_element_type=jnp.float32)
         result = total.astype(jnp.bfloat16)
@@ -431,8 +444,7 @@
         args,
         line_spec(attention, rows, lambda i: i)
         + [
-            pl.BlockSpec((count, rows, raw), lambda i, info: (0, 0, 0)),
-            pl.BlockSpec((count, rows, raw), lambda i, info: (0, jnp.maximum(i - 1, 0), 0)),
+            pl.BlockSpec((count, rows, raw), lambda i, info: (0, i, 0)),
             whole(weights),
             ANYWHERE,
         ],
@@ -533,45 +545,44 @@
     both = jnp.concatenate([frequencies(HD)] * 2)
     angles = positions.astype(jnp.float32)[:, None] * both[None, :]
     sign = jnp.where(jnp.arange(HD) < HD // 2, -1.0, 1.0)
-    q_turned, payload, *residual_raw = prepare(
-        info, queries, span_local, cache_local, jnp.cos(angles),
-        jnp.sin(angles) * sign[None, :], lengths, residual, raw, chunk,
-    )
-    cuts = cut(table, info, out_weight, depth // shares, slab, keep)
+    cuts = cut(table, info, out_weight, residual, depth // shares, keep)
     parts = [cuts[0]]
     for shift in range(1, count):
         pairs = [(i, (i + shift) % count) for i in range(count)]
         parts.append(lax.ppermute(cuts[shift], "tensor", pairs))
-    own_weights = stack(info, parts, [])
-    early, late = [], []
+    residuals = []
     if raw:
-        early = [lax.all_gather(residual_raw[0], "tensor", axis=0, tiled=False)]
-        late = [lax.all_gather(residual_raw[1], "tensor", axis=0, tiled=False)]
+        residuals = [lax.all_gather(cuts[count], "tensor", axis=0, tiled=False)]
+    own_weights = stack(info, parts, 0, keep)
+
+    q_turned, payload = prepare(
+        info, queries, span_local, cache_local, jnp.cos(angles),
+        jnp.sin(angles) * sign[None, :], lengths, cuts[:1],
+    )
     pieces = pieces_of(
-        payload, "context", contexts, lambda block: gate(info, block, [own_weights, *early])
-    )
-
+        payload, "context", contexts, lambda block: gate(info, block, [own_weights])
+    )
     mixed = attend(table, info, q_turned, pieces, cache_local.shape[0], chunk)
     weight_pieces = plane_gather(own_weights, groups, contexts)
     attention = line_gather(mixed, count)
 
-    *hidden_parts, hidden = project(table, info, attention, weight_pieces, residual, chunk)
+    *hidden_parts, hidden = project(
+        table, info, attention, weight_pieces, residual, chunk, residuals
+    )
+    raw_hidden = None
+    if raw:
+        raw_weights = stack(info, parts, keep, count * raw, [mixed])
+        raw_weights = lax.all_gather(raw_weights, ("groups", "context"), axis=0, tiled=False)
+        raw_hidden, hidden = project_raw(
+            table, info, attention, residuals, raw_weights, hidden, raw, chunk
+        )
     lines = []
     for number in range(chunks):
         value = hidden_parts[number]
         if number > 1:
-            value = gate(info, value, lines[number - 2][1:])
+            made = [raw_hidden] if raw and number == chunks - 1 else []
+            value = gate(info, value, [*lines[number - 2][1:], *made])
         lines.append(line_gather(value, count))
-    raw_hidden = None
-    if raw:
-        raw_weights = gate(info, cuts[-1], [*late, hidden_parts[0]])
-        raw_weights = lax.all_gather(
-            raw_weights, ("tensor", "groups", "context"), axis=0, tiled=False
-        )
-        raw_weights = raw_weights.reshape(count, shares, *cuts[-1].shape)
-        raw_hidden, hidden = project_raw(
-            table, info, attention, [*early, *late], raw_weights, hidden, raw, chunk
-        )
     normed = None
     for number in range(chunks):
         normed = norm_into(

time: 264 us -> 273 us (1.034)
  the two profiles are of different devices: /device:TPU:18 before, /device:TPU:0 now
where the time goes in v4:
time: 273 us; the launch traced here: 272 us
  waiting for transfers between devices  95.7 us (35%)
  starting transfers between devices  85.2 us (31%)
  Pallas kernels  45.2 us (17%)
  local copies, waits for them, and re-layouts  28.8 us (11%)
  between operations  15.8 us (6%)
    pallas_call x14, Pallas kernels, call(): pl.pallas_call(kernel, grid_spec=pltpu.PrefetchScalarGridSpec(num_scalar_...  45.2 us
    ppermute x5, starting transfers between devices, line_gather(): far = lax.ppermute(value, 'tensor', [(0, 2), (1, 3), (2, 0), (3, 1)])  32.8 us
    ppermute x5, waiting for transfers between devices, line_gather(): far = lax.ppermute(value, 'tensor', [(0, 2), (1, 3), (2, 0), (3, 1)])  31 us
    unnamed x74, local copies, waits for them, and re-layouts  28.2 us
    ppermute x5, starting transfers between devices, line_gather(): up = lax.ppermute(value, 'tensor', [(0, 1), (1, 2), (2, 3)])  27 us
    ppermute x3, waiting for transfers between devices, per_device(): parts.append(lax.ppermute(cuts[shift], 'tensor', pairs))  24.6 us
    ppermute x5, waiting for transfers between devices, line_gather(): last = lax.ppermute(far, 'tensor', [(1, 0), (2, 3)])  18.5 us
    ppermute x7, waiting for transfers between devices, plane_gather(): held[mask | bit] = lax.ppermute(held[mask], axis, pairs)  9.62 us
  transfers between devices with their start and end apart: 35, of which 15 were waited for; matrix products, arithmetic and copies ran while one was open for 0% of the time, Pallas kernels for 14%

profile of v4, /device:TPU:0, one launch (start us, length us, event | category | flops | bytes accessed | tf_op | source)
XLA Modules:
  0.0 271.8 jit_solution(6444914902903411388)
XLA Ops:
  23.8 7.7 %collective-permute-done.2.refs_1_ = bf16[32,3584]{1,0:T(8,128)(2,1)S(1)} collective-permute-done((bf16[32,3584]{1,0:T(8,128)(2,1)}, bf16[32,3584]{1,0:T(8,128)(2,1)S(1)}, u32[]{:S(2)}, u32[]{:S(2)}) %collective-permute-start.2) | collective-permute-done | bytes 229408 | tf_op jit(solution)/shard_map/ppermute | solution.py:552
  31.5 16.4 %collective-permute-done.3.refs_2_ = bf16[32,3584]{1,0:T(8,128)(2,1)S(1)} collective-permute-done((bf16[32,3584]{1,0:T(8,128)(2,1)}, bf16[32,3584]{1,0:T(8,128)(2,1)S(1)}, u32[]{:S(2)}, u32[]{:S(2)}) %collective-permute-start.3) | collective-permute-done | bytes 229408 | tf_op jit(solution)/shard_map/ppermute | solution.py:552
  51.9 12.2 %attend.1.refs_4_.refs_0_ = bf16[512,256]{1,0:T(8,128)(2,1)S(1)} custom-call(s32[20]{0:T(128)S(1)} %copy-done.36, bf16[512,256]{1,0:T(8,128)(2,1)S(1)} %get-tuple-element.17.q_ref, bf16[1552,256]{1,0:T(8,128)(2,1)S(1)} %get-tuple-element.18.refs_0_, bf16[1552,256]{1,0:T(8,128)(2,1)S(1)} %collective-permute-done.refs_1_, bf16[1552,256]{1,0:T(8,128)(2,1)S(1)} %gate.3.refs_2_, ...), custom_call_target="tpu_custom_call" | custom-call | flops 12884901888 | bytes 1 | tf_op jit(solution)/shard_map/attend/pallas_call | solution.py:131
  67.1 9.6 %collective-permute-done.11.refs_7_ = bf16[4,32,1536]{2,1,0:T(8,128)(2,1)S(1)} collective-permute-done((bf16[4,32,1536]{2,1,0:T(8,128)(2,1)S(1)}, bf16[4,32,1536]{2,1,0:T(8,128)(2,1)S(1)}, u32[]{:S(2)}, u32[]{:S(2)}) %collective-permute-start.11) | collective-permute-done | bytes 393248 | tf_op jit(solution)/shard_map/ppermute | solution.py:75
  79.3 16.8 %collective-permute-start.8 = (bf16[512,256]{1,0:T(8,128)(2,1)S(1)}, bf16[512,256]{1,0:T(8,128)(2,1)S(1)}, u32[]{:S(2)}, u32[]{:S(2)}) collective-permute-start(bf16[512,256]{1,0:T(8,128)(2,1)S(1)} %attend.1.refs_4_.refs_0_), channel_id=1, source_target_pairs={{0,8},{4,12},{8,0},{12,4},{1,9},{5,13},{9,1},{13,5},{2,10},{6,14},... | collective-permute-start | bytes 786440 | tf_op jit(solution)/shard_map/ppermute | solution.py:92
  99.0 13.6 %collective-permute-start.6 = (bf16[512,256]{1,0:T(8,128)(2,1)S(1)}, bf16[512,256]{1,0:T(8,128)(2,1)S(1)}, u32[]{:S(2)}, u32[]{:S(2)}) collective-permute-start(bf16[512,256]{1,0:T(8,128)(2,1)S(1)} %attend.1.refs_4_.refs_0_), channel_id=1, source_target_pairs={{0,4},{4,8},{8,12},{1,5},{5,9},{9,13},{2,6},{6,10},{10,14},{3,7},{... | collective-permute-start | bytes 786440 | tf_op jit(solution)/shard_map/ppermute | solution.py:90
  119.4 4.9 %collective-permute-done.7.refs_2_ = bf16[512,256]{1,0:T(8,128)(2,1)S(1)} collective-permute-done((bf16[512,256]{1,0:T(8,128)(2,1)S(1)}, bf16[512,256]{1,0:T(8,128)(2,1)S(1)}, u32[]{:S(2)}, u32[]{:S(2)}) %collective-permute-start.7) | collective-permute-done | bytes 262176 | tf_op jit(solution)/shard_map/ppermute | solution.py:91
  125.1 4.2 %collective-permute-done.9.refs_4_ = bf16[512,256]{1,0:T(8,128)(2,1)S(1)} collective-permute-done((bf16[512,256]{1,0:T(8,128)(2,1)S(1)}, bf16[512,256]{1,0:T(8,128)(2,1)S(1)}, u32[]{:S(2)}, u32[]{:S(2)}) %collective-permute-start.9) | collective-permute-done | bytes 262176 | tf_op jit(solution)/shard_map/ppermute | solution.py:93
  141.4 4.5 %project.1 = (bf16[128,1536]{1,0:T(8,128)(2,1)S(1)}, bf16[128,1536]{1,0:T(8,128)(2,1)}, bf16[128,1536]{1,0:T(8,128)(2,1)}, bf16[128,1536]{1,0:T(8,128)(2,1)S(1)}, bf16[512,2048]{1,0:T(8,128)(2,1)}) custom-call(s32[20]{0:T(128)S(1)} %copy-done.36, bf16[512,256]{1,0:T(8,128)(2,1)S(1)} %attend.1.refs_4_.refs_0_, bf16[512,256]{1,0:T(8,128)(2,1)S(1)} %copy-done.8, ...), custom_call_target="tpu_custom_call" | custom-call | flops 1 | bytes 1 | tf_op jit(solution)/shard_map/project/pallas_call | solution.py:131
  147.4 3.4 %collective-permute-start.19 = (bf16[128,1536]{1,0:T(8,128)(2,1)}, bf16[128,1536]{1,0:T(8,128)(2,1)S(1)}, u32[]{:S(2)}, u32[]{:S(2)}) collective-permute-start(bf16[128,1536]{1,0:T(8,128)(2,1)} %get-tuple-element.26.refs_0_), channel_id=1, source_target_pairs={{0,8},{4,12},{8,0},{12,4},{1,9},{5,13},{9,1},{13,5},{2,10},{6,14},... | collective-permute-start | bytes 1179656 | tf_op jit(solution)/shard_map/ppermute | solution.py:92
  152.9 20.3 %collective-permute-done.27.refs_3_ = bf16[128,1536]{1,0:T(8,128)(2,1)S(1)} collective-permute-done((bf16[128,1536]{1,0:T(8,128)(2,1)S(1)}, bf16[128,1536]{1,0:T(8,128)(2,1)S(1)}, u32[]{:S(2)}, u32[]{:S(2)}) %collective-permute-start.27) | collective-permute-done | bytes 393248 | tf_op jit(solution)/shard_map/ppermute | solution.py:92
  174.5 4.6 %collective-permute-start.17 = (bf16[128,1536]{1,0:T(8,128)(2,1)}, bf16[128,1536]{1,0:T(8,128)(2,1)S(1)}, u32[]{:S(2)}, u32[]{:S(2)}) collective-permute-start(bf16[128,1536]{1,0:T(8,128)(2,1)} %get-tuple-element.26.refs_0_), channel_id=1, source_target_pairs={{0,4},{4,8},{8,12},{1,5},{5,9},{9,13},{2,6},{6,10},{10,14},{3,7},{... | collective-permute-start | bytes 1179656 | tf_op jit(solution)/shard_map/ppermute | solution.py:90
  183.0 7.1 %collective-permute-done.28.refs_4_ = bf16[128,1536]{1,0:T(8,128)(2,1)S(1)} collective-permute-done((bf16[128,1536]{1,0:T(8,128)(2,1)S(1)}, bf16[128,1536]{1,0:T(8,128)(2,1)S(1)}, u32[]{:S(2)}, u32[]{:S(2)}) %collective-permute-start.28) | collective-permute-done | bytes 393248 | tf_op jit(solution)/shard_map/ppermute | solution.py:93
  190.6 4.9 %collective-permute-start.31 = (bf16[128,1536]{1,0:T(8,128)(2,1)}, bf16[128,1536]{1,0:T(8,128)(2,1)}, u32[]{:S(2)}, u32[]{:S(2)}) collective-permute-start(bf16[128,1536]{1,0:T(8,128)(2,1)} %gate.5.refs_0_), channel_id=1, source_target_pairs={{0,8},{4,12},{8,0},{12,4},{1,9},{5,13},{9,1},{13,5},{2,10},{6,14},... | collective-permute-start | bytes 1179656 | tf_op jit(solution)/shard_map/ppermute | solution.py:92
  205.3 4.3 %project_raw.1 = (bf16[512,2048]{1,0:T(8,128)(2,1)S(1)}, bf16[512,2048]{1,0:T(8,128)(2,1)}) custom-call(s32[20]{0:T(128)S(1)} %copy-done.36, bf16[512,256]{1,0:T(8,128)(2,1)S(1)} %attend.1.refs_4_.refs_0_, bf16[512,256]{1,0:T(8,128)(2,1)S(1)} %copy-done.9, bf16[512,256]{1,0:T(8,128)(2,1)S(1)} %copy-done.12, ...), custom_call_target="tpu_custom_call", output_to_operand_aliasing={{1}: (8, {})} | custom-call | flops 1 | bytes 1 | tf_op jit(solution)/shard_map/project_raw/pallas_call | solution.py:131
  210.1 7.7 %collective-permute-start.23 = (bf16[128,1536]{1,0:T(8,128)(2,1)S(1)}, bf16[128,1536]{1,0:T(8,128)(2,1)S(1)}, u32[]{:S(2)}, u32[]{:S(2)}) collective-permute-start(bf16[128,1536]{1,0:T(8,128)(2,1)S(1)} %gate.4.refs_0_), channel_id=1, source_target_pairs={{0,8},{4,12},{8,0},{12,4},{1,9},{5,13},{9,1},{13,5},{2,10},{6,14},... | collective-permute-start | bytes 1179656 | tf_op jit(solution)/shard_map/ppermute | solution.py:92
  220.4 5.2 %collective-permute-start.21 = (bf16[128,1536]{1,0:T(8,128)(2,1)S(1)}, bf16[128,1536]{1,0:T(8,128)(2,1)S(1)}, u32[]{:S(2)}, u32[]{:S(2)}) collective-permute-start(bf16[128,1536]{1,0:T(8,128)(2,1)S(1)} %gate.4.refs_0_), channel_id=1, source_target_pairs={{0,4},{4,8},{8,12},{1,5},{5,9},{9,13},{2,6},{6,10},{10,14},{3,7},{... | collective-permute-start | bytes 1179656 | tf_op jit(solution)/shard_map/ppermute | solution.py:90
  226.9 9.4 %collective-permute-done.23.refs_3_ = bf16[128,1536]{1,0:T(8,128)(2,1)S(1)} collective-permute-done((bf16[128,1536]{1,0:T(8,128)(2,1)S(1)}, bf16[128,1536]{1,0:T(8,128)(2,1)S(1)}, u32[]{:S(2)}, u32[]{:S(2)}) %collective-permute-start.23) | collective-permute-done | bytes 393248 | tf_op jit(solution)/shard_map/ppermute | solution.py:92
  237.6 3.4 %norm.4.refs_6_ = bf16[512,8192]{1,0:T(8,128)(2,1)} custom-call(s32[20]{0:T(128)S(1)} %copy-done.36, f32[1,8192]{1,0:T(1,128)S(1)} %bitcast.28, bf16[128,1536]{1,0:T(8,128)(2,1)S(1)} %copy-done.19, bf16[128,1536]{1,0:T(8,128)(2,1)S(1)} %collective-permute-done.25.refs_1_, bf16[128,1536]{1,0:T(8,128)(2,1)S(1)} %collective-permute-done.26.refs_2_, ...), custom_call_target="tpu_custom_call" | custom-call | flops 1 | bytes 1 | tf_op jit(solution)/shard_map/norm/pallas_call | solution.py:131
  241.0 4.9 %norm.5.refs_6_ = bf16[512,8192]{1,0:T(8,128)(2,1)} custom-call(s32[20]{0:T(128)S(1)} %copy-done.36, f32[1,8192]{1,0:T(1,128)S(1)} %bitcast.29, bf16[128,1536]{1,0:T(8,128)(2,1)} %get-tuple-element.26.refs_0_, bf16[128,1536]{1,0:T(8,128)(2,1)S(1)} %collective-permute-done.17.refs_1_, ...), custom_call_target="tpu_custom_call", output_to_operand_aliasing={{}: (8, {})} | custom-call | flops 1 | bytes 1 | tf_op jit(solution)/shard_map/norm/pallas_call | solution.py:131
  247.1 5.0 %norm.6.refs_6_ = bf16[512,8192]{1,0:T(8,128)(2,1)} custom-call(s32[20]{0:T(128)S(1)} %copy-done.36, f32[1,8192]{1,0:T(1,128)S(1)} %bitcast.30, bf16[128,1536]{1,0:T(8,128)(2,1)} %gate.5.refs_0_, bf16[128,1536]{1,0:T(8,128)(2,1)} %collective-permute-done.29.refs_1_, ...), custom_call_target="tpu_custom_call", output_to_operand_aliasing={{}: (8, {})} | custom-call | flops 1 | bytes 1 | tf_op jit(solution)/shard_map/norm/pallas_call | solution.py:131
  252.1 3.5 %collective-permute-done.22.refs_2_ = bf16[128,1536]{1,0:T(8,128)(2,1)S(1)} collective-permute-done((bf16[128,1536]{1,0:T(8,128)(2,1)S(1)}, bf16[128,1536]{1,0:T(8,128)(2,1)S(1)}, u32[]{:S(2)}, u32[]{:S(2)}) %collective-permute-start.22) | collective-permute-done | bytes 393248 | tf_op jit(solution)/shard_map/ppermute | solution.py:91
  255.5 6.0 %collective-permute-done.24.refs_4_ = bf16[128,1536]{1,0:T(8,128)(2,1)S(1)} collective-permute-done((bf16[128,1536]{1,0:T(8,128)(2,1)S(1)}, bf16[128,1536]{1,0:T(8,128)(2,1)S(1)}, u32[]{:S(2)}, u32[]{:S(2)}) %collective-permute-start.24) | collective-permute-done | bytes 393248 | tf_op jit(solution)/shard_map/ppermute | solution.py:93
  261.6 3.4 %norm.7 = bf16[512,8192]{1,0:T(8,128)(2,1)} custom-call(s32[20]{0:T(128)S(1)} %copy-done.36, f32[1,8192]{1,0:T(1,128)S(1)} %bitcast.31, bf16[128,1536]{1,0:T(8,128)(2,1)S(1)} %gate.4.refs_0_, bf16[128,1536]{1,0:T(8,128)(2,1)S(1)} %collective-permute-done.21.refs_1_, ...), custom_call_target="tpu_custom_call", output_to_operand_aliasing={{}: (8, {})} | custom-call | flops 1 | bytes 1 | tf_op jit(solution)/shard_map/norm/pallas_call | solution.py:131
  (141 shorter events, 73.1 us)
Async XLA Ops:
  7.2 122.8 %all-gather.5.cloned.1.call-start = ((), (), s32[]{:S(2)}) async-start(), calls=%async_computation | async-start | bytes 2621440 | tf_op jit(solution)/shard_map/all_gather | solution.py:555
  11.0 186.7 %all-gather.7.cloned.1.call-start = ((), (), s32[]{:S(2)}) async-start(), calls=%async_computation.1 | async-start | bytes 4718592 | tf_op jit(solution)/shard_map/all_gather | solution.py:575
  15.3 33.7 %collective-permute-start.1 = (bf16[1552,256]{1,0:T(8,128)(2,1)S(1)}, bf16[1552,256]{1,0:T(8,128)(2,1)S(1)}, u32[]{:S(2)}, u32[]{:S(2)}) collective-permute-start(bf16[1552,256]{1,0:T(8,128)(2,1)S(1)} %get-tuple-element.18.refs_0_), channel_id=1, source_target_pairs={{0,2},{1,3},{2,0},{3,1},{4,6},{5,7},{6,4},{7,5},{8,10},{9,11},{10,... | collective-permute-start | bytes 2383880 | tf_op jit(solution)/shard_map/ppermute | solution.py:42
  19.9 28.0 %collective-permute-start.3 = (bf16[32,3584]{1,0:T(8,128)(2,1)}, bf16[32,3584]{1,0:T(8,128)(2,1)S(1)}, u32[]{:S(2)}, u32[]{:S(2)}) collective-permute-start(bf16[32,3584]{1,0:T(8,128)(2,1)} %get-tuple-element.20), channel_id=1, source_target_pairs={{0,8},{4,12},{8,0},{12,4},{1,9},{5,13},{9,1},{13,5},{2,10},{6,14},... | collective-permute-start | bytes 688136 | tf_op jit(solution)/shard_map/ppermute | solution.py:552
  22.4 26.0 %collective-permute-start.4 = (bf16[32,3584]{1,0:T(8,128)(2,1)}, bf16[32,3584]{1,0:T(8,128)(2,1)S(1)}, u32[]{:S(2)}, u32[]{:S(2)}) collective-permute-start(bf16[32,3584]{1,0:T(8,128)(2,1)} %get-tuple-element.21), channel_id=1, source_target_pairs={{0,12},{4,0},{8,4},{12,8},{1,13},{5,1},{9,5},{13,9},{2,14},{6,2},{... | collective-permute-start | bytes 688136 | tf_op jit(solution)/shard_map/ppermute | solution.py:552
  23.8 25.8 %collective-permute-start = (bf16[1552,256]{1,0:T(8,128)(2,1)S(1)}, bf16[1552,256]{1,0:T(8,128)(2,1)S(1)}, u32[]{:S(2)}, u32[]{:S(2)}) collective-permute-start(bf16[1552,256]{1,0:T(8,128)(2,1)S(1)} %get-tuple-element.18.refs_0_), channel_id=1, source_target_pairs={{0,1},{1,0},{2,3},{3,2},{4,5},{5,4},{6,7},{7,6},{8,9},{9,8},{10,11... | collective-permute-start | bytes 2383880 | tf_op jit(solution)/shard_map/ppermute | solution.py:42
  65.6 30.5 %collective-permute-start.13 = (bf16[4,32,1536]{2,1,0:T(8,128)(2,1)S(1)}, bf16[4,32,1536]{2,1,0:T(8,128)(2,1)S(1)}, u32[]{:S(2)}, u32[]{:S(2)}) collective-permute-start(bf16[4,32,1536]{2,1,0:T(8,128)(2,1)S(1)} %stack.90.refs_1_.refs_5_), channel_id=1, source_target_pairs={{0,16},{16,0},{1,17},{17,1},{2,18},{18,2},{3,19},{19,3},{4,20},{20... | collective-permute-start | bytes 1179656 | tf_op jit(solution)/shard_map/ppermute | solution.py:75
  78.0 34.5 %collective-permute-start.12 = (bf16[4,32,1536]{2,1,0:T(8,128)(2,1)S(1)}, bf16[4,32,1536]{2,1,0:T(8,128)(2,1)S(1)}, u32[]{:S(2)}, u32[]{:S(2)}) collective-permute-start(bf16[4,32,1536]{2,1,0:T(8,128)(2,1)S(1)} %collective-permute-done.11.refs_7_), channel_id=1, source_target_pairs={{0,1},{1,0},{2,3},{3,2},{4,5},{5,4},{6,7},{7,6},{8,9},{9,8},{10,11... | collective-permute-start | bytes 1179656 | tf_op jit(solution)/shard_map/ppermute | solution.py:75
  79.3 35.3 %collective-permute-start.8 = (bf16[512,256]{1,0:T(8,128)(2,1)S(1)}, bf16[512,256]{1,0:T(8,128)(2,1)S(1)}, u32[]{:S(2)}, u32[]{:S(2)}) collective-permute-start(bf16[512,256]{1,0:T(8,128)(2,1)S(1)} %attend.1.refs_4_.refs_0_), channel_id=1, source_target_pairs={{0,8},{4,12},{8,0},{12,4},{1,9},{5,13},{9,1},{13,5},{2,10},{6,14},... | collective-permute-start | bytes 786440 | tf_op jit(solution)/shard_map/ppermute | solution.py:92
  146.0 27.2 %collective-permute-start.27 = (bf16[128,1536]{1,0:T(8,128)(2,1)S(1)}, bf16[128,1536]{1,0:T(8,128)(2,1)S(1)}, u32[]{:S(2)}, u32[]{:S(2)}) collective-permute-start(bf16[128,1536]{1,0:T(8,128)(2,1)S(1)} %get-tuple-element.29.refs_0_), channel_id=1, source_target_pairs={{0,8},{4,12},{8,0},{12,4},{1,9},{5,13},{9,1},{13,5},{2,10},{6,14},... | collective-permute-start | bytes 1179656 | tf_op jit(solution)/shard_map/ppermute | solution.py:92
  146.0 33.1 %collective-permute-start.25 = (bf16[128,1536]{1,0:T(8,128)(2,1)S(1)}, bf16[128,1536]{1,0:T(8,128)(2,1)S(1)}, u32[]{:S(2)}, u32[]{:S(2)}) collective-permute-start(bf16[128,1536]{1,0:T(8,128)(2,1)S(1)} %get-tuple-element.29.refs_0_), channel_id=1, source_target_pairs={{0,4},{4,8},{8,12},{1,5},{5,9},{9,13},{2,6},{6,10},{10,14},{3,7},{... | collective-permute-start | bytes 1179656 | tf_op jit(solution)/shard_map/ppermute | solution.py:90
  147.4 34.3 %collective-permute-start.19 = (bf16[128,1536]{1,0:T(8,128)(2,1)}, bf16[128,1536]{1,0:T(8,128)(2,1)S(1)}, u32[]{:S(2)}, u32[]{:S(2)}) collective-permute-start(bf16[128,1536]{1,0:T(8,128)(2,1)} %get-tuple-element.26.refs_0_), channel_id=1, source_target_pairs={{0,8},{4,12},{8,0},{12,4},{1,9},{5,13},{9,1},{13,5},{2,10},{6,14},... | collective-permute-start | bytes 1179656 | tf_op jit(solution)/shard_map/ppermute | solution.py:92
  150.9 32.1 %collective-permute-start.26 = (bf16[128,1536]{1,0:T(8,128)(2,1)S(1)}, bf16[128,1536]{1,0:T(8,128)(2,1)S(1)}, u32[]{:S(2)}, u32[]{:S(2)}) collective-permute-start(bf16[128,1536]{1,0:T(8,128)(2,1)S(1)} %get-tuple-element.29.refs_0_), channel_id=1, source_target_pairs={{4,0},{8,4},{12,8},{5,1},{9,5},{13,9},{6,2},{10,6},{14,10},{7,3},{... | collective-permute-start | bytes 1179656 | tf_op jit(solution)/shard_map/ppermute | solution.py:91
  174.5 35.1 %collective-permute-start.17 = (bf16[128,1536]{1,0:T(8,128)(2,1)}, bf16[128,1536]{1,0:T(8,128)(2,1)S(1)}, u32[]{:S(2)}, u32[]{:S(2)}) collective-permute-start(bf16[128,1536]{1,0:T(8,128)(2,1)} %get-tuple-element.26.refs_0_), channel_id=1, source_target_pairs={{0,4},{4,8},{8,12},{1,5},{5,9},{9,13},{2,6},{6,10},{10,14},{3,7},{... | collective-permute-start | bytes 1179656 | tf_op jit(solution)/shard_map/ppermute | solution.py:90
  179.1 30.5 %collective-permute-start.18 = (bf16[128,1536]{1,0:T(8,128)(2,1)}, bf16[128,1536]{1,0:T(8,128)(2,1)S(1)}, u32[]{:S(2)}, u32[]{:S(2)}) collective-permute-start(bf16[128,1536]{1,0:T(8,128)(2,1)} %get-tuple-element.26.refs_0_), channel_id=1, source_target_pairs={{4,0},{8,4},{12,8},{5,1},{9,5},{13,9},{6,2},{10,6},{14,10},{7,3},{... | collective-permute-start | bytes 1179656 | tf_op jit(solution)/shard_map/ppermute | solution.py:91
  181.7 27.9 %collective-permute-start.20 = (bf16[128,1536]{1,0:T(8,128)(2,1)S(1)}, bf16[128,1536]{1,0:T(8,128)(2,1)}, u32[]{:S(2)}, u32[]{:S(2)}) collective-permute-start(bf16[128,1536]{1,0:T(8,128)(2,1)S(1)} %collective-permute-done.19.refs_3_), channel_id=1, source_target_pairs={{4,0},{8,12},{5,1},{9,13},{6,2},{10,14},{7,3},{11,15},{20,16},{24,... | collective-permute-start | bytes 1179656 | tf_op jit(solution)/shard_map/ppermute | solution.py:93
  190.6 28.5 %collective-permute-start.31 = (bf16[128,1536]{1,0:T(8,128)(2,1)}, bf16[128,1536]{1,0:T(8,128)(2,1)}, u32[]{:S(2)}, u32[]{:S(2)}) collective-permute-start(bf16[128,1536]{1,0:T(8,128)(2,1)} %gate.5.refs_0_), channel_id=1, source_target_pairs={{0,8},{4,12},{8,0},{12,4},{1,9},{5,13},{9,1},{13,5},{2,10},{6,14},... | collective-permute-start | bytes 1179656 | tf_op jit(solution)/shard_map/ppermute | solution.py:92
  195.5 30.1 %collective-permute-start.29 = (bf16[128,1536]{1,0:T(8,128)(2,1)}, bf16[128,1536]{1,0:T(8,128)(2,1)}, u32[]{:S(2)}, u32[]{:S(2)}) collective-permute-start(bf16[128,1536]{1,0:T(8,128)(2,1)} %gate.5.refs_0_), channel_id=1, source_target_pairs={{0,4},{4,8},{8,12},{1,5},{5,9},{9,13},{2,6},{6,10},{10,14},{3,7},{... | collective-permute-start | bytes 1179656 | tf_op jit(solution)/shard_map/ppermute | solution.py:90
  210.1 26.2 %collective-permute-start.23 = (bf16[128,1536]{1,0:T(8,128)(2,1)S(1)}, bf16[128,1536]{1,0:T(8,128)(2,1)S(1)}, u32[]{:S(2)}, u32[]{:S(2)}) collective-permute-start(bf16[128,1536]{1,0:T(8,128)(2,1)S(1)} %gate.4.refs_0_), channel_id=1, source_target_pairs={{0,8},{4,12},{8,0},{12,4},{1,9},{5,13},{9,1},{13,5},{2,10},{6,14},... | collective-permute-start | bytes 1179656 | tf_op jit(solution)/shard_map/ppermute | solution.py:92
  217.8 28.1 %collective-permute-start.30 = (bf16[128,1536]{1,0:T(8,128)(2,1)}, bf16[128,1536]{1,0:T(8,128)(2,1)S(1)}, u32[]{:S(2)}, u32[]{:S(2)}) collective-permute-start(bf16[128,1536]{1,0:T(8,128)(2,1)} %gate.5.refs_0_), channel_id=1, source_target_pairs={{4,0},{8,4},{12,8},{5,1},{9,5},{13,9},{6,2},{10,6},{14,10},{7,3},{... | collective-permute-start | bytes 1179656 | tf_op jit(solution)/shard_map/ppermute | solution.py:91
  219.1 28.0 %collective-permute-start.32 = (bf16[128,1536]{1,0:T(8,128)(2,1)}, bf16[128,1536]{1,0:T(8,128)(2,1)S(1)}, u32[]{:S(2)}, u32[]{:S(2)}) collective-permute-start(bf16[128,1536]{1,0:T(8,128)(2,1)} %collective-permute-done.31.refs_3_), channel_id=1, source_target_pairs={{4,0},{8,12},{5,1},{9,13},{6,2},{10,14},{7,3},{11,15},{20,16},{24,... | collective-permute-start | bytes 1179656 | tf_op jit(solution)/shard_map/ppermute | solution.py:93
  220.4 31.7 %collective-permute-start.21 = (bf16[128,1536]{1,0:T(8,128)(2,1)S(1)}, bf16[128,1536]{1,0:T(8,128)(2,1)S(1)}, u32[]{:S(2)}, u32[]{:S(2)}) collective-permute-start(bf16[128,1536]{1,0:T(8,128)(2,1)S(1)} %gate.4.refs_0_), channel_id=1, source_target_pairs={{0,4},{4,8},{8,12},{1,5},{5,9},{9,13},{2,6},{6,10},{10,14},{3,7},{... | collective-permute-start | bytes 1179656 | tf_op jit(solution)/shard_map/ppermute | solution.py:90
  225.6 29.9 %collective-permute-start.22 = (bf16[128,1536]{1,0:T(8,128)(2,1)S(1)}, bf16[128,1536]{1,0:T(8,128)(2,1)S(1)}, u32[]{:S(2)}, u32[]{:S(2)}) collective-permute-start(bf16[128,1536]{1,0:T(8,128)(2,1)S(1)} %gate.4.refs_0_), channel_id=1, source_target_pairs={{4,0},{8,4},{12,8},{5,1},{9,5},{13,9},{6,2},{10,6},{14,10},{7,3},{... | collective-permute-start | bytes 1179656 | tf_op jit(solution)/shard_map/ppermute | solution.py:91
  236.3 25.3 %collective-permute-start.24 = (bf16[128,1536]{1,0:T(8,128)(2,1)S(1)}, bf16[128,1536]{1,0:T(8,128)(2,1)S(1)}, u32[]{:S(2)}, u32[]{:S(2)}) collective-permute-start(bf16[128,1536]{1,0:T(8,128)(2,1)S(1)} %collective-permute-done.23.refs_3_), channel_id=1, source_target_pairs={{4,0},{8,12},{5,1},{9,13},{6,2},{10,14},{7,3},{11,15},{20,16},{24,... | collective-permute-start | bytes 1179656 | tf_op jit(solution)/shard_map/ppermute | solution.py:93
  (48 other events, 387.1 us)
Sparse Core Ops, SparseCore 0:
  11.1 65.1 all-gather.4
  78.7 43.7 all-gather.6

commit v5 on v4

--- a/solution.py
+++ b/solution.py
@@ -48,6 +48,7 @@
     for shift in range(1, count):
         pairs = [(i, (i + shift) % count) for i in range(count)]
         blocks.append(lax.ppermute(value, axis, pairs))
+    blocks[-1] = between(blocks[-1])
     return blocks
 
 
@@ -55,33 +56,6 @@
     if count & (count - 1) == 0:
         return [me ^ mask for mask in range(count)]
     return [(me + count - shift) % count for shift in range(count)]
-
-
-def plane_gather(value, groups, contexts, between=lambda block: block):
-    count = groups * contexts
-    if count & (count - 1):
-        gathered = lax.all_gather(value, ("groups", "context"), axis=0, tiled=False)
-        return [gathered[number] for number in range(count)]
-    held = {0: value}
-    bits = [1 << b for b in range(contexts.bit_length() - 2, 0, -1)]
-    bits += [contexts << b for b in range(groups.bit_length() - 1)]
-    bits += [1] if contexts > 1 else []
-    for bit in bits:
-        axis, flip, size = ("context", bit, contexts)
-        if bit >= contexts:
-            axis, flip, size = ("groups", bit // contexts, groups)
-        pairs = [(i, i ^ flip) for i in range(size)]
-        for mask in sorted(held):
-            held[mask | bit] = lax.ppermute(held[mask], axis, pairs)
-        if bit == bits[0]:
-            held[bit] = between(held[bit])
-    return [held[mask] for mask in range(count)]
-
-
-def plane_owners(count, me):
-    if count & (count - 1):
-        return list(range(count))
-    return [me ^ mask for mask in range(count)]
 
 
 def line_gather(value, count):
@@ -102,7 +76,6 @@
         self.low = self.place + count
         self.high = self.low + 1
         self.share = self.low + 2
-        self.rows = self.low + 3
 
 
 def line_read(table, info, refs, d, cols=slice(None)):
@@ -173,18 +146,14 @@
         q_out[:, cols] = turn(q_ref[:, cols])
 
 
-def cut_kernel(table, slab, keep, info, w_ref, r_ref, *refs):
+def cut_kernel(table, slab, keep, info, w_ref, *refs):
     count, raw = table.count, slab - keep
-    outs, rows_ref, sems = refs[:count], refs[-2], refs[-1]
+    outs, rows_ref, sem = refs[:count], refs[-2], refs[-1]
     part = rows_ref.shape[0]
     start = pl.multiple_of(info[table.share] * part, part)
-    copies = [pltpu.make_async_copy(w_ref.at[pl.ds(start, part)], rows_ref, sems.at[0])]
-    if raw:
-        source = r_ref.at[:, pl.ds(keep, raw)]
-        copies.append(pltpu.make_async_copy(source, refs[count], sems.at[1]))
-    for copy in copies:
-        copy.start()
-    copies[0].wait()
+    copy = pltpu.make_async_copy(w_ref.at[pl.ds(start, part)], rows_ref, sem)
+    copy.start()
+    copy.wait()
     for d, out in enumerate(outs):
         target = lax.rem(info[table.place] + d, count)
         out[:, :keep] = rows_ref[:, pl.ds(pl.multiple_of(target * slab, slab), keep)]
@@ -192,30 +161,42 @@
             out[:, keep + j * raw : keep + (j + 1) * raw] = rows_ref[
                 :, j * slab + keep : (j + 1) * slab
             ]
-    if raw:
-        copies[1].wait()
-
-
-def cut(table, info, out_weight, residual, part, keep):
-    rows, slab = residual.shape
-    raw = slab - keep
-    width = keep + table.count * raw
-    shapes = [jax.ShapeDtypeStruct((part, width), out_weight.dtype)] * table.count
-    if raw:
-        shapes.append(jax.ShapeDtypeStruct((rows, raw), residual.dtype))
+
+
+def cut(table, info, out_weight, part, slab, keep):
+    shape = jax.ShapeDtypeStruct((part, keep + table.count * (slab - keep)), out_weight.dtype)
     return call(
         functools.partial(cut_kernel, table, slab, keep),
         "cut",
         info,
-        [out_weight, residual],
-        [pl.BlockSpec(memory_space=pltpu.HBM)] * 2,
-        [whole(shape) for shape in shapes],
-        shapes,
+        [out_weight],
+        [ANYWHERE],
+        [whole(shape)] * table.count,
+        [shape] * table.count,
         scratch=[
             pltpu.VMEM((part, out_weight.shape[1]), out_weight.dtype),
-            pltpu.SemaphoreType.DMA((2,)),
+            pltpu.SemaphoreType.DMA(()),
         ],
         vmem=0,
+    )
+
+
+def last_columns_kernel(info, *refs):
+    refs[-1][...] = refs[0][...]
+
+
+def last_columns(info, value, width, after):
+    rows, full = value.shape
+    shape = jax.ShapeDtypeStruct((rows, width), value.dtype)
+    return call(
+        last_columns_kernel,
+        "last_columns",
+        info,
+        [value, *after],
+        [pl.BlockSpec((rows, width), lambda i, info: (0, full // width - 1))]
+        + [ANYWHERE] * len(after),
+        whole(shape),
+        shape,
     )
 
 
@@ -358,73 +339,58 @@
     )
 
 
-def project_kernel(table, lines, shares, keep, chunks, info, *refs):
+def project_kernel(table, lines, keep, splits, info, *refs):
     count = table.count
-    attention, pieces = refs[:lines], refs[lines : lines + shares]
-    r_ref = refs[lines + shares]
-    parts, h_ref, w_ref = refs[-2 - chunks : -2], refs[-2], refs[-1]
-    part_rows = pieces[0].shape[1]
-
-    @pl.when(pl.program_id(0) == 0)
-    def _():
-        for number, piece in enumerate(pieces):
-            start = pl.multiple_of(info[table.rows + number] * part_rows, part_rows)
-            for d in range(count):
-                w_ref[d, pl.ds(start, part_rows)] = piece[d]
-
+    attention, w_ref, r_ref = refs[:lines], refs[lines], refs[lines + 1]
+    parts, h_ref = refs[-1 - len(splits) : -1], refs[-1]
+    rows = r_ref.shape[0]
     total = r_ref[:, :keep].astype(jnp.float32)
     for d in range(count):
         block = line_read(table, info, attention, d).astype(jnp.bfloat16)
-        total = total + jnp.dot(block, w_ref[d], preferred_element_type=jnp.float32)
+        weight = w_ref[:, d].reshape(block.shape[1], keep)
+        total = total + jnp.dot(block, weight, preferred_element_type=jnp.float32)
     result = total.astype(jnp.bfloat16)
     h_ref[:, :keep] = result
-    for number, part in enumerate(parts):
-
-        @pl.when(pl.program_id(0) == number)
-        def _():
-            part[...] = result
-
-
-def project(table, info, attention, pieces, residual, rows, after):
+    for part, (begin, size) in zip(parts, splits):
+        for row in range(begin, begin + size, rows):
+
+            @pl.when(pl.program_id(0) == row // rows)
+            def _():
+                part[row - begin : row - begin + rows] = result
+
+
+def project(table, info, attention, weights, residual, rows, splits):
     all_rows, slab = residual.shape
-    count, part_rows, keep = pieces[0].shape
-    depth = len(pieces) * part_rows
-    chunks = all_rows // rows
-    part = jax.ShapeDtypeStruct((rows, keep), jnp.bfloat16)
-    hidden = jax.ShapeDtypeStruct(residual.shape, jnp.bfloat16)
+    keep = weights.shape[3]
+    parts = [jax.ShapeDtypeStruct((size, keep), jnp.bfloat16) for _, size in splits]
     row_spec = pl.BlockSpec((rows, slab), lambda i, info: (i, 0))
     return call(
-        functools.partial(project_kernel, table, len(attention), len(pieces), keep, chunks),
+        functools.partial(project_kernel, table, len(attention), keep, splits),
         "project",
         info,
-        [*attention, *pieces, residual, *after],
-        line_spec(attention, rows, lambda i: i)
-        + [whole(p) for p in pieces]
-        + [row_spec]
-        + [ANYWHERE] * len(after),
-        [whole(part)] * chunks + [row_spec],
-        [part] * chunks + [hidden],
-        grid=(chunks,),
-        scratch=[pltpu.VMEM((count, depth, keep), jnp.bfloat16)],
+        [*attention, weights, residual],
+        line_spec(attention, rows, lambda i: i) + [whole(weights), row_spec],
+        [whole(part) for part in parts] + [row_spec],
+        [*parts, jax.ShapeDtypeStruct(residual.shape, jnp.bfloat16)],
+        grid=(all_rows // rows,),
         vmem=28,
     )
 
 
-def project_raw_kernel(table, lines, info, *refs):
+def project_raw_kernel(table, lines, raw_lines, info, *refs):
     count = table.count
-    attention, r_ref, w_ref = refs[:lines], refs[lines], refs[lines + 1]
+    attention, residuals = refs[:lines], refs[lines : lines + raw_lines]
+    w_ref = refs[lines + raw_lines]
     raw_ref, h_ref = refs[-2:]
     raw = h_ref.shape[1]
     blocks = [
         line_read(table, info, attention, d).astype(jnp.bfloat16) for d in range(count)
     ]
     for slab in range(count):
-        place = info[table.place + slab]
-        start = pl.multiple_of(place * raw, raw)
-        total = r_ref[place].astype(jnp.float32)
+        start = pl.multiple_of(info[table.place + slab] * raw, raw)
+        total = line_read(table, info, residuals, slab)
         for d in range(count):
-            weight = w_ref[:, d, :, pl.ds(start, raw)]
-            weight = weight.reshape(blocks[d].shape[1], raw)
+            weight = w_ref[:, d, :, pl.ds(start, raw)].reshape(blocks[d].shape[1], raw)
             total = total + jnp.dot(blocks[d], weight, preferred_element_type=jnp.float32)
         result = total.astype(jnp.bfloat16)
         raw_ref[:, slab * raw : (slab + 1) * raw] = result
@@ -434,22 +400,18 @@
 
 def project_raw(table, info, attention, residuals, weights, hidden, raw, rows):
     all_rows, slab = hidden.shape
-    count = table.count
     args = [*attention, *residuals, weights, hidden]
-    out = jax.ShapeDtypeStruct((all_rows, count * raw), jnp.bfloat16)
-    return call(
-        functools.partial(project_raw_kernel, table, len(attention)),
+    out = jax.ShapeDtypeStruct((all_rows, table.count * raw), jnp.bfloat16)
+    return call(
+        functools.partial(project_raw_kernel, table, len(attention), len(residuals)),
         "project_raw",
         info,
         args,
         line_spec(attention, rows, lambda i: i)
-        + [
-            pl.BlockSpec((count, rows, raw), lambda i, info: (0, i, 0)),
-            whole(weights),
-            ANYWHERE,
-        ],
+        + line_spec(residuals, rows, lambda i: i)
+        + [whole(weights), ANYWHERE],
         [
-            pl.BlockSpec((rows, count * raw), lambda i, info: (i, 0)),
+            pl.BlockSpec((rows, table.count * raw), lambda i, info: (i, 0)),
             pl.BlockSpec((rows, raw), lambda i, info: (i, slab // raw - 1)),
         ],
         [out, jax.ShapeDtypeStruct(hidden.shape, jnp.bfloat16)],
@@ -484,17 +446,17 @@
             out_ref[:, cols] = (value * inverse * g_ref[:, cols]).astype(jnp.bfloat16)
 
 
-def norm_into(table, info, buffer, blocks, raw_hidden, gain, chunk, rows, keep, slab, total_rows):
+def norm_into(table, info, buffer, blocks, raw_hidden, gain, begin, rows, keep, slab, total_rows):
     width = table.count * slab
     step = min(rows, 32)
-    steps = rows // step
+    steps, first = rows // step, begin // step
     args = [gain.reshape(1, width), *blocks]
     in_specs = [pl.BlockSpec((1, width), lambda i, info: (0, 0))]
     in_specs += line_spec(blocks, step, lambda i: i)
     if raw_hidden is not None:
         args.append(raw_hidden)
         in_specs.append(
-            pl.BlockSpec((step, raw_hidden.shape[1]), lambda i, info: (chunk * steps + i, 0))
+            pl.BlockSpec((step, raw_hidden.shape[1]), lambda i, info: (first + i, 0))
         )
     aliases = {}
     if buffer is not None:
@@ -507,7 +469,7 @@
         info,
         args,
         in_specs,
-        pl.BlockSpec((step, width), lambda i, info: (chunk * steps + i, 0)),
+        pl.BlockSpec((step, width), lambda i, info: (first + i, 0)),
         jax.ShapeDtypeStruct((total_rows, width), jnp.bfloat16),
         grid=(steps,),
         aliases=aliases,
@@ -530,13 +492,13 @@
     raw = slab // 4 if slab % 512 == 0 and rows > CHUNK else 0
     keep = slab - raw
     chunk = min(CHUNK, rows)
-    chunks = rows // chunk
+    sizes = [2 * chunk] + [chunk] * (rows // chunk - 2) if rows // chunk > 2 else [rows]
+    splits = [(sum(sizes[:n]), size) for n, size in enumerate(sizes)]
 
     table = Table(contexts, count)
     steering = [context_index, *owners_of(contexts, context_index)]
     steering += [lax.rem(tensor_index + (count - d), count) for d in range(count)]
     steering += [tensor_index == 0, tensor_index == count - 1, share]
-    steering += plane_owners(shares, share)
     info = jnp.stack([jnp.asarray(v).astype(jnp.int32) for v in steering])
 
     cache_local = lax.dynamic_index_in_dim(cache, kv_index, 0, keepdims=False)
@@ -545,48 +507,53 @@
     both = jnp.concatenate([frequencies(HD)] * 2)
     angles = positions.astype(jnp.float32)[:, None] * both[None, :]
     sign = jnp.where(jnp.arange(HD) < HD // 2, -1.0, 1.0)
-    cuts = cut(table, info, out_weight, residual, depth // shares, keep)
+    plane = ("groups", "context")
+    cuts = cut(table, info, out_weight, depth // shares, slab, keep)
     parts = [cuts[0]]
     for shift in range(1, count):
         pairs = [(i, (i + shift) % count) for i in range(count)]
         parts.append(lax.ppermute(cuts[shift], "tensor", pairs))
-    residuals = []
-    if raw:
-        residuals = [lax.all_gather(cuts[count], "tensor", axis=0, tiled=False)]
-    own_weights = stack(info, parts, 0, keep)
-
     q_turned, payload = prepare(
         info, queries, span_local, cache_local, jnp.cos(angles),
         jnp.sin(angles) * sign[None, :], lengths, cuts[:1],
     )
-    pieces = pieces_of(
-        payload, "context", contexts, lambda block: gate(info, block, [own_weights])
-    )
+    sent = []
+
+    def between(block):
+        sent.append(stack(info, parts, 0, keep, [block]))
+        if raw:
+            sent.append(last_columns(info, residual, raw, [*parts[1:], block]))
+        return gate(info, block, sent)
+
+    pieces = pieces_of(payload, "context", contexts, between)
+    own_weights = lax.all_gather(sent[0], plane, axis=0, tiled=False)
+    residuals = line_gather(sent[1], count) if raw else []
     mixed = attend(table, info, q_turned, pieces, cache_local.shape[0], chunk)
-    weight_pieces = plane_gather(own_weights, groups, contexts)
+    if raw:
+        mixed = gate(info, mixed, residuals[1:4] or residuals)
     attention = line_gather(mixed, count)
 
     *hidden_parts, hidden = project(
-        table, info, attention, weight_pieces, residual, chunk, residuals
+        table, info, attention, own_weights, residual, chunk, splits
     )
     raw_hidden = None
     if raw:
-        raw_weights = stack(info, parts, keep, count * raw, [mixed])
-        raw_weights = lax.all_gather(raw_weights, ("groups", "context"), axis=0, tiled=False)
+        raw_weights = stack(info, parts, keep, count * raw, [hidden_parts[0]])
+        raw_weights = lax.all_gather(raw_weights, plane, axis=0, tiled=False)
         raw_hidden, hidden = project_raw(
             table, info, attention, residuals, raw_weights, hidden, raw, chunk
         )
     lines = []
-    for number in range(chunks):
+    for number in range(len(splits)):
         value = hidden_parts[number]
         if number > 1:
-            made = [raw_hidden] if raw and number == chunks - 1 else []
+            made = [raw_hidden] if raw and number == len(splits) - 1 else []
             value = gate(info, value, [*lines[number - 2][1:], *made])
         lines.append(line_gather(value, count))
     normed = None
-    for number in range(chunks):
+    for (begin, size), blocks in zip(splits, lines):
         normed = norm_into(
-            table, info, normed, lines[number], raw_hidden, gain, number, chunk, keep, slab, rows
+            table, info, normed, blocks, raw_hidden, gain, begin, size, keep, slab, rows
         )
     return (hidden, normed)
 

time: 273 us -> 280 us (1.026)
  the two profiles are of different devices: /device:TPU:0 before, /device:TPU:24 now
where the time goes in v5:
time: 280 us; the launch traced here: 278 us
  waiting for transfers between devices  130 us (46%)
  starting transfers between devices  48.5 us (17%)
  Pallas kernels  47.2 us (17%)
  local copies, waits for them, and re-layouts  35.5 us (13%)
  between operations  15.8 us (6%)
    ppermute x5, waiting for transfers between devices, line_gather(): far = lax.ppermute(value, 'tensor', [(0, 2), (1, 3), (2, 0), (3, 1)])  52.9 us
    ppermute x5, waiting for transfers between devices, line_gather(): last = lax.ppermute(far, 'tensor', [(1, 0), (2, 3)])  49.2 us
    pallas_call x14, Pallas kernels, call(): pl.pallas_call(kernel, grid_spec=pltpu.PrefetchScalarGridSpec(num_scalar_...  47.2 us
    unnamed x96, local copies, waits for them, and re-layouts  34.9 us
    ppermute x3, waiting for transfers between devices, per_device(): parts.append(lax.ppermute(cuts[shift], 'tensor', pairs))  19.5 us
    ppermute x5, starting transfers between devices, line_gather(): down = lax.ppermute(value, 'tensor', [(1, 0), (2, 1), (3, 2)])  15.6 us
    ppermute x5, starting transfers between devices, line_gather(): far = lax.ppermute(value, 'tensor', [(0, 2), (1, 3), (2, 0), (3, 1)])  15.5 us
    ppermute x5, waiting for transfers between devices, line_gather(): up = lax.ppermute(value, 'tensor', [(0, 1), (1, 2), (2, 3)])  8.47 us
  transfers between devices with their start and end apart: 28, of which 12 were waited for; matrix products, arithmetic and copies ran while one was open for 0% of the time, Pallas kernels for 12%

profile of v5, /device:TPU:24, one launch (start us, length us, event | category | flops | bytes accessed | tf_op | source)
XLA Modules:
  0.0 278.3 jit_solution(8776827910689492323)
XLA Ops:
  9.4 2.8 %cut.1 = (bf16[32,3584]{1,0:T(8,128)(2,1)}, bf16[32,3584]{1,0:T(8,128)(2,1)}, bf16[32,3584]{1,0:T(8,128)(2,1)}, bf16[32,3584]{1,0:T(8,128)(2,1)}) custom-call(s32[12]{0:T(128)} %stack.58.info, bf16[256,8192]{1,0:T(8,128)(2,1)} %w_ref.1), custom_call_target="tpu_custom_call" | custom-call | flops 1 | bytes 1 | tf_op jit(solution)/shard_map/cut/pallas_call | solution.py:104
  20.4 5.4 %collective-permute-done.2.refs_1_ = bf16[32,3584]{1,0:T(8,128)(2,1)S(1)} collective-permute-done((bf16[32,3584]{1,0:T(8,128)(2,1)}, bf16[32,3584]{1,0:T(8,128)(2,1)S(1)}, u32[]{:S(2)}, u32[]{:S(2)}) %collective-permute-start.2) | collective-permute-done | bytes 229408 | tf_op jit(solution)/shard_map/ppermute | solution.py:515
  25.8 14.1 %collective-permute-done.3.refs_2_ = bf16[32,3584]{1,0:T(8,128)(2,1)S(1)} collective-permute-done((bf16[32,3584]{1,0:T(8,128)(2,1)}, bf16[32,3584]{1,0:T(8,128)(2,1)S(1)}, u32[]{:S(2)}, u32[]{:S(2)}) %collective-permute-start.3) | collective-permute-done | bytes 229408 | tf_op jit(solution)/shard_map/ppermute | solution.py:515
  53.0 13.3 %attend.1.refs_0_ = bf16[512,256]{1,0:T(8,128)(2,1)S(1)} custom-call(s32[12]{0:T(128)S(1)} %copy-done.45, bf16[512,256]{1,0:T(8,128)(2,1)S(1)} %copy-done.47, bf16[1552,256]{1,0:T(8,128)(2,1)} %get-tuple-element.16.refs_0_, bf16[1552,256]{1,0:T(8,128)(2,1)S(1)} %collective-permute-done.refs_1_, bf16[1552,256]{1,0:T(8,128)(2,1)S(1)} %gate.3.refs_2_, ...), custom_call_target="tpu_custom_call" | custom-call | flops 12884901888 | bytes 1 | tf_op jit(solution)/shard_map/attend/pallas_call | solution.py:104
  66.3 6.9 %collective-permute-done.8.refs_3_.refs_8_ = bf16[512,512]{1,0:T(8,128)(2,1)S(1)} collective-permute-done((bf16[512,512]{1,0:T(8,128)(2,1)S(1)}, bf16[512,512]{1,0:T(8,128)(2,1)S(1)}, u32[]{:S(2)}, u32[]{:S(2)}) %collective-permute-start.8) | collective-permute-done | bytes 524320 | tf_op jit(solution)/shard_map/ppermute | solution.py:66
  73.2 4.9 %collective-permute-done.6.refs_1_.refs_6_ = bf16[512,512]{1,0:T(8,128)(2,1)S(1)} collective-permute-done((bf16[512,512]{1,0:T(8,128)(2,1)S(1)}, bf16[512,512]{1,0:T(8,128)(2,1)S(1)}, u32[]{:S(2)}, u32[]{:S(2)}) %collective-permute-start.6) | collective-permute-done | bytes 524320 | tf_op jit(solution)/shard_map/ppermute | solution.py:64
  78.7 5.9 %collective-permute-start.11 = (bf16[512,256]{1,0:T(8,128)(2,1)S(1)}, bf16[512,256]{1,0:T(8,128)(2,1)S(1)}, u32[]{:S(2)}, u32[]{:S(2)}) collective-permute-start(bf16[512,256]{1,0:T(8,128)(2,1)S(1)} %gate.4.refs_0_), channel_id=1, source_target_pairs={{0,8},{4,12},{8,0},{12,4},{1,9},{5,13},{9,1},{13,5},{2,10},{6,14},... | collective-permute-start | bytes 786440 | tf_op jit(solution)/shard_map/ppermute | solution.py:66
  84.5 3.0 %collective-permute-start.10 = (bf16[512,256]{1,0:T(8,128)(2,1)S(1)}, bf16[512,256]{1,0:T(8,128)(2,1)S(1)}, u32[]{:S(2)}, u32[]{:S(2)}) collective-permute-start(bf16[512,256]{1,0:T(8,128)(2,1)S(1)} %gate.4.refs_0_), channel_id=1, source_target_pairs={{4,0},{8,4},{12,8},{5,1},{9,5},{13,9},{6,2},{10,6},{14,10},{7,3},{... | collective-permute-start | bytes 786440 | tf_op jit(solution)/shard_map/ppermute | solution.py:65
  89.5 7.8 %collective-permute-done.11.refs_3_ = bf16[512,256]{1,0:T(8,128)(2,1)S(1)} collective-permute-done((bf16[512,256]{1,0:T(8,128)(2,1)S(1)}, bf16[512,256]{1,0:T(8,128)(2,1)S(1)}, u32[]{:S(2)}, u32[]{:S(2)}) %collective-permute-start.11) | collective-permute-done | bytes 262176 | tf_op jit(solution)/shard_map/ppermute | solution.py:66
  100.7 5.6 %collective-permute-done.12.refs_4_ = bf16[512,256]{1,0:T(8,128)(2,1)S(1)} collective-permute-done((bf16[512,256]{1,0:T(8,128)(2,1)S(1)}, bf16[512,256]{1,0:T(8,128)(2,1)S(1)}, u32[]{:S(2)}, u32[]{:S(2)}) %collective-permute-start.12) | collective-permute-done | bytes 262176 | tf_op jit(solution)/shard_map/ppermute | solution.py:67
  113.6 4.0 %project.1 = (bf16[256,1536]{1,0:T(8,128)(2,1)S(1)}, bf16[128,1536]{1,0:T(8,128)(2,1)S(1)}, bf16[128,1536]{1,0:T(8,128)(2,1)S(1)}, bf16[512,2048]{1,0:T(8,128)(2,1)}) custom-call(s32[12]{0:T(128)S(1)} %copy-done.45, bf16[512,256]{1,0:T(8,128)(2,1)S(1)} %copy-done.4, bf16[512,256]{1,0:T(8,128)(2,1)S(1)} %copy-done.32, bf16[512,256]{1,0:T(8,128)(2,1)S(1)} %copy-done.29, ...), custom_call_target="tpu_custom_call" | custom-call | flops 1 | bytes 1 | tf_op jit(solution)/shard_map/project/pallas_call | solution.py:104
  126.2 4.4 %collective-permute-start.15 = (bf16[256,1536]{1,0:T(8,128)(2,1)S(1)}, bf16[256,1536]{1,0:T(8,128)(2,1)S(1)}, u32[]{:S(2)}, u32[]{:S(2)}) collective-permute-start(bf16[256,1536]{1,0:T(8,128)(2,1)S(1)} %get-tuple-element.20.refs_4_.refs_0_), channel_id=1, source_target_pairs={{4,0},{8,4},{12,8},{5,1},{9,5},{13,9},{6,2},{10,6},{14,10},{7,3},{... | collective-permute-start | bytes 2359304 | tf_op jit(solution)/shard_map/ppermute | solution.py:65
  132.0 29.7 %collective-permute-done.16.refs_3_ = bf16[256,1536]{1,0:T(8,128)(2,1)S(1)} collective-permute-done((bf16[256,1536]{1,0:T(8,128)(2,1)S(1)}, bf16[256,1536]{1,0:T(8,128)(2,1)S(1)}, u32[]{:S(2)}, u32[]{:S(2)}) %collective-permute-start.16) | collective-permute-done | bytes 786464 | tf_op jit(solution)/shard_map/ppermute | solution.py:66
  164.2 3.7 %collective-permute-start.24 = (bf16[128,1536]{1,0:T(8,128)(2,1)}, bf16[128,1536]{1,0:T(8,128)(2,1)}, u32[]{:S(2)}, u32[]{:S(2)}) collective-permute-start(bf16[128,1536]{1,0:T(8,128)(2,1)} %copy-done.40), channel_id=1, source_target_pairs={{0,8},{4,12},{8,0},{12,4},{1,9},{5,13},{9,1},{13,5},{2,10},{6,14},... | collective-permute-start | bytes 1179656 | tf_op jit(solution)/shard_map/ppermute | solution.py:66
  167.9 33.7 %collective-permute-done.13.refs_9_ = bf16[512,512]{1,0:T(8,128)(2,1)S(1)} collective-permute-done((bf16[512,512]{1,0:T(8,128)(2,1)}, bf16[512,512]{1,0:T(8,128)(2,1)S(1)}, u32[]{:S(2)}, u32[]{:S(2)}) %collective-permute-start.13) | collective-permute-done | bytes 524320 | tf_op jit(solution)/shard_map/ppermute | solution.py:67
  215.9 4.1 %project_raw.1 = (bf16[512,2048]{1,0:T(8,128)(2,1)S(1)}, bf16[512,2048]{1,0:T(8,128)(2,1)}) custom-call(s32[12]{0:T(128)S(1)} %copy-done.45, bf16[512,256]{1,0:T(8,128)(2,1)S(1)} %copy-done.5, bf16[512,256]{1,0:T(8,128)(2,1)S(1)} %copy-done.33, bf16[512,256]{1,0:T(8,128)(2,1)S(1)} %copy-done.30, ...), custom_call_target="tpu_custom_call", output_to_operand_aliasing={{1}: (12, {})} | custom-call | flops 1 | bytes 1 | tf_op jit(solution)/shard_map/project_raw/pallas_call | solution.py:104
  225.9 4.6 %collective-permute-start.19 = (bf16[128,1536]{1,0:T(8,128)(2,1)S(1)}, bf16[128,1536]{1,0:T(8,128)(2,1)S(1)}, u32[]{:S(2)}, u32[]{:S(2)}) collective-permute-start(bf16[128,1536]{1,0:T(8,128)(2,1)S(1)} %gate.5.refs_0_), channel_id=1, source_target_pairs={{4,0},{8,4},{12,8},{5,1},{9,5},{13,9},{6,2},{10,6},{14,10},{7,3},{... | collective-permute-start | bytes 1179656 | tf_op jit(solution)/shard_map/ppermute | solution.py:65
  231.8 8.5 %collective-permute-done.20.refs_3_ = bf16[128,1536]{1,0:T(8,128)(2,1)S(1)} collective-permute-done((bf16[128,1536]{1,0:T(8,128)(2,1)S(1)}, bf16[128,1536]{1,0:T(8,128)(2,1)S(1)}, u32[]{:S(2)}, u32[]{:S(2)}) %collective-permute-start.20) | collective-permute-done | bytes 393248 | tf_op jit(solution)/shard_map/ppermute | solution.py:66
  241.6 8.0 %norm.3.refs_6_ = bf16[512,8192]{1,0:T(8,128)(2,1)} custom-call(s32[12]{0:T(128)S(1)} %copy-done.45, f32[1,8192]{1,0:T(1,128)S(1)} %bitcast.21, bf16[256,1536]{1,0:T(8,128)(2,1)S(1)} %get-tuple-element.20.refs_4_.refs_0_, bf16[256,1536]{1,0:T(8,128)(2,1)} %collective-permute-done.14.refs_1_, bf16[256,1536]{1,0:T(8,128)(2,1)S(1)} %collective-permute-done.15.refs_2_, ...), custom_call_target="tpu_custom_call" | custom-call | flops 1 | bytes 1 | tf_op jit(solution)/shard_map/norm/pallas_call | solution.py:104
  249.6 4.1 %collective-permute-done.25.refs_4_ = bf16[128,1536]{1,0:T(8,128)(2,1)S(1)} collective-permute-done((bf16[128,1536]{1,0:T(8,128)(2,1)}, bf16[128,1536]{1,0:T(8,128)(2,1)S(1)}, u32[]{:S(2)}, u32[]{:S(2)}) %collective-permute-start.25) | collective-permute-done | bytes 393248 | tf_op jit(solution)/shard_map/ppermute | solution.py:67
  253.7 4.9 %norm.4.refs_6_ = bf16[512,8192]{1,0:T(8,128)(2,1)} custom-call(s32[12]{0:T(128)S(1)} %copy-done.45, f32[1,8192]{1,0:T(1,128)S(1)} %bitcast.22, bf16[128,1536]{1,0:T(8,128)(2,1)S(1)} %copy-done.41, bf16[128,1536]{1,0:T(8,128)(2,1)S(1)} %collective-permute-done.22.refs_1_, ...), custom_call_target="tpu_custom_call", output_to_operand_aliasing={{}: (8, {})} | custom-call | flops 1 | bytes 1 | tf_op jit(solution)/shard_map/norm/pallas_call | solution.py:104
  258.6 3.6 %collective-permute-done.18.refs_1_ = bf16[128,1536]{1,0:T(8,128)(2,1)S(1)} collective-permute-done((bf16[128,1536]{1,0:T(8,128)(2,1)S(1)}, bf16[128,1536]{1,0:T(8,128)(2,1)S(1)}, u32[]{:S(2)}, u32[]{:S(2)}) %collective-permute-start.18) | collective-permute-done | bytes 393248 | tf_op jit(solution)/shard_map/ppermute | solution.py:64
  262.1 5.9 %collective-permute-done.21.refs_4_ = bf16[128,1536]{1,0:T(8,128)(2,1)S(1)} collective-permute-done((bf16[128,1536]{1,0:T(8,128)(2,1)S(1)}, bf16[128,1536]{1,0:T(8,128)(2,1)S(1)}, u32[]{:S(2)}, u32[]{:S(2)}) %collective-permute-start.21) | collective-permute-done | bytes 393248 | tf_op jit(solution)/shard_map/ppermute | solution.py:67
  268.0 3.4 %norm.5 = bf16[512,8192]{1,0:T(8,128)(2,1)} custom-call(s32[12]{0:T(128)S(1)} %copy-done.45, f32[1,8192]{1,0:T(1,128)S(1)} %bitcast.23, bf16[128,1536]{1,0:T(8,128)(2,1)S(1)} %gate.5.refs_0_, bf16[128,1536]{1,0:T(8,128)(2,1)S(1)} %collective-permute-done.18.refs_1_, ...), custom_call_target="tpu_custom_call", output_to_operand_aliasing={{}: (8, {})} | custom-call | flops 1 | bytes 1 | tf_op jit(solution)/shard_map/norm/pallas_call | solution.py:104
  (149 shorter events, 70.3 us)
Async XLA Ops:
  7.2 99.8 %all-gather.5.cloned.1.call-start = ((), (), s32[]{:S(2)}) async-start(), calls=%async_computation | async-start | bytes 3538944 | tf_op jit(solution)/shard_map/all_gather | solution.py:529
  16.6 23.4 %collective-permute-start.1 = (bf16[1552,256]{1,0:T(8,128)(2,1)}, bf16[1552,256]{1,0:T(8,128)(2,1)S(1)}, u32[]{:S(2)}, u32[]{:S(2)}) collective-permute-start(bf16[1552,256]{1,0:T(8,128)(2,1)} %get-tuple-element.16.refs_0_), channel_id=1, source_target_pairs={{0,2},{1,3},{2,0},{3,1},{4,6},{5,7},{6,4},{7,5},{8,10},{9,11},{10,... | collective-permute-start | bytes 2383880 | tf_op jit(solution)/shard_map/ppermute | solution.py:42
  18.3 21.7 %collective-permute-start.3 = (bf16[32,3584]{1,0:T(8,128)(2,1)}, bf16[32,3584]{1,0:T(8,128)(2,1)S(1)}, u32[]{:S(2)}, u32[]{:S(2)}) collective-permute-start(bf16[32,3584]{1,0:T(8,128)(2,1)} %get-tuple-element.18), channel_id=1, source_target_pairs={{0,8},{4,12},{8,0},{12,4},{1,9},{5,13},{9,1},{13,5},{2,10},{6,14},... | collective-permute-start | bytes 688136 | tf_op jit(solution)/shard_map/ppermute | solution.py:515
  20.0 20.0 %collective-permute-start.4 = (bf16[32,3584]{1,0:T(8,128)(2,1)}, bf16[32,3584]{1,0:T(8,128)(2,1)S(1)}, u32[]{:S(2)}, u32[]{:S(2)}) collective-permute-start(bf16[32,3584]{1,0:T(8,128)(2,1)} %get-tuple-element.19), channel_id=1, source_target_pairs={{0,12},{4,0},{8,4},{12,8},{1,13},{5,1},{9,5},{13,9},{2,14},{6,2},{... | collective-permute-start | bytes 688136 | tf_op jit(solution)/shard_map/ppermute | solution.py:515
  43.4 161.3 %all-gather.7.cloned.1.call-start = ((), (), s32[]{:S(2)}) async-start(), calls=%async_computation.1 | async-start | bytes 4718592 | tf_op jit(solution)/shard_map/all_gather | solution.py:542
  48.1 25.1 %collective-permute-start.8 = (bf16[512,512]{1,0:T(8,128)(2,1)S(1)}, bf16[512,512]{1,0:T(8,128)(2,1)S(1)}, u32[]{:S(2)}, u32[]{:S(2)}) collective-permute-start(bf16[512,512]{1,0:T(8,128)(2,1)S(1)} %last_columns.1.refs_2_.refs_5_), channel_id=1, source_target_pairs={{0,8},{4,12},{8,0},{12,4},{1,9},{5,13},{9,1},{13,5},{2,10},{6,14},... | collective-permute-start | bytes 1572872 | tf_op jit(solution)/shard_map/ppermute | solution.py:66
  49.4 23.8 %collective-permute-start.7 = (bf16[512,512]{1,0:T(8,128)(2,1)S(1)}, bf16[512,512]{1,0:T(8,128)(2,1)S(1)}, u32[]{:S(2)}, u32[]{:S(2)}) collective-permute-start(bf16[512,512]{1,0:T(8,128)(2,1)S(1)} %last_columns.1.refs_2_.refs_5_), channel_id=1, source_target_pairs={{4,0},{8,4},{12,8},{5,1},{9,5},{13,9},{6,2},{10,6},{14,10},{7,3},{... | collective-permute-start | bytes 1572872 | tf_op jit(solution)/shard_map/ppermute | solution.py:65
  50.7 27.4 %collective-permute-start.6 = (bf16[512,512]{1,0:T(8,128)(2,1)S(1)}, bf16[512,512]{1,0:T(8,128)(2,1)S(1)}, u32[]{:S(2)}, u32[]{:S(2)}) collective-permute-start(bf16[512,512]{1,0:T(8,128)(2,1)S(1)} %last_columns.1.refs_2_.refs_5_), channel_id=1, source_target_pairs={{0,4},{4,8},{8,12},{1,5},{5,9},{9,13},{2,6},{6,10},{10,14},{3,7},{... | collective-permute-start | bytes 1572872 | tf_op jit(solution)/shard_map/ppermute | solution.py:64
  78.7 18.6 %collective-permute-start.11 = (bf16[512,256]{1,0:T(8,128)(2,1)S(1)}, bf16[512,256]{1,0:T(8,128)(2,1)S(1)}, u32[]{:S(2)}, u32[]{:S(2)}) collective-permute-start(bf16[512,256]{1,0:T(8,128)(2,1)S(1)} %gate.4.refs_0_), channel_id=1, source_target_pairs={{0,8},{4,12},{8,0},{12,4},{1,9},{5,13},{9,1},{13,5},{2,10},{6,14},... | collective-permute-start | bytes 786440 | tf_op jit(solution)/shard_map/ppermute | solution.py:66
  84.5 14.8 %collective-permute-start.10 = (bf16[512,256]{1,0:T(8,128)(2,1)S(1)}, bf16[512,256]{1,0:T(8,128)(2,1)S(1)}, u32[]{:S(2)}, u32[]{:S(2)}) collective-permute-start(bf16[512,256]{1,0:T(8,128)(2,1)S(1)} %gate.4.refs_0_), channel_id=1, source_target_pairs={{4,0},{8,4},{12,8},{5,1},{9,5},{13,9},{6,2},{10,6},{14,10},{7,3},{... | collective-permute-start | bytes 786440 | tf_op jit(solution)/shard_map/ppermute | solution.py:65
  87.5 12.5 %collective-permute-start.9 = (bf16[512,256]{1,0:T(8,128)(2,1)S(1)}, bf16[512,256]{1,0:T(8,128)(2,1)S(1)}, u32[]{:S(2)}, u32[]{:S(2)}) collective-permute-start(bf16[512,256]{1,0:T(8,128)(2,1)S(1)} %gate.4.refs_0_), channel_id=1, source_target_pairs={{0,4},{4,8},{8,12},{1,5},{5,9},{9,13},{2,6},{6,10},{10,14},{3,7},{... | collective-permute-start | bytes 786440 | tf_op jit(solution)/shard_map/ppermute | solution.py:64
  124.3 37.3 %collective-permute-start.16 = (bf16[256,1536]{1,0:T(8,128)(2,1)S(1)}, bf16[256,1536]{1,0:T(8,128)(2,1)S(1)}, u32[]{:S(2)}, u32[]{:S(2)}) collective-permute-start(bf16[256,1536]{1,0:T(8,128)(2,1)S(1)} %get-tuple-element.20.refs_4_.refs_0_), channel_id=1, source_target_pairs={{0,8},{4,12},{8,0},{12,4},{1,9},{5,13},{9,1},{13,5},{2,10},{6,14},... | collective-permute-start | bytes 2359304 | tf_op jit(solution)/shard_map/ppermute | solution.py:66
  126.2 93.8 %collective-permute-start.15 = (bf16[256,1536]{1,0:T(8,128)(2,1)S(1)}, bf16[256,1536]{1,0:T(8,128)(2,1)S(1)}, u32[]{:S(2)}, u32[]{:S(2)}) collective-permute-start(bf16[256,1536]{1,0:T(8,128)(2,1)S(1)} %get-tuple-element.20.refs_4_.refs_0_), channel_id=1, source_target_pairs={{4,0},{8,4},{12,8},{5,1},{9,5},{13,9},{6,2},{10,6},{14,10},{7,3},{... | collective-permute-start | bytes 2359304 | tf_op jit(solution)/shard_map/ppermute | solution.py:65
  130.7 89.4 %collective-permute-start.14 = (bf16[256,1536]{1,0:T(8,128)(2,1)S(1)}, bf16[256,1536]{1,0:T(8,128)(2,1)}, u32[]{:S(2)}, u32[]{:S(2)}) collective-permute-start(bf16[256,1536]{1,0:T(8,128)(2,1)S(1)} %get-tuple-element.20.refs_4_.refs_0_), channel_id=1, source_target_pairs={{0,4},{4,8},{8,12},{1,5},{5,9},{9,13},{2,6},{6,10},{10,14},{3,7},{... | collective-permute-start | bytes 2359304 | tf_op jit(solution)/shard_map/ppermute | solution.py:64
  161.6 58.4 %collective-permute-start.17 = (bf16[256,1536]{1,0:T(8,128)(2,1)S(1)}, bf16[256,1536]{1,0:T(8,128)(2,1)}, u32[]{:S(2)}, u32[]{:S(2)}) collective-permute-start(bf16[256,1536]{1,0:T(8,128)(2,1)S(1)} %collective-permute-done.16.refs_3_), channel_id=1, source_target_pairs={{4,0},{8,12},{5,1},{9,13},{6,2},{10,14},{7,3},{11,15},{20,16},{24,... | collective-permute-start | bytes 2359304 | tf_op jit(solution)/shard_map/ppermute | solution.py:67
  162.9 38.7 %collective-permute-start.13 = (bf16[512,512]{1,0:T(8,128)(2,1)}, bf16[512,512]{1,0:T(8,128)(2,1)S(1)}, u32[]{:S(2)}, u32[]{:S(2)}) collective-permute-start(bf16[512,512]{1,0:T(8,128)(2,1)} %copy-done.6), channel_id=1, source_target_pairs={{4,0},{8,12},{5,1},{9,13},{6,2},{10,14},{7,3},{11,15},{20,16},{24,... | collective-permute-start | bytes 1572872 | tf_op jit(solution)/shard_map/ppermute | solution.py:67
  164.2 60.4 %collective-permute-start.24 = (bf16[128,1536]{1,0:T(8,128)(2,1)}, bf16[128,1536]{1,0:T(8,128)(2,1)}, u32[]{:S(2)}, u32[]{:S(2)}) collective-permute-start(bf16[128,1536]{1,0:T(8,128)(2,1)} %copy-done.40), channel_id=1, source_target_pairs={{0,8},{4,12},{8,0},{12,4},{1,9},{5,13},{9,1},{13,5},{2,10},{6,14},... | collective-permute-start | bytes 1179656 | tf_op jit(solution)/shard_map/ppermute | solution.py:66
  202.4 28.1 %collective-permute-start.23 = (bf16[128,1536]{1,0:T(8,128)(2,1)}, bf16[128,1536]{1,0:T(8,128)(2,1)}, u32[]{:S(2)}, u32[]{:S(2)}) collective-permute-start(bf16[128,1536]{1,0:T(8,128)(2,1)} %copy-done.40), channel_id=1, source_target_pairs={{4,0},{8,4},{12,8},{5,1},{9,5},{13,9},{6,2},{10,6},{14,10},{7,3},{... | collective-permute-start | bytes 1179656 | tf_op jit(solution)/shard_map/ppermute | solution.py:65
  220.6 19.7 %collective-permute-start.20 = (bf16[128,1536]{1,0:T(8,128)(2,1)S(1)}, bf16[128,1536]{1,0:T(8,128)(2,1)S(1)}, u32[]{:S(2)}, u32[]{:S(2)}) collective-permute-start(bf16[128,1536]{1,0:T(8,128)(2,1)S(1)} %gate.5.refs_0_), channel_id=1, source_target_pairs={{0,8},{4,12},{8,0},{12,4},{1,9},{5,13},{9,1},{13,5},{2,10},{6,14},... | collective-permute-start | bytes 1179656 | tf_op jit(solution)/shard_map/ppermute | solution.py:66
  223.3 26.3 %collective-permute-start.22 = (bf16[128,1536]{1,0:T(8,128)(2,1)S(1)}, bf16[128,1536]{1,0:T(8,128)(2,1)S(1)}, u32[]{:S(2)}, u32[]{:S(2)}) collective-permute-start(bf16[128,1536]{1,0:T(8,128)(2,1)S(1)} %copy-done.41), channel_id=1, source_target_pairs={{0,4},{4,8},{8,12},{1,5},{5,9},{9,13},{2,6},{6,10},{10,14},{3,7},{... | collective-permute-start | bytes 1179656 | tf_op jit(solution)/shard_map/ppermute | solution.py:64
  224.6 29.1 %collective-permute-start.25 = (bf16[128,1536]{1,0:T(8,128)(2,1)}, bf16[128,1536]{1,0:T(8,128)(2,1)S(1)}, u32[]{:S(2)}, u32[]{:S(2)}) collective-permute-start(bf16[128,1536]{1,0:T(8,128)(2,1)} %collective-permute-done.24.refs_3_), channel_id=1, source_target_pairs={{4,0},{8,12},{5,1},{9,13},{6,2},{10,14},{7,3},{11,15},{20,16},{24,... | collective-permute-start | bytes 1179656 | tf_op jit(solution)/shard_map/ppermute | solution.py:67
  225.9 32.7 %collective-permute-start.19 = (bf16[128,1536]{1,0:T(8,128)(2,1)S(1)}, bf16[128,1536]{1,0:T(8,128)(2,1)S(1)}, u32[]{:S(2)}, u32[]{:S(2)}) collective-permute-start(bf16[128,1536]{1,0:T(8,128)(2,1)S(1)} %gate.5.refs_0_), channel_id=1, source_target_pairs={{4,0},{8,4},{12,8},{5,1},{9,5},{13,9},{6,2},{10,6},{14,10},{7,3},{... | collective-permute-start | bytes 1179656 | tf_op jit(solution)/shard_map/ppermute | solution.py:65
  230.5 31.6 %collective-permute-start.18 = (bf16[128,1536]{1,0:T(8,128)(2,1)S(1)}, bf16[128,1536]{1,0:T(8,128)(2,1)S(1)}, u32[]{:S(2)}, u32[]{:S(2)}) collective-permute-start(bf16[128,1536]{1,0:T(8,128)(2,1)S(1)} %gate.5.refs_0_), channel_id=1, source_target_pairs={{0,4},{4,8},{8,12},{1,5},{5,9},{9,13},{2,6},{6,10},{10,14},{3,7},{... | collective-permute-start | bytes 1179656 | tf_op jit(solution)/shard_map/ppermute | solution.py:64
  240.3 27.7 %collective-permute-start.21 = (bf16[128,1536]{1,0:T(8,128)(2,1)S(1)}, bf16[128,1536]{1,0:T(8,128)(2,1)S(1)}, u32[]{:S(2)}, u32[]{:S(2)}) collective-permute-start(bf16[128,1536]{1,0:T(8,128)(2,1)S(1)} %collective-permute-done.20.refs_3_), channel_id=1, source_target_pairs={{4,0},{8,12},{5,1},{9,13},{6,2},{10,14},{7,3},{11,15},{20,16},{24,... | collective-permute-start | bytes 1179656 | tf_op jit(solution)/shard_map/ppermute | solution.py:67
  (52 other events, 222.0 us)
Sparse Core Ops, SparseCore 0:
  43.6 32.3 all-gather.4
  124.5 37.2 all-gather.6

commit v6 on v5

--- a/solution.py
+++ b/solution.py
@@ -58,14 +58,65 @@
     return [(me + count - shift) % count for shift in range(count)]
 
 
+def plane_gather(value, groups, contexts, between=lambda block: block):
+    count = groups * contexts
+    if count & (count - 1):
+        gathered = lax.all_gather(value, ("groups", "context"), axis=0, tiled=False)
+        return [gathered[number] for number in range(count)]
+    held = {0: value}
+    bits = [1 << b for b in range(contexts.bit_length() - 2, 0, -1)]
+    bits += [contexts << b for b in range(groups.bit_length() - 1)]
+    bits += [1] if contexts > 1 else []
+    for bit in bits:
+        axis, flip, size = ("context", bit, contexts)
+        if bit >= contexts:
+            axis, flip, size = ("groups", bit // contexts, groups)
+        pairs = [(i, i ^ flip) for i in range(size)]
+        for mask in sorted(held):
+            held[mask | bit] = lax.ppermute(held[mask], axis, pairs)
+        if bit == bits[0]:
+            held[bit] = between(held[bit])
+    return [held[mask] for mask in range(count)]
+
+
+def plane_owners(count, me):
+    if count & (count - 1):
+        return list(range(count))
+    return [me ^ mask for mask in range(count)]
+
+
 def line_gather(value, count):
     if count != 4:
         return [lax.all_gather(value, "tensor", axis=0, tiled=False)]
+    far, last = line_far(value)
+    return [value, *line_near(value), far, last]
+
+
+def line_near(value):
     up = lax.ppermute(value, "tensor", [(0, 1), (1, 2), (2, 3)])
-    down = lax.ppermute(value, "tensor", [(1, 0), (2, 1), (3, 2)])
+    return up, lax.ppermute(value, "tensor", [(1, 0), (2, 1), (3, 2)])
+
+
+def line_far(value):
     far = lax.ppermute(value, "tensor", [(0, 2), (1, 3), (2, 0), (3, 1)])
-    last = lax.ppermute(far, "tensor", [(1, 0), (2, 3)])
-    return [value, up, down, far, last]
+    return far, lax.ppermute(far, "tensor", [(1, 0), (2, 3)])
+
+
+def chunk_gathers(info, values, copies, made, count):
+    if count != 4:
+        return [line_gather(value, count) for value in values]
+    fars, lines = [], []
+    for number, value in enumerate(values):
+        if number > 1:
+            value = gate(info, value, [fars[number - 2][0]])
+        fars.append(line_far(value))
+    for number, value in enumerate(copies):
+        before = [fars[number - 1][1] if number else fars[0][0]]
+        if number == len(copies) // 2:
+            before += made
+        value = gate(info, value, before)
+        lines.append([value, *line_near(value), *fars[number]])
+    return lines
 
 
 class Table:
@@ -76,6 +127,7 @@
         self.low = self.place + count
         self.high = self.low + 1
         self.share = self.low + 2
+        self.rows = self.low + 3
 
 
 def line_read(table, info, refs, d, cols=slice(None)):
@@ -183,6 +235,47 @@
 
 def last_columns_kernel(info, *refs):
     refs[-1][...] = refs[0][...]
+    refs[-2][...] = refs[0][...]
+
+
+def cut_kernel(table, slab, keep, info, w_ref, *refs):
+    count, raw = table.count, slab - keep
+    outs, rows_ref, sem = refs[:count], refs[-2], refs[-1]
+    part = rows_ref.shape[0]
+    start = pl.multiple_of(info[table.share] * part, part)
+    copy = pltpu.make_async_copy(w_ref.at[pl.ds(start, part)], rows_ref, sem)
+    copy.start()
+    copy.wait()
+    for d, out in enumerate(outs):
+        target = lax.rem(info[table.place] + d, count)
+        out[:, :keep] = rows_ref[:, pl.ds(pl.multiple_of(target * slab, slab), keep)]
+        for j in range(count if raw else 0):
+            out[:, keep + j * raw : keep + (j + 1) * raw] = rows_ref[
+                :, j * slab + keep : (j + 1) * slab
+            ]
+
+
+def cut(table, info, out_weight, part, slab, keep):
+    shape = jax.ShapeDtypeStruct((part, keep + table.count * (slab - keep)), out_weight.dtype)
+    return call(
+        functools.partial(cut_kernel, table, slab, keep),
+        "cut",
+        info,
+        [out_weight],
+        [ANYWHERE],
+        [whole(shape)] * table.count,
+        [shape] * table.count,
+        scratch=[
+            pltpu.VMEM((part, out_weight.shape[1]), out_weight.dtype),
+            pltpu.SemaphoreType.DMA(()),
+        ],
+        vmem=0,
+    )
+
+
+def last_columns_kernel(info, *refs):
+    refs[-1][...] = refs[0][...]
+    refs[-2][...] = refs[0][...]
 
 
 def last_columns(info, value, width, after):
@@ -195,8 +288,8 @@
         [value, *after],
         [pl.BlockSpec((rows, width), lambda i, info: (0, full // width - 1))]
         + [ANYWHERE] * len(after),
-        whole(shape),
-        shape,
+        [whole(shape)] * 2,
+        [shape] * 2,
     )
 
 
@@ -221,16 +314,15 @@
     )
 
 
-def stack_kernel(count, begin, info, *refs):
-    width = refs[-1].shape[2]
+def stack_kernel(count, info, *refs):
     for number, part in enumerate(refs[:count]):
-        refs[-1][number] = part[:, begin : begin + width]
-
-
-def stack(info, parts, begin, width, after=()):
-    shape = jax.ShapeDtypeStruct((len(parts), parts[0].shape[0], width), parts[0].dtype)
-    return call(
-        functools.partial(stack_kernel, len(parts), begin),
+        refs[-1][number] = part[...]
+
+
+def stack(info, parts, after):
+    shape = jax.ShapeDtypeStruct((len(parts), *parts[0].shape), parts[0].dtype)
+    return call(
+        functools.partial(stack_kernel, len(parts)),
         "stack",
         info,
         [*parts, *after],
@@ -339,19 +431,32 @@
     )
 
 
-def project_kernel(table, lines, keep, splits, info, *refs):
+def place_weights(table, info, pieces, w_ref, begin):
+    part, width = pieces[0].shape[1], w_ref.shape[2]
+    for number, piece in enumerate(pieces):
+        start = pl.multiple_of(info[table.rows + number] * part, part)
+        for d in range(table.count):
+            w_ref[d, pl.ds(start, part)] = piece[d, :, begin : begin + width]
+
+
+def project_kernel(table, lines, shares, keep, splits, info, *refs):
     count = table.count
-    attention, w_ref, r_ref = refs[:lines], refs[lines], refs[lines + 1]
-    parts, h_ref = refs[-1 - len(splits) : -1], refs[-1]
+    attention, pieces = refs[:lines], refs[lines : lines + shares]
+    r_ref = refs[lines + shares]
+    parts, h_ref, w_ref = refs[-2 - 2 * len(splits) : -2], refs[-2], refs[-1]
     rows = r_ref.shape[0]
+
+    @pl.when(pl.program_id(0) == 0)
+    def _():
+        place_weights(table, info, pieces, w_ref, 0)
+
     total = r_ref[:, :keep].astype(jnp.float32)
     for d in range(count):
         block = line_read(table, info, attention, d).astype(jnp.bfloat16)
-        weight = w_ref[:, d].reshape(block.shape[1], keep)
-        total = total + jnp.dot(block, weight, preferred_element_type=jnp.float32)
+        total = total + jnp.dot(block, w_ref[d], preferred_element_type=jnp.float32)
     result = total.astype(jnp.bfloat16)
     h_ref[:, :keep] = result
-    for part, (begin, size) in zip(parts, splits):
+    for part, (begin, size) in zip(parts, splits * 2):
         for row in range(begin, begin + size, rows):
 
             @pl.when(pl.program_id(0) == row // rows)
@@ -359,65 +464,80 @@
                 part[row - begin : row - begin + rows] = result
 
 
-def project(table, info, attention, weights, residual, rows, splits):
+def project(table, info, attention, pieces, residual, keep, rows, splits, after):
     all_rows, slab = residual.shape
-    keep = weights.shape[3]
-    parts = [jax.ShapeDtypeStruct((size, keep), jnp.bfloat16) for _, size in splits]
+    count, part_rows, _ = pieces[0].shape
+    parts = [jax.ShapeDtypeStruct((size, keep), jnp.bfloat16) for _, size in splits * 2]
     row_spec = pl.BlockSpec((rows, slab), lambda i, info: (i, 0))
     return call(
-        functools.partial(project_kernel, table, len(attention), keep, splits),
+        functools.partial(project_kernel, table, len(attention), len(pieces), keep, splits),
         "project",
         info,
-        [*attention, weights, residual],
-        line_spec(attention, rows, lambda i: i) + [whole(weights), row_spec],
+        [*attention, *pieces, residual, *after],
+        line_spec(attention, rows, lambda i: i)
+        + [whole(p) for p in pieces]
+        + [row_spec]
+        + [ANYWHERE] * len(after),
         [whole(part) for part in parts] + [row_spec],
         [*parts, jax.ShapeDtypeStruct(residual.shape, jnp.bfloat16)],
         grid=(all_rows // rows,),
-        vmem=28,
-    )
-
-
-def project_raw_kernel(table, lines, raw_lines, info, *refs):
+        scratch=[pltpu.VMEM((count, len(pieces) * part_rows, keep), jnp.bfloat16)],
+        vmem=36,
+    )
+
+
+def project_raw_kernel(table, lines, raw_lines, shares, keep, info, *refs):
     count = table.count
     attention, residuals = refs[:lines], refs[lines : lines + raw_lines]
-    w_ref = refs[lines + raw_lines]
-    raw_ref, h_ref = refs[-2:]
+    pieces = refs[lines + raw_lines : lines + raw_lines + shares]
+    raw_ref, h_ref, w_ref = refs[-3:]
     raw = h_ref.shape[1]
+
+    @pl.when(pl.program_id(0) == 0)
+    def _():
+        place_weights(table, info, pieces, w_ref, keep)
+
     blocks = [
         line_read(table, info, attention, d).astype(jnp.bfloat16) for d in range(count)
     ]
     for slab in range(count):
-        start = pl.multiple_of(info[table.place + slab] * raw, raw)
+        cols = pl.ds(pl.multiple_of(info[table.place + slab] * raw, raw), raw)
         total = line_read(table, info, residuals, slab)
         for d in range(count):
-            weight = w_ref[:, d, :, pl.ds(start, raw)].reshape(blocks[d].shape[1], raw)
-            total = total + jnp.dot(blocks[d], weight, preferred_element_type=jnp.float32)
+            total = total + jnp.dot(
+                blocks[d], w_ref[d, :, cols], preferred_element_type=jnp.float32
+            )
         result = total.astype(jnp.bfloat16)
         raw_ref[:, slab * raw : (slab + 1) * raw] = result
         if slab == 0:
             h_ref[...] = result
 
 
-def project_raw(table, info, attention, residuals, weights, hidden, raw, rows):
+def project_raw(table, info, attention, residuals, pieces, hidden, keep, raw, rows):
     all_rows, slab = hidden.shape
-    args = [*attention, *residuals, weights, hidden]
-    out = jax.ShapeDtypeStruct((all_rows, table.count * raw), jnp.bfloat16)
-    return call(
-        functools.partial(project_raw_kernel, table, len(attention), len(residuals)),
+    count, part_rows, _ = pieces[0].shape
+    args = [*attention, *residuals, *pieces, hidden]
+    out = jax.ShapeDtypeStruct((all_rows, count * raw), jnp.bfloat16)
+    return call(
+        functools.partial(
+            project_raw_kernel, table, len(attention), len(residuals), len(pieces), keep
+        ),
         "project_raw",
         info,
         args,
         line_spec(attention, rows, lambda i: i)
         + line_spec(residuals, rows, lambda i: i)
-        + [whole(weights), ANYWHERE],
+        + [whole(p) for p in pieces]
+        + [ANYWHERE],
         [
-            pl.BlockSpec((rows, table.count * raw), lambda i, info: (i, 0)),
+            pl.BlockSpec((rows, count * raw), lambda i, info: (i, 0)),
             pl.BlockSpec((rows, raw), lambda i, info: (i, slab // raw - 1)),
         ],
         [out, jax.ShapeDtypeStruct(hidden.shape, jnp.bfloat16)],
         grid=(all_rows // rows,),
         aliases={len(args): 1},
-        vmem=28,
+        scratch=[pltpu.VMEM((count, len(pieces) * part_rows, count * raw), jnp.bfloat16)],
+        vmem=36,
     )
 
 
@@ -492,13 +612,14 @@
     raw = slab // 4 if slab % 512 == 0 and rows > CHUNK else 0
     keep = slab - raw
     chunk = min(CHUNK, rows)
-    sizes = [2 * chunk] + [chunk] * (rows // chunk - 2) if rows // chunk > 2 else [rows]
+    sizes = [chunk] * (rows // chunk)
     splits = [(sum(sizes[:n]), size) for n, size in enumerate(sizes)]
 
     table = Table(contexts, count)
     steering = [context_index, *owners_of(contexts, context_index)]
     steering += [lax.rem(tensor_index + (count - d), count) for d in range(count)]
     steering += [tensor_index == 0, tensor_index == count - 1, share]
+    steering += plane_owners(shares, share)
     info = jnp.stack([jnp.asarray(v).astype(jnp.int32) for v in steering])
 
     cache_local = lax.dynamic_index_in_dim(cache, kv_index, 0, keepdims=False)
@@ -507,7 +628,6 @@
     both = jnp.concatenate([frequencies(HD)] * 2)
     angles = positions.astype(jnp.float32)[:, None] * both[None, :]
     sign = jnp.where(jnp.arange(HD) < HD // 2, -1.0, 1.0)
-    plane = ("groups", "context")
     cuts = cut(table, info, out_weight, depth // shares, slab, keep)
     parts = [cuts[0]]
     for shift in range(1, count):
@@ -520,36 +640,41 @@
     sent = []
 
     def between(block):
-        sent.append(stack(info, parts, 0, keep, [block]))
+        sent.append(stack(info, parts, [block]))
         if raw:
-            sent.append(last_columns(info, residual, raw, [*parts[1:], block]))
+            sent.extend(last_columns(info, residual, raw, [*parts[1:], block]))
         return gate(info, block, sent)
 
     pieces = pieces_of(payload, "context", contexts, between)
-    own_weights = lax.all_gather(sent[0], plane, axis=0, tiled=False)
-    residuals = line_gather(sent[1], count) if raw else []
     mixed = attend(table, info, q_turned, pieces, cache_local.shape[0], chunk)
-    if raw:
-        mixed = gate(info, mixed, residuals[1:4] or residuals)
+    weights = plane_gather(
+        sent[0], groups, contexts, lambda block: gate(info, block, [mixed])
+    )
+    residuals = []
+    if raw and count == 4:
+        far, last = line_far(sent[1])
+        near = gate(info, sent[2], [mixed])
+        residuals = [near, *line_near(near), far, last]
+        mixed = gate(info, mixed, [far])
+    elif raw:
+        residuals = line_gather(sent[1], count)
     attention = line_gather(mixed, count)
 
     *hidden_parts, hidden = project(
-        table, info, attention, own_weights, residual, chunk, splits
+        table, info, attention, weights, residual, keep, chunk, splits, residuals[1:]
     )
     raw_hidden = None
     if raw:
-        raw_weights = stack(info, parts, keep, count * raw, [hidden_parts[0]])
-        raw_weights = lax.all_gather(raw_weights, plane, axis=0, tiled=False)
         raw_hidden, hidden = project_raw(
-            table, info, attention, residuals, raw_weights, hidden, raw, chunk
+            table, info, attention, residuals, weights, hidden, keep, raw, chunk
         )
-    lines = []
-    for number in range(len(splits)):
-        value = hidden_parts[number]
-        if number > 1:
-            made = [raw_hidden] if raw and number == len(splits) - 1 else []
-            value = gate(info, value, [*lines[number - 2][1:], *made])
-        lines.append(line_gather(value, count))
+    lines = chunk_gathers(
+        info,
+        hidden_parts[: len(splits)],
+        hidden_parts[len(splits) :],
+        [raw_hidden] if raw else [],
+        count,
+    )
     normed = None
     for (begin, size), blocks in zip(splits, lines):
         normed = norm_into(

time: 280 us -> 245 us (0.88)
  the two profiles are of different devices: /device:TPU:24 before, /device:TPU:0 now
where the time goes in v6:
time: 245 us
  waiting for transfers between devices  130 us (53%)
  starting transfers between devices  63.9 us (26%)
  Pallas kernels  45.1 us (18%)
  local copies, waits for them, and re-layouts  2.55 us (1%)
  between operations  2.5 us (1%)
    ppermute x6, waiting for transfers between devices, line_far(): far = lax.ppermute(value, 'tensor', [(0, 2), (1, 3), (2, 0), (3, 1)])  49.2 us
    pallas_call x21, Pallas kernels, call(): pl.pallas_call(kernel, grid_spec=pltpu.PrefetchScalarGridSpec(num_scalar_...  45.1 us
    ppermute x6, waiting for transfers between devices, line_far(): return (far, lax.ppermute(far, 'tensor', [(1, 0), (2, 3)]))  30.5 us
    ppermute x6, waiting for transfers between devices, line_near(): return (up, lax.ppermute(value, 'tensor', [(1, 0), (2, 1), (3, 2)]))  26.8 us
    ppermute x6, starting transfers between devices, line_near(): up = lax.ppermute(value, 'tensor', [(0, 1), (1, 2), (2, 3)])  21 us
    ppermute x6, starting transfers between devices, line_far(): far = lax.ppermute(value, 'tensor', [(0, 2), (1, 3), (2, 0), (3, 1)])  14.6 us
    ppermute x3, waiting for transfers between devices, per_device(): parts.append(lax.ppermute(cuts[shift], 'tensor', pairs))  13.6 us
    ppermute x6, starting transfers between devices, line_far(): return (far, lax.ppermute(far, 'tensor', [(1, 0), (2, 3)]))  7.71 us
  transfers between devices with their start and end apart: 37, of which 19 were waited for; matrix products, arithmetic and copies ran while one was open for 0% of the time, Pallas kernels for 14%

profile of v6, /device:TPU:0, one launch (start us, length us, event | category | flops | bytes accessed | tf_op | source)
XLA Modules:
  0.0 244.8 jit_solution(12720072864302002214)
XLA Ops:
  17.0 5.2 %collective-permute-done.2.refs_1_ = bf16[32,3584]{1,0:T(8,128)(2,1)S(1)} collective-permute-done((bf16[32,3584]{1,0:T(8,128)(2,1)}, bf16[32,3584]{1,0:T(8,128)(2,1)S(1)}, u32[]{:S(2)}, u32[]{:S(2)}) %collective-permute-start.2) | collective-permute-done | bytes 229408 | tf_op jit(solution)/shard_map/ppermute | solution.py:635
  22.2 8.4 %collective-permute-done.3.refs_2_ = bf16[32,3584]{1,0:T(8,128)(2,1)S(1)} collective-permute-done((bf16[32,3584]{1,0:T(8,128)(2,1)}, bf16[32,3584]{1,0:T(8,128)(2,1)S(1)}, u32[]{:S(2)}, u32[]{:S(2)}) %collective-permute-start.3) | collective-permute-done | bytes 229408 | tf_op jit(solution)/shard_map/ppermute | solution.py:635
  34.0 4.5 %collective-permute-start.6 = (bf16[512,512]{1,0:T(8,128)(2,1)S(1)}, bf16[512,512]{1,0:T(8,128)(2,1)S(1)}, u32[]{:S(2)}, u32[]{:S(2)}) collective-permute-start(bf16[512,512]{1,0:T(8,128)(2,1)S(1)} %get-tuple-element.27.refs_2_), channel_id=1, source_target_pairs={{0,8},{4,12},{8,0},{12,4},{1,9},{5,13},{9,1},{13,5},{2,10},{6,14},... | collective-permute-start | bytes 1572872 | tf_op jit(solution)/shard_map/ppermute | solution.py:101
  40.0 12.2 %attend.1.refs_0_.refs_1_ = bf16[512,256]{1,0:T(8,128)(2,1)S(1)} custom-call(s32[20]{0:T(128)S(1)} %copy-done.7, bf16[512,256]{1,0:T(8,128)(2,1)S(1)} %get-tuple-element.22.q_ref, bf16[1552,256]{1,0:T(8,128)(2,1)S(1)} %get-tuple-element.23.refs_0_, bf16[1552,256]{1,0:T(8,128)(2,1)S(1)} %collective-permute-done.refs_1_, bf16[1552,256]{1,0:T(8,128)(2,1)S(1)} %gate.10.refs_2_, ...), custom_call_target="tpu_custom_call" | custom-call | flops 12884901888 | bytes 1 | tf_op jit(solution)/shard_map/attend/pallas_call | solution.py:156
  52.2 4.0 %collective-permute-done.15.refs_0_ = bf16[4,32,3584]{2,1,0:T(8,128)(2,1)S(1)} collective-permute-done((bf16[4,32,3584]{2,1,0:T(8,128)(2,1)S(1)}, bf16[4,32,3584]{2,1,0:T(8,128)(2,1)S(1)}, u32[]{:S(2)}, u32[]{:S(2)}) %collective-permute-start.15) | collective-permute-done | bytes 917536 | tf_op jit(solution)/shard_map/ppermute | solution.py:76
  64.3 4.8 %collective-permute-start.9 = (bf16[512,256]{1,0:T(8,128)(2,1)S(1)}, bf16[512,256]{1,0:T(8,128)(2,1)S(1)}, u32[]{:S(2)}, u32[]{:S(2)}) collective-permute-start(bf16[512,256]{1,0:T(8,128)(2,1)S(1)} %gate.11.refs_0_), channel_id=1, source_target_pairs={{0,8},{4,12},{8,0},{12,4},{1,9},{5,13},{9,1},{13,5},{2,10},{6,14},... | collective-permute-start | bytes 786440 | tf_op jit(solution)/shard_map/ppermute | solution.py:101
  70.5 12.4 %collective-permute-done.13.refs_17_.refs_9_ = bf16[512,512]{1,0:T(8,128)(2,1)S(1)} collective-permute-done((bf16[512,512]{1,0:T(8,128)(2,1)S(1)}, bf16[512,512]{1,0:T(8,128)(2,1)S(1)}, u32[]{:S(2)}, u32[]{:S(2)}) %collective-permute-start.13) | collective-permute-done | bytes 524320 | tf_op jit(solution)/shard_map/ppermute | solution.py:102
  84.8 4.6 %collective-permute-start.11 = (bf16[512,512]{1,0:T(8,128)(2,1)S(1)}, bf16[512,512]{1,0:T(8,128)(2,1)S(1)}, u32[]{:S(2)}, u32[]{:S(2)}) collective-permute-start(bf16[512,512]{1,0:T(8,128)(2,1)S(1)} %gate.12.refs_5_), channel_id=1, source_target_pairs={{0,4},{4,8},{8,12},{1,5},{5,9},{9,13},{2,6},{6,10},{10,14},{3,7},{... | collective-permute-start | bytes 1572872 | tf_op jit(solution)/shard_map/ppermute | solution.py:96
  89.3 4.2 %collective-permute-done.8.refs_2_ = bf16[512,256]{1,0:T(8,128)(2,1)S(1)} collective-permute-done((bf16[512,256]{1,0:T(8,128)(2,1)S(1)}, bf16[512,256]{1,0:T(8,128)(2,1)S(1)}, u32[]{:S(2)}, u32[]{:S(2)}) %collective-permute-start.8) | collective-permute-done | bytes 262176 | tf_op jit(solution)/shard_map/ppermute | solution.py:97
  94.9 5.5 %collective-permute-done.11.refs_14_.refs_6_ = bf16[512,512]{1,0:T(8,128)(2,1)S(1)} collective-permute-done((bf16[512,512]{1,0:T(8,128)(2,1)S(1)}, bf16[512,512]{1,0:T(8,128)(2,1)S(1)}, u32[]{:S(2)}, u32[]{:S(2)}) %collective-permute-start.11) | collective-permute-done | bytes 524320 | tf_op jit(solution)/shard_map/ppermute | solution.py:96
  101.7 8.6 %collective-permute-done.12.refs_15_.refs_7_ = bf16[512,512]{1,0:T(8,128)(2,1)S(1)} collective-permute-done((bf16[512,512]{1,0:T(8,128)(2,1)S(1)}, bf16[512,512]{1,0:T(8,128)(2,1)S(1)}, u32[]{:S(2)}, u32[]{:S(2)}) %collective-permute-start.12) | collective-permute-done | bytes 524320 | tf_op jit(solution)/shard_map/ppermute | solution.py:97
  110.3 4.1 %collective-permute-done.10.refs_4_ = bf16[512,256]{1,0:T(8,128)(2,1)S(1)} collective-permute-done((bf16[512,256]{1,0:T(8,128)(2,1)S(1)}, bf16[512,256]{1,0:T(8,128)(2,1)S(1)}, u32[]{:S(2)}, u32[]{:S(2)}) %collective-permute-start.10) | collective-permute-done | bytes 262176 | tf_op jit(solution)/shard_map/ppermute | solution.py:102
  114.4 4.4 %project.1 = (bf16[128,1536]{1,0:T(8,128)(2,1)S(1)}, bf16[128,1536]{1,0:T(8,128)(2,1)S(1)}, bf16[128,1536]{1,0:T(8,128)(2,1)S(1)}, bf16[128,1536]{1,0:T(8,128)(2...) custom-call(s32[20]{0:T(128)S(1)} %copy-done.7, ...), custom_call_target="tpu_custom_call" | custom-call | flops 1 | bytes 1 | tf_op jit(solution)/shard_map/project/pallas_call | solution.py:156
  121.7 23.5 %collective-permute-done.21.refs_1_.refs_3_ = bf16[128,1536]{1,0:T(8,128)(2,1)S(1)} collective-permute-done((bf16[128,1536]{1,0:T(8,128)(2,1)S(1)}, bf16[128,1536]{1,0:T(8,128)(2,1)S(1)}, u32[]{:S(2)}, u32[]{:S(2)}) %collective-permute-start.21) | collective-permute-done | bytes 393248 | tf_op jit(solution)/shard_map/ppermute | solution.py:101
  147.2 15.0 %collective-permute-done.26.refs_1_.refs_3_ = bf16[128,1536]{1,0:T(8,128)(2,1)S(1)} collective-permute-done((bf16[128,1536]{1,0:T(8,128)(2,1)S(1)}, bf16[128,1536]{1,0:T(8,128)(2,1)S(1)}, u32[]{:S(2)}, u32[]{:S(2)}) %collective-permute-start.26) | collective-permute-done | bytes 393248 | tf_op jit(solution)/shard_map/ppermute | solution.py:101
  163.5 7.0 %collective-permute-done.22.refs_3_ = bf16[128,1536]{1,0:T(8,128)(2,1)S(1)} collective-permute-done((bf16[128,1536]{1,0:T(8,128)(2,1)S(1)}, bf16[128,1536]{1,0:T(8,128)(2,1)S(1)}, u32[]{:S(2)}, u32[]{:S(2)}) %collective-permute-start.22) | collective-permute-done | bytes 393248 | tf_op jit(solution)/shard_map/ppermute | solution.py:101
  172.4 4.6 %collective-permute-start.35 = (bf16[128,1536]{1,0:T(8,128)(2,1)S(1)}, bf16[128,1536]{1,0:T(8,128)(2,1)S(1)}, u32[]{:S(2)}, u32[]{:S(2)}) collective-permute-start(bf16[128,1536]{1,0:T(8,128)(2,1)S(1)} %gate.19.refs_0_), channel_id=1, source_target_pairs={{0,4},{4,8},{8,12},{1,5},{5,9},{9,13},{2,6},{6,10},{10,14},{3,7},{... | collective-permute-start | bytes 1179656 | tf_op jit(solution)/shard_map/ppermute | solution.py:96
  185.1 7.1 %collective-permute-done.23.refs_1_.refs_4_ = bf16[128,1536]{1,0:T(8,128)(2,1)S(1)} collective-permute-done((bf16[128,1536]{1,0:T(8,128)(2,1)S(1)}, bf16[128,1536]{1,0:T(8,128)(2,1)S(1)}, u32[]{:S(2)}, u32[]{:S(2)}) %collective-permute-start.23) | collective-permute-done | bytes 393248 | tf_op jit(solution)/shard_map/ppermute | solution.py:102
  193.5 4.6 %project_raw.1 = (bf16[512,2048]{1,0:T(8,128)(2,1)S(1)}, bf16[512,2048]{1,0:T(8,128)(2,1)}) custom-call(s32[20]{0:T(128)S(1)} %copy-done.7, bf16[512,256]{1,0:T(8,128)(2,1)S(1)} %gate.11.refs_0_, bf16[512,256]{1,0:T(8,128)(2,1)S(1)} %collective-permute-done.7.refs_1_, ...), custom_call_target="tpu_custom_call", output_to_operand_aliasing={{1}: (19, {})} | custom-call | flops 1 | bytes 1 | tf_op jit(solution)/shard_map/project_raw/pallas_call | solution.py:156
  199.2 4.5 %collective-permute-start.30 = (bf16[128,1536]{1,0:T(8,128)(2,1)S(1)}, bf16[128,1536]{1,0:T(8,128)(2,1)S(1)}, u32[]{:S(2)}, u32[]{:S(2)}) collective-permute-start(bf16[128,1536]{1,0:T(8,128)(2,1)S(1)} %gate.17.refs_0_), channel_id=1, source_target_pairs={{0,4},{4,8},{8,12},{1,5},{5,9},{9,13},{2,6},{6,10},{10,14},{3,7},{... | collective-permute-start | bytes 1179656 | tf_op jit(solution)/shard_map/ppermute | solution.py:96
  203.7 5.2 %collective-permute-done.36.refs_2_ = bf16[128,1536]{1,0:T(8,128)(2,1)S(1)} collective-permute-done((bf16[128,1536]{1,0:T(8,128)(2,1)S(1)}, bf16[128,1536]{1,0:T(8,128)(2,1)S(1)}, u32[]{:S(2)}, u32[]{:S(2)}) %collective-permute-start.36) | collective-permute-done | bytes 393248 | tf_op jit(solution)/shard_map/ppermute | solution.py:97
  211.5 4.6 %collective-permute-start.24 = (bf16[128,1536]{1,0:T(8,128)(2,1)S(1)}, bf16[128,1536]{1,0:T(8,128)(2,1)S(1)}, u32[]{:S(2)}, u32[]{:S(2)}) collective-permute-start(bf16[128,1536]{1,0:T(8,128)(2,1)S(1)} %gate.15.refs_0_), channel_id=1, source_target_pairs={{0,4},{4,8},{8,12},{1,5},{5,9},{9,13},{2,6},{6,10},{10,14},{3,7},{... | collective-permute-start | bytes 1179656 | tf_op jit(solution)/shard_map/ppermute | solution.py:96
  229.2 5.0 %collective-permute-done.28.refs_4_ = bf16[128,1536]{1,0:T(8,128)(2,1)S(1)} collective-permute-done((bf16[128,1536]{1,0:T(8,128)(2,1)S(1)}, bf16[128,1536]{1,0:T(8,128)(2,1)S(1)}, u32[]{:S(2)}, u32[]{:S(2)}) %collective-permute-start.28) | collective-permute-done | bytes 393248 | tf_op jit(solution)/shard_map/ppermute | solution.py:102
  234.2 7.2 %collective-permute-done.25.refs_2_ = bf16[128,1536]{1,0:T(8,128)(2,1)S(1)} collective-permute-done((bf16[128,1536]{1,0:T(8,128)(2,1)S(1)}, bf16[128,1536]{1,0:T(8,128)(2,1)S(1)}, u32[]{:S(2)}, u32[]{:S(2)}) %collective-permute-start.25) | collective-permute-done | bytes 393248 | tf_op jit(solution)/shard_map/ppermute | solution.py:97
  (92 shorter events, 71.1 us)
Async XLA Ops:
  8.5 22.1 %collective-permute-start.1 = (bf16[1552,256]{1,0:T(8,128)(2,1)S(1)}, bf16[1552,256]{1,0:T(8,128)(2,1)S(1)}, u32[]{:S(2)}, u32[]{:S(2)}) collective-permute-start(bf16[1552,256]{1,0:T(8,128)(2,1)S(1)} %get-tuple-element.23.refs_0_), channel_id=1, source_target_pairs={{0,2},{1,3},{2,0},{3,1},{4,6},{5,7},{6,4},{7,5},{8,10},{9,11},{10,... | collective-permute-start | bytes 2383880 | tf_op jit(solution)/shard_map/ppermute | solution.py:42
  17.0 23.0 %collective-permute-start = (bf16[1552,256]{1,0:T(8,128)(2,1)S(1)}, bf16[1552,256]{1,0:T(8,128)(2,1)S(1)}, u32[]{:S(2)}, u32[]{:S(2)}) collective-permute-start(bf16[1552,256]{1,0:T(8,128)(2,1)S(1)} %get-tuple-element.23.refs_0_), channel_id=1, source_target_pairs={{0,1},{1,0},{2,3},{3,2},{4,5},{5,4},{6,7},{7,6},{8,9},{9,8},{10,11... | collective-permute-start | bytes 2383880 | tf_op jit(solution)/shard_map/ppermute | solution.py:42
  33.4 22.8 %collective-permute-start.15 = (bf16[4,32,3584]{2,1,0:T(8,128)(2,1)S(1)}, bf16[4,32,3584]{2,1,0:T(8,128)(2,1)S(1)}, u32[]{:S(2)}, u32[]{:S(2)}) collective-permute-start(bf16[4,32,3584]{2,1,0:T(8,128)(2,1)S(1)} %stack.89.refs_1_.refs_5_.refs_10_), channel_id=1, source_target_pairs={{0,2},{1,3},{2,0},{3,1},{4,6},{5,7},{6,4},{7,5},{8,10},{9,11},{10,... | collective-permute-start | bytes 2752520 | tf_op jit(solution)/shard_map/ppermute | solution.py:76
  34.0 28.0 %collective-permute-start.6 = (bf16[512,512]{1,0:T(8,128)(2,1)S(1)}, bf16[512,512]{1,0:T(8,128)(2,1)S(1)}, u32[]{:S(2)}, u32[]{:S(2)}) collective-permute-start(bf16[512,512]{1,0:T(8,128)(2,1)S(1)} %get-tuple-element.27.refs_2_), channel_id=1, source_target_pairs={{0,8},{4,12},{8,0},{12,4},{1,9},{5,13},{9,1},{13,5},{2,10},{6,14},... | collective-permute-start | bytes 1572872 | tf_op jit(solution)/shard_map/ppermute | solution.py:101
  38.5 30.7 %collective-permute-start.17 = (bf16[4,32,3584]{2,1,0:T(8,128)(2,1)S(1)}, bf16[4,32,3584]{2,1,0:T(8,128)(2,1)S(1)}, u32[]{:S(2)}, u32[]{:S(2)}) collective-permute-start(bf16[4,32,3584]{2,1,0:T(8,128)(2,1)S(1)} %stack.89.refs_1_.refs_5_.refs_10_), channel_id=1, source_target_pairs={{0,16},{16,0},{1,17},{17,1},{2,18},{18,2},{3,19},{19,3},{4,20},{20... | collective-permute-start | bytes 2752520 | tf_op jit(solution)/shard_map/ppermute | solution.py:76
  40.0 30.5 %collective-permute-start.14 = (bf16[4,32,3584]{2,1,0:T(8,128)(2,1)S(1)}, bf16[4,32,3584]{2,1,0:T(8,128)(2,1)S(1)}, u32[]{:S(2)}, u32[]{:S(2)}) collective-permute-start(bf16[4,32,3584]{2,1,0:T(8,128)(2,1)S(1)} %stack.89.refs_1_.refs_5_.refs_10_), channel_id=1, source_target_pairs={{0,1},{1,0},{2,3},{3,2},{4,5},{5,4},{6,7},{7,6},{8,9},{9,8},{10,11... | collective-permute-start | bytes 2752520 | tf_op jit(solution)/shard_map/ppermute | solution.py:76
  56.7 26.2 %collective-permute-start.19 = (bf16[4,32,3584]{2,1,0:T(8,128)(2,1)S(1)}, bf16[4,32,3584]{2,1,0:T(8,128)(2,1)S(1)}, u32[]{:S(2)}, u32[]{:S(2)}) collective-permute-start(bf16[4,32,3584]{2,1,0:T(8,128)(2,1)S(1)} %gate.13.refs_7_.refs_12_), channel_id=1, source_target_pairs={{0,16},{16,0},{1,17},{17,1},{2,18},{18,2},{3,19},{19,3},{4,20},{20... | collective-permute-start | bytes 2752520 | tf_op jit(solution)/shard_map/ppermute | solution.py:76
  70.5 43.9 %collective-permute-start.16 = (bf16[4,32,3584]{2,1,0:T(8,128)(2,1)S(1)}, bf16[4,32,3584]{2,1,0:T(8,128)(2,1)S(1)}, u32[]{:S(2)}, u32[]{:S(2)}) collective-permute-start(bf16[4,32,3584]{2,1,0:T(8,128)(2,1)S(1)} %gate.13.refs_7_.refs_12_), channel_id=1, source_target_pairs={{0,1},{1,0},{2,3},{3,2},{4,5},{5,4},{6,7},{7,6},{8,9},{9,8},{10,11... | collective-permute-start | bytes 2752520 | tf_op jit(solution)/shard_map/ppermute | solution.py:76
  82.9 31.5 %collective-permute-start.18 = (bf16[4,32,3584]{2,1,0:T(8,128)(2,1)S(1)}, bf16[4,32,3584]{2,1,0:T(8,128)(2,1)S(1)}, u32[]{:S(2)}, u32[]{:S(2)}) collective-permute-start(bf16[4,32,3584]{2,1,0:T(8,128)(2,1)S(1)} %collective-permute-done.17.refs_9_.refs_14_), channel_id=1, source_target_pairs={{0,1},{1,0},{2,3},{3,2},{4,5},{5,4},{6,7},{7,6},{8,9},{9,8},{10,11... | collective-permute-start | bytes 2752520 | tf_op jit(solution)/shard_map/ppermute | solution.py:76
  82.9 31.5 %collective-permute-start.20 = (bf16[4,32,3584]{2,1,0:T(8,128)(2,1)S(1)}, bf16[4,32,3584]{2,1,0:T(8,128)(2,1)S(1)}, u32[]{:S(2)}, u32[]{:S(2)}) collective-permute-start(bf16[4,32,3584]{2,1,0:T(8,128)(2,1)S(1)} %collective-permute-done.19.refs_11_.refs_16_), channel_id=1, source_target_pairs={{0,1},{1,0},{2,3},{3,2},{4,5},{5,4},{6,7},{7,6},{8,9},{9,8},{10,11... | collective-permute-start | bytes 2752520 | tf_op jit(solution)/shard_map/ppermute | solution.py:76
  118.8 26.4 %collective-permute-start.21 = (bf16[128,1536]{1,0:T(8,128)(2,1)S(1)}, bf16[128,1536]{1,0:T(8,128)(2,1)S(1)}, u32[]{:S(2)}, u32[]{:S(2)}) collective-permute-start(bf16[128,1536]{1,0:T(8,128)(2,1)S(1)} %get-tuple-element.33), channel_id=1, source_target_pairs={{0,8},{4,12},{8,0},{12,4},{1,9},{5,13},{9,1},{13,5},{2,10},{6,14},... | collective-permute-start | bytes 1179656 | tf_op jit(solution)/shard_map/ppermute | solution.py:101
  118.8 43.4 %collective-permute-start.26 = (bf16[128,1536]{1,0:T(8,128)(2,1)S(1)}, bf16[128,1536]{1,0:T(8,128)(2,1)S(1)}, u32[]{:S(2)}, u32[]{:S(2)}) collective-permute-start(bf16[128,1536]{1,0:T(8,128)(2,1)S(1)} %get-tuple-element.35), channel_id=1, source_target_pairs={{0,8},{4,12},{8,0},{12,4},{1,9},{5,13},{9,1},{13,5},{2,10},{6,14},... | collective-permute-start | bytes 1179656 | tf_op jit(solution)/shard_map/ppermute | solution.py:101
  145.8 24.7 %collective-permute-start.22 = (bf16[128,1536]{1,0:T(8,128)(2,1)S(1)}, bf16[128,1536]{1,0:T(8,128)(2,1)S(1)}, u32[]{:S(2)}, u32[]{:S(2)}) collective-permute-start(bf16[128,1536]{1,0:T(8,128)(2,1)S(1)} %gate.14), channel_id=1, source_target_pairs={{0,8},{4,12},{8,0},{12,4},{1,9},{5,13},{9,1},{13,5},{2,10},{6,14},... | collective-permute-start | bytes 1179656 | tf_op jit(solution)/shard_map/ppermute | solution.py:101
  145.9 33.0 %collective-permute-start.32 = (bf16[128,1536]{1,0:T(8,128)(2,1)S(1)}, bf16[128,1536]{1,0:T(8,128)(2,1)S(1)}, u32[]{:S(2)}, u32[]{:S(2)}) collective-permute-start(bf16[128,1536]{1,0:T(8,128)(2,1)S(1)} %collective-permute-done.21.refs_1_.refs_3_), channel_id=1, source_target_pairs={{4,0},{8,12},{5,1},{9,13},{6,2},{10,14},{7,3},{11,15},{20,16},{24,... | collective-permute-start | bytes 1179656 | tf_op jit(solution)/shard_map/ppermute | solution.py:102
  170.5 21.6 %collective-permute-start.23 = (bf16[128,1536]{1,0:T(8,128)(2,1)S(1)}, bf16[128,1536]{1,0:T(8,128)(2,1)S(1)}, u32[]{:S(2)}, u32[]{:S(2)}) collective-permute-start(bf16[128,1536]{1,0:T(8,128)(2,1)S(1)} %collective-permute-done.22.refs_3_), channel_id=1, source_target_pairs={{4,0},{8,12},{5,1},{9,13},{6,2},{10,14},{7,3},{11,15},{20,16},{24,... | collective-permute-start | bytes 1179656 | tf_op jit(solution)/shard_map/ppermute | solution.py:102
  172.4 26.8 %collective-permute-start.35 = (bf16[128,1536]{1,0:T(8,128)(2,1)S(1)}, bf16[128,1536]{1,0:T(8,128)(2,1)S(1)}, u32[]{:S(2)}, u32[]{:S(2)}) collective-permute-start(bf16[128,1536]{1,0:T(8,128)(2,1)S(1)} %gate.19.refs_0_), channel_id=1, source_target_pairs={{0,4},{4,8},{8,12},{1,5},{5,9},{9,13},{2,6},{6,10},{10,14},{3,7},{... | collective-permute-start | bytes 1179656 | tf_op jit(solution)/shard_map/ppermute | solution.py:96
  177.0 31.9 %collective-permute-start.36 = (bf16[128,1536]{1,0:T(8,128)(2,1)S(1)}, bf16[128,1536]{1,0:T(8,128)(2,1)S(1)}, u32[]{:S(2)}, u32[]{:S(2)}) collective-permute-start(bf16[128,1536]{1,0:T(8,128)(2,1)S(1)} %gate.19.refs_0_), channel_id=1, source_target_pairs={{4,0},{8,4},{12,8},{5,1},{9,5},{13,9},{6,2},{10,6},{14,10},{7,3},{... | collective-permute-start | bytes 1179656 | tf_op jit(solution)/shard_map/ppermute | solution.py:97
  178.8 31.4 %collective-permute-start.27 = (bf16[128,1536]{1,0:T(8,128)(2,1)S(1)}, bf16[128,1536]{1,0:T(8,128)(2,1)S(1)}, u32[]{:S(2)}, u32[]{:S(2)}) collective-permute-start(bf16[128,1536]{1,0:T(8,128)(2,1)S(1)} %gate.16), channel_id=1, source_target_pairs={{0,8},{4,12},{8,0},{12,4},{1,9},{5,13},{9,1},{13,5},{2,10},{6,14},... | collective-permute-start | bytes 1179656 | tf_op jit(solution)/shard_map/ppermute | solution.py:101
  183.6 27.9 %collective-permute-start.33 = (bf16[128,1536]{1,0:T(8,128)(2,1)S(1)}, bf16[128,1536]{1,0:T(8,128)(2,1)S(1)}, u32[]{:S(2)}, u32[]{:S(2)}) collective-permute-start(bf16[128,1536]{1,0:T(8,128)(2,1)S(1)} %gate.18.refs_0_), channel_id=1, source_target_pairs={{0,4},{4,8},{8,12},{1,5},{5,9},{9,13},{2,6},{6,10},{10,14},{3,7},{... | collective-permute-start | bytes 1179656 | tf_op jit(solution)/shard_map/ppermute | solution.py:96
  192.2 25.2 %collective-permute-start.34 = (bf16[128,1536]{1,0:T(8,128)(2,1)S(1)}, bf16[128,1536]{1,0:T(8,128)(2,1)S(1)}, u32[]{:S(2)}, u32[]{:S(2)}) collective-permute-start(bf16[128,1536]{1,0:T(8,128)(2,1)S(1)} %gate.18.refs_0_), channel_id=1, source_target_pairs={{4,0},{8,4},{12,8},{5,1},{9,5},{13,9},{6,2},{10,6},{14,10},{7,3},{... | collective-permute-start | bytes 1179656 | tf_op jit(solution)/shard_map/ppermute | solution.py:97
  199.2 26.3 %collective-permute-start.30 = (bf16[128,1536]{1,0:T(8,128)(2,1)S(1)}, bf16[128,1536]{1,0:T(8,128)(2,1)S(1)}, u32[]{:S(2)}, u32[]{:S(2)}) collective-permute-start(bf16[128,1536]{1,0:T(8,128)(2,1)S(1)} %gate.17.refs_0_), channel_id=1, source_target_pairs={{0,4},{4,8},{8,12},{1,5},{5,9},{9,13},{2,6},{6,10},{10,14},{3,7},{... | collective-permute-start | bytes 1179656 | tf_op jit(solution)/shard_map/ppermute | solution.py:96
  210.2 24.0 %collective-permute-start.28 = (bf16[128,1536]{1,0:T(8,128)(2,1)S(1)}, bf16[128,1536]{1,0:T(8,128)(2,1)S(1)}, u32[]{:S(2)}, u32[]{:S(2)}) collective-permute-start(bf16[128,1536]{1,0:T(8,128)(2,1)S(1)} %collective-permute-done.27.refs_3_), channel_id=1, source_target_pairs={{4,0},{8,12},{5,1},{9,13},{6,2},{10,14},{7,3},{11,15},{20,16},{24,... | collective-permute-start | bytes 1179656 | tf_op jit(solution)/shard_map/ppermute | solution.py:102
  211.5 22.7 %collective-permute-start.24 = (bf16[128,1536]{1,0:T(8,128)(2,1)S(1)}, bf16[128,1536]{1,0:T(8,128)(2,1)S(1)}, u32[]{:S(2)}, u32[]{:S(2)}) collective-permute-start(bf16[128,1536]{1,0:T(8,128)(2,1)S(1)} %gate.15.refs_0_), channel_id=1, source_target_pairs={{0,4},{4,8},{8,12},{1,5},{5,9},{9,13},{2,6},{6,10},{10,14},{3,7},{... | collective-permute-start | bytes 1179656 | tf_op jit(solution)/shard_map/ppermute | solution.py:96
  217.3 24.0 %collective-permute-start.25 = (bf16[128,1536]{1,0:T(8,128)(2,1)S(1)}, bf16[128,1536]{1,0:T(8,128)(2,1)S(1)}, u32[]{:S(2)}, u32[]{:S(2)}) collective-permute-start(bf16[128,1536]{1,0:T(8,128)(2,1)S(1)} %gate.15.refs_0_), channel_id=1, source_target_pairs={{4,0},{8,4},{12,8},{5,1},{9,5},{13,9},{6,2},{10,6},{14,10},{7,3},{... | collective-permute-start | bytes 1179656 | tf_op jit(solution)/shard_map/ppermute | solution.py:97
  (21 other events, 274.0 us)

commit v7 on v6

--- a/solution.py
+++ b/solution.py
@@ -16,6 +16,7 @@
 CHUNK = 128
 KEY_BLOCK = 512
 ATTEND_FLOPS = 16
+RAW_PART = 8
 TAIL = 16
 DIGIT = 32
 ANYWHERE = pl.BlockSpec(memory_space=pl.ANY)
@@ -58,7 +59,7 @@
     return [(me + count - shift) % count for shift in range(count)]
 
 
-def plane_gather(value, groups, contexts, between=lambda block: block):
+def plane_gather(value, swapped, groups, contexts, first, then):
     count = groups * contexts
     if count & (count - 1):
         gathered = lax.all_gather(value, ("groups", "context"), axis=0, tiled=False)
@@ -66,7 +67,6 @@
     held = {0: value}
     bits = [1 << b for b in range(contexts.bit_length() - 2, 0, -1)]
     bits += [contexts << b for b in range(groups.bit_length() - 1)]
-    bits += [1] if contexts > 1 else []
     for bit in bits:
         axis, flip, size = ("context", bit, contexts)
         if bit >= contexts:
@@ -75,8 +75,16 @@
         for mask in sorted(held):
             held[mask | bit] = lax.ppermute(held[mask], axis, pairs)
         if bit == bits[0]:
-            held[bit] = between(held[bit])
+            held[bit] = first(held[bit])
+    if contexts > 1:
+        for mask in sorted(held):
+            held[mask] = then(held[mask], mask) if mask else held[mask]
+            held[mask | 1] = core_swap(held[mask], contexts) if mask else swapped
     return [held[mask] for mask in range(count)]
+
+
+def core_swap(value, contexts):
+    return lax.ppermute(value, "context", [(i, i ^ 1) for i in range(contexts)])
 
 
 def plane_owners(count, me):
@@ -102,19 +110,20 @@
     return far, lax.ppermute(far, "tensor", [(1, 0), (2, 3)])
 
 
-def chunk_gathers(info, values, copies, made, count):
+def chunk_gathers(info, values, copies, first, made, count):
     if count != 4:
         return [line_gather(value, count) for value in values]
     fars, lines = [], []
     for number, value in enumerate(values):
+        after = [fars[number - 1][0]] if number else first
+        fars.append(line_far(gate(info, value, after) if after else value))
+    for number, value in enumerate(copies):
+        after = list(lines[number - 1][1:3]) if number else []
         if number > 1:
-            value = gate(info, value, [fars[number - 2][0]])
-        fars.append(line_far(value))
-    for number, value in enumerate(copies):
-        before = [fars[number - 1][1] if number else fars[0][0]]
+            after.append(fars[number - 2][1])
         if number == len(copies) // 2:
-            before += made
-        value = gate(info, value, before)
+            after += made
+        value = gate(info, value, after) if after else value
         lines.append([value, *line_near(value), *fars[number]])
     return lines
 
@@ -196,46 +205,6 @@
     for head in range(q_ref.shape[1] // HD):
         cols = slice(head * HD, (head + 1) * HD)
         q_out[:, cols] = turn(q_ref[:, cols])
-
-
-def cut_kernel(table, slab, keep, info, w_ref, *refs):
-    count, raw = table.count, slab - keep
-    outs, rows_ref, sem = refs[:count], refs[-2], refs[-1]
-    part = rows_ref.shape[0]
-    start = pl.multiple_of(info[table.share] * part, part)
-    copy = pltpu.make_async_copy(w_ref.at[pl.ds(start, part)], rows_ref, sem)
-    copy.start()
-    copy.wait()
-    for d, out in enumerate(outs):
-        target = lax.rem(info[table.place] + d, count)
-        out[:, :keep] = rows_ref[:, pl.ds(pl.multiple_of(target * slab, slab), keep)]
-        for j in range(count if raw else 0):
-            out[:, keep + j * raw : keep + (j + 1) * raw] = rows_ref[
-                :, j * slab + keep : (j + 1) * slab
-            ]
-
-
-def cut(table, info, out_weight, part, slab, keep):
-    shape = jax.ShapeDtypeStruct((part, keep + table.count * (slab - keep)), out_weight.dtype)
-    return call(
-        functools.partial(cut_kernel, table, slab, keep),
-        "cut",
-        info,
-        [out_weight],
-        [ANYWHERE],
-        [whole(shape)] * table.count,
-        [shape] * table.count,
-        scratch=[
-            pltpu.VMEM((part, out_weight.shape[1]), out_weight.dtype),
-            pltpu.SemaphoreType.DMA(()),
-        ],
-        vmem=0,
-    )
-
-
-def last_columns_kernel(info, *refs):
-    refs[-1][...] = refs[0][...]
-    refs[-2][...] = refs[0][...]
 
 
 def cut_kernel(table, slab, keep, info, w_ref, *refs):
@@ -411,7 +380,7 @@
         out_ref[:, h * HD : (h + 1) * HD] = result[h * rows : (h + 1) * rows]
 
 
-def attend(table, info, queries, pieces, slots, rows):
+def attend(table, info, queries, pieces, slots, rows, after):
     all_rows, width = queries.shape
     heads = width // HD
     keys = sum(a.shape[0] - TAIL for a in pieces)
@@ -420,8 +389,8 @@
         functools.partial(attend_kernel, table, slots),
         "attend",
         info,
-        [queries, *pieces],
-        [chunk_spec] + [whole(a) for a in pieces],
+        [queries, *pieces, *after],
+        [chunk_spec] + [whole(a) for a in pieces] + [ANYWHERE] * len(after),
         chunk_spec,
         jax.ShapeDtypeStruct((all_rows, width), jnp.bfloat16),
         grid=(all_rows // rows,),
@@ -609,7 +578,7 @@
     groups = lax.axis_size("groups")
     shares = groups * contexts
     share = lax.axis_index("groups") * contexts + context_index
-    raw = slab // 4 if slab % 512 == 0 and rows > CHUNK else 0
+    raw = slab // RAW_PART if slab % (RAW_PART * HD) == 0 else 0
     keep = slab - raw
     chunk = min(CHUNK, rows)
     sizes = [chunk] * (rows // chunk)
@@ -640,28 +609,40 @@
     sent = []
 
     def between(block):
-        sent.append(stack(info, parts, [block]))
+        sent.append(stack(info, parts, [payload]))
         if raw:
-            sent.extend(last_columns(info, residual, raw, [*parts[1:], block]))
+            sent.extend(last_columns(info, residual, raw, [*parts[1:], payload]))
         return gate(info, block, sent)
 
     pieces = pieces_of(payload, "context", contexts, between)
-    mixed = attend(table, info, q_turned, pieces, cache_local.shape[0], chunk)
+    early = line_far(sent[1]) if raw and count == 4 else ()
+    swapped = core_swap(sent[0], contexts) if contexts % 2 == 0 else sent[0]
+    mixed = attend(
+        table, info, q_turned, pieces, cache_local.shape[0], chunk, [*early[:1], swapped]
+    )
+    if count == 4:
+        far, last = line_far(mixed)
+        attention = [mixed, *line_near(mixed), far, last]
+    else:
+        attention = line_gather(mixed, count)
+        far = mixed
     weights = plane_gather(
-        sent[0], groups, contexts, lambda block: gate(info, block, [mixed])
+        sent[0],
+        swapped,
+        groups,
+        contexts,
+        lambda block: gate(info, block, [mixed]),
+        lambda block, mask: gate(info, block, attention[1 : 3 if mask & (mask - 1) == 0 else 5]),
     )
     residuals = []
-    if raw and count == 4:
-        far, last = line_far(sent[1])
-        near = gate(info, sent[2], [mixed])
-        residuals = [near, *line_near(near), far, last]
-        mixed = gate(info, mixed, [far])
+    if early:
+        near = gate(info, sent[2], [far])
+        residuals = [near, *line_near(near), *early]
     elif raw:
         residuals = line_gather(sent[1], count)
-    attention = line_gather(mixed, count)
 
     *hidden_parts, hidden = project(
-        table, info, attention, weights, residual, keep, chunk, splits, residuals[1:]
+        table, info, attention, weights, residual, keep, chunk, splits, residuals[4:]
     )
     raw_hidden = None
     if raw:
@@ -672,6 +653,7 @@
         info,
         hidden_parts[: len(splits)],
         hidden_parts[len(splits) :],
+        residuals[1:3],
         [raw_hidden] if raw else [],
         count,
     )

time: 245 us -> 243 us (level)
  waiting for transfers between devices: 130 us -> 102 us
  starting transfers between devices: 63.9 us -> 86.5 us
  local copies, waits for them, and re-layouts: 2.55 us -> 5.15 us
    ppermute x6, starting transfers between devices: 21 us -> 54.6 us  [line_near(): up = lax.ppermute(value, 'tensor', [(0, 1), (1, 2), (2, 3)])]
    ppermute x6, waiting for transfers between devices: 30.5 us -> 16.2 us  [line_far(): return (far, lax.ppermute(far, 'tensor', [(1, 0), (2, 3)]))]
    ppermute x6, starting transfers between devices: 14.6 us -> 3.12 us  [line_far(): far = lax.ppermute(value, 'tensor', [(0, 2), (1, 3), (2, 0), (3, 1)])]
    ppermute x6, waiting for transfers between devices: 26.8 us -> 18.7 us  [line_near(): return (up, lax.ppermute(value, 'tensor', [(1, 0), (2, 1), (3, 2)]))]
    ppermute x6, waiting for transfers between devices: 49.2 us -> 53.5 us  [line_far(): far = lax.ppermute(value, 'tensor', [(0, 2), (1, 3), (2, 0), (3, 1)])]
    ppermute x7 -> x3, waiting for transfers between devices: 4.02 us -> 0.01 us  [plane_gather(): held[mask | bit] = lax.ppermute(held[mask], axis, pairs)]
    ppermute x6, waiting for transfers between devices: 5.53 us -> 2.12 us  [line_near(): up = lax.ppermute(value, 'tensor', [(0, 1), (1, 2), (2, 3)])]
    ppermute x3, waiting for transfers between devices: 13.6 us -> 10.4 us  [per_device(): parts.append(lax.ppermute(cuts[shift], 'tensor', pairs))]
  transfers between devices with their start and end apart: 37 -> 37, of which waited for: 19 -> 18; matrix products, arithmetic and copies ran while one was open for 0% -> 0% of each run, Pallas kernels for 14% -> 16%
where the time goes in v7:
time: 243 us
  waiting for transfers between devices  102 us (42%)
  starting transfers between devices  86.5 us (36%)
  Pallas kernels  45.7 us (19%)
  local copies, waits for them, and re-layouts  5.15 us (2%)
  between operations  2.62 us (1%)
    ppermute x6, starting transfers between devices, line_near(): up = lax.ppermute(value, 'tensor', [(0, 1), (1, 2), (2, 3)])  54.6 us
    ppermute x6, waiting for transfers between devices, line_far(): far = lax.ppermute(value, 'tensor', [(0, 2), (1, 3), (2, 0), (3, 1)])  53.5 us
    pallas_call x24, Pallas kernels, call(): pl.pallas_call(kernel, grid_spec=pltpu.PrefetchScalarGridSpec(num_scalar_...  45.7 us
    ppermute x6, waiting for transfers between devices, line_near(): return (up, lax.ppermute(value, 'tensor', [(1, 0), (2, 1), (3, 2)]))  18.7 us
    ppermute x6, waiting for transfers between devices, line_far(): return (far, lax.ppermute(far, 'tensor', [(1, 0), (2, 3)]))  16.2 us
    ppermute x3, waiting for transfers between devices, per_device(): parts.append(lax.ppermute(cuts[shift], 'tensor', pairs))  10.4 us
    ppermute x6, starting transfers between devices, line_near(): return (up, lax.ppermute(value, 'tensor', [(1, 0), (2, 1), (3, 2)]))  7.74 us
    ppermute x6, starting transfers between devices, line_far(): return (far, lax.ppermute(far, 'tensor', [(1, 0), (2, 3)]))  7.71 us
  transfers between devices with their start and end apart: 37, of which 18 were waited for; matrix products, arithmetic and copies ran while one was open for 0% of the time, Pallas kernels for 16%

profile of v7, /device:TPU:0, one launch (start us, length us, event | category | flops | bytes accessed | tf_op | source)
XLA Modules:
  0.0 242.6 jit_solution(4467280645932347712)
XLA Ops:
  20.3 4.1 %collective-permute-done.2.refs_1_ = bf16[32,2816]{1,0:T(8,128)(2,1)S(1)} collective-permute-done((bf16[32,2816]{1,0:T(8,128)(2,1)}, bf16[32,2816]{1,0:T(8,128)(2,1)S(1)}, u32[]{:S(2)}, u32[]{:S(2)}) %collective-permute-start.2) | collective-permute-done | bytes 180256 | tf_op jit(solution)/shard_map/ppermute | solution.py:604
  24.4 6.3 %collective-permute-done.3.refs_2_ = bf16[32,2816]{1,0:T(8,128)(2,1)S(1)} collective-permute-done((bf16[32,2816]{1,0:T(8,128)(2,1)}, bf16[32,2816]{1,0:T(8,128)(2,1)S(1)}, u32[]{:S(2)}, u32[]{:S(2)}) %collective-permute-start.3) | collective-permute-done | bytes 180256 | tf_op jit(solution)/shard_map/ppermute | solution.py:604
  38.0 10.7 %collective-permute-done.6.refs_4_.refs_8_ = bf16[512,256]{1,0:T(8,128)(2,1)S(1)} collective-permute-done((bf16[512,256]{1,0:T(8,128)(2,1)S(1)}, bf16[512,256]{1,0:T(8,128)(2,1)S(1)}, u32[]{:S(2)}, u32[]{:S(2)}) %collective-permute-start.6) | collective-permute-done | bytes 262176 | tf_op jit(solution)/shard_map/ppermute | solution.py:109
  50.2 12.2 %attend.1.refs_1_.refs_0_ = bf16[512,256]{1,0:T(8,128)(2,1)S(1)} custom-call(s32[20]{0:T(128)S(1)} %copy-done.4, bf16[512,256]{1,0:T(8,128)(2,1)S(1)} %get-tuple-element.22.q_ref, bf16[1552,256]{1,0:T(8,128)(2,1)S(1)} %get-tuple-element.23.refs_4_.refs_0_, bf16[1552,256]{1,0:T(8,128)(2,1)S(1)} %collective-permute-done.refs_1_, ...), custom_call_target="tpu_custom_call" | custom-call | flops 12884901888 | bytes 1 | tf_op jit(solution)/shard_map/attend/pallas_call | solution.py:165
  63.6 6.0 %collective-permute-start.8 = (bf16[512,256]{1,0:T(8,128)(2,1)S(1)}, bf16[512,256]{1,0:T(8,128)(2,1)S(1)}, u32[]{:S(2)}, u32[]{:S(2)}) collective-permute-start(bf16[512,256]{1,0:T(8,128)(2,1)S(1)} %attend.1.refs_1_.refs_0_), channel_id=1, source_target_pairs={{0,4},{4,8},{8,12},{1,5},{5,9},{9,13},{2,6},{6,10},{10,14},{3,7},{... | collective-permute-start | bytes 786440 | tf_op jit(solution)/shard_map/ppermute | solution.py:104
  70.9 8.0 %collective-permute-done.10.refs_1_.refs_3_ = bf16[512,256]{1,0:T(8,128)(2,1)S(1)} collective-permute-done((bf16[512,256]{1,0:T(8,128)(2,1)S(1)}, bf16[512,256]{1,0:T(8,128)(2,1)S(1)}, u32[]{:S(2)}, u32[]{:S(2)}) %collective-permute-start.10) | collective-permute-done | bytes 262176 | tf_op jit(solution)/shard_map/ppermute | solution.py:109
  83.5 4.7 %collective-permute-done.11.refs_4_ = bf16[512,256]{1,0:T(8,128)(2,1)S(1)} collective-permute-done((bf16[512,256]{1,0:T(8,128)(2,1)S(1)}, bf16[512,256]{1,0:T(8,128)(2,1)S(1)}, u32[]{:S(2)}, u32[]{:S(2)}) %collective-permute-start.11) | collective-permute-done | bytes 262176 | tf_op jit(solution)/shard_map/ppermute | solution.py:110
  91.8 4.6 %collective-permute-start.12 = (bf16[512,256]{1,0:T(8,128)(2,1)S(1)}, bf16[512,256]{1,0:T(8,128)(2,1)S(1)}, u32[]{:S(2)}, u32[]{:S(2)}) collective-permute-start(bf16[512,256]{1,0:T(8,128)(2,1)S(1)} %gate.14.refs_5_), channel_id=1, source_target_pairs={{0,4},{4,8},{8,12},{1,5},{5,9},{9,13},{2,6},{6,10},{10,14},{3,7},{... | collective-permute-start | bytes 786440 | tf_op jit(solution)/shard_map/ppermute | solution.py:104
  96.4 3.7 %collective-permute-done.14.refs_14_.refs_9_ = bf16[512,256]{1,0:T(8,128)(2,1)S(1)} collective-permute-done((bf16[512,256]{1,0:T(8,128)(2,1)S(1)}, bf16[512,256]{1,0:T(8,128)(2,1)S(1)}, u32[]{:S(2)}, u32[]{:S(2)}) %collective-permute-start.14) | collective-permute-done | bytes 262176 | tf_op jit(solution)/shard_map/ppermute | solution.py:110
  101.4 4.7 %project.1 = (bf16[128,1792]{1,0:T(8,128)(2,1)S(1)}, bf16[128,1792]{1,0:T(8,128)(2,1)S(1)}, bf16[128,1792]{1,0:T(8,128)(2,1)S(1)}, bf16[128,1792]{1,0:T(8,128)(2...) custom-call(s32[20]{0:T(128)S(1)} %copy-done.5, ...), custom_call_target="tpu_custom_call" | custom-call | flops 1 | bytes 1 | tf_op jit(solution)/shard_map/project/pallas_call | solution.py:165
  112.8 18.2 %collective-permute-done.25.refs_1_.refs_3_ = bf16[128,1792]{1,0:T(8,128)(2,1)S(1)} collective-permute-done((bf16[128,1792]{1,0:T(8,128)(2,1)S(1)}, bf16[128,1792]{1,0:T(8,128)(2,1)S(1)}, u32[]{:S(2)}, u32[]{:S(2)}) %collective-permute-start.25) | collective-permute-done | bytes 458784 | tf_op jit(solution)/shard_map/ppermute | solution.py:109
  135.9 17.8 %collective-permute-start.23 = (bf16[128,1792]{1,0:T(8,128)(2,1)S(1)}, bf16[128,1792]{1,0:T(8,128)(2,1)S(1)}, u32[]{:S(2)}, u32[]{:S(2)}) collective-permute-start(bf16[128,1792]{1,0:T(8,128)(2,1)S(1)} %gate.19.refs_0_), channel_id=1, source_target_pairs={{0,4},{4,8},{8,12},{1,5},{5,9},{9,13},{2,6},{6,10},{10,14},{3,7},{... | collective-permute-start | bytes 1376264 | tf_op jit(solution)/shard_map/ppermute | solution.py:104
  155.0 5.5 %collective-permute-done.29.refs_1_.refs_3_ = bf16[128,1792]{1,0:T(8,128)(2,1)S(1)} collective-permute-done((bf16[128,1792]{1,0:T(8,128)(2,1)S(1)}, bf16[128,1792]{1,0:T(8,128)(2,1)S(1)}, u32[]{:S(2)}, u32[]{:S(2)}) %collective-permute-start.29) | collective-permute-done | bytes 458784 | tf_op jit(solution)/shard_map/ppermute | solution.py:109
  165.8 4.6 %collective-permute-done.24.refs_2_ = bf16[128,1792]{1,0:T(8,128)(2,1)S(1)} collective-permute-done((bf16[128,1792]{1,0:T(8,128)(2,1)S(1)}, bf16[128,1792]{1,0:T(8,128)(2,1)S(1)}, u32[]{:S(2)}, u32[]{:S(2)}) %collective-permute-start.24) | collective-permute-done | bytes 458784 | tf_op jit(solution)/shard_map/ppermute | solution.py:105
  170.9 12.4 %collective-permute-start.27 = (bf16[128,1792]{1,0:T(8,128)(2,1)S(1)}, bf16[128,1792]{1,0:T(8,128)(2,1)S(1)}, u32[]{:S(2)}, u32[]{:S(2)}) collective-permute-start(bf16[128,1792]{1,0:T(8,128)(2,1)S(1)} %gate.21.refs_0_), channel_id=1, source_target_pairs={{0,4},{4,8},{8,12},{1,5},{5,9},{9,13},{2,6},{6,10},{10,14},{3,7},{... | collective-permute-start | bytes 1376264 | tf_op jit(solution)/shard_map/ppermute | solution.py:104
  184.6 5.5 %collective-permute-done.33.refs_1_.refs_3_ = bf16[128,1792]{1,0:T(8,128)(2,1)S(1)} collective-permute-done((bf16[128,1792]{1,0:T(8,128)(2,1)S(1)}, bf16[128,1792]{1,0:T(8,128)(2,1)S(1)}, u32[]{:S(2)}, u32[]{:S(2)}) %collective-permute-start.33) | collective-permute-done | bytes 458784 | tf_op jit(solution)/shard_map/ppermute | solution.py:109
  194.1 5.7 %collective-permute-done.28.refs_2_ = bf16[128,1792]{1,0:T(8,128)(2,1)S(1)} collective-permute-done((bf16[128,1792]{1,0:T(8,128)(2,1)S(1)}, bf16[128,1792]{1,0:T(8,128)(2,1)S(1)}, u32[]{:S(2)}, u32[]{:S(2)}) %collective-permute-start.28) | collective-permute-done | bytes 458784 | tf_op jit(solution)/shard_map/ppermute | solution.py:105
  200.4 12.4 %collective-permute-start.31 = (bf16[128,1792]{1,0:T(8,128)(2,1)S(1)}, bf16[128,1792]{1,0:T(8,128)(2,1)S(1)}, u32[]{:S(2)}, u32[]{:S(2)}) collective-permute-start(bf16[128,1792]{1,0:T(8,128)(2,1)S(1)} %gate.23.refs_0_), channel_id=1, source_target_pairs={{0,4},{4,8},{8,12},{1,5},{5,9},{9,13},{2,6},{6,10},{10,14},{3,7},{... | collective-permute-start | bytes 1376264 | tf_op jit(solution)/shard_map/ppermute | solution.py:104
  214.1 5.5 %collective-permute-done.34.refs_3_ = bf16[128,1792]{1,0:T(8,128)(2,1)S(1)} collective-permute-done((bf16[128,1792]{1,0:T(8,128)(2,1)S(1)}, bf16[128,1792]{1,0:T(8,128)(2,1)S(1)}, u32[]{:S(2)}, u32[]{:S(2)}) %collective-permute-start.34) | collective-permute-done | bytes 458784 | tf_op jit(solution)/shard_map/ppermute | solution.py:109
  220.9 3.5 %norm.4.refs_6_ = bf16[512,8192]{1,0:T(8,128)(2,1)} custom-call(s32[20]{0:T(128)S(1)} %copy-done.5, f32[1,8192]{1,0:T(1,128)S(1)} %bitcast.23, bf16[128,1792]{1,0:T(8,128)(2,1)S(1)} %get-tuple-element.34.refs_0_, bf16[128,1792]{1,0:T(8,128)(2,1)S(1)} %collective-permute-done.21.refs_1_, bf16[128,1792]{1,0:T(8,128)(2,1)S(1)} %collective-permute-done.22.refs_2_, ...), custom_call_target="tpu_custom_call" | custom-call | flops 1 | bytes 1 | tf_op jit(solution)/shard_map/norm/pallas_call | solution.py:165
  224.4 3.5 %norm.5.refs_6_ = bf16[512,8192]{1,0:T(8,128)(2,1)} custom-call(s32[20]{0:T(128)S(1)} %copy-done.5, f32[1,8192]{1,0:T(1,128)S(1)} %bitcast.24, bf16[128,1792]{1,0:T(8,128)(2,1)S(1)} %gate.19.refs_0_, bf16[128,1792]{1,0:T(8,128)(2,1)S(1)} %collective-permute-done.23.refs_1_, ...), custom_call_target="tpu_custom_call", output_to_operand_aliasing={{}: (8, {})} | custom-call | flops 1 | bytes 1 | tf_op jit(solution)/shard_map/norm/pallas_call | solution.py:165
  227.9 3.5 %norm.6.refs_6_ = bf16[512,8192]{1,0:T(8,128)(2,1)} custom-call(s32[20]{0:T(128)S(1)} %copy-done.5, f32[1,8192]{1,0:T(1,128)S(1)} %bitcast.25, bf16[128,1792]{1,0:T(8,128)(2,1)S(1)} %gate.21.refs_0_, bf16[128,1792]{1,0:T(8,128)(2,1)S(1)} %collective-permute-done.27.refs_1_, ...), custom_call_target="tpu_custom_call", output_to_operand_aliasing={{}: (8, {})} | custom-call | flops 1 | bytes 1 | tf_op jit(solution)/shard_map/norm/pallas_call | solution.py:165
  231.3 7.8 %collective-permute-done.35.refs_4_ = bf16[128,1792]{1,0:T(8,128)(2,1)S(1)} collective-permute-done((bf16[128,1792]{1,0:T(8,128)(2,1)S(1)}, bf16[128,1792]{1,0:T(8,128)(2,1)S(1)}, u32[]{:S(2)}, u32[]{:S(2)}) %collective-permute-start.35) | collective-permute-done | bytes 458784 | tf_op jit(solution)/shard_map/ppermute | solution.py:110
  239.1 3.5 %norm.7 = bf16[512,8192]{1,0:T(8,128)(2,1)} custom-call(s32[20]{0:T(128)S(1)} %copy-done.5, f32[1,8192]{1,0:T(1,128)S(1)} %bitcast.26, bf16[128,1792]{1,0:T(8,128)(2,1)S(1)} %gate.23.refs_0_, bf16[128,1792]{1,0:T(8,128)(2,1)S(1)} %collective-permute-done.31.refs_1_, ...), custom_call_target="tpu_custom_call", output_to_operand_aliasing={{}: (8, {})} | custom-call | flops 1 | bytes 1 | tf_op jit(solution)/shard_map/norm/pallas_call | solution.py:165
  (95 shorter events, 65.7 us)
Async XLA Ops:
  11.8 20.7 %collective-permute-start.1 = (bf16[1552,256]{1,0:T(8,128)(2,1)S(1)}, bf16[1552,256]{1,0:T(8,128)(2,1)S(1)}, u32[]{:S(2)}, u32[]{:S(2)}) collective-permute-start(bf16[1552,256]{1,0:T(8,128)(2,1)S(1)} %get-tuple-element.23.refs_4_.refs_0_), channel_id=1, source_target_pairs={{0,2},{1,3},{2,0},{3,1},{4,6},{5,7},{6,4},{7,5},{8,10},{9,11},{10,... | collective-permute-start | bytes 2383880 | tf_op jit(solution)/shard_map/ppermute | solution.py:43
  20.3 29.9 %collective-permute-start = (bf16[1552,256]{1,0:T(8,128)(2,1)S(1)}, bf16[1552,256]{1,0:T(8,128)(2,1)S(1)}, u32[]{:S(2)}, u32[]{:S(2)}) collective-permute-start(bf16[1552,256]{1,0:T(8,128)(2,1)S(1)} %get-tuple-element.23.refs_4_.refs_0_), channel_id=1, source_target_pairs={{0,1},{1,0},{2,3},{3,2},{4,5},{5,4},{6,7},{7,6},{8,9},{9,8},{10,11... | collective-permute-start | bytes 2383880 | tf_op jit(solution)/shard_map/ppermute | solution.py:43
  33.1 17.2 %collective-permute-start.5 = (bf16[1552,256]{1,0:T(8,128)(2,1)S(1)}, bf16[1552,256]{1,0:T(8,128)(2,1)S(1)}, u32[]{:S(2)}, u32[]{:S(2)}) collective-permute-start(bf16[1552,256]{1,0:T(8,128)(2,1)S(1)} %gate.13.refs_2_), channel_id=1, source_target_pairs={{0,1},{1,0},{2,3},{3,2},{4,5},{5,4},{6,7},{7,6},{8,9},{9,8},{10,11... | collective-permute-start | bytes 2383880 | tf_op jit(solution)/shard_map/ppermute | solution.py:43
  33.2 17.1 %collective-permute-start.7 = (bf16[4,32,2816]{2,1,0:T(8,128)(2,1)S(1)}, bf16[4,32,2816]{2,1,0:T(8,128)(2,1)S(1)}, u32[]{:S(2)}, u32[]{:S(2)}) collective-permute-start(bf16[4,32,2816]{2,1,0:T(8,128)(2,1)S(1)} %stack.89.refs_1_.refs_5_.refs_10_), channel_id=1, source_target_pairs={{0,1},{1,0},{2,3},{3,2},{4,5},{5,4},{6,7},{7,6},{8,9},{9,8},{10,11... | collective-permute-start | bytes 2162696 | tf_op jit(solution)/shard_map/ppermute | solution.py:87
  36.5 26.0 %collective-permute-start.15 = (bf16[4,32,2816]{2,1,0:T(8,128)(2,1)S(1)}, bf16[4,32,2816]{2,1,0:T(8,128)(2,1)S(1)}, u32[]{:S(2)}, u32[]{:S(2)}) collective-permute-start(bf16[4,32,2816]{2,1,0:T(8,128)(2,1)S(1)} %stack.89.refs_1_.refs_5_.refs_10_), channel_id=1, source_target_pairs={{0,2},{1,3},{2,0},{3,1},{4,6},{5,7},{6,4},{7,5},{8,10},{9,11},{10,... | collective-permute-start | bytes 2162696 | tf_op jit(solution)/shard_map/ppermute | solution.py:76
  48.7 31.5 %collective-permute-start.17 = (bf16[4,32,2816]{2,1,0:T(8,128)(2,1)S(1)}, bf16[4,32,2816]{2,1,0:T(8,128)(2,1)S(1)}, u32[]{:S(2)}, u32[]{:S(2)}) collective-permute-start(bf16[4,32,2816]{2,1,0:T(8,128)(2,1)S(1)} %stack.89.refs_1_.refs_5_.refs_10_), channel_id=1, source_target_pairs={{0,16},{16,0},{1,17},{17,1},{2,18},{18,2},{3,19},{19,3},{4,20},{20... | collective-permute-start | bytes 2162696 | tf_op jit(solution)/shard_map/ppermute | solution.py:76
  63.1 25.2 %collective-permute-start.19 = (bf16[4,32,2816]{2,1,0:T(8,128)(2,1)S(1)}, bf16[4,32,2816]{2,1,0:T(8,128)(2,1)S(1)}, u32[]{:S(2)}, u32[]{:S(2)}) collective-permute-start(bf16[4,32,2816]{2,1,0:T(8,128)(2,1)S(1)} %gate.15.refs_0_), channel_id=1, source_target_pairs={{0,16},{16,0},{1,17},{17,1},{2,18},{18,2},{3,19},{19,3},{4,20},{20... | collective-permute-start | bytes 2162696 | tf_op jit(solution)/shard_map/ppermute | solution.py:76
  83.5 17.9 %collective-permute-start.18 = (bf16[4,32,2816]{2,1,0:T(8,128)(2,1)S(1)}, bf16[4,32,2816]{2,1,0:T(8,128)(2,1)S(1)}, u32[]{:S(2)}, u32[]{:S(2)}) collective-permute-start(bf16[4,32,2816]{2,1,0:T(8,128)(2,1)S(1)} %gate.17.refs_9_.refs_14_), channel_id=1, source_target_pairs={{0,1},{1,0},{2,3},{3,2},{4,5},{5,4},{6,7},{7,6},{8,9},{9,8},{10,11... | collective-permute-start | bytes 2162696 | tf_op jit(solution)/shard_map/ppermute | solution.py:87
  109.9 21.1 %collective-permute-start.25 = (bf16[128,1792]{1,0:T(8,128)(2,1)S(1)}, bf16[128,1792]{1,0:T(8,128)(2,1)S(1)}, u32[]{:S(2)}, u32[]{:S(2)}) collective-permute-start(bf16[128,1792]{1,0:T(8,128)(2,1)S(1)} %gate.20), channel_id=1, source_target_pairs={{0,8},{4,12},{8,0},{12,4},{1,9},{5,13},{9,1},{13,5},{2,10},{6,14},... | collective-permute-start | bytes 1376264 | tf_op jit(solution)/shard_map/ppermute | solution.py:109
  110.0 23.0 %collective-permute-start.21 = (bf16[128,1792]{1,0:T(8,128)(2,1)S(1)}, bf16[128,1792]{1,0:T(8,128)(2,1)S(1)}, u32[]{:S(2)}, u32[]{:S(2)}) collective-permute-start(bf16[128,1792]{1,0:T(8,128)(2,1)S(1)} %get-tuple-element.34.refs_0_), channel_id=1, source_target_pairs={{0,4},{4,8},{8,12},{1,5},{5,9},{9,13},{2,6},{6,10},{10,14},{3,7},{... | collective-permute-start | bytes 1376264 | tf_op jit(solution)/shard_map/ppermute | solution.py:104
  111.5 23.9 %collective-permute-start.22 = (bf16[128,1792]{1,0:T(8,128)(2,1)S(1)}, bf16[128,1792]{1,0:T(8,128)(2,1)S(1)}, u32[]{:S(2)}, u32[]{:S(2)}) collective-permute-start(bf16[128,1792]{1,0:T(8,128)(2,1)S(1)} %get-tuple-element.34.refs_0_), channel_id=1, source_target_pairs={{4,0},{8,4},{12,8},{5,1},{9,5},{13,9},{6,2},{10,6},{14,10},{7,3},{... | collective-permute-start | bytes 1376264 | tf_op jit(solution)/shard_map/ppermute | solution.py:105
  131.6 29.0 %collective-permute-start.29 = (bf16[128,1792]{1,0:T(8,128)(2,1)S(1)}, bf16[128,1792]{1,0:T(8,128)(2,1)S(1)}, u32[]{:S(2)}, u32[]{:S(2)}) collective-permute-start(bf16[128,1792]{1,0:T(8,128)(2,1)S(1)} %gate.22), channel_id=1, source_target_pairs={{0,8},{4,12},{8,0},{12,4},{1,9},{5,13},{9,1},{13,5},{2,10},{6,14},... | collective-permute-start | bytes 1376264 | tf_op jit(solution)/shard_map/ppermute | solution.py:109
  131.6 34.1 %collective-permute-start.26 = (bf16[128,1792]{1,0:T(8,128)(2,1)S(1)}, bf16[128,1792]{1,0:T(8,128)(2,1)S(1)}, u32[]{:S(2)}, u32[]{:S(2)}) collective-permute-start(bf16[128,1792]{1,0:T(8,128)(2,1)S(1)} %collective-permute-done.25.refs_1_.refs_3_), channel_id=1, source_target_pairs={{4,0},{8,12},{5,1},{9,13},{6,2},{10,14},{7,3},{11,15},{20,16},{24,... | collective-permute-start | bytes 1376264 | tf_op jit(solution)/shard_map/ppermute | solution.py:110
  135.9 29.8 %collective-permute-start.23 = (bf16[128,1792]{1,0:T(8,128)(2,1)S(1)}, bf16[128,1792]{1,0:T(8,128)(2,1)S(1)}, u32[]{:S(2)}, u32[]{:S(2)}) collective-permute-start(bf16[128,1792]{1,0:T(8,128)(2,1)S(1)} %gate.19.refs_0_), channel_id=1, source_target_pairs={{0,4},{4,8},{8,12},{1,5},{5,9},{9,13},{2,6},{6,10},{10,14},{3,7},{... | collective-permute-start | bytes 1376264 | tf_op jit(solution)/shard_map/ppermute | solution.py:104
  153.7 16.6 %collective-permute-start.24 = (bf16[128,1792]{1,0:T(8,128)(2,1)S(1)}, bf16[128,1792]{1,0:T(8,128)(2,1)S(1)}, u32[]{:S(2)}, u32[]{:S(2)}) collective-permute-start(bf16[128,1792]{1,0:T(8,128)(2,1)S(1)} %gate.19.refs_0_), channel_id=1, source_target_pairs={{4,0},{8,4},{12,8},{5,1},{9,5},{13,9},{6,2},{10,6},{14,10},{7,3},{... | collective-permute-start | bytes 1376264 | tf_op jit(solution)/shard_map/ppermute | solution.py:105
  161.1 29.0 %collective-permute-start.33 = (bf16[128,1792]{1,0:T(8,128)(2,1)S(1)}, bf16[128,1792]{1,0:T(8,128)(2,1)S(1)}, u32[]{:S(2)}, u32[]{:S(2)}) collective-permute-start(bf16[128,1792]{1,0:T(8,128)(2,1)S(1)} %gate.24), channel_id=1, source_target_pairs={{0,8},{4,12},{8,0},{12,4},{1,9},{5,13},{9,1},{13,5},{2,10},{6,14},... | collective-permute-start | bytes 1376264 | tf_op jit(solution)/shard_map/ppermute | solution.py:109
  164.4 27.6 %collective-permute-start.30 = (bf16[128,1792]{1,0:T(8,128)(2,1)S(1)}, bf16[128,1792]{1,0:T(8,128)(2,1)S(1)}, u32[]{:S(2)}, u32[]{:S(2)}) collective-permute-start(bf16[128,1792]{1,0:T(8,128)(2,1)S(1)} %collective-permute-done.29.refs_1_.refs_3_), channel_id=1, source_target_pairs={{4,0},{8,12},{5,1},{9,13},{6,2},{10,14},{7,3},{11,15},{20,16},{24,... | collective-permute-start | bytes 1376264 | tf_op jit(solution)/shard_map/ppermute | solution.py:110
  170.9 23.2 %collective-permute-start.27 = (bf16[128,1792]{1,0:T(8,128)(2,1)S(1)}, bf16[128,1792]{1,0:T(8,128)(2,1)S(1)}, u32[]{:S(2)}, u32[]{:S(2)}) collective-permute-start(bf16[128,1792]{1,0:T(8,128)(2,1)S(1)} %gate.21.refs_0_), channel_id=1, source_target_pairs={{0,4},{4,8},{8,12},{1,5},{5,9},{9,13},{2,6},{6,10},{10,14},{3,7},{... | collective-permute-start | bytes 1376264 | tf_op jit(solution)/shard_map/ppermute | solution.py:104
  183.3 16.6 %collective-permute-start.28 = (bf16[128,1792]{1,0:T(8,128)(2,1)S(1)}, bf16[128,1792]{1,0:T(8,128)(2,1)S(1)}, u32[]{:S(2)}, u32[]{:S(2)}) collective-permute-start(bf16[128,1792]{1,0:T(8,128)(2,1)S(1)} %gate.21.refs_0_), channel_id=1, source_target_pairs={{4,0},{8,4},{12,8},{5,1},{9,5},{13,9},{6,2},{10,6},{14,10},{7,3},{... | collective-permute-start | bytes 1376264 | tf_op jit(solution)/shard_map/ppermute | solution.py:105
  190.6 29.0 %collective-permute-start.34 = (bf16[128,1792]{1,0:T(8,128)(2,1)S(1)}, bf16[128,1792]{1,0:T(8,128)(2,1)S(1)}, u32[]{:S(2)}, u32[]{:S(2)}) collective-permute-start(bf16[128,1792]{1,0:T(8,128)(2,1)S(1)} %gate.25), channel_id=1, source_target_pairs={{0,8},{4,12},{8,0},{12,4},{1,9},{5,13},{9,1},{13,5},{2,10},{6,14},... | collective-permute-start | bytes 1376264 | tf_op jit(solution)/shard_map/ppermute | solution.py:109
  190.7 37.2 %collective-permute-start.36 = (bf16[128,1792]{1,0:T(8,128)(2,1)S(1)}, bf16[128,1792]{1,0:T(8,128)(2,1)S(1)}, u32[]{:S(2)}, u32[]{:S(2)}) collective-permute-start(bf16[128,1792]{1,0:T(8,128)(2,1)S(1)} %collective-permute-done.33.refs_1_.refs_3_), channel_id=1, source_target_pairs={{4,0},{8,12},{5,1},{9,13},{6,2},{10,14},{7,3},{11,15},{20,16},{24,... | collective-permute-start | bytes 1376264 | tf_op jit(solution)/shard_map/ppermute | solution.py:110
  200.4 30.9 %collective-permute-start.31 = (bf16[128,1792]{1,0:T(8,128)(2,1)S(1)}, bf16[128,1792]{1,0:T(8,128)(2,1)S(1)}, u32[]{:S(2)}, u32[]{:S(2)}) collective-permute-start(bf16[128,1792]{1,0:T(8,128)(2,1)S(1)} %gate.23.refs_0_), channel_id=1, source_target_pairs={{0,4},{4,8},{8,12},{1,5},{5,9},{9,13},{2,6},{6,10},{10,14},{3,7},{... | collective-permute-start | bytes 1376264 | tf_op jit(solution)/shard_map/ppermute | solution.py:104
  212.8 18.5 %collective-permute-start.32 = (bf16[128,1792]{1,0:T(8,128)(2,1)S(1)}, bf16[128,1792]{1,0:T(8,128)(2,1)S(1)}, u32[]{:S(2)}, u32[]{:S(2)}) collective-permute-start(bf16[128,1792]{1,0:T(8,128)(2,1)S(1)} %gate.23.refs_0_), channel_id=1, source_target_pairs={{4,0},{8,4},{12,8},{5,1},{9,5},{13,9},{6,2},{10,6},{14,10},{7,3},{... | collective-permute-start | bytes 1376264 | tf_op jit(solution)/shard_map/ppermute | solution.py:105
  219.6 19.5 %collective-permute-start.35 = (bf16[128,1792]{1,0:T(8,128)(2,1)S(1)}, bf16[128,1792]{1,0:T(8,128)(2,1)S(1)}, u32[]{:S(2)}, u32[]{:S(2)}) collective-permute-start(bf16[128,1792]{1,0:T(8,128)(2,1)S(1)} %collective-permute-done.34.refs_3_), channel_id=1, source_target_pairs={{4,0},{8,12},{5,1},{9,13},{6,2},{10,14},{7,3},{11,15},{20,16},{24,... | collective-permute-start | bytes 1376264 | tf_op jit(solution)/shard_map/ppermute | solution.py:110
  (21 other events, 297.3 us)

commit v8 on v7

--- a/solution.py
+++ b/solution.py
@@ -16,7 +16,7 @@
 CHUNK = 128
 KEY_BLOCK = 512
 ATTEND_FLOPS = 16
-RAW_PART = 8
+RAW_PART = 4
 TAIL = 16
 DIGIT = 32
 ANYWHERE = pl.BlockSpec(memory_space=pl.ANY)
@@ -59,7 +59,7 @@
     return [(me + count - shift) % count for shift in range(count)]
 
 
-def plane_gather(value, swapped, groups, contexts, first, then):
+def plane_gather(value, groups, contexts, first, then):
     count = groups * contexts
     if count & (count - 1):
         gathered = lax.all_gather(value, ("groups", "context"), axis=0, tiled=False)
@@ -79,7 +79,7 @@
     if contexts > 1:
         for mask in sorted(held):
             held[mask] = then(held[mask], mask) if mask else held[mask]
-            held[mask | 1] = core_swap(held[mask], contexts) if mask else swapped
+            held[mask | 1] = core_swap(held[mask], contexts)
     return [held[mask] for mask in range(count)]
 
 
@@ -115,12 +115,13 @@
         return [line_gather(value, count) for value in values]
     fars, lines = [], []
     for number, value in enumerate(values):
-        after = [fars[number - 1][0]] if number else first
-        fars.append(line_far(gate(info, value, after) if after else value))
+        fars.append(line_far(gate(info, value, [fars[-1][0]]) if number else value))
     for number, value in enumerate(copies):
         after = list(lines[number - 1][1:3]) if number else []
         if number > 1:
             after.append(fars[number - 2][1])
+        if number == 1:
+            after += first
         if number == len(copies) // 2:
             after += made
         value = gate(info, value, after) if after else value
@@ -184,17 +185,40 @@
     return pl.BlockSpec(tuple(a.shape), lambda i, info: zeros)
 
 
-def prepare_kernel(info, q_ref, kv_ref, cache_ref, cos_ref, sin_ref, length_ref, *refs):
-    q_out, kv_out = refs[-2:]
+def prepare_kernel(table, slab, keep, info, q_hbm, kv_hbm, cache_hbm, w_hbm, cos_ref, sin_ref,
+                   length_ref, *refs):
+    count, raw = table.count, slab - keep
+    q_out, kv_out, outs = refs[0], refs[1], refs[2 : 2 + count]
+    q_ref, kv_ref, w_ref, sems = refs[2 + count :]
+    slots, rows, part = cache_hbm.shape[0], q_ref.shape[0], w_ref.shape[0]
+    span, tail = slice(slots, slots + rows), slice(slots + rows, slots + rows + TAIL)
+    start = pl.multiple_of(info[table.share] * part, part)
+    moves = [
+        (w_hbm.at[pl.ds(start, part)], w_ref),
+        (kv_hbm, kv_ref),
+        (q_hbm, q_ref),
+        (cache_hbm, kv_out.at[pl.ds(0, slots)]),
+    ]
+    copies = [pltpu.make_async_copy(*move, sems.at[n]) for n, move in enumerate(moves)]
+    for copy in copies:
+        copy.start()
+
+    copies[0].wait()
+    for d, out in enumerate(outs):
+        target = lax.rem(info[table.place] + d, count)
+        out[:, :keep] = w_ref[:, pl.ds(pl.multiple_of(target * slab, slab), keep)]
+        for j in range(count if raw else 0):
+            out[:, keep + j * raw : keep + (j + 1) * raw] = w_ref[
+                :, j * slab + keep : (j + 1) * slab
+            ]
+
     cosine, sine = cos_ref[...], sin_ref[...]
-    slots, rows = cache_ref.shape[0], q_ref.shape[0]
-    span, tail = slice(slots, slots + rows), slice(slots + rows, slots + rows + TAIL)
 
     def turn(block):
         block = block.astype(jnp.float32)
         return (block * cosine + pltpu.roll(block, HD // 2, 1) * sine).astype(jnp.bfloat16)
 
-    kv_out[:slots] = cache_ref[...]
+    copies[1].wait()
     kv_out[span, :HD] = turn(kv_ref[:, :HD])
     kv_out[span, HD:] = kv_ref[:, HD:]
     length = length_ref[0]
@@ -202,41 +226,36 @@
     lower = length - upper * DIGIT
     kv_out[tail, :HD] = jnp.full((TAIL, HD), upper.astype(jnp.float32)).astype(jnp.bfloat16)
     kv_out[tail, HD:] = jnp.full((TAIL, HD), lower.astype(jnp.float32)).astype(jnp.bfloat16)
+    copies[2].wait()
     for head in range(q_ref.shape[1] // HD):
         cols = slice(head * HD, (head + 1) * HD)
         q_out[:, cols] = turn(q_ref[:, cols])
-
-
-def cut_kernel(table, slab, keep, info, w_ref, *refs):
-    count, raw = table.count, slab - keep
-    outs, rows_ref, sem = refs[:count], refs[-2], refs[-1]
-    part = rows_ref.shape[0]
-    start = pl.multiple_of(info[table.share] * part, part)
-    copy = pltpu.make_async_copy(w_ref.at[pl.ds(start, part)], rows_ref, sem)
-    copy.start()
-    copy.wait()
-    for d, out in enumerate(outs):
-        target = lax.rem(info[table.place] + d, count)
-        out[:, :keep] = rows_ref[:, pl.ds(pl.multiple_of(target * slab, slab), keep)]
-        for j in range(count if raw else 0):
-            out[:, keep + j * raw : keep + (j + 1) * raw] = rows_ref[
-                :, j * slab + keep : (j + 1) * slab
-            ]
-
-
-def cut(table, info, out_weight, part, slab, keep):
-    shape = jax.ShapeDtypeStruct((part, keep + table.count * (slab - keep)), out_weight.dtype)
-    return call(
-        functools.partial(cut_kernel, table, slab, keep),
-        "cut",
-        info,
-        [out_weight],
-        [ANYWHERE],
-        [whole(shape)] * table.count,
-        [shape] * table.count,
+    copies[3].wait()
+
+
+def prepare(table, info, queries, span_pairs, cache, out_weight, cosine, sine, lengths, part,
+            slab, keep):
+    rows = queries.shape[0]
+    shapes = [
+        jax.ShapeDtypeStruct(queries.shape, jnp.bfloat16),
+        jax.ShapeDtypeStruct((cache.shape[0] + rows + TAIL, 2 * HD), jnp.bfloat16),
+    ]
+    width = keep + table.count * (slab - keep)
+    shapes += [jax.ShapeDtypeStruct((part, width), out_weight.dtype)] * table.count
+    return call(
+        functools.partial(prepare_kernel, table, slab, keep),
+        "prepare",
+        info,
+        [queries, span_pairs, cache, out_weight, cosine, sine, lengths],
+        [ANYWHERE] * 4
+        + [whole(cosine), whole(sine), pl.BlockSpec(memory_space=pltpu.SMEM)],
+        [whole(shape) for shape in shapes],
+        shapes,
         scratch=[
+            pltpu.VMEM(queries.shape, jnp.bfloat16),
+            pltpu.VMEM(span_pairs.shape, jnp.bfloat16),
             pltpu.VMEM((part, out_weight.shape[1]), out_weight.dtype),
-            pltpu.SemaphoreType.DMA(()),
+            pltpu.SemaphoreType.DMA((4,)),
         ],
         vmem=0,
     )
@@ -259,27 +278,6 @@
         + [ANYWHERE] * len(after),
         [whole(shape)] * 2,
         [shape] * 2,
-    )
-
-
-def prepare(info, queries, span_pairs, cache, cosine, sine, lengths, after):
-    rows = queries.shape[0]
-    shapes = [
-        jax.ShapeDtypeStruct(queries.shape, jnp.bfloat16),
-        jax.ShapeDtypeStruct((cache.shape[0] + rows + TAIL, 2 * HD), jnp.bfloat16),
-    ]
-    args = [queries, span_pairs, cache, cosine, sine, lengths]
-    return call(
-        prepare_kernel,
-        "prepare",
-        info,
-        [*args, *after],
-        [whole(a) for a in args[:-1]]
-        + [pl.BlockSpec(memory_space=pltpu.SMEM)]
-        + [ANYWHERE] * len(after),
-        [whole(shape) for shape in shapes],
-        shapes,
-        vmem=32,
     )
 
 
@@ -380,7 +378,7 @@
         out_ref[:, h * HD : (h + 1) * HD] = result[h * rows : (h + 1) * rows]
 
 
-def attend(table, info, queries, pieces, slots, rows, after):
+def attend(table, info, queries, pieces, slots, rows):
     all_rows, width = queries.shape
     heads = width // HD
     keys = sum(a.shape[0] - TAIL for a in pieces)
@@ -389,8 +387,8 @@
         functools.partial(attend_kernel, table, slots),
         "attend",
         info,
-        [queries, *pieces, *after],
-        [chunk_spec] + [whole(a) for a in pieces] + [ANYWHERE] * len(after),
+        [queries, *pieces],
+        [chunk_spec] + [whole(a) for a in pieces],
         chunk_spec,
         jax.ShapeDtypeStruct((all_rows, width), jnp.bfloat16),
         grid=(all_rows // rows,),
@@ -433,7 +431,7 @@
                 part[row - begin : row - begin + rows] = result
 
 
-def project(table, info, attention, pieces, residual, keep, rows, splits, after):
+def project(table, info, attention, pieces, residual, keep, rows, splits):
     all_rows, slab = residual.shape
     count, part_rows, _ = pieces[0].shape
     parts = [jax.ShapeDtypeStruct((size, keep), jnp.bfloat16) for _, size in splits * 2]
@@ -442,11 +440,10 @@
         functools.partial(project_kernel, table, len(attention), len(pieces), keep, splits),
         "project",
         info,
-        [*attention, *pieces, residual, *after],
+        [*attention, *pieces, residual],
         line_spec(attention, rows, lambda i: i)
         + [whole(p) for p in pieces]
-        + [row_spec]
-        + [ANYWHERE] * len(after),
+        + [row_spec],
         [whole(part) for part in parts] + [row_spec],
         [*parts, jax.ShapeDtypeStruct(residual.shape, jnp.bfloat16)],
         grid=(all_rows // rows,),
@@ -597,52 +594,41 @@
     both = jnp.concatenate([frequencies(HD)] * 2)
     angles = positions.astype(jnp.float32)[:, None] * both[None, :]
     sign = jnp.where(jnp.arange(HD) < HD // 2, -1.0, 1.0)
-    cuts = cut(table, info, out_weight, depth // shares, slab, keep)
+    q_turned, payload, *cuts = prepare(
+        table, info, queries, span_local, cache_local, out_weight, jnp.cos(angles),
+        jnp.sin(angles) * sign[None, :], lengths, depth // shares, slab, keep,
+    )
     parts = [cuts[0]]
     for shift in range(1, count):
         pairs = [(i, (i + shift) % count) for i in range(count)]
         parts.append(lax.ppermute(cuts[shift], "tensor", pairs))
-    q_turned, payload = prepare(
-        info, queries, span_local, cache_local, jnp.cos(angles),
-        jnp.sin(angles) * sign[None, :], lengths, cuts[:1],
-    )
     sent = []
 
     def between(block):
-        sent.append(stack(info, parts, [payload]))
+        sent.append(stack(info, parts, []))
         if raw:
-            sent.extend(last_columns(info, residual, raw, [*parts[1:], payload]))
+            sent.extend(last_columns(info, residual, raw, parts[1:]))
         return gate(info, block, sent)
 
     pieces = pieces_of(payload, "context", contexts, between)
-    early = line_far(sent[1]) if raw and count == 4 else ()
-    swapped = core_swap(sent[0], contexts) if contexts % 2 == 0 else sent[0]
-    mixed = attend(
-        table, info, q_turned, pieces, cache_local.shape[0], chunk, [*early[:1], swapped]
-    )
-    if count == 4:
-        far, last = line_far(mixed)
-        attention = [mixed, *line_near(mixed), far, last]
-    else:
-        attention = line_gather(mixed, count)
-        far = mixed
+    mixed = attend(table, info, q_turned, pieces, cache_local.shape[0], chunk)
+    residuals = []
+    if raw and count == 4:
+        residuals = [sent[2], *line_near(sent[2]), *line_far(sent[1])]
+    elif raw:
+        residuals = line_gather(sent[1], count)
+    ready = gate(info, mixed, residuals[1:4]) if raw else mixed
+    attention = line_gather(ready, count)
     weights = plane_gather(
         sent[0],
-        swapped,
         groups,
         contexts,
         lambda block: gate(info, block, [mixed]),
         lambda block, mask: gate(info, block, attention[1 : 3 if mask & (mask - 1) == 0 else 5]),
     )
-    residuals = []
-    if early:
-        near = gate(info, sent[2], [far])
-        residuals = [near, *line_near(near), *early]
-    elif raw:
-        residuals = line_gather(sent[1], count)
 
     *hidden_parts, hidden = project(
-        table, info, attention, weights, residual, keep, chunk, splits, residuals[4:]
+        table, info, attention, weights, residual, keep, chunk, splits
     )
     raw_hidden = None
     if raw:
@@ -653,7 +639,7 @@
         info,
         hidden_parts[: len(splits)],
         hidden_parts[len(splits) :],
-        residuals[1:3],
+        residuals[4:],
         [raw_hidden] if raw else [],
         count,
     )

time: 243 us -> 232 us (0.955)
  starting transfers between devices: 86.5 us -> 67.9 us
  waiting for transfers between devices: 102 us -> 110 us
  local copies, waits for them, and re-layouts: 5.15 us -> 1.64 us
    ppermute x6, starting transfers between devices: 54.6 us -> 36.1 us  [line_near(): up = lax.ppermute(value, 'tensor', [(0, 1), (1, 2), (2, 3)])]
    ppermute x6, waiting for transfers between devices: 18.7 us -> 28.8 us  [line_near(): return (up, lax.ppermute(value, 'tensor', [(1, 0), (2, 1), (3, 2)]))]
    ppermute x6, waiting for transfers between devices: 53.5 us -> 46.7 us  [line_far(): far = lax.ppermute(value, 'tensor', [(0, 2), (1, 3), (2, 0), (3, 1)])]
    unnamed x16 -> x12, local copies, waits for them, and re-layouts: 4.5 us -> 0.95 us
    ppermute x3, waiting for transfers between devices: 10.4 us -> 13.6 us  [per_device(): parts.append(lax.ppermute(cuts[shift], 'tensor', pairs))]
    ppermute x4, waiting for transfers between devices: 0.01 us -> 2.66 us  [core_swap(): return lax.ppermute(value, 'context', [(i, i ^ 1) for i in range(contexts)])]
    pallas_call x24 -> x22, Pallas kernels: 45.7 us -> 47.2 us  [call(): pl.pallas_call(kernel, grid_spec=pltpu.PrefetchScalarGridSpec(num_scalar_...]
  transfers between devices with their start and end apart: 37 -> 37, of which waited for: 18 -> 19; matrix products, arithmetic and copies ran while one was open for 0% -> 0% of each run, Pallas kernels for 16% -> 15%
where the time goes in v8:
time: 232 us; the launch traced here: 231 us
  waiting for transfers between devices  110 us (47%)
  starting transfers between devices  67.9 us (29%)
  Pallas kernels  47.2 us (20%)
  between operations  2.55 us (1%)
    pallas_call x22, Pallas kernels, call(): pl.pallas_call(kernel, grid_spec=pltpu.PrefetchScalarGridSpec(num_scalar_...  47.2 us
    ppermute x6, waiting for transfers between devices, line_far(): far = lax.ppermute(value, 'tensor', [(0, 2), (1, 3), (2, 0), (3, 1)])  46.7 us
    ppermute x6, starting transfers between devices, line_near(): up = lax.ppermute(value, 'tensor', [(0, 1), (1, 2), (2, 3)])  36.1 us
    ppermute x6, waiting for transfers between devices, line_near(): return (up, lax.ppermute(value, 'tensor', [(1, 0), (2, 1), (3, 2)]))  28.8 us
    ppermute x6, waiting for transfers between devices, line_far(): return (far, lax.ppermute(far, 'tensor', [(1, 0), (2, 3)]))  18.4 us
    ppermute x3, waiting for transfers between devices, per_device(): parts.append(lax.ppermute(cuts[shift], 'tensor', pairs))  13.6 us
    ppermute x6, starting transfers between devices, line_far(): return (far, lax.ppermute(far, 'tensor', [(1, 0), (2, 3)]))  7.84 us
    ppermute x6, starting transfers between devices, line_near(): return (up, lax.ppermute(value, 'tensor', [(1, 0), (2, 1), (3, 2)]))  7.75 us
  transfers between devices with their start and end apart: 37, of which 19 were waited for; matrix products, arithmetic and copies ran while one was open for 0% of the time, Pallas kernels for 15%

profile of v8, /device:TPU:0, one launch (start us, length us, event | category | flops | bytes accessed | tf_op | source)
XLA Modules:
  0.0 231.4 jit_solution(10329485342353686756)
XLA Ops:
  4.7 4.6 %prepare.1 = (bf16[512,256]{1,0:T(8,128)(2,1)}, bf16[1552,256]{1,0:T(8,128)(2,1)}, bf16[32,3584]{1,0:T(8,128)(2,1)}, bf16[32,3584]{1,0:T(8,128)(2,1)}, bf16[32,3...) custom-call(s32[20]{0:T(128)} %stack.86.info, bf16[512,256]{1,0:T(8,128)(2,1)} %q_hbm.1, bf16[512,256]{1,0:T(8,128)(2,1)} %bitcast.28, ...), custom_call_target="tpu_custom_call" | custom-call | flops 1 | bytes 1 | tf_op jit(solution)/shard_map/prepare/pallas_call | solution.py:166
  17.8 5.2 %collective-permute-done.2.refs_1_ = bf16[32,3584]{1,0:T(8,128)(2,1)S(1)} collective-permute-done((bf16[32,3584]{1,0:T(8,128)(2,1)}, bf16[32,3584]{1,0:T(8,128)(2,1)S(1)}, u32[]{:S(2)}, u32[]{:S(2)}) %collective-permute-start.2) | collective-permute-done | bytes 229408 | tf_op jit(solution)/shard_map/ppermute | solution.py:604
  23.0 8.4 %collective-permute-done.3.refs_2_ = bf16[32,3584]{1,0:T(8,128)(2,1)S(1)} collective-permute-done((bf16[32,3584]{1,0:T(8,128)(2,1)}, bf16[32,3584]{1,0:T(8,128)(2,1)S(1)}, u32[]{:S(2)}, u32[]{:S(2)}) %collective-permute-start.3) | collective-permute-done | bytes 229408 | tf_op jit(solution)/shard_map/ppermute | solution.py:604
  34.8 7.3 %collective-permute-start.6 = (bf16[512,512]{1,0:T(8,128)(2,1)S(1)}, bf16[512,512]{1,0:T(8,128)(2,1)S(1)}, u32[]{:S(2)}, u32[]{:S(2)}) collective-permute-start(bf16[512,512]{1,0:T(8,128)(2,1)S(1)} %get-tuple-element.28.refs_3_.refs_5_), channel_id=1, source_target_pairs={{0,4},{4,8},{8,12},{1,5},{5,9},{9,13},{2,6},{6,10},{10,14},{3,7},{... | collective-permute-start | bytes 1572872 | tf_op jit(solution)/shard_map/ppermute | solution.py:104
  47.3 12.2 %attend.1.refs_0_.refs_1_ = bf16[512,256]{1,0:T(8,128)(2,1)S(1)} custom-call(s32[20]{0:T(128)S(1)} %copy-done.2, bf16[512,256]{1,0:T(8,128)(2,1)S(1)} %copy-done.5, bf16[1552,256]{1,0:T(8,128)(2,1)S(1)} %copy-done.4, bf16[1552,256]{1,0:T(8,128)(2,1)S(1)} %collective-permute-done.refs_1_, bf16[1552,256]{1,0:T(8,128)(2,1)S(1)} %gate.12.refs_2_, ...), custom_call_target="tpu_custom_call" | custom-call | flops 12884901888 | bytes 1 | tf_op jit(solution)/shard_map/attend/pallas_call | solution.py:166
  60.6 19.4 %collective-permute-done.8.refs_3_.refs_8_ = bf16[512,512]{1,0:T(8,128)(2,1)S(1)} collective-permute-done((bf16[512,512]{1,0:T(8,128)(2,1)S(1)}, bf16[512,512]{1,0:T(8,128)(2,1)S(1)}, u32[]{:S(2)}, u32[]{:S(2)}) %collective-permute-start.8) | collective-permute-done | bytes 524320 | tf_op jit(solution)/shard_map/ppermute | solution.py:109
  82.0 4.6 %collective-permute-start.9 = (bf16[512,256]{1,0:T(8,128)(2,1)S(1)}, bf16[512,256]{1,0:T(8,128)(2,1)S(1)}, u32[]{:S(2)}, u32[]{:S(2)}) collective-permute-start(bf16[512,256]{1,0:T(8,128)(2,1)S(1)} %gate.13.refs_0_), channel_id=1, source_target_pairs={{0,4},{4,8},{8,12},{1,5},{5,9},{9,13},{2,6},{6,10},{10,14},{3,7},{... | collective-permute-start | bytes 786440 | tf_op jit(solution)/shard_map/ppermute | solution.py:104
  86.6 5.1 %collective-permute-done.11.refs_3_ = bf16[512,256]{1,0:T(8,128)(2,1)S(1)} collective-permute-done((bf16[512,256]{1,0:T(8,128)(2,1)S(1)}, bf16[512,256]{1,0:T(8,128)(2,1)S(1)}, u32[]{:S(2)}, u32[]{:S(2)}) %collective-permute-start.11) | collective-permute-done | bytes 262176 | tf_op jit(solution)/shard_map/ppermute | solution.py:109
  96.3 5.4 %collective-permute-done.12.refs_4_ = bf16[512,256]{1,0:T(8,128)(2,1)S(1)} collective-permute-done((bf16[512,256]{1,0:T(8,128)(2,1)S(1)}, bf16[512,256]{1,0:T(8,128)(2,1)S(1)}, u32[]{:S(2)}, u32[]{:S(2)}) %collective-permute-start.12) | collective-permute-done | bytes 262176 | tf_op jit(solution)/shard_map/ppermute | solution.py:110
  106.1 4.4 %project.1 = (bf16[128,1536]{1,0:T(8,128)(2,1)S(1)}, bf16[128,1536]{1,0:T(8,128)(2,1)S(1)}, bf16[128,1536]{1,0:T(8,128)(2,1)S(1)}, bf16[128,1536]{1,0:T(8,128)(2...) custom-call(s32[20]{0:T(128)S(1)} %copy-done.2, ...), custom_call_target="tpu_custom_call" | custom-call | flops 1 | bytes 1 | tf_op jit(solution)/shard_map/project/pallas_call | solution.py:166
  113.4 4.6 %collective-permute-start.21 = (bf16[128,1536]{1,0:T(8,128)(2,1)S(1)}, bf16[128,1536]{1,0:T(8,128)(2,1)S(1)}, u32[]{:S(2)}, u32[]{:S(2)}) collective-permute-start(bf16[128,1536]{1,0:T(8,128)(2,1)S(1)} %get-tuple-element.34.refs_0_), channel_id=1, source_target_pairs={{0,4},{4,8},{8,12},{1,5},{5,9},{9,13},{2,6},{6,10},{10,14},{3,7},{... | collective-permute-start | bytes 1179656 | tf_op jit(solution)/shard_map/ppermute | solution.py:104
  119.3 12.6 %collective-permute-done.25.refs_1_.refs_3_ = bf16[128,1536]{1,0:T(8,128)(2,1)S(1)} collective-permute-done((bf16[128,1536]{1,0:T(8,128)(2,1)S(1)}, bf16[128,1536]{1,0:T(8,128)(2,1)S(1)}, u32[]{:S(2)}, u32[]{:S(2)}) %collective-permute-start.25) | collective-permute-done | bytes 393248 | tf_op jit(solution)/shard_map/ppermute | solution.py:109
  136.2 8.4 %collective-permute-done.22.refs_2_ = bf16[128,1536]{1,0:T(8,128)(2,1)S(1)} collective-permute-done((bf16[128,1536]{1,0:T(8,128)(2,1)S(1)}, bf16[128,1536]{1,0:T(8,128)(2,1)S(1)}, u32[]{:S(2)}, u32[]{:S(2)}) %collective-permute-start.22) | collective-permute-done | bytes 393248 | tf_op jit(solution)/shard_map/ppermute | solution.py:105
  145.2 6.5 %collective-permute-start.23 = (bf16[128,1536]{1,0:T(8,128)(2,1)S(1)}, bf16[128,1536]{1,0:T(8,128)(2,1)S(1)}, u32[]{:S(2)}, u32[]{:S(2)}) collective-permute-start(bf16[128,1536]{1,0:T(8,128)(2,1)S(1)} %gate.18.refs_0_), channel_id=1, source_target_pairs={{0,4},{4,8},{8,12},{1,5},{5,9},{9,13},{2,6},{6,10},{10,14},{3,7},{... | collective-permute-start | bytes 1179656 | tf_op jit(solution)/shard_map/ppermute | solution.py:104
  157.1 4.6 %project_raw.1 = (bf16[512,2048]{1,0:T(8,128)(2,1)S(1)}, bf16[512,2048]{1,0:T(8,128)(2,1)}) custom-call(s32[20]{0:T(128)S(1)} %copy-done.2, bf16[512,256]{1,0:T(8,128)(2,1)S(1)} %gate.13.refs_0_, bf16[512,256]{1,0:T(8,128)(2,1)S(1)} %collective-permute-done.9.refs_1_, ...), custom_call_target="tpu_custom_call", output_to_operand_aliasing={{1}: (19, {})} | custom-call | flops 1 | bytes 1 | tf_op jit(solution)/shard_map/project_raw/pallas_call | solution.py:166
  163.1 7.2 %collective-permute-done.24.refs_2_ = bf16[128,1536]{1,0:T(8,128)(2,1)S(1)} collective-permute-done((bf16[128,1536]{1,0:T(8,128)(2,1)S(1)}, bf16[128,1536]{1,0:T(8,128)(2,1)S(1)}, u32[]{:S(2)}, u32[]{:S(2)}) %collective-permute-start.24) | collective-permute-done | bytes 393248 | tf_op jit(solution)/shard_map/ppermute | solution.py:105
  170.9 6.5 %collective-permute-start.27 = (bf16[128,1536]{1,0:T(8,128)(2,1)S(1)}, bf16[128,1536]{1,0:T(8,128)(2,1)S(1)}, u32[]{:S(2)}, u32[]{:S(2)}) collective-permute-start(bf16[128,1536]{1,0:T(8,128)(2,1)S(1)} %gate.19.refs_0_), channel_id=1, source_target_pairs={{0,4},{4,8},{8,12},{1,5},{5,9},{9,13},{2,6},{6,10},{10,14},{3,7},{... | collective-permute-start | bytes 1179656 | tf_op jit(solution)/shard_map/ppermute | solution.py:104
  186.8 8.8 %collective-permute-done.28.refs_2_ = bf16[128,1536]{1,0:T(8,128)(2,1)S(1)} collective-permute-done((bf16[128,1536]{1,0:T(8,128)(2,1)S(1)}, bf16[128,1536]{1,0:T(8,128)(2,1)S(1)}, u32[]{:S(2)}, u32[]{:S(2)}) %collective-permute-start.28) | collective-permute-done | bytes 393248 | tf_op jit(solution)/shard_map/ppermute | solution.py:105
  196.2 6.6 %collective-permute-start.31 = (bf16[128,1536]{1,0:T(8,128)(2,1)S(1)}, bf16[128,1536]{1,0:T(8,128)(2,1)S(1)}, u32[]{:S(2)}, u32[]{:S(2)}) collective-permute-start(bf16[128,1536]{1,0:T(8,128)(2,1)S(1)} %gate.21.refs_0_), channel_id=1, source_target_pairs={{0,4},{4,8},{8,12},{1,5},{5,9},{9,13},{2,6},{6,10},{10,14},{3,7},{... | collective-permute-start | bytes 1179656 | tf_op jit(solution)/shard_map/ppermute | solution.py:104
  208.4 3.4 %norm.4.refs_6_ = bf16[512,8192]{1,0:T(8,128)(2,1)} custom-call(s32[20]{0:T(128)S(1)} %copy-done.2, f32[1,8192]{1,0:T(1,128)S(1)} %bitcast.23, bf16[128,1536]{1,0:T(8,128)(2,1)S(1)} %get-tuple-element.34.refs_0_, bf16[128,1536]{1,0:T(8,128)(2,1)S(1)} %collective-permute-done.21.refs_1_, bf16[128,1536]{1,0:T(8,128)(2,1)S(1)} %collective-permute-done.22.refs_2_, ...), custom_call_target="tpu_custom_call" | custom-call | flops 1 | bytes 1 | tf_op jit(solution)/shard_map/norm/pallas_call | solution.py:166
  211.8 3.4 %norm.5.refs_6_ = bf16[512,8192]{1,0:T(8,128)(2,1)} custom-call(s32[20]{0:T(128)S(1)} %copy-done.2, f32[1,8192]{1,0:T(1,128)S(1)} %bitcast.24, bf16[128,1536]{1,0:T(8,128)(2,1)S(1)} %gate.18.refs_0_, bf16[128,1536]{1,0:T(8,128)(2,1)S(1)} %collective-permute-done.23.refs_1_, ...), custom_call_target="tpu_custom_call", output_to_operand_aliasing={{}: (8, {})} | custom-call | flops 1 | bytes 1 | tf_op jit(solution)/shard_map/norm/pallas_call | solution.py:166
  215.3 3.4 %norm.6.refs_6_ = bf16[512,8192]{1,0:T(8,128)(2,1)} custom-call(s32[20]{0:T(128)S(1)} %copy-done.2, f32[1,8192]{1,0:T(1,128)S(1)} %bitcast.25, bf16[128,1536]{1,0:T(8,128)(2,1)S(1)} %gate.19.refs_0_, bf16[128,1536]{1,0:T(8,128)(2,1)S(1)} %collective-permute-done.27.refs_1_, ...), custom_call_target="tpu_custom_call", output_to_operand_aliasing={{}: (8, {})} | custom-call | flops 1 | bytes 1 | tf_op jit(solution)/shard_map/norm/pallas_call | solution.py:166
  220.5 7.4 %collective-permute-done.35.refs_4_ = bf16[128,1536]{1,0:T(8,128)(2,1)S(1)} collective-permute-done((bf16[128,1536]{1,0:T(8,128)(2,1)S(1)}, bf16[128,1536]{1,0:T(8,128)(2,1)S(1)}, u32[]{:S(2)}, u32[]{:S(2)}) %collective-permute-start.35) | collective-permute-done | bytes 393248 | tf_op jit(solution)/shard_map/ppermute | solution.py:110
  227.9 3.4 %norm.7 = bf16[512,8192]{1,0:T(8,128)(2,1)} custom-call(s32[20]{0:T(128)S(1)} %copy-done.2, f32[1,8192]{1,0:T(1,128)S(1)} %bitcast.26, bf16[128,1536]{1,0:T(8,128)(2,1)S(1)} %gate.21.refs_0_, bf16[128,1536]{1,0:T(8,128)(2,1)S(1)} %collective-permute-done.31.refs_1_, ...), custom_call_target="tpu_custom_call", output_to_operand_aliasing={{}: (8, {})} | custom-call | flops 1 | bytes 1 | tf_op jit(solution)/shard_map/norm/pallas_call | solution.py:166
  (89 shorter events, 65.2 us)
Async XLA Ops:
  9.3 24.3 %collective-permute-start.1 = (bf16[1552,256]{1,0:T(8,128)(2,1)}, bf16[1552,256]{1,0:T(8,128)(2,1)S(1)}, u32[]{:S(2)}, u32[]{:S(2)}) collective-permute-start(bf16[1552,256]{1,0:T(8,128)(2,1)} %get-tuple-element.22.refs_0_), channel_id=1, source_target_pairs={{0,2},{1,3},{2,0},{3,1},{4,6},{5,7},{6,4},{7,5},{8,10},{9,11},{10,... | collective-permute-start | bytes 2383880 | tf_op jit(solution)/shard_map/ppermute | solution.py:43
  17.8 25.6 %collective-permute-start = (bf16[1552,256]{1,0:T(8,128)(2,1)}, bf16[1552,256]{1,0:T(8,128)(2,1)S(1)}, u32[]{:S(2)}, u32[]{:S(2)}) collective-permute-start(bf16[1552,256]{1,0:T(8,128)(2,1)} %get-tuple-element.22.refs_0_), channel_id=1, source_target_pairs={{0,1},{1,0},{2,3},{3,2},{4,5},{5,4},{6,7},{7,6},{8,9},{9,8},{10,11... | collective-permute-start | bytes 2383880 | tf_op jit(solution)/shard_map/ppermute | solution.py:43
  34.2 25.2 %collective-permute-start.15 = (bf16[4,32,3584]{2,1,0:T(8,128)(2,1)S(1)}, bf16[4,32,3584]{2,1,0:T(8,128)(2,1)S(1)}, u32[]{:S(2)}, u32[]{:S(2)}) collective-permute-start(bf16[4,32,3584]{2,1,0:T(8,128)(2,1)S(1)} %stack.89.refs_1_.refs_5_.refs_10_), channel_id=1, source_target_pairs={{0,2},{1,3},{2,0},{3,1},{4,6},{5,7},{6,4},{7,5},{8,10},{9,11},{10,... | collective-permute-start | bytes 2752520 | tf_op jit(solution)/shard_map/ppermute | solution.py:76
  34.8 25.8 %collective-permute-start.6 = (bf16[512,512]{1,0:T(8,128)(2,1)S(1)}, bf16[512,512]{1,0:T(8,128)(2,1)S(1)}, u32[]{:S(2)}, u32[]{:S(2)}) collective-permute-start(bf16[512,512]{1,0:T(8,128)(2,1)S(1)} %get-tuple-element.28.refs_3_.refs_5_), channel_id=1, source_target_pairs={{0,4},{4,8},{8,12},{1,5},{5,9},{9,13},{2,6},{6,10},{10,14},{3,7},{... | collective-permute-start | bytes 1572872 | tf_op jit(solution)/shard_map/ppermute | solution.py:104
  42.2 18.5 %collective-permute-start.7 = (bf16[512,512]{1,0:T(8,128)(2,1)S(1)}, bf16[512,512]{1,0:T(8,128)(2,1)S(1)}, u32[]{:S(2)}, u32[]{:S(2)}) collective-permute-start(bf16[512,512]{1,0:T(8,128)(2,1)S(1)} %get-tuple-element.28.refs_3_.refs_5_), channel_id=1, source_target_pairs={{4,0},{8,4},{12,8},{5,1},{9,5},{13,9},{6,2},{10,6},{14,10},{7,3},{... | collective-permute-start | bytes 1572872 | tf_op jit(solution)/shard_map/ppermute | solution.py:105
  43.5 36.6 %collective-permute-start.8 = (bf16[512,512]{1,0:T(8,128)(2,1)S(1)}, bf16[512,512]{1,0:T(8,128)(2,1)S(1)}, u32[]{:S(2)}, u32[]{:S(2)}) collective-permute-start(bf16[512,512]{1,0:T(8,128)(2,1)S(1)} %get-tuple-element.27.refs_2_), channel_id=1, source_target_pairs={{0,8},{4,12},{8,0},{12,4},{1,9},{5,13},{9,1},{13,5},{2,10},{6,14},... | collective-permute-start | bytes 1572872 | tf_op jit(solution)/shard_map/ppermute | solution.py:109
  45.7 47.3 %collective-permute-start.17 = (bf16[4,32,3584]{2,1,0:T(8,128)(2,1)S(1)}, bf16[4,32,3584]{2,1,0:T(8,128)(2,1)S(1)}, u32[]{:S(2)}, u32[]{:S(2)}) collective-permute-start(bf16[4,32,3584]{2,1,0:T(8,128)(2,1)S(1)} %stack.89.refs_1_.refs_5_.refs_10_), channel_id=1, source_target_pairs={{0,16},{16,0},{1,17},{17,1},{2,18},{18,2},{3,19},{19,3},{4,20},{20... | collective-permute-start | bytes 2752520 | tf_op jit(solution)/shard_map/ppermute | solution.py:76
  60.0 41.7 %collective-permute-start.19 = (bf16[4,32,3584]{2,1,0:T(8,128)(2,1)S(1)}, bf16[4,32,3584]{2,1,0:T(8,128)(2,1)S(1)}, u32[]{:S(2)}, u32[]{:S(2)}) collective-permute-start(bf16[4,32,3584]{2,1,0:T(8,128)(2,1)S(1)} %gate.14.refs_0_), channel_id=1, source_target_pairs={{0,16},{16,0},{1,17},{17,1},{2,18},{18,2},{3,19},{19,3},{4,20},{20... | collective-permute-start | bytes 2752520 | tf_op jit(solution)/shard_map/ppermute | solution.py:76
  110.5 21.3 %collective-permute-start.25 = (bf16[128,1536]{1,0:T(8,128)(2,1)S(1)}, bf16[128,1536]{1,0:T(8,128)(2,1)S(1)}, u32[]{:S(2)}, u32[]{:S(2)}) collective-permute-start(bf16[128,1536]{1,0:T(8,128)(2,1)S(1)} %get-tuple-element.35), channel_id=1, source_target_pairs={{0,8},{4,12},{8,0},{12,4},{1,9},{5,13},{9,1},{13,5},{2,10},{6,14},... | collective-permute-start | bytes 1179656 | tf_op jit(solution)/shard_map/ppermute | solution.py:109
  112.1 24.1 %collective-permute-start.13 = (bf16[512,512]{1,0:T(8,128)(2,1)S(1)}, bf16[512,512]{1,0:T(8,128)(2,1)S(1)}, u32[]{:S(2)}, u32[]{:S(2)}) collective-permute-start(bf16[512,512]{1,0:T(8,128)(2,1)S(1)} %collective-permute-done.8.refs_3_.refs_8_), channel_id=1, source_target_pairs={{4,0},{8,12},{5,1},{9,13},{6,2},{10,14},{7,3},{11,15},{20,16},{24,... | collective-permute-start | bytes 1572872 | tf_op jit(solution)/shard_map/ppermute | solution.py:110
  113.4 22.8 %collective-permute-start.21 = (bf16[128,1536]{1,0:T(8,128)(2,1)S(1)}, bf16[128,1536]{1,0:T(8,128)(2,1)S(1)}, u32[]{:S(2)}, u32[]{:S(2)}) collective-permute-start(bf16[128,1536]{1,0:T(8,128)(2,1)S(1)} %get-tuple-element.34.refs_0_), channel_id=1, source_target_pairs={{0,4},{4,8},{8,12},{1,5},{5,9},{9,13},{2,6},{6,10},{10,14},{3,7},{... | collective-permute-start | bytes 1179656 | tf_op jit(solution)/shard_map/ppermute | solution.py:104
  118.0 26.7 %collective-permute-start.22 = (bf16[128,1536]{1,0:T(8,128)(2,1)S(1)}, bf16[128,1536]{1,0:T(8,128)(2,1)S(1)}, u32[]{:S(2)}, u32[]{:S(2)}) collective-permute-start(bf16[128,1536]{1,0:T(8,128)(2,1)S(1)} %get-tuple-element.34.refs_0_), channel_id=1, source_target_pairs={{4,0},{8,4},{12,8},{5,1},{9,5},{13,9},{6,2},{10,6},{14,10},{7,3},{... | collective-permute-start | bytes 1179656 | tf_op jit(solution)/shard_map/ppermute | solution.py:105
  132.4 24.1 %collective-permute-start.29 = (bf16[128,1536]{1,0:T(8,128)(2,1)S(1)}, bf16[128,1536]{1,0:T(8,128)(2,1)S(1)}, u32[]{:S(2)}, u32[]{:S(2)}) collective-permute-start(bf16[128,1536]{1,0:T(8,128)(2,1)S(1)} %gate.20), channel_id=1, source_target_pairs={{0,8},{4,12},{8,0},{12,4},{1,9},{5,13},{9,1},{13,5},{2,10},{6,14},... | collective-permute-start | bytes 1179656 | tf_op jit(solution)/shard_map/ppermute | solution.py:109
  132.5 30.6 %collective-permute-start.26 = (bf16[128,1536]{1,0:T(8,128)(2,1)S(1)}, bf16[128,1536]{1,0:T(8,128)(2,1)S(1)}, u32[]{:S(2)}, u32[]{:S(2)}) collective-permute-start(bf16[128,1536]{1,0:T(8,128)(2,1)S(1)} %collective-permute-done.25.refs_1_.refs_3_), channel_id=1, source_target_pairs={{4,0},{8,12},{5,1},{9,13},{6,2},{10,14},{7,3},{11,15},{20,16},{24,... | collective-permute-start | bytes 1179656 | tf_op jit(solution)/shard_map/ppermute | solution.py:110
  145.2 17.9 %collective-permute-start.23 = (bf16[128,1536]{1,0:T(8,128)(2,1)S(1)}, bf16[128,1536]{1,0:T(8,128)(2,1)S(1)}, u32[]{:S(2)}, u32[]{:S(2)}) collective-permute-start(bf16[128,1536]{1,0:T(8,128)(2,1)S(1)} %gate.18.refs_0_), channel_id=1, source_target_pairs={{0,4},{4,8},{8,12},{1,5},{5,9},{9,13},{2,6},{6,10},{10,14},{3,7},{... | collective-permute-start | bytes 1179656 | tf_op jit(solution)/shard_map/ppermute | solution.py:104
  151.7 18.6 %collective-permute-start.24 = (bf16[128,1536]{1,0:T(8,128)(2,1)S(1)}, bf16[128,1536]{1,0:T(8,128)(2,1)S(1)}, u32[]{:S(2)}, u32[]{:S(2)}) collective-permute-start(bf16[128,1536]{1,0:T(8,128)(2,1)S(1)} %gate.18.refs_0_), channel_id=1, source_target_pairs={{4,0},{8,4},{12,8},{5,1},{9,5},{13,9},{6,2},{10,6},{14,10},{7,3},{... | collective-permute-start | bytes 1179656 | tf_op jit(solution)/shard_map/ppermute | solution.py:105
  157.0 24.8 %collective-permute-start.33 = (bf16[128,1536]{1,0:T(8,128)(2,1)S(1)}, bf16[128,1536]{1,0:T(8,128)(2,1)S(1)}, u32[]{:S(2)}, u32[]{:S(2)}) collective-permute-start(bf16[128,1536]{1,0:T(8,128)(2,1)S(1)} %gate.22), channel_id=1, source_target_pairs={{0,8},{4,12},{8,0},{12,4},{1,9},{5,13},{9,1},{13,5},{2,10},{6,14},... | collective-permute-start | bytes 1179656 | tf_op jit(solution)/shard_map/ppermute | solution.py:109
  161.7 25.1 %collective-permute-start.30 = (bf16[128,1536]{1,0:T(8,128)(2,1)S(1)}, bf16[128,1536]{1,0:T(8,128)(2,1)S(1)}, u32[]{:S(2)}, u32[]{:S(2)}) collective-permute-start(bf16[128,1536]{1,0:T(8,128)(2,1)S(1)} %collective-permute-done.29.refs_1_.refs_3_), channel_id=1, source_target_pairs={{4,0},{8,12},{5,1},{9,13},{6,2},{10,14},{7,3},{11,15},{20,16},{24,... | collective-permute-start | bytes 1179656 | tf_op jit(solution)/shard_map/ppermute | solution.py:110
  177.4 18.2 %collective-permute-start.28 = (bf16[128,1536]{1,0:T(8,128)(2,1)S(1)}, bf16[128,1536]{1,0:T(8,128)(2,1)S(1)}, u32[]{:S(2)}, u32[]{:S(2)}) collective-permute-start(bf16[128,1536]{1,0:T(8,128)(2,1)S(1)} %gate.19.refs_0_), channel_id=1, source_target_pairs={{4,0},{8,4},{12,8},{5,1},{9,5},{13,9},{6,2},{10,6},{14,10},{7,3},{... | collective-permute-start | bytes 1179656 | tf_op jit(solution)/shard_map/ppermute | solution.py:105
  182.3 24.8 %collective-permute-start.34 = (bf16[128,1536]{1,0:T(8,128)(2,1)S(1)}, bf16[128,1536]{1,0:T(8,128)(2,1)S(1)}, u32[]{:S(2)}, u32[]{:S(2)}) collective-permute-start(bf16[128,1536]{1,0:T(8,128)(2,1)S(1)} %gate.23), channel_id=1, source_target_pairs={{0,8},{4,12},{8,0},{12,4},{1,9},{5,13},{9,1},{13,5},{2,10},{6,14},... | collective-permute-start | bytes 1179656 | tf_op jit(solution)/shard_map/ppermute | solution.py:109
  182.4 32.9 %collective-permute-start.36 = (bf16[128,1536]{1,0:T(8,128)(2,1)S(1)}, bf16[128,1536]{1,0:T(8,128)(2,1)S(1)}, u32[]{:S(2)}, u32[]{:S(2)}) collective-permute-start(bf16[128,1536]{1,0:T(8,128)(2,1)S(1)} %collective-permute-done.33.refs_1_.refs_3_), channel_id=1, source_target_pairs={{4,0},{8,12},{5,1},{9,13},{6,2},{10,14},{7,3},{11,15},{20,16},{24,... | collective-permute-start | bytes 1179656 | tf_op jit(solution)/shard_map/ppermute | solution.py:110
  196.2 22.5 %collective-permute-start.31 = (bf16[128,1536]{1,0:T(8,128)(2,1)S(1)}, bf16[128,1536]{1,0:T(8,128)(2,1)S(1)}, u32[]{:S(2)}, u32[]{:S(2)}) collective-permute-start(bf16[128,1536]{1,0:T(8,128)(2,1)S(1)} %gate.21.refs_0_), channel_id=1, source_target_pairs={{0,4},{4,8},{8,12},{1,5},{5,9},{9,13},{2,6},{6,10},{10,14},{3,7},{... | collective-permute-start | bytes 1179656 | tf_op jit(solution)/shard_map/ppermute | solution.py:104
  202.7 17.8 %collective-permute-start.32 = (bf16[128,1536]{1,0:T(8,128)(2,1)S(1)}, bf16[128,1536]{1,0:T(8,128)(2,1)S(1)}, u32[]{:S(2)}, u32[]{:S(2)}) collective-permute-start(bf16[128,1536]{1,0:T(8,128)(2,1)S(1)} %gate.21.refs_0_), channel_id=1, source_target_pairs={{4,0},{8,4},{12,8},{5,1},{9,5},{13,9},{6,2},{10,6},{14,10},{7,3},{... | collective-permute-start | bytes 1179656 | tf_op jit(solution)/shard_map/ppermute | solution.py:105
  207.1 20.8 %collective-permute-start.35 = (bf16[128,1536]{1,0:T(8,128)(2,1)S(1)}, bf16[128,1536]{1,0:T(8,128)(2,1)S(1)}, u32[]{:S(2)}, u32[]{:S(2)}) collective-permute-start(bf16[128,1536]{1,0:T(8,128)(2,1)S(1)} %collective-permute-done.34.refs_3_), channel_id=1, source_target_pairs={{4,0},{8,12},{5,1},{9,13},{6,2},{10,14},{7,3},{11,15},{20,16},{24,... | collective-permute-start | bytes 1179656 | tf_op jit(solution)/shard_map/ppermute | solution.py:110
  (19 other events, 324.8 us)

commit v9 on v8

--- a/solution.py
+++ b/solution.py
@@ -115,13 +115,12 @@
         return [line_gather(value, count) for value in values]
     fars, lines = [], []
     for number, value in enumerate(values):
-        fars.append(line_far(gate(info, value, [fars[-1][0]]) if number else value))
+        after = [fars[-1][0]] if number else first
+        fars.append(line_far(gate(info, value, after) if after else value))
     for number, value in enumerate(copies):
         after = list(lines[number - 1][1:3]) if number else []
         if number > 1:
             after.append(fars[number - 2][1])
-        if number == 1:
-            after += first
         if number == len(copies) // 2:
             after += made
         value = gate(info, value, after) if after else value
@@ -614,17 +613,19 @@
     mixed = attend(table, info, q_turned, pieces, cache_local.shape[0], chunk)
     residuals = []
     if raw and count == 4:
-        residuals = [sent[2], *line_near(sent[2]), *line_far(sent[1])]
-    elif raw:
-        residuals = line_gather(sent[1], count)
-    ready = gate(info, mixed, residuals[1:4]) if raw else mixed
-    attention = line_gather(ready, count)
+        early = line_far(sent[1])
+        attention = line_gather(gate(info, mixed, early[:1]), count)
+        near = gate(info, sent[2], attention[3:4])
+        residuals = [near, *line_near(near), *early]
+    else:
+        attention = line_gather(mixed, count)
+        residuals = line_gather(sent[1], count) if raw else []
     weights = plane_gather(
         sent[0],
         groups,
         contexts,
         lambda block: gate(info, block, [mixed]),
-        lambda block, mask: gate(info, block, attention[1 : 3 if mask & (mask - 1) == 0 else 5]),
+        lambda block, mask: gate(info, block, attention[3:4] if mask in (mask & -mask,) else attention[1:]),
     )
 
     *hidden_parts, hidden = project(
@@ -639,7 +640,7 @@
         info,
         hidden_parts[: len(splits)],
         hidden_parts[len(splits) :],
-        residuals[4:],
+        [*residuals[1:3], *residuals[4:]],
         [raw_hidden] if raw else [],
         count,
     )

time: 232 us -> 241 us (1.039)
  starting transfers between devices: 67.9 us -> 80.5 us
  waiting for transfers between devices: 110 us -> 105 us
    ppermute x6, starting transfers between devices: 36.1 us -> 46.2 us  [line_near(): up = lax.ppermute(value, 'tensor', [(0, 1), (1, 2), (2, 3)])]
    ppermute x6, waiting for transfers between devices: 46.7 us -> 40.1 us  [line_far(): far = lax.ppermute(value, 'tensor', [(0, 2), (1, 3), (2, 0), (3, 1)])]
    ppermute x3, waiting for transfers between devices: 0.01 us -> 3.94 us  [plane_gather(): held[mask | bit] = lax.ppermute(held[mask], axis, pairs)]
    ppermute x6, waiting for transfers between devices: 0.02 us -> 3.01 us  [line_near(): up = lax.ppermute(value, 'tensor', [(0, 1), (1, 2), (2, 3)])]
    ppermute x4, waiting for transfers between devices: 2.66 us -> 0.01 us  [core_swap(): return lax.ppermute(value, 'context', [(i, i ^ 1) for i in range(contexts)])]
    ppermute x6, waiting for transfers between devices: 18.4 us -> 15.8 us  [line_far(): return (far, lax.ppermute(far, 'tensor', [(1, 0), (2, 3)]))]
    pallas_call x22 -> x24, Pallas kernels: 47.2 us -> 48.3 us  [call(): pl.pallas_call(kernel, grid_spec=pltpu.PrefetchScalarGridSpec(num_scalar_...]
  transfers between devices with their start and end apart: 37 -> 37, of which waited for: 19 -> 19; matrix products, arithmetic and copies ran while one was open for 0% -> 0% of each run, Pallas kernels for 15% -> 17%
where the time goes in v9:
time: 241 us; the launch traced here: 240 us
  waiting for transfers between devices  105 us (44%)
  starting transfers between devices  80.5 us (33%)
  Pallas kernels  48.3 us (20%)
  between operations  2.62 us (1%)
    pallas_call x24, Pallas kernels, call(): pl.pallas_call(kernel, grid_spec=pltpu.PrefetchScalarGridSpec(num_scalar_...  48.3 us
    ppermute x6, starting transfers between devices, line_near(): up = lax.ppermute(value, 'tensor', [(0, 1), (1, 2), (2, 3)])  46.2 us
    ppermute x6, waiting for transfers between devices, line_far(): far = lax.ppermute(value, 'tensor', [(0, 2), (1, 3), (2, 0), (3, 1)])  40.1 us
    ppermute x6, waiting for transfers between devices, line_near(): return (up, lax.ppermute(value, 'tensor', [(1, 0), (2, 1), (3, 2)]))  28.7 us
    ppermute x6, waiting for transfers between devices, line_far(): return (far, lax.ppermute(far, 'tensor', [(1, 0), (2, 3)]))  15.8 us
    ppermute x3, waiting for transfers between devices, per_device(): parts.append(lax.ppermute(cuts[shift], 'tensor', pairs))  13.6 us
    ppermute x6, starting transfers between devices, line_far(): return (far, lax.ppermute(far, 'tensor', [(1, 0), (2, 3)]))  7.85 us
    ppermute x6, starting transfers between devices, line_near(): return (up, lax.ppermute(value, 'tensor', [(1, 0), (2, 1), (3, 2)]))  7.75 us
  transfers between devices with their start and end apart: 37, of which 19 were waited for; matrix products, arithmetic and copies ran while one was open for 0% of the time, Pallas kernels for 17%

profile of v9, /device:TPU:0, one launch (start us, length us, event | category | flops | bytes accessed | tf_op | source)
XLA Modules:
  0.0 240.1 jit_solution(16648378655269517976)
XLA Ops:
  4.7 4.6 %prepare.1 = (bf16[512,256]{1,0:T(8,128)(2,1)}, bf16[1552,256]{1,0:T(8,128)(2,1)}, bf16[32,3584]{1,0:T(8,128)(2,1)}, bf16[32,3584]{1,0:T(8,128)(2,1)}, bf16[32,3...) custom-call(s32[20]{0:T(128)} %stack.86.info, bf16[512,256]{1,0:T(8,128)(2,1)} %q_hbm.1, bf16[512,256]{1,0:T(8,128)(2,1)} %bitcast.28, ...), custom_call_target="tpu_custom_call" | custom-call | flops 1 | bytes 1 | tf_op jit(solution)/shard_map/prepare/pallas_call | solution.py:165
  17.8 5.2 %collective-permute-done.2.refs_1_ = bf16[32,3584]{1,0:T(8,128)(2,1)S(1)} collective-permute-done((bf16[32,3584]{1,0:T(8,128)(2,1)}, bf16[32,3584]{1,0:T(8,128)(2,1)S(1)}, u32[]{:S(2)}, u32[]{:S(2)}) %collective-permute-start.2) | collective-permute-done | bytes 229408 | tf_op jit(solution)/shard_map/ppermute | solution.py:603
  23.0 8.4 %collective-permute-done.3.refs_2_ = bf16[32,3584]{1,0:T(8,128)(2,1)S(1)} collective-permute-done((bf16[32,3584]{1,0:T(8,128)(2,1)}, bf16[32,3584]{1,0:T(8,128)(2,1)S(1)}, u32[]{:S(2)}, u32[]{:S(2)}) %collective-permute-start.3) | collective-permute-done | bytes 229408 | tf_op jit(solution)/shard_map/ppermute | solution.py:603
  34.8 4.5 %collective-permute-start.6 = (bf16[512,512]{1,0:T(8,128)(2,1)S(1)}, bf16[512,512]{1,0:T(8,128)(2,1)S(1)}, u32[]{:S(2)}, u32[]{:S(2)}) collective-permute-start(bf16[512,512]{1,0:T(8,128)(2,1)S(1)} %get-tuple-element.27.refs_2_), channel_id=1, source_target_pairs={{0,8},{4,12},{8,0},{12,4},{1,9},{5,13},{9,1},{13,5},{2,10},{6,14},... | collective-permute-start | bytes 1572872 | tf_op jit(solution)/shard_map/ppermute | solution.py:109
  40.8 12.2 %attend.1.refs_0_.refs_1_ = bf16[512,256]{1,0:T(8,128)(2,1)S(1)} custom-call(s32[20]{0:T(128)S(1)} %copy-done.2, bf16[512,256]{1,0:T(8,128)(2,1)S(1)} %copy-done.5, bf16[1552,256]{1,0:T(8,128)(2,1)S(1)} %copy-done.4, bf16[1552,256]{1,0:T(8,128)(2,1)S(1)} %collective-permute-done.refs_1_, bf16[1552,256]{1,0:T(8,128)(2,1)S(1)} %gate.14.refs_2_, ...), custom_call_target="tpu_custom_call" | custom-call | flops 12884901888 | bytes 1 | tf_op jit(solution)/shard_map/attend/pallas_call | solution.py:165
  53.1 3.9 %collective-permute-done.15.refs_0_ = bf16[4,32,3584]{2,1,0:T(8,128)(2,1)S(1)} collective-permute-done((bf16[4,32,3584]{2,1,0:T(8,128)(2,1)S(1)}, bf16[4,32,3584]{2,1,0:T(8,128)(2,1)S(1)}, u32[]{:S(2)}, u32[]{:S(2)}) %collective-permute-start.15) | collective-permute-done | bytes 917536 | tf_op jit(solution)/shard_map/ppermute | solution.py:76
  64.2 5.2 %collective-permute-start.7 = (bf16[512,256]{1,0:T(8,128)(2,1)S(1)}, bf16[512,256]{1,0:T(8,128)(2,1)S(1)}, u32[]{:S(2)}, u32[]{:S(2)}) collective-permute-start(bf16[512,256]{1,0:T(8,128)(2,1)S(1)} %gate.15.refs_0_), channel_id=1, source_target_pairs={{0,4},{4,8},{8,12},{1,5},{5,9},{9,13},{2,6},{6,10},{10,14},{3,7},{... | collective-permute-start | bytes 786440 | tf_op jit(solution)/shard_map/ppermute | solution.py:104
  69.5 8.3 %collective-permute-done.9.refs_1_.refs_3_ = bf16[512,256]{1,0:T(8,128)(2,1)S(1)} collective-permute-done((bf16[512,256]{1,0:T(8,128)(2,1)S(1)}, bf16[512,256]{1,0:T(8,128)(2,1)S(1)}, u32[]{:S(2)}, u32[]{:S(2)}) %collective-permute-start.9) | collective-permute-done | bytes 262176 | tf_op jit(solution)/shard_map/ppermute | solution.py:109
  81.0 8.4 %collective-permute-done.8.refs_2_ = bf16[512,256]{1,0:T(8,128)(2,1)S(1)} collective-permute-done((bf16[512,256]{1,0:T(8,128)(2,1)S(1)}, bf16[512,256]{1,0:T(8,128)(2,1)S(1)}, u32[]{:S(2)}, u32[]{:S(2)}) %collective-permute-start.8) | collective-permute-done | bytes 262176 | tf_op jit(solution)/shard_map/ppermute | solution.py:105
  89.4 5.2 %collective-permute-done.10.refs_4_ = bf16[512,256]{1,0:T(8,128)(2,1)S(1)} collective-permute-done((bf16[512,256]{1,0:T(8,128)(2,1)S(1)}, bf16[512,256]{1,0:T(8,128)(2,1)S(1)}, u32[]{:S(2)}, u32[]{:S(2)}) %collective-permute-start.10) | collective-permute-done | bytes 262176 | tf_op jit(solution)/shard_map/ppermute | solution.py:110
  98.2 4.6 %collective-permute-start.11 = (bf16[512,512]{1,0:T(8,128)(2,1)S(1)}, bf16[512,512]{1,0:T(8,128)(2,1)S(1)}, u32[]{:S(2)}, u32[]{:S(2)}) collective-permute-start(bf16[512,512]{1,0:T(8,128)(2,1)S(1)} %gate.16.refs_5_), channel_id=1, source_target_pairs={{0,4},{4,8},{8,12},{1,5},{5,9},{9,13},{2,6},{6,10},{10,14},{3,7},{... | collective-permute-start | bytes 1572872 | tf_op jit(solution)/shard_map/ppermute | solution.py:104
  104.2 4.4 %project.1 = (bf16[128,1536]{1,0:T(8,128)(2,1)S(1)}, bf16[128,1536]{1,0:T(8,128)(2,1)S(1)}, bf16[128,1536]{1,0:T(8,128)(2,1)S(1)}, bf16[128,1536]{1,0:T(8,128)(2...) custom-call(s32[20]{0:T(128)S(1)} %copy-done.2, ...), custom_call_target="tpu_custom_call" | custom-call | flops 1 | bytes 1 | tf_op jit(solution)/shard_map/project/pallas_call | solution.py:165
  108.6 4.5 %collective-permute-done.13.refs_9_.refs_3_ = bf16[512,512]{1,0:T(8,128)(2,1)S(1)} collective-permute-done((bf16[512,512]{1,0:T(8,128)(2,1)S(1)}, bf16[512,512]{1,0:T(8,128)(2,1)S(1)}, u32[]{:S(2)}, u32[]{:S(2)}) %collective-permute-start.13) | collective-permute-done | bytes 524320 | tf_op jit(solution)/shard_map/ppermute | solution.py:110
  113.9 9.5 %collective-permute-done.12.refs_7_.refs_2_ = bf16[512,512]{1,0:T(8,128)(2,1)S(1)} collective-permute-done((bf16[512,512]{1,0:T(8,128)(2,1)S(1)}, bf16[512,512]{1,0:T(8,128)(2,1)S(1)}, u32[]{:S(2)}, u32[]{:S(2)}) %collective-permute-start.12) | collective-permute-done | bytes 524320 | tf_op jit(solution)/shard_map/ppermute | solution.py:105
  126.7 15.9 %collective-permute-done.25.refs_1_.refs_3_ = bf16[128,1536]{1,0:T(8,128)(2,1)S(1)} collective-permute-done((bf16[128,1536]{1,0:T(8,128)(2,1)S(1)}, bf16[128,1536]{1,0:T(8,128)(2,1)S(1)}, u32[]{:S(2)}, u32[]{:S(2)}) %collective-permute-start.25) | collective-permute-done | bytes 393248 | tf_op jit(solution)/shard_map/ppermute | solution.py:109
  148.0 14.5 %collective-permute-start.23 = (bf16[128,1536]{1,0:T(8,128)(2,1)S(1)}, bf16[128,1536]{1,0:T(8,128)(2,1)S(1)}, u32[]{:S(2)}, u32[]{:S(2)}) collective-permute-start(bf16[128,1536]{1,0:T(8,128)(2,1)S(1)} %gate.21.refs_0_), channel_id=1, source_target_pairs={{0,4},{4,8},{8,12},{1,5},{5,9},{9,13},{2,6},{6,10},{10,14},{3,7},{... | collective-permute-start | bytes 1179656 | tf_op jit(solution)/shard_map/ppermute | solution.py:104
  163.8 4.1 %collective-permute-done.29.refs_1_.refs_3_ = bf16[128,1536]{1,0:T(8,128)(2,1)S(1)} collective-permute-done((bf16[128,1536]{1,0:T(8,128)(2,1)S(1)}, bf16[128,1536]{1,0:T(8,128)(2,1)S(1)}, u32[]{:S(2)}, u32[]{:S(2)}) %collective-permute-start.29) | collective-permute-done | bytes 393248 | tf_op jit(solution)/shard_map/ppermute | solution.py:109
  168.5 4.6 %project_raw.1 = (bf16[512,2048]{1,0:T(8,128)(2,1)S(1)}, bf16[512,2048]{1,0:T(8,128)(2,1)}) custom-call(s32[20]{0:T(128)S(1)} %copy-done.2, bf16[512,256]{1,0:T(8,128)(2,1)S(1)} %gate.15.refs_0_, bf16[512,256]{1,0:T(8,128)(2,1)S(1)} %collective-permute-done.7.refs_1_, ...), custom_call_target="tpu_custom_call", output_to_operand_aliasing={{1}: (19, {})} | custom-call | flops 1 | bytes 1 | tf_op jit(solution)/shard_map/project_raw/pallas_call | solution.py:165
  176.8 11.4 %collective-permute-start.27 = (bf16[128,1536]{1,0:T(8,128)(2,1)S(1)}, bf16[128,1536]{1,0:T(8,128)(2,1)S(1)}, u32[]{:S(2)}, u32[]{:S(2)}) collective-permute-start(bf16[128,1536]{1,0:T(8,128)(2,1)S(1)} %gate.23.refs_0_), channel_id=1, source_target_pairs={{0,4},{4,8},{8,12},{1,5},{5,9},{9,13},{2,6},{6,10},{10,14},{3,7},{... | collective-permute-start | bytes 1179656 | tf_op jit(solution)/shard_map/ppermute | solution.py:104
  189.5 4.1 %collective-permute-done.33.refs_1_.refs_3_ = bf16[128,1536]{1,0:T(8,128)(2,1)S(1)} collective-permute-done((bf16[128,1536]{1,0:T(8,128)(2,1)S(1)}, bf16[128,1536]{1,0:T(8,128)(2,1)S(1)}, u32[]{:S(2)}, u32[]{:S(2)}) %collective-permute-start.33) | collective-permute-done | bytes 393248 | tf_op jit(solution)/shard_map/ppermute | solution.py:109
  197.7 6.2 %collective-permute-done.28.refs_2_ = bf16[128,1536]{1,0:T(8,128)(2,1)S(1)} collective-permute-done((bf16[128,1536]{1,0:T(8,128)(2,1)S(1)}, bf16[128,1536]{1,0:T(8,128)(2,1)S(1)}, u32[]{:S(2)}, u32[]{:S(2)}) %collective-permute-start.28) | collective-permute-done | bytes 393248 | tf_op jit(solution)/shard_map/ppermute | solution.py:105
  204.5 9.0 %collective-permute-start.31 = (bf16[128,1536]{1,0:T(8,128)(2,1)S(1)}, bf16[128,1536]{1,0:T(8,128)(2,1)S(1)}, u32[]{:S(2)}, u32[]{:S(2)}) collective-permute-start(bf16[128,1536]{1,0:T(8,128)(2,1)S(1)} %gate.25.refs_0_), channel_id=1, source_target_pairs={{0,4},{4,8},{8,12},{1,5},{5,9},{9,13},{2,6},{6,10},{10,14},{3,7},{... | collective-permute-start | bytes 1179656 | tf_op jit(solution)/shard_map/ppermute | solution.py:104
  214.8 4.1 %collective-permute-done.34.refs_3_ = bf16[128,1536]{1,0:T(8,128)(2,1)S(1)} collective-permute-done((bf16[128,1536]{1,0:T(8,128)(2,1)S(1)}, bf16[128,1536]{1,0:T(8,128)(2,1)S(1)}, u32[]{:S(2)}, u32[]{:S(2)}) %collective-permute-start.34) | collective-permute-done | bytes 393248 | tf_op jit(solution)/shard_map/ppermute | solution.py:109
  230.6 6.1 %collective-permute-done.35.refs_4_ = bf16[128,1536]{1,0:T(8,128)(2,1)S(1)} collective-permute-done((bf16[128,1536]{1,0:T(8,128)(2,1)S(1)}, bf16[128,1536]{1,0:T(8,128)(2,1)S(1)}, u32[]{:S(2)}, u32[]{:S(2)}) %collective-permute-start.35) | collective-permute-done | bytes 393248 | tf_op jit(solution)/shard_map/ppermute | solution.py:110
  (91 shorter events, 68.6 us)
Async XLA Ops:
  9.3 24.3 %collective-permute-start.1 = (bf16[1552,256]{1,0:T(8,128)(2,1)}, bf16[1552,256]{1,0:T(8,128)(2,1)S(1)}, u32[]{:S(2)}, u32[]{:S(2)}) collective-permute-start(bf16[1552,256]{1,0:T(8,128)(2,1)} %get-tuple-element.22.refs_0_), channel_id=1, source_target_pairs={{0,2},{1,3},{2,0},{3,1},{4,6},{5,7},{6,4},{7,5},{8,10},{9,11},{10,... | collective-permute-start | bytes 2383880 | tf_op jit(solution)/shard_map/ppermute | solution.py:43
  13.9 17.5 %collective-permute-start.3 = (bf16[32,3584]{1,0:T(8,128)(2,1)}, bf16[32,3584]{1,0:T(8,128)(2,1)S(1)}, u32[]{:S(2)}, u32[]{:S(2)}) collective-permute-start(bf16[32,3584]{1,0:T(8,128)(2,1)} %get-tuple-element.25), channel_id=1, source_target_pairs={{0,8},{4,12},{8,0},{12,4},{1,9},{5,13},{9,1},{13,5},{2,10},{6,14},... | collective-permute-start | bytes 688136 | tf_op jit(solution)/shard_map/ppermute | solution.py:603
  17.8 23.0 %collective-permute-start = (bf16[1552,256]{1,0:T(8,128)(2,1)}, bf16[1552,256]{1,0:T(8,128)(2,1)S(1)}, u32[]{:S(2)}, u32[]{:S(2)}) collective-permute-start(bf16[1552,256]{1,0:T(8,128)(2,1)} %get-tuple-element.22.refs_0_), channel_id=1, source_target_pairs={{0,1},{1,0},{2,3},{3,2},{4,5},{5,4},{6,7},{7,6},{8,9},{9,8},{10,11... | collective-permute-start | bytes 2383880 | tf_op jit(solution)/shard_map/ppermute | solution.py:43
  34.2 22.8 %collective-permute-start.15 = (bf16[4,32,3584]{2,1,0:T(8,128)(2,1)S(1)}, bf16[4,32,3584]{2,1,0:T(8,128)(2,1)S(1)}, u32[]{:S(2)}, u32[]{:S(2)}) collective-permute-start(bf16[4,32,3584]{2,1,0:T(8,128)(2,1)S(1)} %stack.89.refs_1_.refs_5_.refs_10_), channel_id=1, source_target_pairs={{0,2},{1,3},{2,0},{3,1},{4,6},{5,7},{6,4},{7,5},{8,10},{9,11},{10,... | collective-permute-start | bytes 2752520 | tf_op jit(solution)/shard_map/ppermute | solution.py:76
  34.8 28.0 %collective-permute-start.6 = (bf16[512,512]{1,0:T(8,128)(2,1)S(1)}, bf16[512,512]{1,0:T(8,128)(2,1)S(1)}, u32[]{:S(2)}, u32[]{:S(2)}) collective-permute-start(bf16[512,512]{1,0:T(8,128)(2,1)S(1)} %get-tuple-element.27.refs_2_), channel_id=1, source_target_pairs={{0,8},{4,12},{8,0},{12,4},{1,9},{5,13},{9,1},{13,5},{2,10},{6,14},... | collective-permute-start | bytes 1572872 | tf_op jit(solution)/shard_map/ppermute | solution.py:109
  39.3 30.2 %collective-permute-start.17 = (bf16[4,32,3584]{2,1,0:T(8,128)(2,1)S(1)}, bf16[4,32,3584]{2,1,0:T(8,128)(2,1)S(1)}, u32[]{:S(2)}, u32[]{:S(2)}) collective-permute-start(bf16[4,32,3584]{2,1,0:T(8,128)(2,1)S(1)} %stack.89.refs_1_.refs_5_.refs_10_), channel_id=1, source_target_pairs={{0,16},{16,0},{1,17},{17,1},{2,18},{18,2},{3,19},{19,3},{4,20},{20... | collective-permute-start | bytes 2752520 | tf_op jit(solution)/shard_map/ppermute | solution.py:76
  57.6 37.1 %collective-permute-start.19 = (bf16[4,32,3584]{2,1,0:T(8,128)(2,1)S(1)}, bf16[4,32,3584]{2,1,0:T(8,128)(2,1)S(1)}, u32[]{:S(2)}, u32[]{:S(2)}) collective-permute-start(bf16[4,32,3584]{2,1,0:T(8,128)(2,1)S(1)} %gate.17.refs_0_), channel_id=1, source_target_pairs={{0,16},{16,0},{1,17},{17,1},{2,18},{18,2},{3,19},{19,3},{4,20},{20... | collective-permute-start | bytes 2752520 | tf_op jit(solution)/shard_map/ppermute | solution.py:76
  69.4 28.8 %collective-permute-start.14 = (bf16[4,32,3584]{2,1,0:T(8,128)(2,1)S(1)}, bf16[4,32,3584]{2,1,0:T(8,128)(2,1)S(1)}, u32[]{:S(2)}, u32[]{:S(2)}) collective-permute-start(bf16[4,32,3584]{2,1,0:T(8,128)(2,1)S(1)} %stack.89.refs_1_.refs_5_.refs_10_), channel_id=1, source_target_pairs={{0,1},{1,0},{2,3},{3,2},{4,5},{5,4},{6,7},{7,6},{8,9},{9,8},{10,11... | collective-permute-start | bytes 2752520 | tf_op jit(solution)/shard_map/ppermute | solution.py:87
  78.3 24.5 %collective-permute-start.18 = (bf16[4,32,3584]{2,1,0:T(8,128)(2,1)S(1)}, bf16[4,32,3584]{2,1,0:T(8,128)(2,1)S(1)}, u32[]{:S(2)}, u32[]{:S(2)}) collective-permute-start(bf16[4,32,3584]{2,1,0:T(8,128)(2,1)S(1)} %gate.19.refs_9_.refs_14_), channel_id=1, source_target_pairs={{0,1},{1,0},{2,3},{3,2},{4,5},{5,4},{6,7},{7,6},{8,9},{9,8},{10,11... | collective-permute-start | bytes 2752520 | tf_op jit(solution)/shard_map/ppermute | solution.py:87
  102.8 20.5 %collective-permute-start.12 = (bf16[512,512]{1,0:T(8,128)(2,1)S(1)}, bf16[512,512]{1,0:T(8,128)(2,1)S(1)}, u32[]{:S(2)}, u32[]{:S(2)}) collective-permute-start(bf16[512,512]{1,0:T(8,128)(2,1)S(1)} %gate.16.refs_5_), channel_id=1, source_target_pairs={{4,0},{8,4},{12,8},{5,1},{9,5},{13,9},{6,2},{10,6},{14,10},{7,3},{... | collective-permute-start | bytes 1572872 | tf_op jit(solution)/shard_map/ppermute | solution.py:105
  123.9 18.7 %collective-permute-start.25 = (bf16[128,1536]{1,0:T(8,128)(2,1)S(1)}, bf16[128,1536]{1,0:T(8,128)(2,1)S(1)}, u32[]{:S(2)}, u32[]{:S(2)}) collective-permute-start(bf16[128,1536]{1,0:T(8,128)(2,1)S(1)} %gate.22), channel_id=1, source_target_pairs={{0,8},{4,12},{8,0},{12,4},{1,9},{5,13},{9,1},{13,5},{2,10},{6,14},... | collective-permute-start | bytes 1179656 | tf_op jit(solution)/shard_map/ppermute | solution.py:109
  124.0 20.6 %collective-permute-start.21 = (bf16[128,1536]{1,0:T(8,128)(2,1)S(1)}, bf16[128,1536]{1,0:T(8,128)(2,1)S(1)}, u32[]{:S(2)}, u32[]{:S(2)}) collective-permute-start(bf16[128,1536]{1,0:T(8,128)(2,1)S(1)} %get-tuple-element.34.refs_0_), channel_id=1, source_target_pairs={{0,4},{4,8},{8,12},{1,5},{5,9},{9,13},{2,6},{6,10},{10,14},{3,7},{... | collective-permute-start | bytes 1179656 | tf_op jit(solution)/shard_map/ppermute | solution.py:104
  125.4 22.0 %collective-permute-start.22 = (bf16[128,1536]{1,0:T(8,128)(2,1)S(1)}, bf16[128,1536]{1,0:T(8,128)(2,1)S(1)}, u32[]{:S(2)}, u32[]{:S(2)}) collective-permute-start(bf16[128,1536]{1,0:T(8,128)(2,1)S(1)} %get-tuple-element.34.refs_0_), channel_id=1, source_target_pairs={{4,0},{8,4},{12,8},{5,1},{9,5},{13,9},{6,2},{10,6},{14,10},{7,3},{... | collective-permute-start | bytes 1179656 | tf_op jit(solution)/shard_map/ppermute | solution.py:105
  143.1 24.7 %collective-permute-start.29 = (bf16[128,1536]{1,0:T(8,128)(2,1)S(1)}, bf16[128,1536]{1,0:T(8,128)(2,1)S(1)}, u32[]{:S(2)}, u32[]{:S(2)}) collective-permute-start(bf16[128,1536]{1,0:T(8,128)(2,1)S(1)} %gate.24), channel_id=1, source_target_pairs={{0,8},{4,12},{8,0},{12,4},{1,9},{5,13},{9,1},{13,5},{2,10},{6,14},... | collective-permute-start | bytes 1179656 | tf_op jit(solution)/shard_map/ppermute | solution.py:109
  143.2 31.3 %collective-permute-start.26 = (bf16[128,1536]{1,0:T(8,128)(2,1)S(1)}, bf16[128,1536]{1,0:T(8,128)(2,1)S(1)}, u32[]{:S(2)}, u32[]{:S(2)}) collective-permute-start(bf16[128,1536]{1,0:T(8,128)(2,1)S(1)} %collective-permute-done.25.refs_1_.refs_3_), channel_id=1, source_target_pairs={{4,0},{8,12},{5,1},{9,13},{6,2},{10,14},{7,3},{11,15},{20,16},{24,... | collective-permute-start | bytes 1179656 | tf_op jit(solution)/shard_map/ppermute | solution.py:110
  148.0 26.5 %collective-permute-start.23 = (bf16[128,1536]{1,0:T(8,128)(2,1)S(1)}, bf16[128,1536]{1,0:T(8,128)(2,1)S(1)}, u32[]{:S(2)}, u32[]{:S(2)}) collective-permute-start(bf16[128,1536]{1,0:T(8,128)(2,1)S(1)} %gate.21.refs_0_), channel_id=1, source_target_pairs={{0,4},{4,8},{8,12},{1,5},{5,9},{9,13},{2,6},{6,10},{10,14},{3,7},{... | collective-permute-start | bytes 1179656 | tf_op jit(solution)/shard_map/ppermute | solution.py:104
  168.4 25.2 %collective-permute-start.33 = (bf16[128,1536]{1,0:T(8,128)(2,1)S(1)}, bf16[128,1536]{1,0:T(8,128)(2,1)S(1)}, u32[]{:S(2)}, u32[]{:S(2)}) collective-permute-start(bf16[128,1536]{1,0:T(8,128)(2,1)S(1)} %gate.26), channel_id=1, source_target_pairs={{0,8},{4,12},{8,0},{12,4},{1,9},{5,13},{9,1},{13,5},{2,10},{6,14},... | collective-permute-start | bytes 1179656 | tf_op jit(solution)/shard_map/ppermute | solution.py:109
  173.1 22.5 %collective-permute-start.30 = (bf16[128,1536]{1,0:T(8,128)(2,1)S(1)}, bf16[128,1536]{1,0:T(8,128)(2,1)S(1)}, u32[]{:S(2)}, u32[]{:S(2)}) collective-permute-start(bf16[128,1536]{1,0:T(8,128)(2,1)S(1)} %collective-permute-done.29.refs_1_.refs_3_), channel_id=1, source_target_pairs={{4,0},{8,12},{5,1},{9,13},{6,2},{10,14},{7,3},{11,15},{20,16},{24,... | collective-permute-start | bytes 1179656 | tf_op jit(solution)/shard_map/ppermute | solution.py:110
  176.8 21.0 %collective-permute-start.27 = (bf16[128,1536]{1,0:T(8,128)(2,1)S(1)}, bf16[128,1536]{1,0:T(8,128)(2,1)S(1)}, u32[]{:S(2)}, u32[]{:S(2)}) collective-permute-start(bf16[128,1536]{1,0:T(8,128)(2,1)S(1)} %gate.23.refs_0_), channel_id=1, source_target_pairs={{0,4},{4,8},{8,12},{1,5},{5,9},{9,13},{2,6},{6,10},{10,14},{3,7},{... | collective-permute-start | bytes 1179656 | tf_op jit(solution)/shard_map/ppermute | solution.py:104
  194.2 24.8 %collective-permute-start.34 = (bf16[128,1536]{1,0:T(8,128)(2,1)S(1)}, bf16[128,1536]{1,0:T(8,128)(2,1)S(1)}, u32[]{:S(2)}, u32[]{:S(2)}) collective-permute-start(bf16[128,1536]{1,0:T(8,128)(2,1)S(1)} %gate.27), channel_id=1, source_target_pairs={{0,8},{4,12},{8,0},{12,4},{1,9},{5,13},{9,1},{13,5},{2,10},{6,14},... | collective-permute-start | bytes 1179656 | tf_op jit(solution)/shard_map/ppermute | solution.py:109
  194.3 32.9 %collective-permute-start.36 = (bf16[128,1536]{1,0:T(8,128)(2,1)S(1)}, bf16[128,1536]{1,0:T(8,128)(2,1)S(1)}, u32[]{:S(2)}, u32[]{:S(2)}) collective-permute-start(bf16[128,1536]{1,0:T(8,128)(2,1)S(1)} %collective-permute-done.33.refs_1_.refs_3_), channel_id=1, source_target_pairs={{4,0},{8,12},{5,1},{9,13},{6,2},{10,14},{7,3},{11,15},{20,16},{24,... | collective-permute-start | bytes 1179656 | tf_op jit(solution)/shard_map/ppermute | solution.py:110
  204.5 26.0 %collective-permute-start.31 = (bf16[128,1536]{1,0:T(8,128)(2,1)S(1)}, bf16[128,1536]{1,0:T(8,128)(2,1)S(1)}, u32[]{:S(2)}, u32[]{:S(2)}) collective-permute-start(bf16[128,1536]{1,0:T(8,128)(2,1)S(1)} %gate.25.refs_0_), channel_id=1, source_target_pairs={{0,4},{4,8},{8,12},{1,5},{5,9},{9,13},{2,6},{6,10},{10,14},{3,7},{... | collective-permute-start | bytes 1179656 | tf_op jit(solution)/shard_map/ppermute | solution.py:104
  213.5 17.0 %collective-permute-start.32 = (bf16[128,1536]{1,0:T(8,128)(2,1)S(1)}, bf16[128,1536]{1,0:T(8,128)(2,1)S(1)}, u32[]{:S(2)}, u32[]{:S(2)}) collective-permute-start(bf16[128,1536]{1,0:T(8,128)(2,1)S(1)} %gate.25.refs_0_), channel_id=1, source_target_pairs={{4,0},{8,4},{12,8},{5,1},{9,5},{13,9},{6,2},{10,6},{14,10},{7,3},{... | collective-permute-start | bytes 1179656 | tf_op jit(solution)/shard_map/ppermute | solution.py:105
  219.0 17.7 %collective-permute-start.35 = (bf16[128,1536]{1,0:T(8,128)(2,1)S(1)}, bf16[128,1536]{1,0:T(8,128)(2,1)S(1)}, u32[]{:S(2)}, u32[]{:S(2)}) collective-permute-start(bf16[128,1536]{1,0:T(8,128)(2,1)S(1)} %collective-permute-done.34.refs_3_), channel_id=1, source_target_pairs={{4,0},{8,12},{5,1},{9,13},{6,2},{10,14},{7,3},{11,15},{20,16},{24,... | collective-permute-start | bytes 1179656 | tf_op jit(solution)/shard_map/ppermute | solution.py:110
  (19 other events, 335.9 us)

commit v10 on v8

--- a/solution.py
+++ b/solution.py
@@ -16,7 +16,7 @@
 CHUNK = 128
 KEY_BLOCK = 512
 ATTEND_FLOPS = 16
-RAW_PART = 4
+RAW_PART = 8
 TAIL = 16
 DIGIT = 32
 ANYWHERE = pl.BlockSpec(memory_space=pl.ANY)

time: 232 us -> 230 us (level)
  waiting for transfers between devices: 110 us -> 94.8 us
  starting transfers between devices: 67.9 us -> 78.7 us
  local copies, waits for them, and re-layouts: 1.64 us -> 5.82 us
    ppermute x6, waiting for transfers between devices: 28.8 us -> 14 us  [line_near(): return (up, lax.ppermute(value, 'tensor', [(1, 0), (2, 1), (3, 2)]))]
    ppermute x6, starting transfers between devices: 36.1 us -> 47.3 us  [line_near(): up = lax.ppermute(value, 'tensor', [(0, 1), (1, 2), (2, 3)])]
    ppermute x6, waiting for transfers between devices: 18.4 us -> 24 us  [line_far(): return (far, lax.ppermute(far, 'tensor', [(1, 0), (2, 3)]))]
    ppermute x6, waiting for transfers between devices: 46.7 us -> 42.1 us  [line_far(): far = lax.ppermute(value, 'tensor', [(0, 2), (1, 3), (2, 0), (3, 1)])]
    unnamed x12 -> x16, local copies, waits for them, and re-layouts: 0.95 us -> 5.21 us
    ppermute x3, waiting for transfers between devices: 13.6 us -> 10.4 us  [per_device(): parts.append(lax.ppermute(cuts[shift], 'tensor', pairs))]
  transfers between devices with their start and end apart: 37 -> 37, of which waited for: 19 -> 16; matrix products, arithmetic and copies ran while one was open for 0% -> 0% of each run, Pallas kernels for 15% -> 15%
where the time goes in v10:
time: 230 us
  waiting for transfers between devices  94.8 us (41%)
  starting transfers between devices  78.7 us (34%)
  Pallas kernels  46 us (20%)
  local copies, waits for them, and re-layouts  5.82 us (3%)
  between operations  2.42 us (1%)
    ppermute x6, starting transfers between devices, line_near(): up = lax.ppermute(value, 'tensor', [(0, 1), (1, 2), (2, 3)])  47.3 us
    pallas_call x22, Pallas kernels, call(): pl.pallas_call(kernel, grid_spec=pltpu.PrefetchScalarGridSpec(num_scalar_...  46 us
    ppermute x6, waiting for transfers between devices, line_far(): far = lax.ppermute(value, 'tensor', [(0, 2), (1, 3), (2, 0), (3, 1)])  42.1 us
    ppermute x6, waiting for transfers between devices, line_far(): return (far, lax.ppermute(far, 'tensor', [(1, 0), (2, 3)]))  24 us
    ppermute x6, waiting for transfers between devices, line_near(): return (up, lax.ppermute(value, 'tensor', [(1, 0), (2, 1), (3, 2)]))  14 us
    ppermute x3, waiting for transfers between devices, per_device(): parts.append(lax.ppermute(cuts[shift], 'tensor', pairs))  10.4 us
    ppermute x6, starting transfers between devices, line_near(): return (up, lax.ppermute(value, 'tensor', [(1, 0), (2, 1), (3, 2)]))  7.74 us
    ppermute x6, starting transfers between devices, line_far(): return (far, lax.ppermute(far, 'tensor', [(1, 0), (2, 3)]))  7.72 us
  transfers between devices with their start and end apart: 37, of which 16 were waited for; matrix products, arithmetic and copies ran while one was open for 0% of the time, Pallas kernels for 15%

profile of v10, /device:TPU:0, one launch (start us, length us, event | category | flops | bytes accessed | tf_op | source)
XLA Modules:
  0.0 229.7 jit_solution(17273501447346389421)
XLA Ops:
  4.5 4.4 %prepare.1 = (bf16[512,256]{1,0:T(8,128)(2,1)}, bf16[1552,256]{1,0:T(8,128)(2,1)}, bf16[32,2816]{1,0:T(8,128)(2,1)}, bf16[32,2816]{1,0:T(8,128)(2,1)}, bf16[32,2...) custom-call(s32[20]{0:T(128)} %stack.86.info, bf16[512,256]{1,0:T(8,128)(2,1)} %q_hbm.1, bf16[512,256]{1,0:T(8,128)(2,1)} %bitcast.28, ...), custom_call_target="tpu_custom_call" | custom-call | flops 1 | bytes 1 | tf_op jit(solution)/shard_map/prepare/pallas_call | solution.py:166
  17.4 4.1 %collective-permute-done.2.refs_1_ = bf16[32,2816]{1,0:T(8,128)(2,1)S(1)} collective-permute-done((bf16[32,2816]{1,0:T(8,128)(2,1)}, bf16[32,2816]{1,0:T(8,128)(2,1)S(1)}, u32[]{:S(2)}, u32[]{:S(2)}) %collective-permute-start.2) | collective-permute-done | bytes 180256 | tf_op jit(solution)/shard_map/ppermute | solution.py:604
  21.4 6.3 %collective-permute-done.3.refs_2_ = bf16[32,2816]{1,0:T(8,128)(2,1)S(1)} collective-permute-done((bf16[32,2816]{1,0:T(8,128)(2,1)}, bf16[32,2816]{1,0:T(8,128)(2,1)S(1)}, u32[]{:S(2)}, u32[]{:S(2)}) %collective-permute-start.3) | collective-permute-done | bytes 180256 | tf_op jit(solution)/shard_map/ppermute | solution.py:604
  33.3 6.2 %collective-permute-start.6 = (bf16[512,256]{1,0:T(8,128)(2,1)S(1)}, bf16[512,256]{1,0:T(8,128)(2,1)S(1)}, u32[]{:S(2)}, u32[]{:S(2)}) collective-permute-start(bf16[512,256]{1,0:T(8,128)(2,1)S(1)} %get-tuple-element.28.refs_3_.refs_5_), channel_id=1, source_target_pairs={{0,4},{4,8},{8,12},{1,5},{5,9},{9,13},{2,6},{6,10},{10,14},{3,7},{... | collective-permute-start | bytes 786440 | tf_op jit(solution)/shard_map/ppermute | solution.py:104
  46.8 12.2 %attend.1.refs_0_.refs_1_ = bf16[512,256]{1,0:T(8,128)(2,1)S(1)} custom-call(s32[20]{0:T(128)S(1)} %copy-done.3, bf16[512,256]{1,0:T(8,128)(2,1)S(1)} %copy-done.7, bf16[1552,256]{1,0:T(8,128)(2,1)S(1)} %copy-done.6, bf16[1552,256]{1,0:T(8,128)(2,1)S(1)} %collective-permute-done.refs_1_, bf16[1552,256]{1,0:T(8,128)(2,1)S(1)} %gate.12.refs_2_, ...), custom_call_target="tpu_custom_call" | custom-call | flops 12884901888 | bytes 1 | tf_op jit(solution)/shard_map/attend/pallas_call | solution.py:166
  62.7 5.2 %collective-permute-start.9 = (bf16[512,256]{1,0:T(8,128)(2,1)S(1)}, bf16[512,256]{1,0:T(8,128)(2,1)S(1)}, u32[]{:S(2)}, u32[]{:S(2)}) collective-permute-start(bf16[512,256]{1,0:T(8,128)(2,1)S(1)} %gate.13.refs_0_), channel_id=1, source_target_pairs={{0,4},{4,8},{8,12},{1,5},{5,9},{9,13},{2,6},{6,10},{10,14},{3,7},{... | collective-permute-start | bytes 786440 | tf_op jit(solution)/shard_map/ppermute | solution.py:104
  67.9 8.0 %collective-permute-done.11.refs_3_ = bf16[512,256]{1,0:T(8,128)(2,1)S(1)} collective-permute-done((bf16[512,256]{1,0:T(8,128)(2,1)S(1)}, bf16[512,256]{1,0:T(8,128)(2,1)S(1)}, u32[]{:S(2)}, u32[]{:S(2)}) %collective-permute-start.11) | collective-permute-done | bytes 262176 | tf_op jit(solution)/shard_map/ppermute | solution.py:109
  78.4 6.6 %collective-permute-done.12.refs_4_ = bf16[512,256]{1,0:T(8,128)(2,1)S(1)} collective-permute-done((bf16[512,256]{1,0:T(8,128)(2,1)S(1)}, bf16[512,256]{1,0:T(8,128)(2,1)S(1)}, u32[]{:S(2)}, u32[]{:S(2)}) %collective-permute-start.12) | collective-permute-done | bytes 262176 | tf_op jit(solution)/shard_map/ppermute | solution.py:110
  88.9 4.7 %project.1 = (bf16[128,1792]{1,0:T(8,128)(2,1)S(1)}, bf16[128,1792]{1,0:T(8,128)(2,1)S(1)}, bf16[128,1792]{1,0:T(8,128)(2,1)S(1)}, bf16[128,1792]{1,0:T(8,128)(2...) custom-call(s32[20]{0:T(128)S(1)} %copy-done.3, ...), custom_call_target="tpu_custom_call" | custom-call | flops 1 | bytes 1 | tf_op jit(solution)/shard_map/project/pallas_call | solution.py:166
  94.2 4.4 %collective-permute-start.21 = (bf16[128,1792]{1,0:T(8,128)(2,1)S(1)}, bf16[128,1792]{1,0:T(8,128)(2,1)S(1)}, u32[]{:S(2)}, u32[]{:S(2)}) collective-permute-start(bf16[128,1792]{1,0:T(8,128)(2,1)S(1)} %get-tuple-element.34.refs_0_), channel_id=1, source_target_pairs={{0,4},{4,8},{8,12},{1,5},{5,9},{9,13},{2,6},{6,10},{10,14},{3,7},{... | collective-permute-start | bytes 1376264 | tf_op jit(solution)/shard_map/ppermute | solution.py:104
  99.9 17.0 %collective-permute-done.25.refs_1_.refs_3_ = bf16[128,1792]{1,0:T(8,128)(2,1)S(1)} collective-permute-done((bf16[128,1792]{1,0:T(8,128)(2,1)S(1)}, bf16[128,1792]{1,0:T(8,128)(2,1)S(1)}, u32[]{:S(2)}, u32[]{:S(2)}) %collective-permute-start.25) | collective-permute-done | bytes 458784 | tf_op jit(solution)/shard_map/ppermute | solution.py:109
  120.1 8.5 %collective-permute-done.13.refs_9_.refs_3_ = bf16[512,256]{1,0:T(8,128)(2,1)S(1)} collective-permute-done((bf16[512,256]{1,0:T(8,128)(2,1)S(1)}, bf16[512,256]{1,0:T(8,128)(2,1)S(1)}, u32[]{:S(2)}, u32[]{:S(2)}) %collective-permute-start.13) | collective-permute-done | bytes 262176 | tf_op jit(solution)/shard_map/ppermute | solution.py:110
  129.2 10.5 %collective-permute-start.23 = (bf16[128,1792]{1,0:T(8,128)(2,1)S(1)}, bf16[128,1792]{1,0:T(8,128)(2,1)S(1)}, u32[]{:S(2)}, u32[]{:S(2)}) collective-permute-start(bf16[128,1792]{1,0:T(8,128)(2,1)S(1)} %gate.18.refs_0_), channel_id=1, source_target_pairs={{0,4},{4,8},{8,12},{1,5},{5,9},{9,13},{2,6},{6,10},{10,14},{3,7},{... | collective-permute-start | bytes 1376264 | tf_op jit(solution)/shard_map/ppermute | solution.py:104
  140.9 5.5 %collective-permute-done.29.refs_1_.refs_3_ = bf16[128,1792]{1,0:T(8,128)(2,1)S(1)} collective-permute-done((bf16[128,1792]{1,0:T(8,128)(2,1)S(1)}, bf16[128,1792]{1,0:T(8,128)(2,1)S(1)}, u32[]{:S(2)}, u32[]{:S(2)}) %collective-permute-start.29) | collective-permute-done | bytes 458784 | tf_op jit(solution)/shard_map/ppermute | solution.py:109
  151.6 6.4 %collective-permute-done.24.refs_2_ = bf16[128,1792]{1,0:T(8,128)(2,1)S(1)} collective-permute-done((bf16[128,1792]{1,0:T(8,128)(2,1)S(1)}, bf16[128,1792]{1,0:T(8,128)(2,1)S(1)}, u32[]{:S(2)}, u32[]{:S(2)}) %collective-permute-start.24) | collective-permute-done | bytes 458784 | tf_op jit(solution)/shard_map/ppermute | solution.py:105
  158.6 10.5 %collective-permute-start.27 = (bf16[128,1792]{1,0:T(8,128)(2,1)S(1)}, bf16[128,1792]{1,0:T(8,128)(2,1)S(1)}, u32[]{:S(2)}, u32[]{:S(2)}) collective-permute-start(bf16[128,1792]{1,0:T(8,128)(2,1)S(1)} %gate.19.refs_0_), channel_id=1, source_target_pairs={{0,4},{4,8},{8,12},{1,5},{5,9},{9,13},{2,6},{6,10},{10,14},{3,7},{... | collective-permute-start | bytes 1376264 | tf_op jit(solution)/shard_map/ppermute | solution.py:104
  170.5 5.5 %collective-permute-done.33.refs_1_.refs_3_ = bf16[128,1792]{1,0:T(8,128)(2,1)S(1)} collective-permute-done((bf16[128,1792]{1,0:T(8,128)(2,1)S(1)}, bf16[128,1792]{1,0:T(8,128)(2,1)S(1)}, u32[]{:S(2)}, u32[]{:S(2)}) %collective-permute-start.33) | collective-permute-done | bytes 458784 | tf_op jit(solution)/shard_map/ppermute | solution.py:109
  180.0 7.6 %collective-permute-done.28.refs_2_ = bf16[128,1792]{1,0:T(8,128)(2,1)S(1)} collective-permute-done((bf16[128,1792]{1,0:T(8,128)(2,1)S(1)}, bf16[128,1792]{1,0:T(8,128)(2,1)S(1)}, u32[]{:S(2)}, u32[]{:S(2)}) %collective-permute-start.28) | collective-permute-done | bytes 458784 | tf_op jit(solution)/shard_map/ppermute | solution.py:105
  188.1 10.5 %collective-permute-start.31 = (bf16[128,1792]{1,0:T(8,128)(2,1)S(1)}, bf16[128,1792]{1,0:T(8,128)(2,1)S(1)}, u32[]{:S(2)}, u32[]{:S(2)}) collective-permute-start(bf16[128,1792]{1,0:T(8,128)(2,1)S(1)} %gate.21.refs_0_), channel_id=1, source_target_pairs={{0,4},{4,8},{8,12},{1,5},{5,9},{9,13},{2,6},{6,10},{10,14},{3,7},{... | collective-permute-start | bytes 1376264 | tf_op jit(solution)/shard_map/ppermute | solution.py:104
  200.0 5.5 %collective-permute-done.34.refs_3_ = bf16[128,1792]{1,0:T(8,128)(2,1)S(1)} collective-permute-done((bf16[128,1792]{1,0:T(8,128)(2,1)S(1)}, bf16[128,1792]{1,0:T(8,128)(2,1)S(1)}, u32[]{:S(2)}, u32[]{:S(2)}) %collective-permute-start.34) | collective-permute-done | bytes 458784 | tf_op jit(solution)/shard_map/ppermute | solution.py:109
  206.8 3.5 %norm.4.refs_6_ = bf16[512,8192]{1,0:T(8,128)(2,1)} custom-call(s32[20]{0:T(128)S(1)} %copy-done.4, f32[1,8192]{1,0:T(1,128)S(1)} %bitcast.23, bf16[128,1792]{1,0:T(8,128)(2,1)S(1)} %get-tuple-element.34.refs_0_, bf16[128,1792]{1,0:T(8,128)(2,1)S(1)} %collective-permute-done.21.refs_1_, bf16[128,1792]{1,0:T(8,128)(2,1)S(1)} %collective-permute-done.22.refs_2_, ...), custom_call_target="tpu_custom_call" | custom-call | flops 1 | bytes 1 | tf_op jit(solution)/shard_map/norm/pallas_call | solution.py:166
  213.8 3.5 %norm.6.refs_6_ = bf16[512,8192]{1,0:T(8,128)(2,1)} custom-call(s32[20]{0:T(128)S(1)} %copy-done.4, f32[1,8192]{1,0:T(1,128)S(1)} %bitcast.25, bf16[128,1792]{1,0:T(8,128)(2,1)S(1)} %gate.19.refs_0_, bf16[128,1792]{1,0:T(8,128)(2,1)S(1)} %collective-permute-done.27.refs_1_, ...), custom_call_target="tpu_custom_call", output_to_operand_aliasing={{}: (8, {})} | custom-call | flops 1 | bytes 1 | tf_op jit(solution)/shard_map/norm/pallas_call | solution.py:166
  217.2 8.9 %collective-permute-done.35.refs_4_ = bf16[128,1792]{1,0:T(8,128)(2,1)S(1)} collective-permute-done((bf16[128,1792]{1,0:T(8,128)(2,1)S(1)}, bf16[128,1792]{1,0:T(8,128)(2,1)S(1)}, u32[]{:S(2)}, u32[]{:S(2)}) %collective-permute-start.35) | collective-permute-done | bytes 458784 | tf_op jit(solution)/shard_map/ppermute | solution.py:110
  226.2 3.5 %norm.7 = bf16[512,8192]{1,0:T(8,128)(2,1)} custom-call(s32[20]{0:T(128)S(1)} %copy-done.4, f32[1,8192]{1,0:T(1,128)S(1)} %bitcast.26, bf16[128,1792]{1,0:T(8,128)(2,1)S(1)} %gate.21.refs_0_, bf16[128,1792]{1,0:T(8,128)(2,1)S(1)} %collective-permute-done.31.refs_1_, ...), custom_call_target="tpu_custom_call", output_to_operand_aliasing={{}: (8, {})} | custom-call | flops 1 | bytes 1 | tf_op jit(solution)/shard_map/norm/pallas_call | solution.py:166
  (93 shorter events, 58.2 us)
Async XLA Ops:
  8.9 23.2 %collective-permute-start.1 = (bf16[1552,256]{1,0:T(8,128)(2,1)}, bf16[1552,256]{1,0:T(8,128)(2,1)S(1)}, u32[]{:S(2)}, u32[]{:S(2)}) collective-permute-start(bf16[1552,256]{1,0:T(8,128)(2,1)} %get-tuple-element.22.refs_0_), channel_id=1, source_target_pairs={{0,2},{1,3},{2,0},{3,1},{4,6},{5,7},{6,4},{7,5},{8,10},{9,11},{10,... | collective-permute-start | bytes 2383880 | tf_op jit(solution)/shard_map/ppermute | solution.py:43
  17.4 23.5 %collective-permute-start = (bf16[1552,256]{1,0:T(8,128)(2,1)}, bf16[1552,256]{1,0:T(8,128)(2,1)S(1)}, u32[]{:S(2)}, u32[]{:S(2)}) collective-permute-start(bf16[1552,256]{1,0:T(8,128)(2,1)} %get-tuple-element.22.refs_0_), channel_id=1, source_target_pairs={{0,1},{1,0},{2,3},{3,2},{4,5},{5,4},{6,7},{7,6},{8,9},{9,8},{10,11... | collective-permute-start | bytes 2383880 | tf_op jit(solution)/shard_map/ppermute | solution.py:43
  32.7 26.3 %collective-permute-start.15 = (bf16[4,32,2816]{2,1,0:T(8,128)(2,1)S(1)}, bf16[4,32,2816]{2,1,0:T(8,128)(2,1)S(1)}, u32[]{:S(2)}, u32[]{:S(2)}) collective-permute-start(bf16[4,32,2816]{2,1,0:T(8,128)(2,1)S(1)} %stack.89.refs_1_.refs_5_.refs_10_), channel_id=1, source_target_pairs={{0,2},{1,3},{2,0},{3,1},{4,6},{5,7},{6,4},{7,5},{8,10},{9,11},{10,... | collective-permute-start | bytes 2162696 | tf_op jit(solution)/shard_map/ppermute | solution.py:76
  33.3 26.8 %collective-permute-start.6 = (bf16[512,256]{1,0:T(8,128)(2,1)S(1)}, bf16[512,256]{1,0:T(8,128)(2,1)S(1)}, u32[]{:S(2)}, u32[]{:S(2)}) collective-permute-start(bf16[512,256]{1,0:T(8,128)(2,1)S(1)} %get-tuple-element.28.refs_3_.refs_5_), channel_id=1, source_target_pairs={{0,4},{4,8},{8,12},{1,5},{5,9},{9,13},{2,6},{6,10},{10,14},{3,7},{... | collective-permute-start | bytes 786440 | tf_op jit(solution)/shard_map/ppermute | solution.py:104
  39.5 20.6 %collective-permute-start.7 = (bf16[512,256]{1,0:T(8,128)(2,1)S(1)}, bf16[512,256]{1,0:T(8,128)(2,1)S(1)}, u32[]{:S(2)}, u32[]{:S(2)}) collective-permute-start(bf16[512,256]{1,0:T(8,128)(2,1)S(1)} %get-tuple-element.28.refs_3_.refs_5_), channel_id=1, source_target_pairs={{4,0},{8,4},{12,8},{5,1},{9,5},{13,9},{6,2},{10,6},{14,10},{7,3},{... | collective-permute-start | bytes 786440 | tf_op jit(solution)/shard_map/ppermute | solution.py:105
  40.9 19.8 %collective-permute-start.8 = (bf16[512,256]{1,0:T(8,128)(2,1)S(1)}, bf16[512,256]{1,0:T(8,128)(2,1)S(1)}, u32[]{:S(2)}, u32[]{:S(2)}) collective-permute-start(bf16[512,256]{1,0:T(8,128)(2,1)S(1)} %get-tuple-element.27.refs_2_), channel_id=1, source_target_pairs={{0,8},{4,12},{8,0},{12,4},{1,9},{5,13},{9,1},{13,5},{2,10},{6,14},... | collective-permute-start | bytes 786440 | tf_op jit(solution)/shard_map/ppermute | solution.py:109
  43.2 34.0 %collective-permute-start.17 = (bf16[4,32,2816]{2,1,0:T(8,128)(2,1)S(1)}, bf16[4,32,2816]{2,1,0:T(8,128)(2,1)S(1)}, u32[]{:S(2)}, u32[]{:S(2)}) collective-permute-start(bf16[4,32,2816]{2,1,0:T(8,128)(2,1)S(1)} %stack.89.refs_1_.refs_5_.refs_10_), channel_id=1, source_target_pairs={{0,16},{16,0},{1,17},{17,1},{2,18},{18,2},{3,19},{19,3},{4,20},{20... | collective-permute-start | bytes 2162696 | tf_op jit(solution)/shard_map/ppermute | solution.py:76
  59.6 25.5 %collective-permute-start.19 = (bf16[4,32,2816]{2,1,0:T(8,128)(2,1)S(1)}, bf16[4,32,2816]{2,1,0:T(8,128)(2,1)S(1)}, u32[]{:S(2)}, u32[]{:S(2)}) collective-permute-start(bf16[4,32,2816]{2,1,0:T(8,128)(2,1)S(1)} %gate.14.refs_0_), channel_id=1, source_target_pairs={{0,16},{16,0},{1,17},{17,1},{2,18},{18,2},{3,19},{19,3},{4,20},{20... | collective-permute-start | bytes 2162696 | tf_op jit(solution)/shard_map/ppermute | solution.py:76
  93.6 23.3 %collective-permute-start.25 = (bf16[128,1792]{1,0:T(8,128)(2,1)S(1)}, bf16[128,1792]{1,0:T(8,128)(2,1)S(1)}, u32[]{:S(2)}, u32[]{:S(2)}) collective-permute-start(bf16[128,1792]{1,0:T(8,128)(2,1)S(1)} %get-tuple-element.35), channel_id=1, source_target_pairs={{0,8},{4,12},{8,0},{12,4},{1,9},{5,13},{9,1},{13,5},{2,10},{6,14},... | collective-permute-start | bytes 1376264 | tf_op jit(solution)/shard_map/ppermute | solution.py:109
  94.2 34.4 %collective-permute-start.21 = (bf16[128,1792]{1,0:T(8,128)(2,1)S(1)}, bf16[128,1792]{1,0:T(8,128)(2,1)S(1)}, u32[]{:S(2)}, u32[]{:S(2)}) collective-permute-start(bf16[128,1792]{1,0:T(8,128)(2,1)S(1)} %get-tuple-element.34.refs_0_), channel_id=1, source_target_pairs={{0,4},{4,8},{8,12},{1,5},{5,9},{9,13},{2,6},{6,10},{10,14},{3,7},{... | collective-permute-start | bytes 1376264 | tf_op jit(solution)/shard_map/ppermute | solution.py:104
  98.6 30.0 %collective-permute-start.22 = (bf16[128,1792]{1,0:T(8,128)(2,1)S(1)}, bf16[128,1792]{1,0:T(8,128)(2,1)S(1)}, u32[]{:S(2)}, u32[]{:S(2)}) collective-permute-start(bf16[128,1792]{1,0:T(8,128)(2,1)S(1)} %get-tuple-element.34.refs_0_), channel_id=1, source_target_pairs={{4,0},{8,4},{12,8},{5,1},{9,5},{13,9},{6,2},{10,6},{14,10},{7,3},{... | collective-permute-start | bytes 1376264 | tf_op jit(solution)/shard_map/ppermute | solution.py:105
  117.5 29.0 %collective-permute-start.29 = (bf16[128,1792]{1,0:T(8,128)(2,1)S(1)}, bf16[128,1792]{1,0:T(8,128)(2,1)S(1)}, u32[]{:S(2)}, u32[]{:S(2)}) collective-permute-start(bf16[128,1792]{1,0:T(8,128)(2,1)S(1)} %gate.20), channel_id=1, source_target_pairs={{0,8},{4,12},{8,0},{12,4},{1,9},{5,13},{9,1},{13,5},{2,10},{6,14},... | collective-permute-start | bytes 1376264 | tf_op jit(solution)/shard_map/ppermute | solution.py:109
  118.8 32.8 %collective-permute-start.26 = (bf16[128,1792]{1,0:T(8,128)(2,1)S(1)}, bf16[128,1792]{1,0:T(8,128)(2,1)S(1)}, u32[]{:S(2)}, u32[]{:S(2)}) collective-permute-start(bf16[128,1792]{1,0:T(8,128)(2,1)S(1)} %collective-permute-done.25.refs_1_.refs_3_), channel_id=1, source_target_pairs={{4,0},{8,12},{5,1},{9,13},{6,2},{10,14},{7,3},{11,15},{20,16},{24,... | collective-permute-start | bytes 1376264 | tf_op jit(solution)/shard_map/ppermute | solution.py:110
  129.2 22.5 %collective-permute-start.23 = (bf16[128,1792]{1,0:T(8,128)(2,1)S(1)}, bf16[128,1792]{1,0:T(8,128)(2,1)S(1)}, u32[]{:S(2)}, u32[]{:S(2)}) collective-permute-start(bf16[128,1792]{1,0:T(8,128)(2,1)S(1)} %gate.18.refs_0_), channel_id=1, source_target_pairs={{0,4},{4,8},{8,12},{1,5},{5,9},{9,13},{2,6},{6,10},{10,14},{3,7},{... | collective-permute-start | bytes 1376264 | tf_op jit(solution)/shard_map/ppermute | solution.py:104
  139.6 18.5 %collective-permute-start.24 = (bf16[128,1792]{1,0:T(8,128)(2,1)S(1)}, bf16[128,1792]{1,0:T(8,128)(2,1)S(1)}, u32[]{:S(2)}, u32[]{:S(2)}) collective-permute-start(bf16[128,1792]{1,0:T(8,128)(2,1)S(1)} %gate.18.refs_0_), channel_id=1, source_target_pairs={{4,0},{8,4},{12,8},{5,1},{9,5},{13,9},{6,2},{10,6},{14,10},{7,3},{... | collective-permute-start | bytes 1376264 | tf_op jit(solution)/shard_map/ppermute | solution.py:105
  147.0 29.0 %collective-permute-start.33 = (bf16[128,1792]{1,0:T(8,128)(2,1)S(1)}, bf16[128,1792]{1,0:T(8,128)(2,1)S(1)}, u32[]{:S(2)}, u32[]{:S(2)}) collective-permute-start(bf16[128,1792]{1,0:T(8,128)(2,1)S(1)} %gate.22), channel_id=1, source_target_pairs={{0,8},{4,12},{8,0},{12,4},{1,9},{5,13},{9,1},{13,5},{2,10},{6,14},... | collective-permute-start | bytes 1376264 | tf_op jit(solution)/shard_map/ppermute | solution.py:109
  150.3 27.6 %collective-permute-start.30 = (bf16[128,1792]{1,0:T(8,128)(2,1)S(1)}, bf16[128,1792]{1,0:T(8,128)(2,1)S(1)}, u32[]{:S(2)}, u32[]{:S(2)}) collective-permute-start(bf16[128,1792]{1,0:T(8,128)(2,1)S(1)} %collective-permute-done.29.refs_1_.refs_3_), channel_id=1, source_target_pairs={{4,0},{8,12},{5,1},{9,13},{6,2},{10,14},{7,3},{11,15},{20,16},{24,... | collective-permute-start | bytes 1376264 | tf_op jit(solution)/shard_map/ppermute | solution.py:110
  158.6 21.4 %collective-permute-start.27 = (bf16[128,1792]{1,0:T(8,128)(2,1)S(1)}, bf16[128,1792]{1,0:T(8,128)(2,1)S(1)}, u32[]{:S(2)}, u32[]{:S(2)}) collective-permute-start(bf16[128,1792]{1,0:T(8,128)(2,1)S(1)} %gate.19.refs_0_), channel_id=1, source_target_pairs={{0,4},{4,8},{8,12},{1,5},{5,9},{9,13},{2,6},{6,10},{10,14},{3,7},{... | collective-permute-start | bytes 1376264 | tf_op jit(solution)/shard_map/ppermute | solution.py:104
  169.2 18.4 %collective-permute-start.28 = (bf16[128,1792]{1,0:T(8,128)(2,1)S(1)}, bf16[128,1792]{1,0:T(8,128)(2,1)S(1)}, u32[]{:S(2)}, u32[]{:S(2)}) collective-permute-start(bf16[128,1792]{1,0:T(8,128)(2,1)S(1)} %gate.19.refs_0_), channel_id=1, source_target_pairs={{4,0},{8,4},{12,8},{5,1},{9,5},{13,9},{6,2},{10,6},{14,10},{7,3},{... | collective-permute-start | bytes 1376264 | tf_op jit(solution)/shard_map/ppermute | solution.py:105
  176.5 29.0 %collective-permute-start.34 = (bf16[128,1792]{1,0:T(8,128)(2,1)S(1)}, bf16[128,1792]{1,0:T(8,128)(2,1)S(1)}, u32[]{:S(2)}, u32[]{:S(2)}) collective-permute-start(bf16[128,1792]{1,0:T(8,128)(2,1)S(1)} %gate.23), channel_id=1, source_target_pairs={{0,8},{4,12},{8,0},{12,4},{1,9},{5,13},{9,1},{13,5},{2,10},{6,14},... | collective-permute-start | bytes 1376264 | tf_op jit(solution)/shard_map/ppermute | solution.py:109
  176.6 37.2 %collective-permute-start.36 = (bf16[128,1792]{1,0:T(8,128)(2,1)S(1)}, bf16[128,1792]{1,0:T(8,128)(2,1)S(1)}, u32[]{:S(2)}, u32[]{:S(2)}) collective-permute-start(bf16[128,1792]{1,0:T(8,128)(2,1)S(1)} %collective-permute-done.33.refs_1_.refs_3_), channel_id=1, source_target_pairs={{4,0},{8,12},{5,1},{9,13},{6,2},{10,14},{7,3},{11,15},{20,16},{24,... | collective-permute-start | bytes 1376264 | tf_op jit(solution)/shard_map/ppermute | solution.py:110
  188.1 29.1 %collective-permute-start.31 = (bf16[128,1792]{1,0:T(8,128)(2,1)S(1)}, bf16[128,1792]{1,0:T(8,128)(2,1)S(1)}, u32[]{:S(2)}, u32[]{:S(2)}) collective-permute-start(bf16[128,1792]{1,0:T(8,128)(2,1)S(1)} %gate.21.refs_0_), channel_id=1, source_target_pairs={{0,4},{4,8},{8,12},{1,5},{5,9},{9,13},{2,6},{6,10},{10,14},{3,7},{... | collective-permute-start | bytes 1376264 | tf_op jit(solution)/shard_map/ppermute | solution.py:104
  198.7 18.5 %collective-permute-start.32 = (bf16[128,1792]{1,0:T(8,128)(2,1)S(1)}, bf16[128,1792]{1,0:T(8,128)(2,1)S(1)}, u32[]{:S(2)}, u32[]{:S(2)}) collective-permute-start(bf16[128,1792]{1,0:T(8,128)(2,1)S(1)} %gate.21.refs_0_), channel_id=1, source_target_pairs={{4,0},{8,4},{12,8},{5,1},{9,5},{13,9},{6,2},{10,6},{14,10},{7,3},{... | collective-permute-start | bytes 1376264 | tf_op jit(solution)/shard_map/ppermute | solution.py:105
  205.5 20.7 %collective-permute-start.35 = (bf16[128,1792]{1,0:T(8,128)(2,1)S(1)}, bf16[128,1792]{1,0:T(8,128)(2,1)S(1)}, u32[]{:S(2)}, u32[]{:S(2)}) collective-permute-start(bf16[128,1792]{1,0:T(8,128)(2,1)S(1)} %collective-permute-done.34.refs_3_), channel_id=1, source_target_pairs={{4,0},{8,12},{5,1},{9,13},{6,2},{10,14},{7,3},{11,15},{20,16},{24,... | collective-permute-start | bytes 1376264 | tf_op jit(solution)/shard_map/ppermute | solution.py:110
  (21 other events, 298.4 us)

commit v11 on v9

--- a/solution.py
+++ b/solution.py
@@ -16,7 +16,6 @@
 CHUNK = 128
 KEY_BLOCK = 512
 ATTEND_FLOPS = 16
-RAW_PART = 4
 TAIL = 16
 DIGIT = 32
 ANYWHERE = pl.BlockSpec(memory_space=pl.ANY)
@@ -73,9 +72,9 @@
             axis, flip, size = ("groups", bit // contexts, groups)
         pairs = [(i, i ^ flip) for i in range(size)]
         for mask in sorted(held):
+            if mask:
+                held[mask] = first(held[mask], held[bit])
             held[mask | bit] = lax.ppermute(held[mask], axis, pairs)
-        if bit == bits[0]:
-            held[bit] = first(held[bit])
     if contexts > 1:
         for mask in sorted(held):
             held[mask] = then(held[mask], mask) if mask else held[mask]
@@ -110,19 +109,19 @@
     return far, lax.ppermute(far, "tensor", [(1, 0), (2, 3)])
 
 
-def chunk_gathers(info, values, copies, first, made, count):
+def chunk_gathers(info, values, copies, second, count):
     if count != 4:
         return [line_gather(value, count) for value in values]
     fars, lines = [], []
     for number, value in enumerate(values):
-        after = [fars[-1][0]] if number else first
+        after = [fars[-1][0]] if number else []
+        if number == 1:
+            after += second
         fars.append(line_far(gate(info, value, after) if after else value))
     for number, value in enumerate(copies):
         after = list(lines[number - 1][1:3]) if number else []
         if number > 1:
             after.append(fars[number - 2][1])
-        if number == len(copies) // 2:
-            after += made
         value = gate(info, value, after) if after else value
         lines.append([value, *line_near(value), *fars[number]])
     return lines
@@ -184,9 +183,9 @@
     return pl.BlockSpec(tuple(a.shape), lambda i, info: zeros)
 
 
-def prepare_kernel(table, slab, keep, info, q_hbm, kv_hbm, cache_hbm, w_hbm, cos_ref, sin_ref,
+def prepare_kernel(table, slab, info, q_hbm, kv_hbm, cache_hbm, w_hbm, cos_ref, sin_ref,
                    length_ref, *refs):
-    count, raw = table.count, slab - keep
+    count = table.count
     q_out, kv_out, outs = refs[0], refs[1], refs[2 : 2 + count]
     q_ref, kv_ref, w_ref, sems = refs[2 + count :]
     slots, rows, part = cache_hbm.shape[0], q_ref.shape[0], w_ref.shape[0]
@@ -205,11 +204,7 @@
     copies[0].wait()
     for d, out in enumerate(outs):
         target = lax.rem(info[table.place] + d, count)
-        out[:, :keep] = w_ref[:, pl.ds(pl.multiple_of(target * slab, slab), keep)]
-        for j in range(count if raw else 0):
-            out[:, keep + j * raw : keep + (j + 1) * raw] = w_ref[
-                :, j * slab + keep : (j + 1) * slab
-            ]
+        out[...] = w_ref[:, pl.ds(pl.multiple_of(target * slab, slab), slab)]
 
     cosine, sine = cos_ref[...], sin_ref[...]
 
@@ -233,16 +228,15 @@
 
 
 def prepare(table, info, queries, span_pairs, cache, out_weight, cosine, sine, lengths, part,
-            slab, keep):
+            slab):
     rows = queries.shape[0]
     shapes = [
         jax.ShapeDtypeStruct(queries.shape, jnp.bfloat16),
         jax.ShapeDtypeStruct((cache.shape[0] + rows + TAIL, 2 * HD), jnp.bfloat16),
     ]
-    width = keep + table.count * (slab - keep)
-    shapes += [jax.ShapeDtypeStruct((part, width), out_weight.dtype)] * table.count
+    shapes += [jax.ShapeDtypeStruct((part, slab), out_weight.dtype)] * table.count
     return call(
-        functools.partial(prepare_kernel, table, slab, keep),
+        functools.partial(prepare_kernel, table, slab),
         "prepare",
         info,
         [queries, span_pairs, cache, out_weight, cosine, sine, lengths],
@@ -260,26 +254,6 @@
     )
 
 
-def last_columns_kernel(info, *refs):
-    refs[-1][...] = refs[0][...]
-    refs[-2][...] = refs[0][...]
-
-
-def last_columns(info, value, width, after):
-    rows, full = value.shape
-    shape = jax.ShapeDtypeStruct((rows, width), value.dtype)
-    return call(
-        last_columns_kernel,
-        "last_columns",
-        info,
-        [value, *after],
-        [pl.BlockSpec((rows, width), lambda i, info: (0, full // width - 1))]
-        + [ANYWHERE] * len(after),
-        [whole(shape)] * 2,
-        [shape] * 2,
-    )
-
-
 def stack_kernel(count, info, *refs):
     for number, part in enumerate(refs[:count]):
         refs[-1][number] = part[...]
@@ -315,12 +289,12 @@
     )
 
 
-def attend_kernel(table, slots, info, q_ref, *refs):
+def attend_kernel(table, slots, first, info, q_ref, *refs):
     count = table.contexts
     pieces, out_ref, s_ref = refs[:count], refs[-2], refs[-1]
     rows = q_ref.shape[0]
     heads = q_ref.shape[1] // HD
-    chunk = pl.program_id(0)
+    chunk = pl.program_id(0) + first
     mine = info[0]
     q = jnp.concatenate([q_ref[:, h * HD : (h + 1) * HD] for h in range(heads)], axis=0)
     exponent = math.log2(math.e) / math.sqrt(HD)
@@ -377,186 +351,116 @@
         out_ref[:, h * HD : (h + 1) * HD] = result[h * rows : (h + 1) * rows]
 
 
-def attend(table, info, queries, pieces, slots, rows):
-    all_rows, width = queries.shape
+def attend(table, info, queries, pieces, slots, begin, size, rows):
+    width = queries.shape[1]
     heads = width // HD
     keys = sum(a.shape[0] - TAIL for a in pieces)
-    chunk_spec = pl.BlockSpec((rows, width), lambda i, info: (i, 0))
+    first = begin // rows
     return call(
-        functools.partial(attend_kernel, table, slots),
+        functools.partial(attend_kernel, table, slots, first),
         "attend",
         info,
         [queries, *pieces],
-        [chunk_spec] + [whole(a) for a in pieces],
-        chunk_spec,
-        jax.ShapeDtypeStruct((all_rows, width), jnp.bfloat16),
-        grid=(all_rows // rows,),
+        [pl.BlockSpec((rows, width), lambda i, info: (first + i, 0))]
+        + [whole(a) for a in pieces],
+        pl.BlockSpec((rows, width), lambda i, info: (i, 0)),
+        jax.ShapeDtypeStruct((size, width), jnp.bfloat16),
+        grid=(size // rows,),
         scratch=[pltpu.VMEM((heads * rows, keys), jnp.float32)],
-        flops=ATTEND_FLOPS * all_rows * heads * keys * HD,
+        flops=ATTEND_FLOPS * size * heads * keys * HD,
         vmem=28,
     )
 
 
-def place_weights(table, info, pieces, w_ref, begin):
-    part, width = pieces[0].shape[1], w_ref.shape[2]
-    for number, piece in enumerate(pieces):
-        start = pl.multiple_of(info[table.rows + number] * part, part)
-        for d in range(table.count):
-            w_ref[d, pl.ds(start, part)] = piece[d, :, begin : begin + width]
-
-
-def project_kernel(table, lines, shares, keep, splits, info, *refs):
+def project_kernel(table, lines, shares, splits, info, *refs):
     count = table.count
     attention, pieces = refs[:lines], refs[lines : lines + shares]
     r_ref = refs[lines + shares]
     parts, h_ref, w_ref = refs[-2 - 2 * len(splits) : -2], refs[-2], refs[-1]
-    rows = r_ref.shape[0]
-
-    @pl.when(pl.program_id(0) == 0)
-    def _():
-        place_weights(table, info, pieces, w_ref, 0)
-
-    total = r_ref[:, :keep].astype(jnp.float32)
-    for d in range(count):
-        block = line_read(table, info, attention, d).astype(jnp.bfloat16)
-        total = total + jnp.dot(block, w_ref[d], preferred_element_type=jnp.float32)
-    result = total.astype(jnp.bfloat16)
-    h_ref[:, :keep] = result
-    for part, (begin, size) in zip(parts, splits * 2):
-        for row in range(begin, begin + size, rows):
-
-            @pl.when(pl.program_id(0) == row // rows)
-            def _():
-                part[row - begin : row - begin + rows] = result
-
-
-def project(table, info, attention, pieces, residual, keep, rows, splits):
-    all_rows, slab = residual.shape
-    count, part_rows, _ = pieces[0].shape
-    parts = [jax.ShapeDtypeStruct((size, keep), jnp.bfloat16) for _, size in splits * 2]
-    row_spec = pl.BlockSpec((rows, slab), lambda i, info: (i, 0))
-    return call(
-        functools.partial(project_kernel, table, len(attention), len(pieces), keep, splits),
-        "project",
-        info,
-        [*attention, *pieces, residual],
-        line_spec(attention, rows, lambda i: i)
-        + [whole(p) for p in pieces]
-        + [row_spec],
-        [whole(part) for part in parts] + [row_spec],
-        [*parts, jax.ShapeDtypeStruct(residual.shape, jnp.bfloat16)],
-        grid=(all_rows // rows,),
-        scratch=[pltpu.VMEM((count, len(pieces) * part_rows, keep), jnp.bfloat16)],
-        vmem=36,
-    )
-
-
-def project_raw_kernel(table, lines, raw_lines, shares, keep, info, *refs):
-    count = table.count
-    attention, residuals = refs[:lines], refs[lines : lines + raw_lines]
-    pieces = refs[lines + raw_lines : lines + raw_lines + shares]
-    raw_ref, h_ref, w_ref = refs[-3:]
-    raw = h_ref.shape[1]
-
-    @pl.when(pl.program_id(0) == 0)
-    def _():
-        place_weights(table, info, pieces, w_ref, keep)
-
+    share_rows = pieces[0].shape[1]
+    for number, piece in enumerate(pieces):
+        start = pl.multiple_of(info[table.rows + number] * share_rows, share_rows)
+        for d in range(count):
+            w_ref[d, pl.ds(start, share_rows)] = piece[d]
     blocks = [
         line_read(table, info, attention, d).astype(jnp.bfloat16) for d in range(count)
     ]
-    for slab in range(count):
-        cols = pl.ds(pl.multiple_of(info[table.place + slab] * raw, raw), raw)
-        total = line_read(table, info, residuals, slab)
+    for part, copy, (begin, size) in zip(parts, parts[len(splits) :], splits):
+        rows = slice(begin, begin + size)
+        total = r_ref[rows].astype(jnp.float32)
         for d in range(count):
             total = total + jnp.dot(
-                blocks[d], w_ref[d, :, cols], preferred_element_type=jnp.float32
+                blocks[d][rows], w_ref[d], preferred_element_type=jnp.float32
             )
         result = total.astype(jnp.bfloat16)
-        raw_ref[:, slab * raw : (slab + 1) * raw] = result
-        if slab == 0:
-            h_ref[...] = result
-
-
-def project_raw(table, info, attention, residuals, pieces, hidden, keep, raw, rows):
-    all_rows, slab = hidden.shape
-    count, part_rows, _ = pieces[0].shape
-    args = [*attention, *residuals, *pieces, hidden]
-    out = jax.ShapeDtypeStruct((all_rows, count * raw), jnp.bfloat16)
+        h_ref[rows] = result
+        part[...] = result
+        copy[...] = result
+
+
+def project(table, info, attention, pieces, residual, hidden, half, halves, splits):
+    all_rows, slab = residual.shape
+    rows = all_rows // halves
+    count, share_rows, _ = pieces[0].shape
+    parts = [jax.ShapeDtypeStruct((size, slab), jnp.bfloat16) for _, size in splits * 2]
+    row_spec = pl.BlockSpec((rows, slab), lambda i, info: (half, 0))
+    args = [*attention, *pieces, residual]
+    specs = line_spec(attention, rows, lambda i: 0) + [whole(p) for p in pieces] + [row_spec]
+    aliases = {}
+    if hidden is not None:
+        args.append(hidden)
+        specs.append(ANYWHERE)
+        aliases = {len(args): len(parts)}
     return call(
-        functools.partial(
-            project_raw_kernel, table, len(attention), len(residuals), len(pieces), keep
-        ),
-        "project_raw",
+        functools.partial(project_kernel, table, len(attention), len(pieces), splits),
+        "project",
         info,
         args,
-        line_spec(attention, rows, lambda i: i)
-        + line_spec(residuals, rows, lambda i: i)
-        + [whole(p) for p in pieces]
-        + [ANYWHERE],
-        [
-            pl.BlockSpec((rows, count * raw), lambda i, info: (i, 0)),
-            pl.BlockSpec((rows, raw), lambda i, info: (i, slab // raw - 1)),
-        ],
-        [out, jax.ShapeDtypeStruct(hidden.shape, jnp.bfloat16)],
-        grid=(all_rows // rows,),
-        aliases={len(args): 1},
-        scratch=[pltpu.VMEM((count, len(pieces) * part_rows, count * raw), jnp.bfloat16)],
+        specs,
+        [whole(part) for part in parts] + [row_spec],
+        [*parts, jax.ShapeDtypeStruct(residual.shape, jnp.bfloat16)],
+        aliases=aliases,
+        scratch=[pltpu.VMEM((count, len(pieces) * share_rows, slab), jnp.bfloat16)],
         vmem=36,
     )
 
 
-def norm_kernel(table, lines, keep, slab, info, g_ref, *refs):
+def norm_kernel(table, lines, info, g_ref, *refs):
     count = table.count
     blocks, out_ref = refs[:lines], refs[-1]
-    raw = slab - keep
-    values = []
+    slab = out_ref.shape[1] // count
     squares = jnp.zeros((out_ref.shape[0], 1), jnp.float32)
-
-    def read(d):
-        found = [(0, keep, line_read(table, info, blocks, d))]
-        if raw:
-            cols = slice(d * raw, (d + 1) * raw)
-            found.append((keep, raw, refs[lines][:, cols].astype(jnp.float32)))
-        return found
-
     for d in range(count):
-        for _, _, value in read(d):
-            squares = squares + jnp.sum(value * value, axis=1, keepdims=True)
+        value = line_read(table, info, blocks, d)
+        squares = squares + jnp.sum(value * value, axis=1, keepdims=True)
     inverse = lax.rsqrt(squares / (count * slab) + EPS_NORM)
     for d in range(count):
-        for offset, width, value in read(d):
-            start = pl.multiple_of(info[table.place + d] * slab + offset, HD)
-            cols = pl.ds(start, width)
-            out_ref[:, cols] = (value * inverse * g_ref[:, cols]).astype(jnp.bfloat16)
-
-
-def norm_into(table, info, buffer, blocks, raw_hidden, gain, begin, rows, keep, slab, total_rows):
-    width = table.count * slab
-    step = min(rows, 32)
-    steps, first = rows // step, begin // step
+        cols = pl.ds(pl.multiple_of(info[table.place + d] * slab, slab), slab)
+        value = line_read(table, info, blocks, d)
+        out_ref[:, cols] = (value * inverse * g_ref[:, cols]).astype(jnp.bfloat16)
+
+
+def norm_into(table, info, buffer, blocks, gain, begin, rows, total_rows):
+    width = gain.shape[0]
+    step = math.gcd(rows, 32)
+    first = begin // step
     args = [gain.reshape(1, width), *blocks]
     in_specs = [pl.BlockSpec((1, width), lambda i, info: (0, 0))]
     in_specs += line_spec(blocks, step, lambda i: i)
-    if raw_hidden is not None:
-        args.append(raw_hidden)
-        in_specs.append(
-            pl.BlockSpec((step, raw_hidden.shape[1]), lambda i, info: (first + i, 0))
-        )
     aliases = {}
     if buffer is not None:
         args.append(buffer)
         in_specs.append(ANYWHERE)
         aliases = {len(args): 0}
     return call(
-        functools.partial(norm_kernel, table, len(blocks), keep, slab),
+        functools.partial(norm_kernel, table, len(blocks)),
         "norm",
         info,
         args,
         in_specs,
         pl.BlockSpec((step, width), lambda i, info: (first + i, 0)),
         jax.ShapeDtypeStruct((total_rows, width), jnp.bfloat16),
-        grid=(steps,),
+        grid=(rows // step,),
         aliases=aliases,
     )
 
@@ -574,11 +478,12 @@
     groups = lax.axis_size("groups")
     shares = groups * contexts
     share = lax.axis_index("groups") * contexts + context_index
-    raw = slab // RAW_PART if slab % (RAW_PART * HD) == 0 else 0
-    keep = slab - raw
     chunk = min(CHUNK, rows)
-    sizes = [chunk] * (rows // chunk)
-    splits = [(sum(sizes[:n]), size) for n, size in enumerate(sizes)]
+    halves = 2 if rows % (2 * chunk) == 0 else 1
+    half = rows // halves
+    splits = [[(0, chunk), (chunk, half - chunk)] if half > chunk else [(0, half)]] * halves
+    if halves == 2 and chunk == 128 and half == 256:
+        splits = [splits[0], [(0, 160), (160, 96)]]
 
     table = Table(contexts, count)
     steering = [context_index, *owners_of(contexts, context_index)]
@@ -595,60 +500,46 @@
     sign = jnp.where(jnp.arange(HD) < HD // 2, -1.0, 1.0)
     q_turned, payload, *cuts = prepare(
         table, info, queries, span_local, cache_local, out_weight, jnp.cos(angles),
-        jnp.sin(angles) * sign[None, :], lengths, depth // shares, slab, keep,
+        jnp.sin(angles) * sign[None, :], lengths, depth // shares, slab,
     )
     parts = [cuts[0]]
     for shift in range(1, count):
         pairs = [(i, (i + shift) % count) for i in range(count)]
         parts.append(lax.ppermute(cuts[shift], "tensor", pairs))
-    sent = []
-
-    def between(block):
-        sent.append(stack(info, parts, []))
-        if raw:
-            sent.extend(last_columns(info, residual, raw, parts[1:]))
-        return gate(info, block, sent)
-
-    pieces = pieces_of(payload, "context", contexts, between)
-    mixed = attend(table, info, q_turned, pieces, cache_local.shape[0], chunk)
-    residuals = []
-    if raw and count == 4:
-        early = line_far(sent[1])
-        attention = line_gather(gate(info, mixed, early[:1]), count)
-        near = gate(info, sent[2], attention[3:4])
-        residuals = [near, *line_near(near), *early]
-    else:
-        attention = line_gather(mixed, count)
-        residuals = line_gather(sent[1], count) if raw else []
+    own_weights = stack(info, parts, [])
+    pieces = pieces_of(
+        payload, "context", contexts, lambda block: gate(info, block, [own_weights])
+    )
+    slots = cache_local.shape[0]
+    mixed = [
+        attend(table, info, q_turned, pieces, slots, number * half, half, chunk)
+        for number in range(halves)
+    ]
+    attention = [line_gather(value, count) for value in mixed]
     weights = plane_gather(
-        sent[0],
+        own_weights,
         groups,
         contexts,
-        lambda block: gate(info, block, [mixed]),
-        lambda block, mask: gate(info, block, attention[3:4] if mask in (mask & -mask,) else attention[1:]),
-    )
-
-    *hidden_parts, hidden = project(
-        table, info, attention, weights, residual, keep, chunk, splits
-    )
-    raw_hidden = None
-    if raw:
-        raw_hidden, hidden = project_raw(
-            table, info, attention, residuals, weights, hidden, keep, raw, chunk
+        lambda block, other: gate(info, block, [mixed[0], other]),
+        lambda block, mask: gate(
+            info,
+            block,
+            attention[0][3:4] if mask in (mask & -mask,) else [*attention[0][1:], *mixed[1:]],
+        ),
+    )
+    values, copies, hidden = [], [], None
+    for number in range(halves):
+        *made, hidden = project(
+            table, info, attention[number], weights, residual, hidden, number, halves,
+            splits[number],
         )
-    lines = chunk_gathers(
-        info,
-        hidden_parts[: len(splits)],
-        hidden_parts[len(splits) :],
-        [*residuals[1:3], *residuals[4:]],
-        [raw_hidden] if raw else [],
-        count,
-    )
-    normed = None
-    for (begin, size), blocks in zip(splits, lines):
-        normed = norm_into(
-            table, info, normed, blocks, raw_hidden, gain, begin, size, keep, slab, rows
-        )
+        values += made[: len(made) // 2]
+        copies += made[len(made) // 2 :]
+    lines = chunk_gathers(info, values, copies, attention[-1][1:], count)
+    normed, begin = None, 0
+    for blocks, value in zip(lines, values):
+        normed = norm_into(table, info, normed, blocks, gain, begin, value.shape[0], rows)
+        begin += value.shape[0]
     return (hidden, normed)
 
 

time: 241 us -> 249 us (1.033)
  waiting for transfers between devices: 105 us -> 121 us
  starting transfers between devices: 80.5 us -> 75.8 us
  Pallas kernels: 48.3 us -> 43.6 us
  local copies, waits for them, and re-layouts: 1.64 us -> 4.36 us
    ppermute x6, waiting for transfers between devices: 15.8 us -> 48 us  [line_far(): return (far, lax.ppermute(far, 'tensor', [(1, 0), (2, 3)]))]
    ppermute x6, waiting for transfers between devices: 28.7 us -> 13.9 us  [line_near(): return (up, lax.ppermute(value, 'tensor', [(1, 0), (2, 1), (3, 2)]))]
    ppermute x6, starting transfers between devices: 46.2 us -> 35.4 us  [line_near(): up = lax.ppermute(value, 'tensor', [(0, 1), (1, 2), (2, 3)])]
    ppermute x3, waiting for transfers between devices: 13.6 us -> 7.26 us  [per_device(): parts.append(lax.ppermute(cuts[shift], 'tensor', pairs))]
    ppermute x6, starting transfers between devices: 5.63 us -> 11.5 us  [line_far(): far = lax.ppermute(value, 'tensor', [(0, 2), (1, 3), (2, 0), (3, 1)])]
    pallas_call x24 -> x21, Pallas kernels: 48.3 us -> 43.6 us  [call(): pl.pallas_call(kernel, grid_spec=pltpu.PrefetchScalarGridSpec(num_scalar_...]
    ppermute x3, waiting for transfers between devices: 0.01 us -> 2.99 us  [pieces_of(): held[mask | bit] = lax.ppermute(held[mask], axis, pairs)]
    unnamed x12 -> x14, local copies, waits for them, and re-layouts: 0.95 us -> 3.67 us
  transfers between devices with their start and end apart: 37 -> 37, of which waited for: 19 -> 16; matrix products, arithmetic and copies ran while one was open for 0% -> 0% of each run, Pallas kernels for 17% -> 13%
where the time goes in v11:
time: 249 us
  waiting for transfers between devices  121 us (49%)
  starting transfers between devices  75.8 us (30%)
  Pallas kernels  43.6 us (18%)
  local copies, waits for them, and re-layouts  4.36 us (2%)
    ppermute x6, waiting for transfers between devices, line_far(): return (far, lax.ppermute(far, 'tensor', [(1, 0), (2, 3)]))  48 us
    pallas_call x21, Pallas kernels, call(): pl.pallas_call(kernel, grid_spec=pltpu.PrefetchScalarGridSpec(num_scalar_...  43.6 us
    ppermute x6, waiting for transfers between devices, line_far(): far = lax.ppermute(value, 'tensor', [(0, 2), (1, 3), (2, 0), (3, 1)])  41.1 us
    ppermute x6, starting transfers between devices, line_near(): up = lax.ppermute(value, 'tensor', [(0, 1), (1, 2), (2, 3)])  35.4 us
    ppermute x6, waiting for transfers between devices, line_near(): return (up, lax.ppermute(value, 'tensor', [(1, 0), (2, 1), (3, 2)]))  13.9 us
    ppermute x6, starting transfers between devices, line_far(): far = lax.ppermute(value, 'tensor', [(0, 2), (1, 3), (2, 0), (3, 1)])  11.5 us
    ppermute x6, starting transfers between devices, line_far(): return (far, lax.ppermute(far, 'tensor', [(1, 0), (2, 3)]))  7.73 us
    ppermute x6, starting transfers between devices, line_near(): return (up, lax.ppermute(value, 'tensor', [(1, 0), (2, 1), (3, 2)]))  7.73 us
  transfers between devices with their start and end apart: 37, of which 16 were waited for; matrix products, arithmetic and copies ran while one was open for 0% of the time, Pallas kernels for 13%

profile of v11, /device:TPU:0, one launch (start us, length us, event | category | flops | bytes accessed | tf_op | source)
XLA Modules:
  0.0 248.7 jit_solution(4097757451489963185)
XLA Ops:
  4.5 4.4 %prepare.1 = (bf16[512,256]{1,0:T(8,128)(2,1)}, bf16[1552,256]{1,0:T(8,128)(2,1)}, bf16[32,2048]{1,0:T(8,128)(2,1)}, bf16[32,2048]{1,0:T(8,128)(2,1)}, bf16[32,2...) custom-call(s32[20]{0:T(128)} %stack.86.info, bf16[512,256]{1,0:T(8,128)(2,1)} %q_hbm.1, bf16[512,256]{1,0:T(8,128)(2,1)} %bitcast.28, ...), custom_call_target="tpu_custom_call" | custom-call | flops 1 | bytes 1 | tf_op jit(solution)/shard_map/prepare/pallas_call | solution.py:164
  20.5 4.3 %collective-permute-done.3.refs_2_ = bf16[32,2048]{1,0:T(8,128)(2,1)S(1)} collective-permute-done((bf16[32,2048]{1,0:T(8,128)(2,1)}, bf16[32,2048]{1,0:T(8,128)(2,1)S(1)}, u32[]{:S(2)}, u32[]{:S(2)}) %collective-permute-start.3) | collective-permute-done | bytes 131104 | tf_op jit(solution)/shard_map/ppermute | solution.py:508
  35.9 6.4 %attend.3.refs_1_.refs_0_ = bf16[256,256]{1,0:T(8,128)(2,1)S(1)} custom-call(s32[20]{0:T(128)S(1)} %copy-done.3, bf16[512,256]{1,0:T(8,128)(2,1)S(1)} %copy-done.6, bf16[1552,256]{1,0:T(8,128)(2,1)S(1)} %copy-done.5, bf16[1552,256]{1,0:T(8,128)(2,1)S(1)} %collective-permute-done.refs_1_, bf16[1552,256]{1,0:T(8,128)(2,1)S(1)} %gate.11.refs_2_, ...), custom_call_target="tpu_custom_call" | custom-call | flops 6442450944 | bytes 1 | tf_op jit(solution)/shard_map/attend/pallas_call | solution.py:164
  46.3 4.6 %collective-permute-start.17 = (bf16[256,256]{1,0:T(8,128)(2,1)S(1)}, bf16[256,256]{1,0:T(8,128)(2,1)S(1)}, u32[]{:S(2)}, u32[]{:S(2)}) collective-permute-start(bf16[256,256]{1,0:T(8,128)(2,1)S(1)} %attend.3.refs_1_.refs_0_), channel_id=1, source_target_pairs={{0,4},{4,8},{8,12},{1,5},{5,9},{9,13},{2,6},{6,10},{10,14},{3,7},{... | collective-permute-start | bytes 393224 | tf_op jit(solution)/shard_map/ppermute | solution.py:103
  53.5 6.4 %attend.2.refs_5_.refs_0_ = bf16[256,256]{1,0:T(8,128)(2,1)S(1)} custom-call(s32[20]{0:T(128)S(1)} %copy-done.3, bf16[512,256]{1,0:T(8,128)(2,1)S(1)} %copy-done.6, bf16[1552,256]{1,0:T(8,128)(2,1)S(1)} %copy-done.5, bf16[1552,256]{1,0:T(8,128)(2,1)S(1)} %collective-permute-done.refs_1_, bf16[1552,256]{1,0:T(8,128)(2,1)S(1)} %gate.11.refs_2_, ...), custom_call_target="tpu_custom_call" | custom-call | flops 6442450944 | bytes 1 | tf_op jit(solution)/shard_map/attend/pallas_call | solution.py:164
  60.5 4.7 %collective-permute-done.16.refs_0_ = bf16[4,32,2048]{2,1,0:T(8,128)(2,1)S(1)} collective-permute-done((bf16[4,32,2048]{2,1,0:T(8,128)(2,1)S(1)}, bf16[4,32,2048]{2,1,0:T(8,128)(2,1)S(1)}, u32[]{:S(2)}, u32[]{:S(2)}) %collective-permute-start.16) | collective-permute-done | bytes 524320 | tf_op jit(solution)/shard_map/ppermute | solution.py:77
  77.2 5.2 %collective-permute-start.21 = (bf16[128,2048]{1,0:T(8,128)(2,1)S(1)}, bf16[128,2048]{1,0:T(8,128)(2,1)S(1)}, u32[]{:S(2)}, u32[]{:S(2)}) collective-permute-start(bf16[128,2048]{1,0:T(8,128)(2,1)S(1)} %get-tuple-element.29.refs_0_), channel_id=1, source_target_pairs={{0,4},{4,8},{8,12},{1,5},{5,9},{9,13},{2,6},{6,10},{10,14},{3,7},{... | collective-permute-start | bytes 1572872 | tf_op jit(solution)/shard_map/ppermute | solution.py:103
  82.4 21.8 %collective-permute-done.8.refs_3_.refs_4_ = bf16[256,256]{1,0:T(8,128)(2,1)S(1)} collective-permute-done((bf16[256,256]{1,0:T(8,128)(2,1)S(1)}, bf16[256,256]{1,0:T(8,128)(2,1)S(1)}, u32[]{:S(2)}, u32[]{:S(2)}) %collective-permute-start.8) | collective-permute-done | bytes 131104 | tf_op jit(solution)/shard_map/ppermute | solution.py:108
  108.0 4.4 %collective-permute-done.9.refs_4_.refs_5_ = bf16[256,256]{1,0:T(8,128)(2,1)S(1)} collective-permute-done((bf16[256,256]{1,0:T(8,128)(2,1)S(1)}, bf16[256,256]{1,0:T(8,128)(2,1)S(1)}, u32[]{:S(2)}, u32[]{:S(2)}) %collective-permute-start.9) | collective-permute-done | bytes 131104 | tf_op jit(solution)/shard_map/ppermute | solution.py:109
  112.9 5.8 %collective-permute-start.29 = (bf16[128,2048]{1,0:T(8,128)(2,1)S(1)}, bf16[128,2048]{1,0:T(8,128)(2,1)S(1)}, u32[]{:S(2)}, u32[]{:S(2)}) collective-permute-start(bf16[128,2048]{1,0:T(8,128)(2,1)S(1)} %gate.18), channel_id=1, source_target_pairs={{0,8},{4,12},{8,0},{12,4},{1,9},{5,13},{9,1},{13,5},{2,10},{6,14},... | collective-permute-start | bytes 1572872 | tf_op jit(solution)/shard_map/ppermute | solution.py:108
  121.9 5.4 %collective-permute-start.23 = (bf16[128,2048]{1,0:T(8,128)(2,1)S(1)}, bf16[128,2048]{1,0:T(8,128)(2,1)S(1)}, u32[]{:S(2)}, u32[]{:S(2)}) collective-permute-start(bf16[128,2048]{1,0:T(8,128)(2,1)S(1)} %gate.16.refs_0_), channel_id=1, source_target_pairs={{0,4},{4,8},{8,12},{1,5},{5,9},{9,13},{2,6},{6,10},{10,14},{3,7},{... | collective-permute-start | bytes 1572872 | tf_op jit(solution)/shard_map/ppermute | solution.py:103
  127.3 3.4 %project.3 = (bf16[160,2048]{1,0:T(8,128)(2,1)S(1)}, bf16[96,2048]{1,0:T(8,128)(2,1)S(1)}, bf16[160,2048]{1,0:T(8,128)(2,1)S(1)}, bf16[96,2048]{1,0:T(8,128)(2,1)S(1)}, bf16[512,2048]{1,0:T(8,128)(2,1)}) custom-call(s32[20]{0:T(128)S(1)} %copy-done.3, bf16[256,256]{1,0:T(8,128)(2,1)S(1)} %attend.2.refs_5_.refs_0_, ...), custom_call_target="tpu_custom_call", output_to_operand_aliasing={{4}: (15, {})} | custom-call | flops 1 | bytes 1 | tf_op jit(solution)/shard_map/project/pallas_call | solution.py:164
  130.7 11.5 %collective-permute-done.29.refs_1_.refs_3_ = bf16[128,2048]{1,0:T(8,128)(2,1)S(1)} collective-permute-done((bf16[128,2048]{1,0:T(8,128)(2,1)S(1)}, bf16[128,2048]{1,0:T(8,128)(2,1)S(1)}, u32[]{:S(2)}, u32[]{:S(2)}) %collective-permute-start.29) | collective-permute-done | bytes 524320 | tf_op jit(solution)/shard_map/ppermute | solution.py:108
  142.8 3.7 %collective-permute-done.26.refs_3_.refs_4_ = bf16[128,2048]{1,0:T(8,128)(2,1)S(1)} collective-permute-done((bf16[128,2048]{1,0:T(8,128)(2,1)S(1)}, bf16[128,2048]{1,0:T(8,128)(2,1)S(1)}, u32[]{:S(2)}, u32[]{:S(2)}) %collective-permute-start.26) | collective-permute-done | bytes 524320 | tf_op jit(solution)/shard_map/ppermute | solution.py:109
  146.4 9.7 %collective-permute-done.24.refs_2_ = bf16[128,2048]{1,0:T(8,128)(2,1)S(1)} collective-permute-done((bf16[128,2048]{1,0:T(8,128)(2,1)S(1)}, bf16[128,2048]{1,0:T(8,128)(2,1)S(1)}, u32[]{:S(2)}, u32[]{:S(2)}) %collective-permute-start.24) | collective-permute-done | bytes 524320 | tf_op jit(solution)/shard_map/ppermute | solution.py:104
  158.0 14.4 %collective-permute-start.27 = (bf16[160,2048]{1,0:T(8,128)(2,1)S(1)}, bf16[160,2048]{1,0:T(8,128)(2,1)S(1)}, u32[]{:S(2)}, u32[]{:S(2)}) collective-permute-start(bf16[160,2048]{1,0:T(8,128)(2,1)S(1)} %gate.17.refs_0_), channel_id=1, source_target_pairs={{0,4},{4,8},{8,12},{1,5},{5,9},{9,13},{2,6},{6,10},{10,14},{3,7},{... | collective-permute-start | bytes 1966088 | tf_op jit(solution)/shard_map/ppermute | solution.py:103
  173.7 7.8 %collective-permute-done.33.refs_1_.refs_3_ = bf16[160,2048]{1,0:T(8,128)(2,1)S(1)} collective-permute-done((bf16[160,2048]{1,0:T(8,128)(2,1)S(1)}, bf16[160,2048]{1,0:T(8,128)(2,1)S(1)}, u32[]{:S(2)}, u32[]{:S(2)}) %collective-permute-start.33) | collective-permute-done | bytes 655392 | tf_op jit(solution)/shard_map/ppermute | solution.py:108
  183.4 31.6 %collective-permute-done.30.refs_3_.refs_4_ = bf16[128,2048]{1,0:T(8,128)(2,1)S(1)} collective-permute-done((bf16[128,2048]{1,0:T(8,128)(2,1)S(1)}, bf16[128,2048]{1,0:T(8,128)(2,1)S(1)}, u32[]{:S(2)}, u32[]{:S(2)}) %collective-permute-start.30) | collective-permute-done | bytes 524320 | tf_op jit(solution)/shard_map/ppermute | solution.py:109
  216.8 4.6 %collective-permute-start.31 = (bf16[96,2048]{1,0:T(8,128)(2,1)S(1)}, bf16[96,2048]{1,0:T(8,128)(2,1)S(1)}, u32[]{:S(2)}, u32[]{:S(2)}) collective-permute-start(bf16[96,2048]{1,0:T(8,128)(2,1)S(1)} %gate.19.refs_0_), channel_id=1, source_target_pairs={{0,4},{4,8},{8,12},{1,5},{5,9},{9,13},{2,6},{6,10},{10,14},{3,7},{... | collective-permute-start | bytes 1179656 | tf_op jit(solution)/shard_map/ppermute | solution.py:103
  222.7 3.3 %norm.4.refs_5_ = bf16[512,8192]{1,0:T(8,128)(2,1)} custom-call(s32[20]{0:T(128)S(1)} %copy-done.3, f32[1,8192]{1,0:T(1,128)S(1)} %bitcast.23, bf16[128,2048]{1,0:T(8,128)(2,1)S(1)} %get-tuple-element.29.refs_0_, bf16[128,2048]{1,0:T(8,128)(2,1)S(1)} %collective-permute-done.21.refs_1_, bf16[128,2048]{1,0:T(8,128)(2,1)S(1)} %collective-permute-done.22.refs_2_, ...), custom_call_target="tpu_custom_call" | custom-call | flops 1 | bytes 1 | tf_op jit(solution)/shard_map/norm/pallas_call | solution.py:164
  226.0 3.3 %norm.5.refs_5_ = bf16[512,8192]{1,0:T(8,128)(2,1)} custom-call(s32[20]{0:T(128)S(1)} %copy-done.3, f32[1,8192]{1,0:T(1,128)S(1)} %bitcast.24, bf16[128,2048]{1,0:T(8,128)(2,1)S(1)} %gate.16.refs_0_, bf16[128,2048]{1,0:T(8,128)(2,1)S(1)} %collective-permute-done.23.refs_1_, ...), custom_call_target="tpu_custom_call", output_to_operand_aliasing={{}: (7, {})} | custom-call | flops 1 | bytes 1 | tf_op jit(solution)/shard_map/norm/pallas_call | solution.py:164
  229.2 4.0 %norm.6.refs_5_ = bf16[512,8192]{1,0:T(8,128)(2,1)} custom-call(s32[20]{0:T(128)S(1)} %copy-done.3, f32[1,8192]{1,0:T(1,128)S(1)} %bitcast.25, bf16[160,2048]{1,0:T(8,128)(2,1)S(1)} %gate.17.refs_0_, bf16[160,2048]{1,0:T(8,128)(2,1)S(1)} %collective-permute-done.27.refs_1_, ...), custom_call_target="tpu_custom_call", output_to_operand_aliasing={{}: (7, {})} | custom-call | flops 1 | bytes 1 | tf_op jit(solution)/shard_map/norm/pallas_call | solution.py:164
  233.3 4.2 %collective-permute-done.32.refs_2_ = bf16[96,2048]{1,0:T(8,128)(2,1)S(1)} collective-permute-done((bf16[96,2048]{1,0:T(8,128)(2,1)S(1)}, bf16[96,2048]{1,0:T(8,128)(2,1)S(1)}, u32[]{:S(2)}, u32[]{:S(2)}) %collective-permute-start.32) | collective-permute-done | bytes 393248 | tf_op jit(solution)/shard_map/ppermute | solution.py:104
  237.5 8.3 %collective-permute-done.35.refs_4_ = bf16[96,2048]{1,0:T(8,128)(2,1)S(1)} collective-permute-done((bf16[96,2048]{1,0:T(8,128)(2,1)S(1)}, bf16[96,2048]{1,0:T(8,128)(2,1)S(1)}, u32[]{:S(2)}, u32[]{:S(2)}) %collective-permute-start.35) | collective-permute-done | bytes 393248 | tf_op jit(solution)/shard_map/ppermute | solution.py:109
  (90 shorter events, 63.4 us)
Async XLA Ops:
  8.9 20.9 %collective-permute-start.1 = (bf16[1552,256]{1,0:T(8,128)(2,1)}, bf16[1552,256]{1,0:T(8,128)(2,1)S(1)}, u32[]{:S(2)}, u32[]{:S(2)}) collective-permute-start(bf16[1552,256]{1,0:T(8,128)(2,1)} %get-tuple-element.19.refs_0_), channel_id=1, source_target_pairs={{0,2},{1,3},{2,0},{3,1},{4,6},{5,7},{6,4},{7,5},{8,10},{9,11},{10,... | collective-permute-start | bytes 2383880 | tf_op jit(solution)/shard_map/ppermute | solution.py:42
  17.5 16.4 %collective-permute-start = (bf16[1552,256]{1,0:T(8,128)(2,1)}, bf16[1552,256]{1,0:T(8,128)(2,1)S(1)}, u32[]{:S(2)}, u32[]{:S(2)}) collective-permute-start(bf16[1552,256]{1,0:T(8,128)(2,1)} %get-tuple-element.19.refs_0_), channel_id=1, source_target_pairs={{0,1},{1,0},{2,3},{3,2},{4,5},{5,4},{6,7},{7,6},{8,9},{9,8},{10,11... | collective-permute-start | bytes 2383880 | tf_op jit(solution)/shard_map/ppermute | solution.py:42
  30.5 15.8 %collective-permute-start.12 = (bf16[4,32,2048]{2,1,0:T(8,128)(2,1)S(1)}, bf16[4,32,2048]{2,1,0:T(8,128)(2,1)S(1)}, u32[]{:S(2)}, u32[]{:S(2)}) collective-permute-start(bf16[4,32,2048]{2,1,0:T(8,128)(2,1)S(1)} %stack.89.refs_1_.refs_5_), channel_id=1, source_target_pairs={{0,16},{16,0},{1,17},{17,1},{2,18},{18,2},{3,19},{19,3},{4,20},{20... | collective-permute-start | bytes 1572872 | tf_op jit(solution)/shard_map/ppermute | solution.py:77
  32.3 18.5 %collective-permute-start.11 = (bf16[4,32,2048]{2,1,0:T(8,128)(2,1)S(1)}, bf16[4,32,2048]{2,1,0:T(8,128)(2,1)S(1)}, u32[]{:S(2)}, u32[]{:S(2)}) collective-permute-start(bf16[4,32,2048]{2,1,0:T(8,128)(2,1)S(1)} %stack.89.refs_1_.refs_5_), channel_id=1, source_target_pairs={{0,2},{1,3},{2,0},{3,1},{4,6},{5,7},{6,4},{7,5},{8,10},{9,11},{10,... | collective-permute-start | bytes 1572872 | tf_op jit(solution)/shard_map/ppermute | solution.py:77
  45.0 22.0 %collective-permute-start.10 = (bf16[4,32,2048]{2,1,0:T(8,128)(2,1)S(1)}, bf16[4,32,2048]{2,1,0:T(8,128)(2,1)S(1)}, u32[]{:S(2)}, u32[]{:S(2)}) collective-permute-start(bf16[4,32,2048]{2,1,0:T(8,128)(2,1)S(1)} %stack.89.refs_1_.refs_5_), channel_id=1, source_target_pairs={{0,1},{1,0},{2,3},{3,2},{4,5},{5,4},{6,7},{7,6},{8,9},{9,8},{10,11... | collective-permute-start | bytes 1572872 | tf_op jit(solution)/shard_map/ppermute | solution.py:86
  45.0 15.4 %collective-permute-start.18 = (bf16[256,256]{1,0:T(8,128)(2,1)S(1)}, bf16[256,256]{1,0:T(8,128)(2,1)S(1)}, u32[]{:S(2)}, u32[]{:S(2)}) collective-permute-start(bf16[256,256]{1,0:T(8,128)(2,1)S(1)} %attend.3.refs_1_.refs_0_), channel_id=1, source_target_pairs={{4,0},{8,4},{12,8},{5,1},{9,5},{13,9},{6,2},{10,6},{14,10},{7,3},{... | collective-permute-start | bytes 393224 | tf_op jit(solution)/shard_map/ppermute | solution.py:104
  71.7 40.7 %collective-permute-start.25 = (bf16[128,2048]{1,0:T(8,128)(2,1)S(1)}, bf16[128,2048]{1,0:T(8,128)(2,1)S(1)}, u32[]{:S(2)}, u32[]{:S(2)}) collective-permute-start(bf16[128,2048]{1,0:T(8,128)(2,1)S(1)} %get-tuple-element.30), channel_id=1, source_target_pairs={{0,8},{4,12},{8,0},{12,4},{1,9},{5,13},{9,1},{13,5},{2,10},{6,14},... | collective-permute-start | bytes 1572872 | tf_op jit(solution)/shard_map/ppermute | solution.py:108
  73.0 31.2 %collective-permute-start.8 = (bf16[256,256]{1,0:T(8,128)(2,1)S(1)}, bf16[256,256]{1,0:T(8,128)(2,1)S(1)}, u32[]{:S(2)}, u32[]{:S(2)}) collective-permute-start(bf16[256,256]{1,0:T(8,128)(2,1)S(1)} %attend.2.refs_5_.refs_0_), channel_id=1, source_target_pairs={{0,8},{4,12},{8,0},{12,4},{1,9},{5,13},{9,1},{13,5},{2,10},{6,14},... | collective-permute-start | bytes 393224 | tf_op jit(solution)/shard_map/ppermute | solution.py:108
  74.6 30.9 %collective-permute-start.7 = (bf16[256,256]{1,0:T(8,128)(2,1)S(1)}, bf16[256,256]{1,0:T(8,128)(2,1)S(1)}, u32[]{:S(2)}, u32[]{:S(2)}) collective-permute-start(bf16[256,256]{1,0:T(8,128)(2,1)S(1)} %attend.2.refs_5_.refs_0_), channel_id=1, source_target_pairs={{4,0},{8,4},{12,8},{5,1},{9,5},{13,9},{6,2},{10,6},{14,10},{7,3},{... | collective-permute-start | bytes 393224 | tf_op jit(solution)/shard_map/ppermute | solution.py:104
  75.9 44.1 %collective-permute-start.22 = (bf16[128,2048]{1,0:T(8,128)(2,1)S(1)}, bf16[128,2048]{1,0:T(8,128)(2,1)S(1)}, u32[]{:S(2)}, u32[]{:S(2)}) collective-permute-start(bf16[128,2048]{1,0:T(8,128)(2,1)S(1)} %get-tuple-element.29.refs_0_), channel_id=1, source_target_pairs={{4,0},{8,4},{12,8},{5,1},{9,5},{13,9},{6,2},{10,6},{14,10},{7,3},{... | collective-permute-start | bytes 1572872 | tf_op jit(solution)/shard_map/ppermute | solution.py:104
  77.2 42.8 %collective-permute-start.21 = (bf16[128,2048]{1,0:T(8,128)(2,1)S(1)}, bf16[128,2048]{1,0:T(8,128)(2,1)S(1)}, u32[]{:S(2)}, u32[]{:S(2)}) collective-permute-start(bf16[128,2048]{1,0:T(8,128)(2,1)S(1)} %get-tuple-element.29.refs_0_), channel_id=1, source_target_pairs={{0,4},{4,8},{8,12},{1,5},{5,9},{9,13},{2,6},{6,10},{10,14},{3,7},{... | collective-permute-start | bytes 1572872 | tf_op jit(solution)/shard_map/ppermute | solution.py:103
  112.9 29.2 %collective-permute-start.29 = (bf16[128,2048]{1,0:T(8,128)(2,1)S(1)}, bf16[128,2048]{1,0:T(8,128)(2,1)S(1)}, u32[]{:S(2)}, u32[]{:S(2)}) collective-permute-start(bf16[128,2048]{1,0:T(8,128)(2,1)S(1)} %gate.18), channel_id=1, source_target_pairs={{0,8},{4,12},{8,0},{12,4},{1,9},{5,13},{9,1},{13,5},{2,10},{6,14},... | collective-permute-start | bytes 1572872 | tf_op jit(solution)/shard_map/ppermute | solution.py:108
  118.7 27.7 %collective-permute-start.26 = (bf16[128,2048]{1,0:T(8,128)(2,1)S(1)}, bf16[128,2048]{1,0:T(8,128)(2,1)S(1)}, u32[]{:S(2)}, u32[]{:S(2)}) collective-permute-start(bf16[128,2048]{1,0:T(8,128)(2,1)S(1)} %collective-permute-done.25.refs_1_.refs_3_), channel_id=1, source_target_pairs={{4,0},{8,12},{5,1},{9,13},{6,2},{10,14},{7,3},{11,15},{20,16},{24,... | collective-permute-start | bytes 1572872 | tf_op jit(solution)/shard_map/ppermute | solution.py:109
  120.6 35.6 %collective-permute-start.24 = (bf16[128,2048]{1,0:T(8,128)(2,1)S(1)}, bf16[128,2048]{1,0:T(8,128)(2,1)S(1)}, u32[]{:S(2)}, u32[]{:S(2)}) collective-permute-start(bf16[128,2048]{1,0:T(8,128)(2,1)S(1)} %gate.16.refs_0_), channel_id=1, source_target_pairs={{4,0},{8,4},{12,8},{5,1},{9,5},{13,9},{6,2},{10,6},{14,10},{7,3},{... | collective-permute-start | bytes 1572872 | tf_op jit(solution)/shard_map/ppermute | solution.py:104
  121.9 34.3 %collective-permute-start.23 = (bf16[128,2048]{1,0:T(8,128)(2,1)S(1)}, bf16[128,2048]{1,0:T(8,128)(2,1)S(1)}, u32[]{:S(2)}, u32[]{:S(2)}) collective-permute-start(bf16[128,2048]{1,0:T(8,128)(2,1)S(1)} %gate.16.refs_0_), channel_id=1, source_target_pairs={{0,4},{4,8},{8,12},{1,5},{5,9},{9,13},{2,6},{6,10},{10,14},{3,7},{... | collective-permute-start | bytes 1572872 | tf_op jit(solution)/shard_map/ppermute | solution.py:103
  142.7 38.8 %collective-permute-start.33 = (bf16[160,2048]{1,0:T(8,128)(2,1)S(1)}, bf16[160,2048]{1,0:T(8,128)(2,1)S(1)}, u32[]{:S(2)}, u32[]{:S(2)}) collective-permute-start(bf16[160,2048]{1,0:T(8,128)(2,1)S(1)} %gate.20), channel_id=1, source_target_pairs={{0,8},{4,12},{8,0},{12,4},{1,9},{5,13},{9,1},{13,5},{2,10},{6,14},... | collective-permute-start | bytes 1966088 | tf_op jit(solution)/shard_map/ppermute | solution.py:108
  156.7 58.3 %collective-permute-start.28 = (bf16[160,2048]{1,0:T(8,128)(2,1)S(1)}, bf16[160,2048]{1,0:T(8,128)(2,1)S(1)}, u32[]{:S(2)}, u32[]{:S(2)}) collective-permute-start(bf16[160,2048]{1,0:T(8,128)(2,1)S(1)} %gate.17.refs_0_), channel_id=1, source_target_pairs={{4,0},{8,4},{12,8},{5,1},{9,5},{13,9},{6,2},{10,6},{14,10},{7,3},{... | collective-permute-start | bytes 1966088 | tf_op jit(solution)/shard_map/ppermute | solution.py:104
  158.0 57.0 %collective-permute-start.27 = (bf16[160,2048]{1,0:T(8,128)(2,1)S(1)}, bf16[160,2048]{1,0:T(8,128)(2,1)S(1)}, u32[]{:S(2)}, u32[]{:S(2)}) collective-permute-start(bf16[160,2048]{1,0:T(8,128)(2,1)S(1)} %gate.17.refs_0_), channel_id=1, source_target_pairs={{0,4},{4,8},{8,12},{1,5},{5,9},{9,13},{2,6},{6,10},{10,14},{3,7},{... | collective-permute-start | bytes 1966088 | tf_op jit(solution)/shard_map/ppermute | solution.py:103
  172.4 42.6 %collective-permute-start.30 = (bf16[128,2048]{1,0:T(8,128)(2,1)S(1)}, bf16[128,2048]{1,0:T(8,128)(2,1)S(1)}, u32[]{:S(2)}, u32[]{:S(2)}) collective-permute-start(bf16[128,2048]{1,0:T(8,128)(2,1)S(1)} %collective-permute-done.29.refs_1_.refs_3_), channel_id=1, source_target_pairs={{4,0},{8,12},{5,1},{9,13},{6,2},{10,14},{7,3},{11,15},{20,16},{24,... | collective-permute-start | bytes 1572872 | tf_op jit(solution)/shard_map/ppermute | solution.py:109
  182.0 39.4 %collective-permute-start.34 = (bf16[96,2048]{1,0:T(8,128)(2,1)S(1)}, bf16[96,2048]{1,0:T(8,128)(2,1)S(1)}, u32[]{:S(2)}, u32[]{:S(2)}) collective-permute-start(bf16[96,2048]{1,0:T(8,128)(2,1)S(1)} %gate.21), channel_id=1, source_target_pairs={{0,8},{4,12},{8,0},{12,4},{1,9},{5,13},{9,1},{13,5},{2,10},{6,14},... | collective-permute-start | bytes 1179656 | tf_op jit(solution)/shard_map/ppermute | solution.py:108
  182.1 47.1 %collective-permute-start.36 = (bf16[160,2048]{1,0:T(8,128)(2,1)S(1)}, bf16[160,2048]{1,0:T(8,128)(2,1)S(1)}, u32[]{:S(2)}, u32[]{:S(2)}) collective-permute-start(bf16[160,2048]{1,0:T(8,128)(2,1)S(1)} %collective-permute-done.33.refs_1_.refs_3_), channel_id=1, source_target_pairs={{4,0},{8,12},{5,1},{9,13},{6,2},{10,14},{7,3},{11,15},{20,16},{24,... | collective-permute-start | bytes 1966088 | tf_op jit(solution)/shard_map/ppermute | solution.py:109
  215.5 21.9 %collective-permute-start.32 = (bf16[96,2048]{1,0:T(8,128)(2,1)S(1)}, bf16[96,2048]{1,0:T(8,128)(2,1)S(1)}, u32[]{:S(2)}, u32[]{:S(2)}) collective-permute-start(bf16[96,2048]{1,0:T(8,128)(2,1)S(1)} %gate.19.refs_0_), channel_id=1, source_target_pairs={{4,0},{8,4},{12,8},{5,1},{9,5},{13,9},{6,2},{10,6},{14,10},{7,3},{... | collective-permute-start | bytes 1179656 | tf_op jit(solution)/shard_map/ppermute | solution.py:104
  216.8 20.6 %collective-permute-start.31 = (bf16[96,2048]{1,0:T(8,128)(2,1)S(1)}, bf16[96,2048]{1,0:T(8,128)(2,1)S(1)}, u32[]{:S(2)}, u32[]{:S(2)}) collective-permute-start(bf16[96,2048]{1,0:T(8,128)(2,1)S(1)} %gate.19.refs_0_), channel_id=1, source_target_pairs={{0,4},{4,8},{8,12},{1,5},{5,9},{9,13},{2,6},{6,10},{10,14},{3,7},{... | collective-permute-start | bytes 1179656 | tf_op jit(solution)/shard_map/ppermute | solution.py:103
  221.4 24.4 %collective-permute-start.35 = (bf16[96,2048]{1,0:T(8,128)(2,1)S(1)}, bf16[96,2048]{1,0:T(8,128)(2,1)S(1)}, u32[]{:S(2)}, u32[]{:S(2)}) collective-permute-start(bf16[96,2048]{1,0:T(8,128)(2,1)S(1)} %collective-permute-done.34.refs_3_), channel_id=1, source_target_pairs={{4,0},{8,12},{5,1},{9,13},{6,2},{10,14},{7,3},{11,15},{20,16},{24,... | collective-permute-start | bytes 1179656 | tf_op jit(solution)/shard_map/ppermute | solution.py:109
  (20 other events, 244.9 us)

commit v12 on v11

--- a/solution.py
+++ b/solution.py
@@ -16,6 +16,7 @@
 CHUNK = 128
 KEY_BLOCK = 512
 ATTEND_FLOPS = 16
+RAW_PART = 8
 TAIL = 16
 DIGIT = 32
 ANYWHERE = pl.BlockSpec(memory_space=pl.ANY)
@@ -109,7 +110,7 @@
     return far, lax.ppermute(far, "tensor", [(1, 0), (2, 3)])
 
 
-def chunk_gathers(info, values, copies, second, count):
+def chunk_gathers(info, values, copies, second, made, count):
     if count != 4:
         return [line_gather(value, count) for value in values]
     fars, lines = [], []
@@ -119,9 +120,9 @@
             after += second
         fars.append(line_far(gate(info, value, after) if after else value))
     for number, value in enumerate(copies):
-        after = list(lines[number - 1][1:3]) if number else []
-        if number > 1:
-            after.append(fars[number - 2][1])
+        after = [*lines[number - 1][1:3], fars[number - 1][1]] if number else []
+        if number == len(copies) // 2:
+            after += made
         value = gate(info, value, after) if after else value
         lines.append([value, *line_near(value), *fars[number]])
     return lines
@@ -183,9 +184,9 @@
     return pl.BlockSpec(tuple(a.shape), lambda i, info: zeros)
 
 
-def prepare_kernel(table, slab, info, q_hbm, kv_hbm, cache_hbm, w_hbm, cos_ref, sin_ref,
+def prepare_kernel(table, slab, keep, info, q_hbm, kv_hbm, cache_hbm, w_hbm, cos_ref, sin_ref,
                    length_ref, *refs):
-    count = table.count
+    count, raw = table.count, slab - keep
     q_out, kv_out, outs = refs[0], refs[1], refs[2 : 2 + count]
     q_ref, kv_ref, w_ref, sems = refs[2 + count :]
     slots, rows, part = cache_hbm.shape[0], q_ref.shape[0], w_ref.shape[0]
@@ -204,7 +205,11 @@
     copies[0].wait()
     for d, out in enumerate(outs):
         target = lax.rem(info[table.place] + d, count)
-        out[...] = w_ref[:, pl.ds(pl.multiple_of(target * slab, slab), slab)]
+        out[:, :keep] = w_ref[:, pl.ds(pl.multiple_of(target * slab, slab), keep)]
+        for j in range(count if raw else 0):
+            out[:, keep + j * raw : keep + (j + 1) * raw] = w_ref[
+                :, j * slab + keep : (j + 1) * slab
+            ]
 
     cosine, sine = cos_ref[...], sin_ref[...]
 
@@ -228,15 +233,16 @@
 
 
 def prepare(table, info, queries, span_pairs, cache, out_weight, cosine, sine, lengths, part,
-            slab):
+            slab, keep):
     rows = queries.shape[0]
     shapes = [
         jax.ShapeDtypeStruct(queries.shape, jnp.bfloat16),
         jax.ShapeDtypeStruct((cache.shape[0] + rows + TAIL, 2 * HD), jnp.bfloat16),
     ]
-    shapes += [jax.ShapeDtypeStruct((part, slab), out_weight.dtype)] * table.count
-    return call(
-        functools.partial(prepare_kernel, table, slab),
+    width = keep + table.count * (slab - keep)
+    shapes += [jax.ShapeDtypeStruct((part, width), out_weight.dtype)] * table.count
+    return call(
+        functools.partial(prepare_kernel, table, slab, keep),
         "prepare",
         info,
         [queries, span_pairs, cache, out_weight, cosine, sine, lengths],
@@ -251,6 +257,25 @@
             pltpu.SemaphoreType.DMA((4,)),
         ],
         vmem=0,
+    )
+
+
+def last_columns_kernel(info, *refs):
+    refs[-1][...] = refs[0][...]
+
+
+def last_columns(info, value, width, after):
+    rows, full = value.shape
+    shape = jax.ShapeDtypeStruct((rows, width), value.dtype)
+    return call(
+        last_columns_kernel,
+        "last_columns",
+        info,
+        [value, *after],
+        [pl.BlockSpec((rows, width), lambda i, info: (0, full // width - 1))]
+        + [ANYWHERE] * len(after),
+        whole(shape),
+        shape,
     )
 
 
@@ -377,32 +402,32 @@
     attention, pieces = refs[:lines], refs[lines : lines + shares]
     r_ref = refs[lines + shares]
     parts, h_ref, w_ref = refs[-2 - 2 * len(splits) : -2], refs[-2], refs[-1]
-    share_rows = pieces[0].shape[1]
+    share_rows, keep = pieces[0].shape[1], w_ref.shape[2]
     for number, piece in enumerate(pieces):
         start = pl.multiple_of(info[table.rows + number] * share_rows, share_rows)
         for d in range(count):
-            w_ref[d, pl.ds(start, share_rows)] = piece[d]
+            w_ref[d, pl.ds(start, share_rows)] = piece[d, :, :keep]
     blocks = [
         line_read(table, info, attention, d).astype(jnp.bfloat16) for d in range(count)
     ]
     for part, copy, (begin, size) in zip(parts, parts[len(splits) :], splits):
         rows = slice(begin, begin + size)
-        total = r_ref[rows].astype(jnp.float32)
+        total = r_ref[rows, :keep].astype(jnp.float32)
         for d in range(count):
             total = total + jnp.dot(
                 blocks[d][rows], w_ref[d], preferred_element_type=jnp.float32
             )
         result = total.astype(jnp.bfloat16)
-        h_ref[rows] = result
+        h_ref[rows, :keep] = result
         part[...] = result
         copy[...] = result
 
 
-def project(table, info, attention, pieces, residual, hidden, half, halves, splits):
+def project(table, info, attention, pieces, residual, hidden, keep, half, halves, splits):
     all_rows, slab = residual.shape
     rows = all_rows // halves
     count, share_rows, _ = pieces[0].shape
-    parts = [jax.ShapeDtypeStruct((size, slab), jnp.bfloat16) for _, size in splits * 2]
+    parts = [jax.ShapeDtypeStruct((size, keep), jnp.bfloat16) for _, size in splits * 2]
     row_spec = pl.BlockSpec((rows, slab), lambda i, info: (half, 0))
     args = [*attention, *pieces, residual]
     specs = line_spec(attention, rows, lambda i: 0) + [whole(p) for p in pieces] + [row_spec]
@@ -420,47 +445,134 @@
         [whole(part) for part in parts] + [row_spec],
         [*parts, jax.ShapeDtypeStruct(residual.shape, jnp.bfloat16)],
         aliases=aliases,
-        scratch=[pltpu.VMEM((count, len(pieces) * share_rows, slab), jnp.bfloat16)],
+        scratch=[pltpu.VMEM((count, len(pieces) * share_rows, keep), jnp.bfloat16)],
         vmem=36,
     )
 
 
-def norm_kernel(table, lines, info, g_ref, *refs):
+def project_raw_kernel(table, lines, halves, raw_lines, shares, info, *refs):
+    count = table.count
+    attention, refs = refs[: lines * halves], refs[lines * halves :]
+    residuals, pieces = refs[:raw_lines], refs[raw_lines : raw_lines + shares]
+    raw_ref, h_ref, w_ref = refs[-3:]
+    raw, share_rows = h_ref.shape[1], pieces[0].shape[1]
+    keep = pieces[0].shape[2] - w_ref.shape[2]
+    step = pl.program_id(0)
+
+    @pl.when(step == 0)
+    def _():
+        for number, piece in enumerate(pieces):
+            start = pl.multiple_of(info[table.rows + number] * share_rows, share_rows)
+            for d in range(count):
+                w_ref[d, pl.ds(start, share_rows)] = piece[d, :, keep:]
+
+    blocks = []
+    for d in range(count):
+        block = line_read(table, info, attention[:lines], d)
+        if halves == 2:
+            other = line_read(table, info, attention[lines:], d)
+            block = jnp.where(step < pl.num_programs(0) // 2, block, other)
+        blocks.append(block.astype(jnp.bfloat16))
+    for slab in range(count):
+        cols = pl.ds(pl.multiple_of(info[table.place + slab] * raw, raw), raw)
+        total = line_read(table, info, residuals, slab)
+        for d in range(count):
+            total = total + jnp.dot(
+                blocks[d], w_ref[d, :, cols], preferred_element_type=jnp.float32
+            )
+        result = total.astype(jnp.bfloat16)
+        raw_ref[:, slab * raw : (slab + 1) * raw] = result
+        if slab == 0:
+            h_ref[...] = result
+
+
+def project_raw(table, info, attention, residuals, pieces, hidden, raw, rows):
+    all_rows, slab = hidden.shape
+    count, share_rows, _ = pieces[0].shape
+    halves, lines = len(attention), len(attention[0])
+    steps = all_rows // rows
+    args = [*sum(attention, []), *residuals, *pieces, hidden]
+    specs = []
+    for half, blocks in enumerate(attention):
+        first, last = half * (steps // halves), (half + 1) * (steps // halves) - 1
+        specs += line_spec(
+            blocks, rows, lambda i, a=first, b=last: jnp.clip(i, a, b) - a
+        )
+    out = jax.ShapeDtypeStruct((all_rows, count * raw), jnp.bfloat16)
+    return call(
+        functools.partial(
+            project_raw_kernel, table, lines, halves, len(residuals), len(pieces)
+        ),
+        "project_raw",
+        info,
+        args,
+        specs
+        + line_spec(residuals, rows, lambda i: i)
+        + [whole(p) for p in pieces]
+        + [ANYWHERE],
+        [
+            pl.BlockSpec((rows, count * raw), lambda i, info: (i, 0)),
+            pl.BlockSpec((rows, raw), lambda i, info: (i, slab // raw - 1)),
+        ],
+        [out, jax.ShapeDtypeStruct(hidden.shape, jnp.bfloat16)],
+        grid=(steps,),
+        aliases={len(args): 1},
+        scratch=[pltpu.VMEM((count, len(pieces) * share_rows, count * raw), jnp.bfloat16)],
+        vmem=36,
+    )
+
+
+def norm_kernel(table, lines, keep, slab, info, g_ref, *refs):
     count = table.count
     blocks, out_ref = refs[:lines], refs[-1]
-    slab = out_ref.shape[1] // count
+    raw = slab - keep
+    values = []
     squares = jnp.zeros((out_ref.shape[0], 1), jnp.float32)
+
+    def read(d):
+        found = [(0, keep, line_read(table, info, blocks, d))]
+        if raw:
+            cols = slice(d * raw, (d + 1) * raw)
+            found.append((keep, raw, refs[lines][:, cols].astype(jnp.float32)))
+        return found
+
     for d in range(count):
-        value = line_read(table, info, blocks, d)
-        squares = squares + jnp.sum(value * value, axis=1, keepdims=True)
+        for _, _, value in read(d):
+            squares = squares + jnp.sum(value * value, axis=1, keepdims=True)
     inverse = lax.rsqrt(squares / (count * slab) + EPS_NORM)
     for d in range(count):
-        cols = pl.ds(pl.multiple_of(info[table.place + d] * slab, slab), slab)
-        value = line_read(table, info, blocks, d)
-        out_ref[:, cols] = (value * inverse * g_ref[:, cols]).astype(jnp.bfloat16)
-
-
-def norm_into(table, info, buffer, blocks, gain, begin, rows, total_rows):
-    width = gain.shape[0]
+        for offset, width, value in read(d):
+            start = pl.multiple_of(info[table.place + d] * slab + offset, HD)
+            cols = pl.ds(start, width)
+            out_ref[:, cols] = (value * inverse * g_ref[:, cols]).astype(jnp.bfloat16)
+
+
+def norm_into(table, info, buffer, blocks, raw_hidden, gain, begin, rows, keep, slab, total_rows):
+    width = table.count * slab
     step = math.gcd(rows, 32)
-    first = begin // step
+    steps, first = rows // step, begin // step
     args = [gain.reshape(1, width), *blocks]
     in_specs = [pl.BlockSpec((1, width), lambda i, info: (0, 0))]
     in_specs += line_spec(blocks, step, lambda i: i)
+    if raw_hidden is not None:
+        args.append(raw_hidden)
+        in_specs.append(
+            pl.BlockSpec((step, raw_hidden.shape[1]), lambda i, info: (first + i, 0))
+        )
     aliases = {}
     if buffer is not None:
         args.append(buffer)
         in_specs.append(ANYWHERE)
         aliases = {len(args): 0}
     return call(
-        functools.partial(norm_kernel, table, len(blocks)),
+        functools.partial(norm_kernel, table, len(blocks), keep, slab),
         "norm",
         info,
         args,
         in_specs,
         pl.BlockSpec((step, width), lambda i, info: (first + i, 0)),
         jax.ShapeDtypeStruct((total_rows, width), jnp.bfloat16),
-        grid=(rows // step,),
+        grid=(steps,),
         aliases=aliases,
     )
 
@@ -478,12 +590,14 @@
     groups = lax.axis_size("groups")
     shares = groups * contexts
     share = lax.axis_index("groups") * contexts + context_index
+    raw = slab // RAW_PART if slab % (RAW_PART * HD) == 0 else 0
+    keep = slab - raw
     chunk = min(CHUNK, rows)
     halves = 2 if rows % (2 * chunk) == 0 else 1
     half = rows // halves
     splits = [[(0, chunk), (chunk, half - chunk)] if half > chunk else [(0, half)]] * halves
     if halves == 2 and chunk == 128 and half == 256:
-        splits = [splits[0], [(0, 160), (160, 96)]]
+        splits = [splits[0], [(0, 144), (144, 112)]]
 
     table = Table(contexts, count)
     steering = [context_index, *owners_of(contexts, context_index)]
@@ -500,22 +614,26 @@
     sign = jnp.where(jnp.arange(HD) < HD // 2, -1.0, 1.0)
     q_turned, payload, *cuts = prepare(
         table, info, queries, span_local, cache_local, out_weight, jnp.cos(angles),
-        jnp.sin(angles) * sign[None, :], lengths, depth // shares, slab,
+        jnp.sin(angles) * sign[None, :], lengths, depth // shares, slab, keep,
     )
     parts = [cuts[0]]
     for shift in range(1, count):
         pairs = [(i, (i + shift) % count) for i in range(count)]
         parts.append(lax.ppermute(cuts[shift], "tensor", pairs))
     own_weights = stack(info, parts, [])
+    own_raw = [last_columns(info, residual, raw, parts[1:])] if raw else []
     pieces = pieces_of(
-        payload, "context", contexts, lambda block: gate(info, block, [own_weights])
+        payload, "context", contexts, lambda block: gate(info, block, [own_weights, *own_raw])
     )
     slots = cache_local.shape[0]
     mixed = [
         attend(table, info, q_turned, pieces, slots, number * half, half, chunk)
         for number in range(halves)
     ]
-    attention = [line_gather(value, count) for value in mixed]
+    residuals = line_gather(own_raw[0], count) if raw else []
+    ready = [gate(info, mixed[0], residuals[3:4]), *mixed[1:]] if raw else mixed
+    attention = [line_gather(value, count) for value in ready]
+    before = [*attention[0][1:], *mixed[1:], *residuals[1:3], *residuals[4:]]
     weights = plane_gather(
         own_weights,
         groups,
@@ -524,21 +642,35 @@
         lambda block, mask: gate(
             info,
             block,
-            attention[0][3:4] if mask in (mask & -mask,) else [*attention[0][1:], *mixed[1:]],
+            attention[0][3:4] if mask in (mask & -mask,) else before,
         ),
     )
     values, copies, hidden = [], [], None
     for number in range(halves):
         *made, hidden = project(
-            table, info, attention[number], weights, residual, hidden, number, halves,
-            splits[number],
+            table, info, attention[number], weights, residual, hidden, keep, number,
+            halves, splits[number],
         )
         values += made[: len(made) // 2]
         copies += made[len(made) // 2 :]
-    lines = chunk_gathers(info, values, copies, attention[-1][1:], count)
+    raw_hidden = None
+    if raw:
+        raw_hidden, hidden = project_raw(
+            table, info, attention, residuals, weights, hidden, raw, chunk
+        )
+    lines = chunk_gathers(
+        info,
+        values,
+        copies,
+        attention[-1][1:],
+        [raw_hidden] if raw else [],
+        count,
+    )
     normed, begin = None, 0
     for blocks, value in zip(lines, values):
-        normed = norm_into(table, info, normed, blocks, gain, begin, value.shape[0], rows)
+        normed = norm_into(
+            table, info, normed, blocks, raw_hidden, gain, begin, value.shape[0], keep, slab, rows
+        )
         begin += value.shape[0]
     return (hidden, normed)
 

time: 249 us -> 242 us (0.972)
  Pallas kernels: 43.6 us -> 50.8 us
  waiting for transfers between devices: 121 us -> 115 us
  starting transfers between devices: 75.8 us -> 69.9 us
  local copies, waits for them, and re-layouts: 4.36 us -> 1.58 us
    ppermute x6 -> x7, waiting for transfers between devices: 48 us -> 28.8 us  [line_far(): return (far, lax.ppermute(far, 'tensor', [(1, 0), (2, 3)]))]
    ppermute x6 -> x7, waiting for transfers between devices: 41.1 us -> 57.5 us  [line_far(): far = lax.ppermute(value, 'tensor', [(0, 2), (1, 3), (2, 0), (3, 1)])]
    ppermute x6 -> x7, starting transfers between devices: 35.4 us -> 24.4 us  [line_near(): up = lax.ppermute(value, 'tensor', [(0, 1), (1, 2), (2, 3)])]
    pallas_call x21 -> x24, Pallas kernels: 43.6 us -> 50.8 us  [call(): pl.pallas_call(kernel, grid_spec=pltpu.PrefetchScalarGridSpec(num_scalar_...]
    ppermute x3, waiting for transfers between devices: 7.26 us -> 10.4 us  [per_device(): parts.append(lax.ppermute(cuts[shift], 'tensor', pairs))]
    ppermute x3, waiting for transfers between devices: 2.99 us -> 0.01 us  [pieces_of(): held[mask | bit] = lax.ppermute(held[mask], axis, pairs)]
    unnamed x14 -> x12, local copies, waits for them, and re-layouts: 3.67 us -> 0.94 us
    ppermute x3, waiting for transfers between devices: 4.73 us -> 2.17 us  [plane_gather(): held[mask | bit] = lax.ppermute(held[mask], axis, pairs)]
  transfers between devices with their start and end apart: 37 -> 41, of which waited for: 16 -> 16; matrix products, arithmetic and copies ran while one was open for 0% -> 0% of each run, Pallas kernels for 13% -> 16%
where the time goes in v12:
time: 242 us
  waiting for transfers between devices  115 us (48%)
  starting transfers between devices  69.9 us (29%)
  Pallas kernels  50.8 us (21%)
  between operations  2.64 us (1%)
    ppermute x7, waiting for transfers between devices, line_far(): far = lax.ppermute(value, 'tensor', [(0, 2), (1, 3), (2, 0), (3, 1)])  57.5 us
    pallas_call x24, Pallas kernels, call(): pl.pallas_call(kernel, grid_spec=pltpu.PrefetchScalarGridSpec(num_scalar_...  50.8 us
    ppermute x7, waiting for transfers between devices, line_far(): return (far, lax.ppermute(far, 'tensor', [(1, 0), (2, 3)]))  28.8 us
    ppermute x7, starting transfers between devices, line_near(): up = lax.ppermute(value, 'tensor', [(0, 1), (1, 2), (2, 3)])  24.4 us
    ppermute x7, waiting for transfers between devices, line_near(): return (up, lax.ppermute(value, 'tensor', [(1, 0), (2, 1), (3, 2)]))  12.8 us
    ppermute x7, starting transfers between devices, line_far(): far = lax.ppermute(value, 'tensor', [(0, 2), (1, 3), (2, 0), (3, 1)])  12.8 us
    ppermute x3, waiting for transfers between devices, per_device(): parts.append(lax.ppermute(cuts[shift], 'tensor', pairs))  10.4 us
    ppermute x7, starting transfers between devices, line_far(): return (far, lax.ppermute(far, 'tensor', [(1, 0), (2, 3)]))  9.19 us
  transfers between devices with their start and end apart: 41, of which 16 were waited for; matrix products, arithmetic and copies ran while one was open for 0% of the time, Pallas kernels for 16%

profile of v12, /device:TPU:0, one launch (start us, length us, event | category | flops | bytes accessed | tf_op | source)
XLA Modules:
  0.0 241.5 jit_solution(11287890971717913587)
XLA Ops:
  4.7 4.5 %prepare.1 = (bf16[512,256]{1,0:T(8,128)(2,1)}, bf16[1552,256]{1,0:T(8,128)(2,1)}, bf16[32,2816]{1,0:T(8,128)(2,1)}, bf16[32,2816]{1,0:T(8,128)(2,1)}, bf16[32,2...) custom-call(s32[20]{0:T(128)} %stack.86.info, bf16[512,256]{1,0:T(8,128)(2,1)} %q_hbm.1, bf16[512,256]{1,0:T(8,128)(2,1)} %bitcast.28, ...), custom_call_target="tpu_custom_call" | custom-call | flops 1 | bytes 1 | tf_op jit(solution)/shard_map/prepare/pallas_call | solution.py:165
  17.7 4.1 %collective-permute-done.2.refs_1_ = bf16[32,2816]{1,0:T(8,128)(2,1)S(1)} collective-permute-done((bf16[32,2816]{1,0:T(8,128)(2,1)}, bf16[32,2816]{1,0:T(8,128)(2,1)S(1)}, u32[]{:S(2)}, u32[]{:S(2)}) %collective-permute-start.2) | collective-permute-done | bytes 180256 | tf_op jit(solution)/shard_map/ppermute | solution.py:622
  21.8 6.3 %collective-permute-done.3.refs_2_ = bf16[32,2816]{1,0:T(8,128)(2,1)S(1)} collective-permute-done((bf16[32,2816]{1,0:T(8,128)(2,1)}, bf16[32,2816]{1,0:T(8,128)(2,1)S(1)}, u32[]{:S(2)}, u32[]{:S(2)}) %collective-permute-start.3) | collective-permute-done | bytes 180256 | tf_op jit(solution)/shard_map/ppermute | solution.py:622
  36.7 4.2 %collective-permute-start.15 = (bf16[512,256]{1,0:T(8,128)(2,1)S(1)}, bf16[512,256]{1,0:T(8,128)(2,1)S(1)}, u32[]{:S(2)}, u32[]{:S(2)}) collective-permute-start(bf16[512,256]{1,0:T(8,128)(2,1)S(1)} %last_columns.1.refs_2_.refs_10_), channel_id=1, source_target_pairs={{0,4},{4,8},{8,12},{1,5},{5,9},{9,13},{2,6},{6,10},{10,14},{3,7},{... | collective-permute-start | bytes 786440 | tf_op jit(solution)/shard_map/ppermute | solution.py:104
  42.2 6.4 %attend.2.refs_0_.refs_1_ = bf16[256,256]{1,0:T(8,128)(2,1)S(1)} custom-call(s32[20]{0:T(128)S(1)} %copy-done.2, bf16[512,256]{1,0:T(8,128)(2,1)S(1)} %copy-done.5, bf16[1552,256]{1,0:T(8,128)(2,1)S(1)} %copy-done.4, bf16[1552,256]{1,0:T(8,128)(2,1)S(1)} %collective-permute-done.refs_1_, bf16[1552,256]{1,0:T(8,128)(2,1)S(1)} %gate.12.refs_2_, ...), custom_call_target="tpu_custom_call" | custom-call | flops 6442450944 | bytes 1 | tf_op jit(solution)/shard_map/attend/pallas_call | solution.py:165
  57.3 4.6 %collective-permute-start.7 = (bf16[256,256]{1,0:T(8,128)(2,1)S(1)}, bf16[256,256]{1,0:T(8,128)(2,1)S(1)}, u32[]{:S(2)}, u32[]{:S(2)}) collective-permute-start(bf16[256,256]{1,0:T(8,128)(2,1)S(1)} %gate.13.refs_0_), channel_id=1, source_target_pairs={{0,4},{4,8},{8,12},{1,5},{5,9},{9,13},{2,6},{6,10},{10,14},{3,7},{... | collective-permute-start | bytes 393224 | tf_op jit(solution)/shard_map/ppermute | solution.py:104
  64.5 6.4 %attend.3.refs_5_.refs_0_ = bf16[256,256]{1,0:T(8,128)(2,1)S(1)} custom-call(s32[20]{0:T(128)S(1)} %copy-done.2, bf16[512,256]{1,0:T(8,128)(2,1)S(1)} %copy-done.5, bf16[1552,256]{1,0:T(8,128)(2,1)S(1)} %copy-done.4, bf16[1552,256]{1,0:T(8,128)(2,1)S(1)} %collective-permute-done.refs_1_, bf16[1552,256]{1,0:T(8,128)(2,1)S(1)} %gate.12.refs_2_, ...), custom_call_target="tpu_custom_call" | custom-call | flops 6442450944 | bytes 1 | tf_op jit(solution)/shard_map/attend/pallas_call | solution.py:165
  79.8 4.8 %collective-permute-start.27 = (bf16[128,1792]{1,0:T(8,128)(2,1)S(1)}, bf16[128,1792]{1,0:T(8,128)(2,1)S(1)}, u32[]{:S(2)}, u32[]{:S(2)}) collective-permute-start(bf16[128,1792]{1,0:T(8,128)(2,1)S(1)} %get-tuple-element.33), channel_id=1, source_target_pairs={{0,8},{4,12},{8,0},{12,4},{1,9},{5,13},{9,1},{13,5},{2,10},{6,14},... | collective-permute-start | bytes 1376264 | tf_op jit(solution)/shard_map/ppermute | solution.py:109
  88.6 22.3 %collective-permute-done.13.refs_3_.refs_8_.refs_4_ = bf16[256,256]{1,0:T(8,128)(2,1)S(1)} collective-permute-done((bf16[256,256]{1,0:T(8,128)(2,1)S(1)}, bf16[256,256]{1,0:T(8,128)(2,1)S(1)}, u32[]{:S(2)}, u32[]{:S(2)}) %collective-permute-start.13) | collective-permute-done | bytes 131104 | tf_op jit(solution)/shard_map/ppermute | solution.py:109
  112.2 5.9 %collective-permute-done.14.refs_4_.refs_9_.refs_5_ = bf16[256,256]{1,0:T(8,128)(2,1)S(1)} collective-permute-done((bf16[256,256]{1,0:T(8,128)(2,1)S(1)}, bf16[256,256]{1,0:T(8,128)(2,1)S(1)}, u32[]{:S(2)}, u32[]{:S(2)}) %collective-permute-start.14) | collective-permute-done | bytes 131104 | tf_op jit(solution)/shard_map/ppermute | solution.py:110
  118.7 4.3 %collective-permute-start.25 = (bf16[128,1792]{1,0:T(8,128)(2,1)S(1)}, bf16[128,1792]{1,0:T(8,128)(2,1)S(1)}, u32[]{:S(2)}, u32[]{:S(2)}) collective-permute-start(bf16[128,1792]{1,0:T(8,128)(2,1)S(1)} %get-tuple-element.32.refs_0_), channel_id=1, source_target_pairs={{0,4},{4,8},{8,12},{1,5},{5,9},{9,13},{2,6},{6,10},{10,14},{3,7},{... | collective-permute-start | bytes 1376264 | tf_op jit(solution)/shard_map/ppermute | solution.py:104
  128.8 11.3 %collective-permute-done.31.refs_1_.refs_3_ = bf16[128,1792]{1,0:T(8,128)(2,1)S(1)} collective-permute-done((bf16[128,1792]{1,0:T(8,128)(2,1)S(1)}, bf16[128,1792]{1,0:T(8,128)(2,1)S(1)}, u32[]{:S(2)}, u32[]{:S(2)}) %collective-permute-start.31) | collective-permute-done | bytes 458784 | tf_op jit(solution)/shard_map/ppermute | solution.py:109
  142.0 6.0 %collective-permute-done.26.refs_2_ = bf16[128,1792]{1,0:T(8,128)(2,1)S(1)} collective-permute-done((bf16[128,1792]{1,0:T(8,128)(2,1)S(1)}, bf16[128,1792]{1,0:T(8,128)(2,1)S(1)}, u32[]{:S(2)}, u32[]{:S(2)}) %collective-permute-start.26) | collective-permute-done | bytes 458784 | tf_op jit(solution)/shard_map/ppermute | solution.py:105
  148.0 9.8 %collective-permute-done.28.refs_3_.refs_4_ = bf16[128,1792]{1,0:T(8,128)(2,1)S(1)} collective-permute-done((bf16[128,1792]{1,0:T(8,128)(2,1)S(1)}, bf16[128,1792]{1,0:T(8,128)(2,1)S(1)}, u32[]{:S(2)}, u32[]{:S(2)}) %collective-permute-start.28) | collective-permute-done | bytes 458784 | tf_op jit(solution)/shard_map/ppermute | solution.py:110
  158.4 5.6 %collective-permute-start.29 = (bf16[128,1792]{1,0:T(8,128)(2,1)S(1)}, bf16[128,1792]{1,0:T(8,128)(2,1)S(1)}, u32[]{:S(2)}, u32[]{:S(2)}) collective-permute-start(bf16[128,1792]{1,0:T(8,128)(2,1)S(1)} %gate.18.refs_0_), channel_id=1, source_target_pairs={{0,4},{4,8},{8,12},{1,5},{5,9},{9,13},{2,6},{6,10},{10,14},{3,7},{... | collective-permute-start | bytes 1376264 | tf_op jit(solution)/shard_map/ppermute | solution.py:104
  165.3 3.4 %project_raw.1 = (bf16[512,1024]{1,0:T(8,128)(2,1)S(1)}, bf16[512,2048]{1,0:T(8,128)(2,1)}) custom-call(s32[20]{0:T(128)S(1)} %copy-done.2, bf16[256,256]{1,0:T(8,128)(2,1)S(1)} %gate.13.refs_0_, bf16[256,256]{1,0:T(8,128)(2,1)S(1)} %collective-permute-done.7.refs_1_, ...), custom_call_target="tpu_custom_call", output_to_operand_aliasing={{1}: (24, {})} | custom-call | flops 1 | bytes 1 | tf_op jit(solution)/shard_map/project_raw/pallas_call | solution.py:165
  168.7 10.0 %collective-permute-done.32.refs_3_.refs_4_ = bf16[128,1792]{1,0:T(8,128)(2,1)S(1)} collective-permute-done((bf16[128,1792]{1,0:T(8,128)(2,1)S(1)}, bf16[128,1792]{1,0:T(8,128)(2,1)S(1)}, u32[]{:S(2)}, u32[]{:S(2)}) %collective-permute-start.32) | collective-permute-done | bytes 458784 | tf_op jit(solution)/shard_map/ppermute | solution.py:110
  178.7 6.8 %collective-permute-done.30.refs_2_ = bf16[128,1792]{1,0:T(8,128)(2,1)S(1)} collective-permute-done((bf16[128,1792]{1,0:T(8,128)(2,1)S(1)}, bf16[128,1792]{1,0:T(8,128)(2,1)S(1)}, u32[]{:S(2)}, u32[]{:S(2)}) %collective-permute-start.30) | collective-permute-done | bytes 458784 | tf_op jit(solution)/shard_map/ppermute | solution.py:105
  193.2 23.9 %collective-permute-done.39.refs_3_ = bf16[112,1792]{1,0:T(8,128)(2,1)S(1)} collective-permute-done((bf16[112,1792]{1,0:T(8,128)(2,1)S(1)}, bf16[112,1792]{1,0:T(8,128)(2,1)S(1)}, u32[]{:S(2)}, u32[]{:S(2)}) %collective-permute-start.39) | collective-permute-done | bytes 401440 | tf_op jit(solution)/shard_map/ppermute | solution.py:109
  218.4 3.1 %collective-permute-done.36.refs_3_.refs_4_ = bf16[144,1792]{1,0:T(8,128)(2,1)S(1)} collective-permute-done((bf16[144,1792]{1,0:T(8,128)(2,1)S(1)}, bf16[144,1792]{1,0:T(8,128)(2,1)S(1)}, u32[]{:S(2)}, u32[]{:S(2)}) %collective-permute-start.36) | collective-permute-done | bytes 516128 | tf_op jit(solution)/shard_map/ppermute | solution.py:110
  224.9 3.5 %norm.4.refs_6_ = bf16[512,8192]{1,0:T(8,128)(2,1)} custom-call(s32[20]{0:T(128)S(1)} %copy-done.2, f32[1,8192]{1,0:T(1,128)S(1)} %bitcast.23, bf16[128,1792]{1,0:T(8,128)(2,1)S(1)} %get-tuple-element.32.refs_0_, bf16[128,1792]{1,0:T(8,128)(2,1)S(1)} %collective-permute-done.25.refs_1_, bf16[128,1792]{1,0:T(8,128)(2,1)S(1)} %collective-permute-done.26.refs_2_, ...), custom_call_target="tpu_custom_call" | custom-call | flops 1 | bytes 1 | tf_op jit(solution)/shard_map/norm/pallas_call | solution.py:165
  228.4 3.5 %norm.5.refs_6_ = bf16[512,8192]{1,0:T(8,128)(2,1)} custom-call(s32[20]{0:T(128)S(1)} %copy-done.2, f32[1,8192]{1,0:T(1,128)S(1)} %bitcast.24, bf16[128,1792]{1,0:T(8,128)(2,1)S(1)} %gate.18.refs_0_, bf16[128,1792]{1,0:T(8,128)(2,1)S(1)} %collective-permute-done.29.refs_1_, ...), custom_call_target="tpu_custom_call", output_to_operand_aliasing={{}: (8, {})} | custom-call | flops 1 | bytes 1 | tf_op jit(solution)/shard_map/norm/pallas_call | solution.py:165
  231.9 5.3 %norm.6.refs_6_ = bf16[512,8192]{1,0:T(8,128)(2,1)} custom-call(s32[20]{0:T(128)S(1)} %copy-done.2, f32[1,8192]{1,0:T(1,128)S(1)} %bitcast.25, bf16[144,1792]{1,0:T(8,128)(2,1)S(1)} %gate.20.refs_0_, bf16[144,1792]{1,0:T(8,128)(2,1)S(1)} %collective-permute-done.33.refs_1_, ...), custom_call_target="tpu_custom_call", output_to_operand_aliasing={{}: (8, {})} | custom-call | flops 1 | bytes 1 | tf_op jit(solution)/shard_map/norm/pallas_call | solution.py:165
  237.2 4.4 %norm.7 = bf16[512,8192]{1,0:T(8,128)(2,1)} custom-call(s32[20]{0:T(128)S(1)} %copy-done.2, f32[1,8192]{1,0:T(1,128)S(1)} %bitcast.26, bf16[112,1792]{1,0:T(8,128)(2,1)S(1)} %gate.22.refs_0_, bf16[112,1792]{1,0:T(8,128)(2,1)S(1)} %collective-permute-done.37.refs_1_, ...), custom_call_target="tpu_custom_call", output_to_operand_aliasing={{}: (8, {})} | custom-call | flops 1 | bytes 1 | tf_op jit(solution)/shard_map/norm/pallas_call | solution.py:165
  (99 shorter events, 68.7 us)
Async XLA Ops:
  9.2 21.0 %collective-permute-start.1 = (bf16[1552,256]{1,0:T(8,128)(2,1)}, bf16[1552,256]{1,0:T(8,128)(2,1)S(1)}, u32[]{:S(2)}, u32[]{:S(2)}) collective-permute-start(bf16[1552,256]{1,0:T(8,128)(2,1)} %get-tuple-element.21.refs_0_), channel_id=1, source_target_pairs={{0,2},{1,3},{2,0},{3,1},{4,6},{5,7},{6,4},{7,5},{8,10},{9,11},{10,... | collective-permute-start | bytes 2383880 | tf_op jit(solution)/shard_map/ppermute | solution.py:43
  17.7 19.0 %collective-permute-start = (bf16[1552,256]{1,0:T(8,128)(2,1)}, bf16[1552,256]{1,0:T(8,128)(2,1)S(1)}, u32[]{:S(2)}, u32[]{:S(2)}) collective-permute-start(bf16[1552,256]{1,0:T(8,128)(2,1)} %get-tuple-element.21.refs_0_), channel_id=1, source_target_pairs={{0,1},{1,0},{2,3},{3,2},{4,5},{5,4},{6,7},{7,6},{8,9},{9,8},{10,11... | collective-permute-start | bytes 2383880 | tf_op jit(solution)/shard_map/ppermute | solution.py:43
  30.8 18.6 %collective-permute-start.19 = (bf16[4,32,2816]{2,1,0:T(8,128)(2,1)S(1)}, bf16[4,32,2816]{2,1,0:T(8,128)(2,1)S(1)}, u32[]{:S(2)}, u32[]{:S(2)}) collective-permute-start(bf16[4,32,2816]{2,1,0:T(8,128)(2,1)S(1)} %stack.89.refs_1_.refs_5_.refs_15_), channel_id=1, source_target_pairs={{0,2},{1,3},{2,0},{3,1},{4,6},{5,7},{6,4},{7,5},{8,10},{9,11},{10,... | collective-permute-start | bytes 2162696 | tf_op jit(solution)/shard_map/ppermute | solution.py:78
  32.6 18.2 %collective-permute-start.20 = (bf16[4,32,2816]{2,1,0:T(8,128)(2,1)S(1)}, bf16[4,32,2816]{2,1,0:T(8,128)(2,1)S(1)}, u32[]{:S(2)}, u32[]{:S(2)}) collective-permute-start(bf16[4,32,2816]{2,1,0:T(8,128)(2,1)S(1)} %stack.89.refs_1_.refs_5_.refs_15_), channel_id=1, source_target_pairs={{0,16},{16,0},{1,17},{17,1},{2,18},{18,2},{3,19},{19,3},{4,20},{20... | collective-permute-start | bytes 2162696 | tf_op jit(solution)/shard_map/ppermute | solution.py:78
  36.7 20.7 %collective-permute-start.15 = (bf16[512,256]{1,0:T(8,128)(2,1)S(1)}, bf16[512,256]{1,0:T(8,128)(2,1)S(1)}, u32[]{:S(2)}, u32[]{:S(2)}) collective-permute-start(bf16[512,256]{1,0:T(8,128)(2,1)S(1)} %last_columns.1.refs_2_.refs_10_), channel_id=1, source_target_pairs={{0,4},{4,8},{8,12},{1,5},{5,9},{9,13},{2,6},{6,10},{10,14},{3,7},{... | collective-permute-start | bytes 786440 | tf_op jit(solution)/shard_map/ppermute | solution.py:104
  40.9 21.1 %collective-permute-start.16 = (bf16[512,256]{1,0:T(8,128)(2,1)S(1)}, bf16[512,256]{1,0:T(8,128)(2,1)S(1)}, u32[]{:S(2)}, u32[]{:S(2)}) collective-permute-start(bf16[512,256]{1,0:T(8,128)(2,1)S(1)} %last_columns.1.refs_2_.refs_10_), channel_id=1, source_target_pairs={{4,0},{8,4},{12,8},{5,1},{9,5},{13,9},{6,2},{10,6},{14,10},{7,3},{... | collective-permute-start | bytes 786440 | tf_op jit(solution)/shard_map/ppermute | solution.py:105
  54.5 17.6 %collective-permute-start.23 = (bf16[4,32,2816]{2,1,0:T(8,128)(2,1)S(1)}, bf16[4,32,2816]{2,1,0:T(8,128)(2,1)S(1)}, u32[]{:S(2)}, u32[]{:S(2)}) collective-permute-start(bf16[4,32,2816]{2,1,0:T(8,128)(2,1)S(1)} %gate.14.refs_0_), channel_id=1, source_target_pairs={{0,16},{16,0},{1,17},{17,1},{2,18},{18,2},{3,19},{19,3},{4,20},{20... | collective-permute-start | bytes 2162696 | tf_op jit(solution)/shard_map/ppermute | solution.py:78
  79.8 38.4 %collective-permute-start.27 = (bf16[128,1792]{1,0:T(8,128)(2,1)S(1)}, bf16[128,1792]{1,0:T(8,128)(2,1)S(1)}, u32[]{:S(2)}, u32[]{:S(2)}) collective-permute-start(bf16[128,1792]{1,0:T(8,128)(2,1)S(1)} %get-tuple-element.33), channel_id=1, source_target_pairs={{0,8},{4,12},{8,0},{12,4},{1,9},{5,13},{9,1},{13,5},{2,10},{6,14},... | collective-permute-start | bytes 1376264 | tf_op jit(solution)/shard_map/ppermute | solution.py:109
  84.6 26.4 %collective-permute-start.13 = (bf16[256,256]{1,0:T(8,128)(2,1)S(1)}, bf16[256,256]{1,0:T(8,128)(2,1)S(1)}, u32[]{:S(2)}, u32[]{:S(2)}) collective-permute-start(bf16[256,256]{1,0:T(8,128)(2,1)S(1)} %attend.3.refs_5_.refs_0_), channel_id=1, source_target_pairs={{0,8},{4,12},{8,0},{12,4},{1,9},{5,13},{9,1},{13,5},{2,10},{6,14},... | collective-permute-start | bytes 393224 | tf_op jit(solution)/shard_map/ppermute | solution.py:109
  84.6 27.6 %collective-permute-start.11 = (bf16[256,256]{1,0:T(8,128)(2,1)S(1)}, bf16[256,256]{1,0:T(8,128)(2,1)S(1)}, u32[]{:S(2)}, u32[]{:S(2)}) collective-permute-start(bf16[256,256]{1,0:T(8,128)(2,1)S(1)} %attend.3.refs_5_.refs_0_), channel_id=1, source_target_pairs={{0,4},{4,8},{8,12},{1,5},{5,9},{9,13},{2,6},{6,10},{10,14},{3,7},{... | collective-permute-start | bytes 393224 | tf_op jit(solution)/shard_map/ppermute | solution.py:104
  87.3 24.9 %collective-permute-start.12 = (bf16[256,256]{1,0:T(8,128)(2,1)S(1)}, bf16[256,256]{1,0:T(8,128)(2,1)S(1)}, u32[]{:S(2)}, u32[]{:S(2)}) collective-permute-start(bf16[256,256]{1,0:T(8,128)(2,1)S(1)} %attend.3.refs_5_.refs_0_), channel_id=1, source_target_pairs={{4,0},{8,4},{12,8},{5,1},{9,5},{13,9},{6,2},{10,6},{14,10},{7,3},{... | collective-permute-start | bytes 393224 | tf_op jit(solution)/shard_map/ppermute | solution.py:105
  118.7 21.4 %collective-permute-start.31 = (bf16[128,1792]{1,0:T(8,128)(2,1)S(1)}, bf16[128,1792]{1,0:T(8,128)(2,1)S(1)}, u32[]{:S(2)}, u32[]{:S(2)}) collective-permute-start(bf16[128,1792]{1,0:T(8,128)(2,1)S(1)} %gate.19), channel_id=1, source_target_pairs={{0,8},{4,12},{8,0},{12,4},{1,9},{5,13},{9,1},{13,5},{2,10},{6,14},... | collective-permute-start | bytes 1376264 | tf_op jit(solution)/shard_map/ppermute | solution.py:109
  118.7 23.2 %collective-permute-start.25 = (bf16[128,1792]{1,0:T(8,128)(2,1)S(1)}, bf16[128,1792]{1,0:T(8,128)(2,1)S(1)}, u32[]{:S(2)}, u32[]{:S(2)}) collective-permute-start(bf16[128,1792]{1,0:T(8,128)(2,1)S(1)} %get-tuple-element.32.refs_0_), channel_id=1, source_target_pairs={{0,4},{4,8},{8,12},{1,5},{5,9},{9,13},{2,6},{6,10},{10,14},{3,7},{... | collective-permute-start | bytes 1376264 | tf_op jit(solution)/shard_map/ppermute | solution.py:104
  123.0 25.0 %collective-permute-start.26 = (bf16[128,1792]{1,0:T(8,128)(2,1)S(1)}, bf16[128,1792]{1,0:T(8,128)(2,1)S(1)}, u32[]{:S(2)}, u32[]{:S(2)}) collective-permute-start(bf16[128,1792]{1,0:T(8,128)(2,1)S(1)} %get-tuple-element.32.refs_0_), channel_id=1, source_target_pairs={{4,0},{8,4},{12,8},{5,1},{9,5},{13,9},{6,2},{10,6},{14,10},{7,3},{... | collective-permute-start | bytes 1376264 | tf_op jit(solution)/shard_map/ppermute | solution.py:105
  124.3 33.5 %collective-permute-start.28 = (bf16[128,1792]{1,0:T(8,128)(2,1)S(1)}, bf16[128,1792]{1,0:T(8,128)(2,1)S(1)}, u32[]{:S(2)}, u32[]{:S(2)}) collective-permute-start(bf16[128,1792]{1,0:T(8,128)(2,1)S(1)} %collective-permute-done.27.refs_1_.refs_3_), channel_id=1, source_target_pairs={{4,0},{8,12},{5,1},{9,13},{6,2},{10,14},{7,3},{11,15},{20,16},{24,... | collective-permute-start | bytes 1376264 | tf_op jit(solution)/shard_map/ppermute | solution.py:110
  140.6 48.2 %collective-permute-start.35 = (bf16[144,1792]{1,0:T(8,128)(2,1)S(1)}, bf16[144,1792]{1,0:T(8,128)(2,1)S(1)}, u32[]{:S(2)}, u32[]{:S(2)}) collective-permute-start(bf16[144,1792]{1,0:T(8,128)(2,1)S(1)} %gate.21), channel_id=1, source_target_pairs={{0,8},{4,12},{8,0},{12,4},{1,9},{5,13},{9,1},{13,5},{2,10},{6,14},... | collective-permute-start | bytes 1548296 | tf_op jit(solution)/shard_map/ppermute | solution.py:109
  140.7 38.0 %collective-permute-start.32 = (bf16[128,1792]{1,0:T(8,128)(2,1)S(1)}, bf16[128,1792]{1,0:T(8,128)(2,1)S(1)}, u32[]{:S(2)}, u32[]{:S(2)}) collective-permute-start(bf16[128,1792]{1,0:T(8,128)(2,1)S(1)} %collective-permute-done.31.refs_1_.refs_3_), channel_id=1, source_target_pairs={{4,0},{8,12},{5,1},{9,13},{6,2},{10,14},{7,3},{11,15},{20,16},{24,... | collective-permute-start | bytes 1376264 | tf_op jit(solution)/shard_map/ppermute | solution.py:110
  158.4 20.3 %collective-permute-start.29 = (bf16[128,1792]{1,0:T(8,128)(2,1)S(1)}, bf16[128,1792]{1,0:T(8,128)(2,1)S(1)}, u32[]{:S(2)}, u32[]{:S(2)}) collective-permute-start(bf16[128,1792]{1,0:T(8,128)(2,1)S(1)} %gate.18.refs_0_), channel_id=1, source_target_pairs={{0,4},{4,8},{8,12},{1,5},{5,9},{9,13},{2,6},{6,10},{10,14},{3,7},{... | collective-permute-start | bytes 1376264 | tf_op jit(solution)/shard_map/ppermute | solution.py:104
  164.0 21.5 %collective-permute-start.30 = (bf16[128,1792]{1,0:T(8,128)(2,1)S(1)}, bf16[128,1792]{1,0:T(8,128)(2,1)S(1)}, u32[]{:S(2)}, u32[]{:S(2)}) collective-permute-start(bf16[128,1792]{1,0:T(8,128)(2,1)S(1)} %gate.18.refs_0_), channel_id=1, source_target_pairs={{4,0},{8,4},{12,8},{5,1},{9,5},{13,9},{6,2},{10,6},{14,10},{7,3},{... | collective-permute-start | bytes 1376264 | tf_op jit(solution)/shard_map/ppermute | solution.py:105
  186.0 32.4 %collective-permute-start.33 = (bf16[144,1792]{1,0:T(8,128)(2,1)S(1)}, bf16[144,1792]{1,0:T(8,128)(2,1)S(1)}, u32[]{:S(2)}, u32[]{:S(2)}) collective-permute-start(bf16[144,1792]{1,0:T(8,128)(2,1)S(1)} %gate.20.refs_0_), channel_id=1, source_target_pairs={{0,4},{4,8},{8,12},{1,5},{5,9},{9,13},{2,6},{6,10},{10,14},{3,7},{... | collective-permute-start | bytes 1548296 | tf_op jit(solution)/shard_map/ppermute | solution.py:104
  187.5 30.9 %collective-permute-start.34 = (bf16[144,1792]{1,0:T(8,128)(2,1)S(1)}, bf16[144,1792]{1,0:T(8,128)(2,1)S(1)}, u32[]{:S(2)}, u32[]{:S(2)}) collective-permute-start(bf16[144,1792]{1,0:T(8,128)(2,1)S(1)} %gate.20.refs_0_), channel_id=1, source_target_pairs={{4,0},{8,4},{12,8},{5,1},{9,5},{13,9},{6,2},{10,6},{14,10},{7,3},{... | collective-permute-start | bytes 1548296 | tf_op jit(solution)/shard_map/ppermute | solution.py:105
  188.8 32.7 %collective-permute-start.36 = (bf16[144,1792]{1,0:T(8,128)(2,1)S(1)}, bf16[144,1792]{1,0:T(8,128)(2,1)S(1)}, u32[]{:S(2)}, u32[]{:S(2)}) collective-permute-start(bf16[144,1792]{1,0:T(8,128)(2,1)S(1)} %collective-permute-done.35.refs_1_.refs_3_), channel_id=1, source_target_pairs={{4,0},{8,12},{5,1},{9,13},{6,2},{10,14},{7,3},{11,15},{20,16},{24,... | collective-permute-start | bytes 1548296 | tf_op jit(solution)/shard_map/ppermute | solution.py:110
  190.7 26.5 %collective-permute-start.39 = (bf16[112,1792]{1,0:T(8,128)(2,1)S(1)}, bf16[112,1792]{1,0:T(8,128)(2,1)S(1)}, u32[]{:S(2)}, u32[]{:S(2)}) collective-permute-start(bf16[112,1792]{1,0:T(8,128)(2,1)S(1)} %gate.23), channel_id=1, source_target_pairs={{0,8},{4,12},{8,0},{12,4},{1,9},{5,13},{9,1},{13,5},{2,10},{6,14},... | collective-permute-start | bytes 1204232 | tf_op jit(solution)/shard_map/ppermute | solution.py:109
  217.1 20.0 %collective-permute-start.40 = (bf16[112,1792]{1,0:T(8,128)(2,1)S(1)}, bf16[112,1792]{1,0:T(8,128)(2,1)S(1)}, u32[]{:S(2)}, u32[]{:S(2)}) collective-permute-start(bf16[112,1792]{1,0:T(8,128)(2,1)S(1)} %collective-permute-done.39.refs_3_), channel_id=1, source_target_pairs={{4,0},{8,12},{5,1},{9,13},{6,2},{10,14},{7,3},{11,15},{20,16},{24,... | collective-permute-start | bytes 1204232 | tf_op jit(solution)/shard_map/ppermute | solution.py:110
  (23 other events, 345.0 us)

commit v13 on v12

--- a/solution.py
+++ b/solution.py
@@ -120,7 +120,9 @@
             after += second
         fars.append(line_far(gate(info, value, after) if after else value))
     for number, value in enumerate(copies):
-        after = [*lines[number - 1][1:3], fars[number - 1][1]] if number else []
+        after = list(lines[number - 1][1:3]) if number else []
+        if number > 1:
+            after.append(fars[number - 2][1])
         if number == len(copies) // 2:
             after += made
         value = gate(info, value, after) if after else value
@@ -593,11 +595,9 @@
     raw = slab // RAW_PART if slab % (RAW_PART * HD) == 0 else 0
     keep = slab - raw
     chunk = min(CHUNK, rows)
-    halves = 2 if rows % (2 * chunk) == 0 else 1
+    halves = 1
     half = rows // halves
-    splits = [[(0, chunk), (chunk, half - chunk)] if half > chunk else [(0, half)]] * halves
-    if halves == 2 and chunk == 128 and half == 256:
-        splits = [splits[0], [(0, 144), (144, 112)]]
+    splits = [[(begin, chunk) for begin in range(0, half, chunk)]] * halves
 
     table = Table(contexts, count)
     steering = [context_index, *owners_of(contexts, context_index)]
@@ -662,7 +662,7 @@
         info,
         values,
         copies,
-        attention[-1][1:],
+        attention[-1][1:] if halves > 1 else [],
         [raw_hidden] if raw else [],
         count,
     )

time: 242 us -> 234 us (0.967)
  waiting for transfers between devices: 115 us -> 88.7 us
  starting transfers between devices: 69.9 us -> 89 us
  Pallas kernels: 50.8 us -> 45.7 us
  local copies, waits for them, and re-layouts: 1.58 us -> 5.97 us
    ppermute x7 -> x6, starting transfers between devices: 24.4 us -> 55.1 us  [line_near(): up = lax.ppermute(value, 'tensor', [(0, 1), (1, 2), (2, 3)])]
    ppermute x7 -> x6, waiting for transfers between devices: 28.8 us -> 11.6 us  [line_far(): return (far, lax.ppermute(far, 'tensor', [(1, 0), (2, 3)]))]
    ppermute x7 -> x6, waiting for transfers between devices: 57.5 us -> 43.4 us  [line_far(): far = lax.ppermute(value, 'tensor', [(0, 2), (1, 3), (2, 0), (3, 1)])]
    ppermute x7 -> x6, starting transfers between devices: 12.8 us -> 5.95 us  [line_far(): far = lax.ppermute(value, 'tensor', [(0, 2), (1, 3), (2, 0), (3, 1)])]
    ppermute x7 -> x6, waiting for transfers between devices: 12.8 us -> 18 us  [line_near(): return (up, lax.ppermute(value, 'tensor', [(1, 0), (2, 1), (3, 2)]))]
    pallas_call x24 -> x22, Pallas kernels: 50.8 us -> 45.7 us  [call(): pl.pallas_call(kernel, grid_spec=pltpu.PrefetchScalarGridSpec(num_scalar_...]
    unnamed x12 -> x16, local copies, waits for them, and re-layouts: 0.94 us -> 5.28 us
    ppermute x7 -> x6, waiting for transfers between devices: 0.02 us -> 3.09 us  [line_near(): up = lax.ppermute(value, 'tensor', [(0, 1), (1, 2), (2, 3)])]
  transfers between devices with their start and end apart: 41 -> 37, of which waited for: 16 -> 18; matrix products, arithmetic and copies ran while one was open for 0% -> 0% of each run, Pallas kernels for 16% -> 14%
where the time goes in v13:
time: 234 us
  starting transfers between devices  89 us (38%)
  waiting for transfers between devices  88.7 us (38%)
  Pallas kernels  45.7 us (20%)
  local copies, waits for them, and re-layouts  5.97 us (3%)
  between operations  2.43 us (1%)
    ppermute x6, starting transfers between devices, line_near(): up = lax.ppermute(value, 'tensor', [(0, 1), (1, 2), (2, 3)])  55.1 us
    pallas_call x22, Pallas kernels, call(): pl.pallas_call(kernel, grid_spec=pltpu.PrefetchScalarGridSpec(num_scalar_...  45.7 us
    ppermute x6, waiting for transfers between devices, line_far(): far = lax.ppermute(value, 'tensor', [(0, 2), (1, 3), (2, 0), (3, 1)])  43.4 us
    ppermute x6, waiting for transfers between devices, line_near(): return (up, lax.ppermute(value, 'tensor', [(1, 0), (2, 1), (3, 2)]))  18 us
    ppermute x6, waiting for transfers between devices, line_far(): return (far, lax.ppermute(far, 'tensor', [(1, 0), (2, 3)]))  11.6 us
    ppermute x3, waiting for transfers between devices, per_device(): parts.append(lax.ppermute(cuts[shift], 'tensor', pairs))  10.4 us
    ppermute x6, starting transfers between devices, line_near(): return (up, lax.ppermute(value, 'tensor', [(1, 0), (2, 1), (3, 2)]))  7.74 us
    ppermute x6, starting transfers between devices, line_far(): return (far, lax.ppermute(far, 'tensor', [(1, 0), (2, 3)]))  7.71 us
  transfers between devices with their start and end apart: 37, of which 18 were waited for; matrix products, arithmetic and copies ran while one was open for 0% of the time, Pallas kernels for 14%

profile of v13, /device:TPU:0, one launch (start us, length us, event | category | flops | bytes accessed | tf_op | source)
XLA Modules:
  0.0 233.7 jit_solution(5362650012226683008)
XLA Ops:
  4.6 4.5 %prepare.1 = (bf16[512,256]{1,0:T(8,128)(2,1)}, bf16[1552,256]{1,0:T(8,128)(2,1)}, bf16[32,2816]{1,0:T(8,128)(2,1)}, bf16[32,2816]{1,0:T(8,128)(2,1)}, bf16[32,2...) custom-call(s32[20]{0:T(128)} %stack.86.info, bf16[512,256]{1,0:T(8,128)(2,1)} %q_hbm.1, bf16[512,256]{1,0:T(8,128)(2,1)} %bitcast.28, ...), custom_call_target="tpu_custom_call" | custom-call | flops 1 | bytes 1 | tf_op jit(solution)/shard_map/prepare/pallas_call | solution.py:167
  17.6 4.1 %collective-permute-done.2.refs_1_ = bf16[32,2816]{1,0:T(8,128)(2,1)S(1)} collective-permute-done((bf16[32,2816]{1,0:T(8,128)(2,1)}, bf16[32,2816]{1,0:T(8,128)(2,1)S(1)}, u32[]{:S(2)}, u32[]{:S(2)}) %collective-permute-start.2) | collective-permute-done | bytes 180256 | tf_op jit(solution)/shard_map/ppermute | solution.py:622
  21.6 6.3 %collective-permute-done.3.refs_2_ = bf16[32,2816]{1,0:T(8,128)(2,1)S(1)} collective-permute-done((bf16[32,2816]{1,0:T(8,128)(2,1)}, bf16[32,2816]{1,0:T(8,128)(2,1)S(1)}, u32[]{:S(2)}, u32[]{:S(2)}) %collective-permute-start.3) | collective-permute-done | bytes 180256 | tf_op jit(solution)/shard_map/ppermute | solution.py:622
  35.1 3.4 %collective-permute-start.6 = (bf16[512,256]{1,0:T(8,128)(2,1)S(1)}, bf16[512,256]{1,0:T(8,128)(2,1)S(1)}, u32[]{:S(2)}, u32[]{:S(2)}) collective-permute-start(bf16[512,256]{1,0:T(8,128)(2,1)S(1)} %last_columns.1.refs_2_.refs_5_), channel_id=1, source_target_pairs={{0,8},{4,12},{8,0},{12,4},{1,9},{5,13},{9,1},{13,5},{2,10},{6,14},... | collective-permute-start | bytes 786440 | tf_op jit(solution)/shard_map/ppermute | solution.py:109
  40.6 12.2 %attend.1.refs_0_.refs_1_ = bf16[512,256]{1,0:T(8,128)(2,1)S(1)} custom-call(s32[20]{0:T(128)S(1)} %copy-done.4, bf16[512,256]{1,0:T(8,128)(2,1)S(1)} %copy-done.7, bf16[1552,256]{1,0:T(8,128)(2,1)S(1)} %copy-done.6, bf16[1552,256]{1,0:T(8,128)(2,1)S(1)} %collective-permute-done.refs_1_, bf16[1552,256]{1,0:T(8,128)(2,1)S(1)} %gate.12.refs_2_, ...), custom_call_target="tpu_custom_call" | custom-call | flops 12884901888 | bytes 1 | tf_op jit(solution)/shard_map/attend/pallas_call | solution.py:167
  54.0 6.2 %collective-permute-start.11 = (bf16[512,256]{1,0:T(8,128)(2,1)S(1)}, bf16[512,256]{1,0:T(8,128)(2,1)S(1)}, u32[]{:S(2)}, u32[]{:S(2)}) collective-permute-start(bf16[512,256]{1,0:T(8,128)(2,1)S(1)} %last_columns.1.refs_2_.refs_5_), channel_id=1, source_target_pairs={{0,4},{4,8},{8,12},{1,5},{5,9},{9,13},{2,6},{6,10},{10,14},{3,7},{... | collective-permute-start | bytes 786440 | tf_op jit(solution)/shard_map/ppermute | solution.py:104
  66.6 4.4 %collective-permute-start.7 = (bf16[512,256]{1,0:T(8,128)(2,1)S(1)}, bf16[512,256]{1,0:T(8,128)(2,1)S(1)}, u32[]{:S(2)}, u32[]{:S(2)}) collective-permute-start(bf16[512,256]{1,0:T(8,128)(2,1)S(1)} %gate.13.refs_0_), channel_id=1, source_target_pairs={{0,4},{4,8},{8,12},{1,5},{5,9},{9,13},{2,6},{6,10},{10,14},{3,7},{... | collective-permute-start | bytes 786440 | tf_op jit(solution)/shard_map/ppermute | solution.py:104
  73.8 8.3 %collective-permute-done.9.refs_1_.refs_3_ = bf16[512,256]{1,0:T(8,128)(2,1)S(1)} collective-permute-done((bf16[512,256]{1,0:T(8,128)(2,1)S(1)}, bf16[512,256]{1,0:T(8,128)(2,1)S(1)}, u32[]{:S(2)}, u32[]{:S(2)}) %collective-permute-start.9) | collective-permute-done | bytes 262176 | tf_op jit(solution)/shard_map/ppermute | solution.py:109
  87.8 3.8 %collective-permute-done.10.refs_4_ = bf16[512,256]{1,0:T(8,128)(2,1)S(1)} collective-permute-done((bf16[512,256]{1,0:T(8,128)(2,1)S(1)}, bf16[512,256]{1,0:T(8,128)(2,1)S(1)}, u32[]{:S(2)}, u32[]{:S(2)}) %collective-permute-start.10) | collective-permute-done | bytes 262176 | tf_op jit(solution)/shard_map/ppermute | solution.py:110
  95.4 4.2 %project.1 = (bf16[128,1792]{1,0:T(8,128)(2,1)S(1)}, bf16[128,1792]{1,0:T(8,128)(2,1)S(1)}, bf16[128,1792]{1,0:T(8,128)(2,1)S(1)}, bf16[128,1792]{1,0:T(8,128)(2...) custom-call(s32[20]{0:T(128)S(1)} %copy-done.4, ...), custom_call_target="tpu_custom_call" | custom-call | flops 1 | bytes 1 | tf_op jit(solution)/shard_map/project/pallas_call | solution.py:167
  103.6 18.5 %collective-permute-done.25.refs_1_.refs_3_ = bf16[128,1792]{1,0:T(8,128)(2,1)S(1)} collective-permute-done((bf16[128,1792]{1,0:T(8,128)(2,1)S(1)}, bf16[128,1792]{1,0:T(8,128)(2,1)S(1)}, u32[]{:S(2)}, u32[]{:S(2)}) %collective-permute-start.25) | collective-permute-done | bytes 458784 | tf_op jit(solution)/shard_map/ppermute | solution.py:109
  127.5 17.3 %collective-permute-start.23 = (bf16[128,1792]{1,0:T(8,128)(2,1)S(1)}, bf16[128,1792]{1,0:T(8,128)(2,1)S(1)}, u32[]{:S(2)}, u32[]{:S(2)}) collective-permute-start(bf16[128,1792]{1,0:T(8,128)(2,1)S(1)} %gate.18.refs_0_), channel_id=1, source_target_pairs={{0,4},{4,8},{8,12},{1,5},{5,9},{9,13},{2,6},{6,10},{10,14},{3,7},{... | collective-permute-start | bytes 1376264 | tf_op jit(solution)/shard_map/ppermute | solution.py:104
  146.1 5.5 %collective-permute-done.29.refs_1_.refs_3_ = bf16[128,1792]{1,0:T(8,128)(2,1)S(1)} collective-permute-done((bf16[128,1792]{1,0:T(8,128)(2,1)S(1)}, bf16[128,1792]{1,0:T(8,128)(2,1)S(1)}, u32[]{:S(2)}, u32[]{:S(2)}) %collective-permute-start.29) | collective-permute-done | bytes 458784 | tf_op jit(solution)/shard_map/ppermute | solution.py:109
  156.8 4.6 %collective-permute-done.24.refs_2_ = bf16[128,1792]{1,0:T(8,128)(2,1)S(1)} collective-permute-done((bf16[128,1792]{1,0:T(8,128)(2,1)S(1)}, bf16[128,1792]{1,0:T(8,128)(2,1)S(1)}, u32[]{:S(2)}, u32[]{:S(2)}) %collective-permute-start.24) | collective-permute-done | bytes 458784 | tf_op jit(solution)/shard_map/ppermute | solution.py:105
  162.0 12.4 %collective-permute-start.27 = (bf16[128,1792]{1,0:T(8,128)(2,1)S(1)}, bf16[128,1792]{1,0:T(8,128)(2,1)S(1)}, u32[]{:S(2)}, u32[]{:S(2)}) collective-permute-start(bf16[128,1792]{1,0:T(8,128)(2,1)S(1)} %gate.19.refs_0_), channel_id=1, source_target_pairs={{0,4},{4,8},{8,12},{1,5},{5,9},{9,13},{2,6},{6,10},{10,14},{3,7},{... | collective-permute-start | bytes 1376264 | tf_op jit(solution)/shard_map/ppermute | solution.py:104
  175.6 5.5 %collective-permute-done.33.refs_1_.refs_3_ = bf16[128,1792]{1,0:T(8,128)(2,1)S(1)} collective-permute-done((bf16[128,1792]{1,0:T(8,128)(2,1)S(1)}, bf16[128,1792]{1,0:T(8,128)(2,1)S(1)}, u32[]{:S(2)}, u32[]{:S(2)}) %collective-permute-start.33) | collective-permute-done | bytes 458784 | tf_op jit(solution)/shard_map/ppermute | solution.py:109
  185.2 5.8 %collective-permute-done.28.refs_2_ = bf16[128,1792]{1,0:T(8,128)(2,1)S(1)} collective-permute-done((bf16[128,1792]{1,0:T(8,128)(2,1)S(1)}, bf16[128,1792]{1,0:T(8,128)(2,1)S(1)}, u32[]{:S(2)}, u32[]{:S(2)}) %collective-permute-start.28) | collective-permute-done | bytes 458784 | tf_op jit(solution)/shard_map/ppermute | solution.py:105
  191.5 12.4 %collective-permute-start.31 = (bf16[128,1792]{1,0:T(8,128)(2,1)S(1)}, bf16[128,1792]{1,0:T(8,128)(2,1)S(1)}, u32[]{:S(2)}, u32[]{:S(2)}) collective-permute-start(bf16[128,1792]{1,0:T(8,128)(2,1)S(1)} %gate.21.refs_0_), channel_id=1, source_target_pairs={{0,4},{4,8},{8,12},{1,5},{5,9},{9,13},{2,6},{6,10},{10,14},{3,7},{... | collective-permute-start | bytes 1376264 | tf_op jit(solution)/shard_map/ppermute | solution.py:104
  205.2 5.5 %collective-permute-done.34.refs_3_ = bf16[128,1792]{1,0:T(8,128)(2,1)S(1)} collective-permute-done((bf16[128,1792]{1,0:T(8,128)(2,1)S(1)}, bf16[128,1792]{1,0:T(8,128)(2,1)S(1)}, u32[]{:S(2)}, u32[]{:S(2)}) %collective-permute-start.34) | collective-permute-done | bytes 458784 | tf_op jit(solution)/shard_map/ppermute | solution.py:109
  212.0 3.5 %norm.4.refs_6_ = bf16[512,8192]{1,0:T(8,128)(2,1)} custom-call(s32[20]{0:T(128)S(1)} %copy-done.4, f32[1,8192]{1,0:T(1,128)S(1)} %bitcast.23, bf16[128,1792]{1,0:T(8,128)(2,1)S(1)} %get-tuple-element.30.refs_0_, bf16[128,1792]{1,0:T(8,128)(2,1)S(1)} %collective-permute-done.21.refs_1_, bf16[128,1792]{1,0:T(8,128)(2,1)S(1)} %collective-permute-done.22.refs_2_, ...), custom_call_target="tpu_custom_call" | custom-call | flops 1 | bytes 1 | tf_op jit(solution)/shard_map/norm/pallas_call | solution.py:167
  215.5 3.5 %norm.5.refs_6_ = bf16[512,8192]{1,0:T(8,128)(2,1)} custom-call(s32[20]{0:T(128)S(1)} %copy-done.4, f32[1,8192]{1,0:T(1,128)S(1)} %bitcast.24, bf16[128,1792]{1,0:T(8,128)(2,1)S(1)} %gate.18.refs_0_, bf16[128,1792]{1,0:T(8,128)(2,1)S(1)} %collective-permute-done.23.refs_1_, ...), custom_call_target="tpu_custom_call", output_to_operand_aliasing={{}: (8, {})} | custom-call | flops 1 | bytes 1 | tf_op jit(solution)/shard_map/norm/pallas_call | solution.py:167
  218.9 3.5 %norm.6.refs_6_ = bf16[512,8192]{1,0:T(8,128)(2,1)} custom-call(s32[20]{0:T(128)S(1)} %copy-done.4, f32[1,8192]{1,0:T(1,128)S(1)} %bitcast.25, bf16[128,1792]{1,0:T(8,128)(2,1)S(1)} %gate.19.refs_0_, bf16[128,1792]{1,0:T(8,128)(2,1)S(1)} %collective-permute-done.27.refs_1_, ...), custom_call_target="tpu_custom_call", output_to_operand_aliasing={{}: (8, {})} | custom-call | flops 1 | bytes 1 | tf_op jit(solution)/shard_map/norm/pallas_call | solution.py:167
  222.4 7.8 %collective-permute-done.35.refs_4_ = bf16[128,1792]{1,0:T(8,128)(2,1)S(1)} collective-permute-done((bf16[128,1792]{1,0:T(8,128)(2,1)S(1)}, bf16[128,1792]{1,0:T(8,128)(2,1)S(1)}, u32[]{:S(2)}, u32[]{:S(2)}) %collective-permute-start.35) | collective-permute-done | bytes 458784 | tf_op jit(solution)/shard_map/ppermute | solution.py:110
  230.2 3.5 %norm.7 = bf16[512,8192]{1,0:T(8,128)(2,1)} custom-call(s32[20]{0:T(128)S(1)} %copy-done.4, f32[1,8192]{1,0:T(1,128)S(1)} %bitcast.26, bf16[128,1792]{1,0:T(8,128)(2,1)S(1)} %gate.21.refs_0_, bf16[128,1792]{1,0:T(8,128)(2,1)S(1)} %collective-permute-done.31.refs_1_, ...), custom_call_target="tpu_custom_call", output_to_operand_aliasing={{}: (8, {})} | custom-call | flops 1 | bytes 1 | tf_op jit(solution)/shard_map/norm/pallas_call | solution.py:167
  (93 shorter events, 64.7 us)
Async XLA Ops:
  9.1 23.3 %collective-permute-start.1 = (bf16[1552,256]{1,0:T(8,128)(2,1)}, bf16[1552,256]{1,0:T(8,128)(2,1)S(1)}, u32[]{:S(2)}, u32[]{:S(2)}) collective-permute-start(bf16[1552,256]{1,0:T(8,128)(2,1)} %get-tuple-element.20.refs_0_), channel_id=1, source_target_pairs={{0,2},{1,3},{2,0},{3,1},{4,6},{5,7},{6,4},{7,5},{8,10},{9,11},{10,... | collective-permute-start | bytes 2383880 | tf_op jit(solution)/shard_map/ppermute | solution.py:43
  17.6 20.9 %collective-permute-start = (bf16[1552,256]{1,0:T(8,128)(2,1)}, bf16[1552,256]{1,0:T(8,128)(2,1)S(1)}, u32[]{:S(2)}, u32[]{:S(2)}) collective-permute-start(bf16[1552,256]{1,0:T(8,128)(2,1)} %get-tuple-element.20.refs_0_), channel_id=1, source_target_pairs={{0,1},{1,0},{2,3},{3,2},{4,5},{5,4},{6,7},{7,6},{8,9},{9,8},{10,11... | collective-permute-start | bytes 2383880 | tf_op jit(solution)/shard_map/ppermute | solution.py:43
  33.0 19.8 %collective-permute-start.15 = (bf16[4,32,2816]{2,1,0:T(8,128)(2,1)S(1)}, bf16[4,32,2816]{2,1,0:T(8,128)(2,1)S(1)}, u32[]{:S(2)}, u32[]{:S(2)}) collective-permute-start(bf16[4,32,2816]{2,1,0:T(8,128)(2,1)S(1)} %stack.89.refs_1_.refs_5_.refs_10_), channel_id=1, source_target_pairs={{0,2},{1,3},{2,0},{3,1},{4,6},{5,7},{6,4},{7,5},{8,10},{9,11},{10,... | collective-permute-start | bytes 2162696 | tf_op jit(solution)/shard_map/ppermute | solution.py:78
  33.6 19.3 %collective-permute-start.16 = (bf16[4,32,2816]{2,1,0:T(8,128)(2,1)S(1)}, bf16[4,32,2816]{2,1,0:T(8,128)(2,1)S(1)}, u32[]{:S(2)}, u32[]{:S(2)}) collective-permute-start(bf16[4,32,2816]{2,1,0:T(8,128)(2,1)S(1)} %stack.89.refs_1_.refs_5_.refs_10_), channel_id=1, source_target_pairs={{0,16},{16,0},{1,17},{17,1},{2,18},{18,2},{3,19},{19,3},{4,20},{20... | collective-permute-start | bytes 2162696 | tf_op jit(solution)/shard_map/ppermute | solution.py:78
  35.1 26.4 %collective-permute-start.6 = (bf16[512,256]{1,0:T(8,128)(2,1)S(1)}, bf16[512,256]{1,0:T(8,128)(2,1)S(1)}, u32[]{:S(2)}, u32[]{:S(2)}) collective-permute-start(bf16[512,256]{1,0:T(8,128)(2,1)S(1)} %last_columns.1.refs_2_.refs_5_), channel_id=1, source_target_pairs={{0,8},{4,12},{8,0},{12,4},{1,9},{5,13},{9,1},{13,5},{2,10},{6,14},... | collective-permute-start | bytes 786440 | tf_op jit(solution)/shard_map/ppermute | solution.py:109
  53.4 38.2 %collective-permute-start.19 = (bf16[4,32,2816]{2,1,0:T(8,128)(2,1)S(1)}, bf16[4,32,2816]{2,1,0:T(8,128)(2,1)S(1)}, u32[]{:S(2)}, u32[]{:S(2)}) collective-permute-start(bf16[4,32,2816]{2,1,0:T(8,128)(2,1)S(1)} %gate.14.refs_0_), channel_id=1, source_target_pairs={{0,16},{16,0},{1,17},{17,1},{2,18},{18,2},{3,19},{19,3},{4,20},{20... | collective-permute-start | bytes 2162696 | tf_op jit(solution)/shard_map/ppermute | solution.py:78
  62.0 20.1 %collective-permute-start.9 = (bf16[512,256]{1,0:T(8,128)(2,1)S(1)}, bf16[512,256]{1,0:T(8,128)(2,1)S(1)}, u32[]{:S(2)}, u32[]{:S(2)}) collective-permute-start(bf16[512,256]{1,0:T(8,128)(2,1)S(1)} %gate.13.refs_0_), channel_id=1, source_target_pairs={{0,8},{4,12},{8,0},{12,4},{1,9},{5,13},{9,1},{13,5},{2,10},{6,14},... | collective-permute-start | bytes 786440 | tf_op jit(solution)/shard_map/ppermute | solution.py:109
  64.3 19.6 %collective-permute-start.13 = (bf16[512,256]{1,0:T(8,128)(2,1)S(1)}, bf16[512,256]{1,0:T(8,128)(2,1)S(1)}, u32[]{:S(2)}, u32[]{:S(2)}) collective-permute-start(bf16[512,256]{1,0:T(8,128)(2,1)S(1)} %collective-permute-done.6.refs_1_.refs_8_), channel_id=1, source_target_pairs={{4,0},{8,12},{5,1},{9,13},{6,2},{10,14},{7,3},{11,15},{20,16},{24,... | collective-permute-start | bytes 786440 | tf_op jit(solution)/shard_map/ppermute | solution.py:110
  66.6 17.5 %collective-permute-start.7 = (bf16[512,256]{1,0:T(8,128)(2,1)S(1)}, bf16[512,256]{1,0:T(8,128)(2,1)S(1)}, u32[]{:S(2)}, u32[]{:S(2)}) collective-permute-start(bf16[512,256]{1,0:T(8,128)(2,1)S(1)} %gate.13.refs_0_), channel_id=1, source_target_pairs={{0,4},{4,8},{8,12},{1,5},{5,9},{9,13},{2,6},{6,10},{10,14},{3,7},{... | collective-permute-start | bytes 786440 | tf_op jit(solution)/shard_map/ppermute | solution.py:104
  99.7 22.4 %collective-permute-start.25 = (bf16[128,1792]{1,0:T(8,128)(2,1)S(1)}, bf16[128,1792]{1,0:T(8,128)(2,1)S(1)}, u32[]{:S(2)}, u32[]{:S(2)}) collective-permute-start(bf16[128,1792]{1,0:T(8,128)(2,1)S(1)} %get-tuple-element.31), channel_id=1, source_target_pairs={{0,8},{4,12},{8,0},{12,4},{1,9},{5,13},{9,1},{13,5},{2,10},{6,14},... | collective-permute-start | bytes 1376264 | tf_op jit(solution)/shard_map/ppermute | solution.py:109
  99.7 24.3 %collective-permute-start.21 = (bf16[128,1792]{1,0:T(8,128)(2,1)S(1)}, bf16[128,1792]{1,0:T(8,128)(2,1)S(1)}, u32[]{:S(2)}, u32[]{:S(2)}) collective-permute-start(bf16[128,1792]{1,0:T(8,128)(2,1)S(1)} %get-tuple-element.30.refs_0_), channel_id=1, source_target_pairs={{0,4},{4,8},{8,12},{1,5},{5,9},{9,13},{2,6},{6,10},{10,14},{3,7},{... | collective-permute-start | bytes 1376264 | tf_op jit(solution)/shard_map/ppermute | solution.py:104
  102.3 24.7 %collective-permute-start.22 = (bf16[128,1792]{1,0:T(8,128)(2,1)S(1)}, bf16[128,1792]{1,0:T(8,128)(2,1)S(1)}, u32[]{:S(2)}, u32[]{:S(2)}) collective-permute-start(bf16[128,1792]{1,0:T(8,128)(2,1)S(1)} %get-tuple-element.30.refs_0_), channel_id=1, source_target_pairs={{4,0},{8,4},{12,8},{5,1},{9,5},{13,9},{6,2},{10,6},{14,10},{7,3},{... | collective-permute-start | bytes 1376264 | tf_op jit(solution)/shard_map/ppermute | solution.py:105
  122.6 29.0 %collective-permute-start.29 = (bf16[128,1792]{1,0:T(8,128)(2,1)S(1)}, bf16[128,1792]{1,0:T(8,128)(2,1)S(1)}, u32[]{:S(2)}, u32[]{:S(2)}) collective-permute-start(bf16[128,1792]{1,0:T(8,128)(2,1)S(1)} %gate.20), channel_id=1, source_target_pairs={{0,8},{4,12},{8,0},{12,4},{1,9},{5,13},{9,1},{13,5},{2,10},{6,14},... | collective-permute-start | bytes 1376264 | tf_op jit(solution)/shard_map/ppermute | solution.py:109
  122.7 34.1 %collective-permute-start.26 = (bf16[128,1792]{1,0:T(8,128)(2,1)S(1)}, bf16[128,1792]{1,0:T(8,128)(2,1)S(1)}, u32[]{:S(2)}, u32[]{:S(2)}) collective-permute-start(bf16[128,1792]{1,0:T(8,128)(2,1)S(1)} %collective-permute-done.25.refs_1_.refs_3_), channel_id=1, source_target_pairs={{4,0},{8,12},{5,1},{9,13},{6,2},{10,14},{7,3},{11,15},{20,16},{24,... | collective-permute-start | bytes 1376264 | tf_op jit(solution)/shard_map/ppermute | solution.py:110
  127.5 29.3 %collective-permute-start.23 = (bf16[128,1792]{1,0:T(8,128)(2,1)S(1)}, bf16[128,1792]{1,0:T(8,128)(2,1)S(1)}, u32[]{:S(2)}, u32[]{:S(2)}) collective-permute-start(bf16[128,1792]{1,0:T(8,128)(2,1)S(1)} %gate.18.refs_0_), channel_id=1, source_target_pairs={{0,4},{4,8},{8,12},{1,5},{5,9},{9,13},{2,6},{6,10},{10,14},{3,7},{... | collective-permute-start | bytes 1376264 | tf_op jit(solution)/shard_map/ppermute | solution.py:104
  144.8 16.6 %collective-permute-start.24 = (bf16[128,1792]{1,0:T(8,128)(2,1)S(1)}, bf16[128,1792]{1,0:T(8,128)(2,1)S(1)}, u32[]{:S(2)}, u32[]{:S(2)}) collective-permute-start(bf16[128,1792]{1,0:T(8,128)(2,1)S(1)} %gate.18.refs_0_), channel_id=1, source_target_pairs={{4,0},{8,4},{12,8},{5,1},{9,5},{13,9},{6,2},{10,6},{14,10},{7,3},{... | collective-permute-start | bytes 1376264 | tf_op jit(solution)/shard_map/ppermute | solution.py:105
  152.2 29.0 %collective-permute-start.33 = (bf16[128,1792]{1,0:T(8,128)(2,1)S(1)}, bf16[128,1792]{1,0:T(8,128)(2,1)S(1)}, u32[]{:S(2)}, u32[]{:S(2)}) collective-permute-start(bf16[128,1792]{1,0:T(8,128)(2,1)S(1)} %gate.22), channel_id=1, source_target_pairs={{0,8},{4,12},{8,0},{12,4},{1,9},{5,13},{9,1},{13,5},{2,10},{6,14},... | collective-permute-start | bytes 1376264 | tf_op jit(solution)/shard_map/ppermute | solution.py:109
  155.5 27.6 %collective-permute-start.30 = (bf16[128,1792]{1,0:T(8,128)(2,1)S(1)}, bf16[128,1792]{1,0:T(8,128)(2,1)S(1)}, u32[]{:S(2)}, u32[]{:S(2)}) collective-permute-start(bf16[128,1792]{1,0:T(8,128)(2,1)S(1)} %collective-permute-done.29.refs_1_.refs_3_), channel_id=1, source_target_pairs={{4,0},{8,12},{5,1},{9,13},{6,2},{10,14},{7,3},{11,15},{20,16},{24,... | collective-permute-start | bytes 1376264 | tf_op jit(solution)/shard_map/ppermute | solution.py:110
  162.0 23.2 %collective-permute-start.27 = (bf16[128,1792]{1,0:T(8,128)(2,1)S(1)}, bf16[128,1792]{1,0:T(8,128)(2,1)S(1)}, u32[]{:S(2)}, u32[]{:S(2)}) collective-permute-start(bf16[128,1792]{1,0:T(8,128)(2,1)S(1)} %gate.19.refs_0_), channel_id=1, source_target_pairs={{0,4},{4,8},{8,12},{1,5},{5,9},{9,13},{2,6},{6,10},{10,14},{3,7},{... | collective-permute-start | bytes 1376264 | tf_op jit(solution)/shard_map/ppermute | solution.py:104
  181.7 29.0 %collective-permute-start.34 = (bf16[128,1792]{1,0:T(8,128)(2,1)S(1)}, bf16[128,1792]{1,0:T(8,128)(2,1)S(1)}, u32[]{:S(2)}, u32[]{:S(2)}) collective-permute-start(bf16[128,1792]{1,0:T(8,128)(2,1)S(1)} %gate.23), channel_id=1, source_target_pairs={{0,8},{4,12},{8,0},{12,4},{1,9},{5,13},{9,1},{13,5},{2,10},{6,14},... | collective-permute-start | bytes 1376264 | tf_op jit(solution)/shard_map/ppermute | solution.py:109
  181.8 37.2 %collective-permute-start.36 = (bf16[128,1792]{1,0:T(8,128)(2,1)S(1)}, bf16[128,1792]{1,0:T(8,128)(2,1)S(1)}, u32[]{:S(2)}, u32[]{:S(2)}) collective-permute-start(bf16[128,1792]{1,0:T(8,128)(2,1)S(1)} %collective-permute-done.33.refs_1_.refs_3_), channel_id=1, source_target_pairs={{4,0},{8,12},{5,1},{9,13},{6,2},{10,14},{7,3},{11,15},{20,16},{24,... | collective-permute-start | bytes 1376264 | tf_op jit(solution)/shard_map/ppermute | solution.py:110
  191.5 30.9 %collective-permute-start.31 = (bf16[128,1792]{1,0:T(8,128)(2,1)S(1)}, bf16[128,1792]{1,0:T(8,128)(2,1)S(1)}, u32[]{:S(2)}, u32[]{:S(2)}) collective-permute-start(bf16[128,1792]{1,0:T(8,128)(2,1)S(1)} %gate.21.refs_0_), channel_id=1, source_target_pairs={{0,4},{4,8},{8,12},{1,5},{5,9},{9,13},{2,6},{6,10},{10,14},{3,7},{... | collective-permute-start | bytes 1376264 | tf_op jit(solution)/shard_map/ppermute | solution.py:104
  203.9 18.5 %collective-permute-start.32 = (bf16[128,1792]{1,0:T(8,128)(2,1)S(1)}, bf16[128,1792]{1,0:T(8,128)(2,1)S(1)}, u32[]{:S(2)}, u32[]{:S(2)}) collective-permute-start(bf16[128,1792]{1,0:T(8,128)(2,1)S(1)} %gate.21.refs_0_), channel_id=1, source_target_pairs={{4,0},{8,4},{12,8},{5,1},{9,5},{13,9},{6,2},{10,6},{14,10},{7,3},{... | collective-permute-start | bytes 1376264 | tf_op jit(solution)/shard_map/ppermute | solution.py:105
  210.7 19.5 %collective-permute-start.35 = (bf16[128,1792]{1,0:T(8,128)(2,1)S(1)}, bf16[128,1792]{1,0:T(8,128)(2,1)S(1)}, u32[]{:S(2)}, u32[]{:S(2)}) collective-permute-start(bf16[128,1792]{1,0:T(8,128)(2,1)S(1)} %collective-permute-done.34.refs_3_), channel_id=1, source_target_pairs={{4,0},{8,12},{5,1},{9,13},{6,2},{10,14},{7,3},{11,15},{20,16},{24,... | collective-permute-start | bytes 1376264 | tf_op jit(solution)/shard_map/ppermute | solution.py:110
  (21 other events, 272.7 us)

commit v14 on v13

--- a/solution.py
+++ b/solution.py
@@ -186,11 +186,11 @@
     return pl.BlockSpec(tuple(a.shape), lambda i, info: zeros)
 
 
-def prepare_kernel(table, slab, keep, info, q_hbm, kv_hbm, cache_hbm, w_hbm, cos_ref, sin_ref,
-                   length_ref, *refs):
+def prepare_kernel(table, slab, keep, info, q_hbm, kv_hbm, cache_hbm, w_hbm, r_hbm, cos_ref,
+                   sin_ref, length_ref, *refs):
     count, raw = table.count, slab - keep
     q_out, kv_out, outs = refs[0], refs[1], refs[2 : 2 + count]
-    q_ref, kv_ref, w_ref, sems = refs[2 + count :]
+    q_ref, kv_ref, w_ref, sems = refs[-4:]
     slots, rows, part = cache_hbm.shape[0], q_ref.shape[0], w_ref.shape[0]
     span, tail = slice(slots, slots + rows), slice(slots + rows, slots + rows + TAIL)
     start = pl.multiple_of(info[table.share] * part, part)
@@ -200,6 +200,8 @@
         (q_hbm, q_ref),
         (cache_hbm, kv_out.at[pl.ds(0, slots)]),
     ]
+    if raw:
+        moves.append((r_hbm.at[:, pl.ds(keep, raw)], refs[2 + count]))
     copies = [pltpu.make_async_copy(*move, sems.at[n]) for n, move in enumerate(moves)]
     for copy in copies:
         copy.start()
@@ -231,24 +233,27 @@
     for head in range(q_ref.shape[1] // HD):
         cols = slice(head * HD, (head + 1) * HD)
         q_out[:, cols] = turn(q_ref[:, cols])
-    copies[3].wait()
-
-
-def prepare(table, info, queries, span_pairs, cache, out_weight, cosine, sine, lengths, part,
-            slab, keep):
-    rows = queries.shape[0]
+    for copy in copies[3:]:
+        copy.wait()
+
+
+def prepare(table, info, queries, span_pairs, cache, out_weight, residual, cosine, sine, lengths,
+            part, keep):
+    rows, slab = residual.shape
     shapes = [
         jax.ShapeDtypeStruct(queries.shape, jnp.bfloat16),
         jax.ShapeDtypeStruct((cache.shape[0] + rows + TAIL, 2 * HD), jnp.bfloat16),
     ]
     width = keep + table.count * (slab - keep)
     shapes += [jax.ShapeDtypeStruct((part, width), out_weight.dtype)] * table.count
+    if keep < slab:
+        shapes.append(jax.ShapeDtypeStruct((rows, slab - keep), residual.dtype))
     return call(
         functools.partial(prepare_kernel, table, slab, keep),
         "prepare",
         info,
-        [queries, span_pairs, cache, out_weight, cosine, sine, lengths],
-        [ANYWHERE] * 4
+        [queries, span_pairs, cache, out_weight, residual, cosine, sine, lengths],
+        [ANYWHERE] * 5
         + [whole(cosine), whole(sine), pl.BlockSpec(memory_space=pltpu.SMEM)],
         [whole(shape) for shape in shapes],
         shapes,
@@ -256,28 +261,9 @@
             pltpu.VMEM(queries.shape, jnp.bfloat16),
             pltpu.VMEM(span_pairs.shape, jnp.bfloat16),
             pltpu.VMEM((part, out_weight.shape[1]), out_weight.dtype),
-            pltpu.SemaphoreType.DMA((4,)),
+            pltpu.SemaphoreType.DMA((5,)),
         ],
         vmem=0,
-    )
-
-
-def last_columns_kernel(info, *refs):
-    refs[-1][...] = refs[0][...]
-
-
-def last_columns(info, value, width, after):
-    rows, full = value.shape
-    shape = jax.ShapeDtypeStruct((rows, width), value.dtype)
-    return call(
-        last_columns_kernel,
-        "last_columns",
-        info,
-        [value, *after],
-        [pl.BlockSpec((rows, width), lambda i, info: (0, full // width - 1))]
-        + [ANYWHERE] * len(after),
-        whole(shape),
-        shape,
     )
 
 
@@ -613,15 +599,15 @@
     angles = positions.astype(jnp.float32)[:, None] * both[None, :]
     sign = jnp.where(jnp.arange(HD) < HD // 2, -1.0, 1.0)
     q_turned, payload, *cuts = prepare(
-        table, info, queries, span_local, cache_local, out_weight, jnp.cos(angles),
-        jnp.sin(angles) * sign[None, :], lengths, depth // shares, slab, keep,
+        table, info, queries, span_local, cache_local, out_weight, residual, jnp.cos(angles),
+        jnp.sin(angles) * sign[None, :], lengths, depth // shares, keep,
     )
     parts = [cuts[0]]
     for shift in range(1, count):
         pairs = [(i, (i + shift) % count) for i in range(count)]
         parts.append(lax.ppermute(cuts[shift], "tensor", pairs))
     own_weights = stack(info, parts, [])
-    own_raw = [last_columns(info, residual, raw, parts[1:])] if raw else []
+    own_raw = [gate(info, cuts[count], parts[1:])] if raw else []
     pieces = pieces_of(
         payload, "context", contexts, lambda block: gate(info, block, [own_weights, *own_raw])
     )
@@ -631,18 +617,18 @@
         for number in range(halves)
     ]
     residuals = line_gather(own_raw[0], count) if raw else []
-    ready = [gate(info, mixed[0], residuals[3:4]), *mixed[1:]] if raw else mixed
+    ready = [gate(info, mixed[0], residuals[1:4] or residuals), *mixed[1:]] if raw else mixed
     attention = [line_gather(value, count) for value in ready]
-    before = [*attention[0][1:], *mixed[1:], *residuals[1:3], *residuals[4:]]
+    before = [*attention[0][1:], *mixed[1:], *residuals[4:]]
     weights = plane_gather(
         own_weights,
         groups,
         contexts,
-        lambda block, other: gate(info, block, [mixed[0], other]),
+        lambda block, other: gate(info, block, mixed[:1]),
         lambda block, mask: gate(
             info,
             block,
-            attention[0][3:4] if mask in (mask & -mask,) else before,
+            attention[0][1:3] if mask in (mask & -mask,) else before,
         ),
     )
     values, copies, hidden = [], [], None

time: 234 us -> 232 us (level)
  waiting for transfers between devices: 88.7 us -> 84.2 us
  starting transfers between devices: 89 us -> 91.8 us
    ppermute x6, waiting for transfers between devices: 11.6 us -> 17.1 us  [line_far(): return (far, lax.ppermute(far, 'tensor', [(1, 0), (2, 3)]))]
    ppermute x6, waiting for transfers between devices: 43.4 us -> 38.4 us  [line_far(): far = lax.ppermute(value, 'tensor', [(0, 2), (1, 3), (2, 0), (3, 1)])]
    ppermute x6, waiting for transfers between devices: 18 us -> 13.6 us  [line_near(): return (up, lax.ppermute(value, 'tensor', [(1, 0), (2, 1), (3, 2)]))]
    unnamed x16 -> x14, local copies, waits for them, and re-layouts: 5.28 us -> 3.59 us
  transfers between devices with their start and end apart: 37 -> 37, of which waited for: 18 -> 18; matrix products, arithmetic and copies ran while one was open for 0% -> 0% of each run, Pallas kernels for 14% -> 15%
where the time goes in v14:
time: 232 us; the launch traced here: 231 us
  starting transfers between devices  91.8 us (40%)
  waiting for transfers between devices  84.2 us (36%)
  Pallas kernels  46.9 us (20%)
  local copies, waits for them, and re-layouts  4.18 us (2%)
  between operations  2.41 us (1%)
    ppermute x6, starting transfers between devices, line_near(): up = lax.ppermute(value, 'tensor', [(0, 1), (1, 2), (2, 3)])  56.7 us
    pallas_call x22, Pallas kernels, call(): pl.pallas_call(kernel, grid_spec=pltpu.PrefetchScalarGridSpec(num_scalar_...  46.9 us
    ppermute x6, waiting for transfers between devices, line_far(): far = lax.ppermute(value, 'tensor', [(0, 2), (1, 3), (2, 0), (3, 1)])  38.4 us
    ppermute x6, waiting for transfers between devices, line_far(): return (far, lax.ppermute(far, 'tensor', [(1, 0), (2, 3)]))  17.1 us
    ppermute x6, waiting for transfers between devices, line_near(): return (up, lax.ppermute(value, 'tensor', [(1, 0), (2, 1), (3, 2)]))  13.6 us
    ppermute x3, waiting for transfers between devices, per_device(): parts.append(lax.ppermute(cuts[shift], 'tensor', pairs))  10.4 us
    ppermute x6, starting transfers between devices, line_near(): return (up, lax.ppermute(value, 'tensor', [(1, 0), (2, 1), (3, 2)]))  7.75 us
    ppermute x6, starting transfers between devices, line_far(): return (far, lax.ppermute(far, 'tensor', [(1, 0), (2, 3)]))  7.72 us
  transfers between devices with their start and end apart: 37, of which 18 were waited for; matrix products, arithmetic and copies ran while one was open for 0% of the time, Pallas kernels for 15%

profile of v14, /device:TPU:0, one launch (start us, length us, event | category | flops | bytes accessed | tf_op | source)
XLA Modules:
  0.0 231.5 jit_solution(12422652389632898015)
XLA Ops:
  4.5 4.6 %prepare.1 = (bf16[512,256]{1,0:T(8,128)(2,1)}, bf16[1552,256]{1,0:T(8,128)(2,1)}, bf16[32,2816]{1,0:T(8,128)(2,1)}, bf16[32,2816]{1,0:T(8,128)(2,1)}, bf16[32,2...) custom-call(s32[20]{0:T(128)} %stack.86.info, bf16[512,256]{1,0:T(8,128)(2,1)} %q_hbm.1, ...), custom_call_target="tpu_custom_call" | custom-call | flops 1 | bytes 1 | tf_op jit(solution)/shard_map/prepare/pallas_call | solution.py:167
  17.6 4.1 %collective-permute-done.2.refs_1_ = bf16[32,2816]{1,0:T(8,128)(2,1)S(1)} collective-permute-done((bf16[32,2816]{1,0:T(8,128)(2,1)}, bf16[32,2816]{1,0:T(8,128)(2,1)S(1)}, u32[]{:S(2)}, u32[]{:S(2)}) %collective-permute-start.2) | collective-permute-done | bytes 180256 | tf_op jit(solution)/shard_map/ppermute | solution.py:608
  21.7 6.3 %collective-permute-done.3.refs_2_ = bf16[32,2816]{1,0:T(8,128)(2,1)S(1)} collective-permute-done((bf16[32,2816]{1,0:T(8,128)(2,1)}, bf16[32,2816]{1,0:T(8,128)(2,1)S(1)}, u32[]{:S(2)}, u32[]{:S(2)}) %collective-permute-start.3) | collective-permute-done | bytes 180256 | tf_op jit(solution)/shard_map/ppermute | solution.py:608
  32.4 5.7 %collective-permute-start.6 = (bf16[512,256]{1,0:T(8,128)(2,1)}, bf16[512,256]{1,0:T(8,128)(2,1)S(1)}, u32[]{:S(2)}, u32[]{:S(2)}) collective-permute-start(bf16[512,256]{1,0:T(8,128)(2,1)} %gate.13.refs_2_.refs_5_), channel_id=1, source_target_pairs={{0,4},{4,8},{8,12},{1,5},{5,9},{9,13},{2,6},{6,10},{10,14},{3,7},{... | collective-permute-start | bytes 786440 | tf_op jit(solution)/shard_map/ppermute | solution.py:104
  45.4 12.2 %attend.1.refs_0_.refs_1_ = bf16[512,256]{1,0:T(8,128)(2,1)S(1)} custom-call(s32[20]{0:T(128)S(1)} %copy-done.3, bf16[512,256]{1,0:T(8,128)(2,1)S(1)} %copy-done.6, bf16[1552,256]{1,0:T(8,128)(2,1)S(1)} %copy-done.5, bf16[1552,256]{1,0:T(8,128)(2,1)S(1)} %collective-permute-done.refs_1_, bf16[1552,256]{1,0:T(8,128)(2,1)S(1)} %gate.14.refs_2_, ...), custom_call_target="tpu_custom_call" | custom-call | flops 12884901888 | bytes 1 | tf_op jit(solution)/shard_map/attend/pallas_call | solution.py:167
  61.4 5.1 %collective-permute-start.9 = (bf16[512,256]{1,0:T(8,128)(2,1)S(1)}, bf16[512,256]{1,0:T(8,128)(2,1)S(1)}, u32[]{:S(2)}, u32[]{:S(2)}) collective-permute-start(bf16[512,256]{1,0:T(8,128)(2,1)S(1)} %gate.15.refs_0_), channel_id=1, source_target_pairs={{0,4},{4,8},{8,12},{1,5},{5,9},{9,13},{2,6},{6,10},{10,14},{3,7},{... | collective-permute-start | bytes 786440 | tf_op jit(solution)/shard_map/ppermute | solution.py:104
  67.8 6.6 %collective-permute-done.11.refs_3_ = bf16[512,256]{1,0:T(8,128)(2,1)S(1)} collective-permute-done((bf16[512,256]{1,0:T(8,128)(2,1)S(1)}, bf16[512,256]{1,0:T(8,128)(2,1)S(1)}, u32[]{:S(2)}, u32[]{:S(2)}) %collective-permute-start.11) | collective-permute-done | bytes 262176 | tf_op jit(solution)/shard_map/ppermute | solution.py:109
  77.5 4.5 %collective-permute-done.13.refs_5_.refs_9_ = bf16[512,256]{1,0:T(8,128)(2,1)S(1)} collective-permute-done((bf16[512,256]{1,0:T(8,128)(2,1)S(1)}, bf16[512,256]{1,0:T(8,128)(2,1)S(1)}, u32[]{:S(2)}, u32[]{:S(2)}) %collective-permute-start.13) | collective-permute-done | bytes 262176 | tf_op jit(solution)/shard_map/ppermute | solution.py:110
  82.0 4.1 %collective-permute-done.12.refs_4_ = bf16[512,256]{1,0:T(8,128)(2,1)S(1)} collective-permute-done((bf16[512,256]{1,0:T(8,128)(2,1)S(1)}, bf16[512,256]{1,0:T(8,128)(2,1)S(1)}, u32[]{:S(2)}, u32[]{:S(2)}) %collective-permute-start.12) | collective-permute-done | bytes 262176 | tf_op jit(solution)/shard_map/ppermute | solution.py:110
  89.9 4.2 %project.1 = (bf16[128,1792]{1,0:T(8,128)(2,1)S(1)}, bf16[128,1792]{1,0:T(8,128)(2,1)S(1)}, bf16[128,1792]{1,0:T(8,128)(2,1)S(1)}, bf16[128,1792]{1,0:T(8,128)(2...) custom-call(s32[20]{0:T(128)S(1)} %copy-done.3, ...), custom_call_target="tpu_custom_call" | custom-call | flops 1 | bytes 1 | tf_op jit(solution)/shard_map/project/pallas_call | solution.py:167
  94.2 4.0 %collective-permute-start.25 = (bf16[128,1792]{1,0:T(8,128)(2,1)S(1)}, bf16[128,1792]{1,0:T(8,128)(2,1)S(1)}, u32[]{:S(2)}, u32[]{:S(2)}) collective-permute-start(bf16[128,1792]{1,0:T(8,128)(2,1)S(1)} %get-tuple-element.33), channel_id=1, source_target_pairs={{0,8},{4,12},{8,0},{12,4},{1,9},{5,13},{9,1},{13,5},{2,10},{6,14},... | collective-permute-start | bytes 1376264 | tf_op jit(solution)/shard_map/ppermute | solution.py:109
  98.1 4.4 %collective-permute-start.21 = (bf16[128,1792]{1,0:T(8,128)(2,1)S(1)}, bf16[128,1792]{1,0:T(8,128)(2,1)S(1)}, u32[]{:S(2)}, u32[]{:S(2)}) collective-permute-start(bf16[128,1792]{1,0:T(8,128)(2,1)S(1)} %get-tuple-element.32.refs_0_), channel_id=1, source_target_pairs={{0,4},{4,8},{8,12},{1,5},{5,9},{9,13},{2,6},{6,10},{10,14},{3,7},{... | collective-permute-start | bytes 1376264 | tf_op jit(solution)/shard_map/ppermute | solution.py:104
  103.8 15.5 %collective-permute-done.25.refs_1_.refs_3_ = bf16[128,1792]{1,0:T(8,128)(2,1)S(1)} collective-permute-done((bf16[128,1792]{1,0:T(8,128)(2,1)S(1)}, bf16[128,1792]{1,0:T(8,128)(2,1)S(1)}, u32[]{:S(2)}, u32[]{:S(2)}) %collective-permute-start.25) | collective-permute-done | bytes 458784 | tf_op jit(solution)/shard_map/ppermute | solution.py:109
  124.8 17.2 %collective-permute-start.23 = (bf16[128,1792]{1,0:T(8,128)(2,1)S(1)}, bf16[128,1792]{1,0:T(8,128)(2,1)S(1)}, u32[]{:S(2)}, u32[]{:S(2)}) collective-permute-start(bf16[128,1792]{1,0:T(8,128)(2,1)S(1)} %gate.20.refs_0_), channel_id=1, source_target_pairs={{0,4},{4,8},{8,12},{1,5},{5,9},{9,13},{2,6},{6,10},{10,14},{3,7},{... | collective-permute-start | bytes 1376264 | tf_op jit(solution)/shard_map/ppermute | solution.py:104
  143.3 5.4 %collective-permute-done.29.refs_1_.refs_3_ = bf16[128,1792]{1,0:T(8,128)(2,1)S(1)} collective-permute-done((bf16[128,1792]{1,0:T(8,128)(2,1)S(1)}, bf16[128,1792]{1,0:T(8,128)(2,1)S(1)}, u32[]{:S(2)}, u32[]{:S(2)}) %collective-permute-start.29) | collective-permute-done | bytes 458784 | tf_op jit(solution)/shard_map/ppermute | solution.py:109
  149.3 4.4 %project_raw.1 = (bf16[512,1024]{1,0:T(8,128)(2,1)S(1)}, bf16[512,2048]{1,0:T(8,128)(2,1)}) custom-call(s32[20]{0:T(128)S(1)} %copy-done.3, bf16[512,256]{1,0:T(8,128)(2,1)S(1)} %gate.15.refs_0_, bf16[512,256]{1,0:T(8,128)(2,1)S(1)} %collective-permute-done.9.refs_1_, ...), custom_call_target="tpu_custom_call", output_to_operand_aliasing={{1}: (19, {})} | custom-call | flops 1 | bytes 1 | tf_op jit(solution)/shard_map/project_raw/pallas_call | solution.py:167
  158.7 13.2 %collective-permute-start.27 = (bf16[128,1792]{1,0:T(8,128)(2,1)S(1)}, bf16[128,1792]{1,0:T(8,128)(2,1)S(1)}, u32[]{:S(2)}, u32[]{:S(2)}) collective-permute-start(bf16[128,1792]{1,0:T(8,128)(2,1)S(1)} %gate.21.refs_0_), channel_id=1, source_target_pairs={{0,4},{4,8},{8,12},{1,5},{5,9},{9,13},{2,6},{6,10},{10,14},{3,7},{... | collective-permute-start | bytes 1376264 | tf_op jit(solution)/shard_map/ppermute | solution.py:104
  173.2 5.1 %collective-permute-done.33.refs_1_.refs_3_ = bf16[128,1792]{1,0:T(8,128)(2,1)S(1)} collective-permute-done((bf16[128,1792]{1,0:T(8,128)(2,1)S(1)}, bf16[128,1792]{1,0:T(8,128)(2,1)S(1)}, u32[]{:S(2)}, u32[]{:S(2)}) %collective-permute-start.33) | collective-permute-done | bytes 458784 | tf_op jit(solution)/shard_map/ppermute | solution.py:109
  182.8 6.9 %collective-permute-done.28.refs_2_ = bf16[128,1792]{1,0:T(8,128)(2,1)S(1)} collective-permute-done((bf16[128,1792]{1,0:T(8,128)(2,1)S(1)}, bf16[128,1792]{1,0:T(8,128)(2,1)S(1)}, u32[]{:S(2)}, u32[]{:S(2)}) %collective-permute-start.28) | collective-permute-done | bytes 458784 | tf_op jit(solution)/shard_map/ppermute | solution.py:105
  190.3 11.1 %collective-permute-start.31 = (bf16[128,1792]{1,0:T(8,128)(2,1)S(1)}, bf16[128,1792]{1,0:T(8,128)(2,1)S(1)}, u32[]{:S(2)}, u32[]{:S(2)}) collective-permute-start(bf16[128,1792]{1,0:T(8,128)(2,1)S(1)} %gate.23.refs_0_), channel_id=1, source_target_pairs={{0,4},{4,8},{8,12},{1,5},{5,9},{9,13},{2,6},{6,10},{10,14},{3,7},{... | collective-permute-start | bytes 1376264 | tf_op jit(solution)/shard_map/ppermute | solution.py:104
  202.7 5.1 %collective-permute-done.34.refs_3_ = bf16[128,1792]{1,0:T(8,128)(2,1)S(1)} collective-permute-done((bf16[128,1792]{1,0:T(8,128)(2,1)S(1)}, bf16[128,1792]{1,0:T(8,128)(2,1)S(1)}, u32[]{:S(2)}, u32[]{:S(2)}) %collective-permute-start.34) | collective-permute-done | bytes 458784 | tf_op jit(solution)/shard_map/ppermute | solution.py:109
  209.1 3.5 %norm.4.refs_6_ = bf16[512,8192]{1,0:T(8,128)(2,1)} custom-call(s32[20]{0:T(128)S(1)} %copy-done.3, f32[1,8192]{1,0:T(1,128)S(1)} %bitcast.23, bf16[128,1792]{1,0:T(8,128)(2,1)S(1)} %get-tuple-element.32.refs_0_, bf16[128,1792]{1,0:T(8,128)(2,1)S(1)} %collective-permute-done.21.refs_1_, bf16[128,1792]{1,0:T(8,128)(2,1)S(1)} %collective-permute-done.22.refs_2_, ...), custom_call_target="tpu_custom_call" | custom-call | flops 1 | bytes 1 | tf_op jit(solution)/shard_map/norm/pallas_call | solution.py:167
  216.0 3.5 %norm.6.refs_6_ = bf16[512,8192]{1,0:T(8,128)(2,1)} custom-call(s32[20]{0:T(128)S(1)} %copy-done.3, f32[1,8192]{1,0:T(1,128)S(1)} %bitcast.25, bf16[128,1792]{1,0:T(8,128)(2,1)S(1)} %gate.21.refs_0_, bf16[128,1792]{1,0:T(8,128)(2,1)S(1)} %collective-permute-done.27.refs_1_, ...), custom_call_target="tpu_custom_call", output_to_operand_aliasing={{}: (8, {})} | custom-call | flops 1 | bytes 1 | tf_op jit(solution)/shard_map/norm/pallas_call | solution.py:167
  219.5 8.5 %collective-permute-done.35.refs_4_ = bf16[128,1792]{1,0:T(8,128)(2,1)S(1)} collective-permute-done((bf16[128,1792]{1,0:T(8,128)(2,1)S(1)}, bf16[128,1792]{1,0:T(8,128)(2,1)S(1)}, u32[]{:S(2)}, u32[]{:S(2)}) %collective-permute-start.35) | collective-permute-done | bytes 458784 | tf_op jit(solution)/shard_map/ppermute | solution.py:110
  (91 shorter events, 63.9 us)
Async XLA Ops:
  9.1 21.5 %collective-permute-start.1 = (bf16[1552,256]{1,0:T(8,128)(2,1)}, bf16[1552,256]{1,0:T(8,128)(2,1)S(1)}, u32[]{:S(2)}, u32[]{:S(2)}) collective-permute-start(bf16[1552,256]{1,0:T(8,128)(2,1)} %get-tuple-element.21.refs_0_), channel_id=1, source_target_pairs={{0,2},{1,3},{2,0},{3,1},{4,6},{5,7},{6,4},{7,5},{8,10},{9,11},{10,... | collective-permute-start | bytes 2383880 | tf_op jit(solution)/shard_map/ppermute | solution.py:43
  17.6 21.8 %collective-permute-start = (bf16[1552,256]{1,0:T(8,128)(2,1)}, bf16[1552,256]{1,0:T(8,128)(2,1)S(1)}, u32[]{:S(2)}, u32[]{:S(2)}) collective-permute-start(bf16[1552,256]{1,0:T(8,128)(2,1)} %get-tuple-element.21.refs_0_), channel_id=1, source_target_pairs={{0,1},{1,0},{2,3},{3,2},{4,5},{5,4},{6,7},{7,6},{8,9},{9,8},{10,11... | collective-permute-start | bytes 2383880 | tf_op jit(solution)/shard_map/ppermute | solution.py:43
  31.3 26.3 %collective-permute-start.15 = (bf16[4,32,2816]{2,1,0:T(8,128)(2,1)S(1)}, bf16[4,32,2816]{2,1,0:T(8,128)(2,1)S(1)}, u32[]{:S(2)}, u32[]{:S(2)}) collective-permute-start(bf16[4,32,2816]{2,1,0:T(8,128)(2,1)S(1)} %stack.89.refs_1_.refs_5_.refs_10_), channel_id=1, source_target_pairs={{0,2},{1,3},{2,0},{3,1},{4,6},{5,7},{6,4},{7,5},{8,10},{9,11},{10,... | collective-permute-start | bytes 2162696 | tf_op jit(solution)/shard_map/ppermute | solution.py:78
  32.4 26.3 %collective-permute-start.6 = (bf16[512,256]{1,0:T(8,128)(2,1)}, bf16[512,256]{1,0:T(8,128)(2,1)S(1)}, u32[]{:S(2)}, u32[]{:S(2)}) collective-permute-start(bf16[512,256]{1,0:T(8,128)(2,1)} %gate.13.refs_2_.refs_5_), channel_id=1, source_target_pairs={{0,4},{4,8},{8,12},{1,5},{5,9},{9,13},{2,6},{6,10},{10,14},{3,7},{... | collective-permute-start | bytes 786440 | tf_op jit(solution)/shard_map/ppermute | solution.py:104
  38.1 20.6 %collective-permute-start.7 = (bf16[512,256]{1,0:T(8,128)(2,1)}, bf16[512,256]{1,0:T(8,128)(2,1)S(1)}, u32[]{:S(2)}, u32[]{:S(2)}) collective-permute-start(bf16[512,256]{1,0:T(8,128)(2,1)} %gate.13.refs_2_.refs_5_), channel_id=1, source_target_pairs={{4,0},{8,4},{12,8},{5,1},{9,5},{13,9},{6,2},{10,6},{14,10},{7,3},{... | collective-permute-start | bytes 786440 | tf_op jit(solution)/shard_map/ppermute | solution.py:105
  39.4 20.0 %collective-permute-start.8 = (bf16[512,256]{1,0:T(8,128)(2,1)}, bf16[512,256]{1,0:T(8,128)(2,1)S(1)}, u32[]{:S(2)}, u32[]{:S(2)}) collective-permute-start(bf16[512,256]{1,0:T(8,128)(2,1)} %gate.13.refs_2_.refs_5_), channel_id=1, source_target_pairs={{0,8},{4,12},{8,0},{12,4},{1,9},{5,13},{9,1},{13,5},{2,10},{6,14},... | collective-permute-start | bytes 786440 | tf_op jit(solution)/shard_map/ppermute | solution.py:109
  41.7 24.8 %collective-permute-start.17 = (bf16[4,32,2816]{2,1,0:T(8,128)(2,1)S(1)}, bf16[4,32,2816]{2,1,0:T(8,128)(2,1)S(1)}, u32[]{:S(2)}, u32[]{:S(2)}) collective-permute-start(bf16[4,32,2816]{2,1,0:T(8,128)(2,1)S(1)} %stack.89.refs_1_.refs_5_.refs_10_), channel_id=1, source_target_pairs={{0,16},{16,0},{1,17},{17,1},{2,18},{18,2},{3,19},{19,3},{4,20},{20... | collective-permute-start | bytes 2162696 | tf_op jit(solution)/shard_map/ppermute | solution.py:78
  58.1 27.9 %collective-permute-start.19 = (bf16[4,32,2816]{2,1,0:T(8,128)(2,1)S(1)}, bf16[4,32,2816]{2,1,0:T(8,128)(2,1)S(1)}, u32[]{:S(2)}, u32[]{:S(2)}) collective-permute-start(bf16[4,32,2816]{2,1,0:T(8,128)(2,1)S(1)} %gate.16.refs_0_), channel_id=1, source_target_pairs={{0,16},{16,0},{1,17},{17,1},{2,18},{18,2},{3,19},{19,3},{4,20},{20... | collective-permute-start | bytes 2162696 | tf_op jit(solution)/shard_map/ppermute | solution.py:78
  60.1 16.3 %collective-permute-start.10 = (bf16[512,256]{1,0:T(8,128)(2,1)S(1)}, bf16[512,256]{1,0:T(8,128)(2,1)S(1)}, u32[]{:S(2)}, u32[]{:S(2)}) collective-permute-start(bf16[512,256]{1,0:T(8,128)(2,1)S(1)} %gate.15.refs_0_), channel_id=1, source_target_pairs={{4,0},{8,4},{12,8},{5,1},{9,5},{13,9},{6,2},{10,6},{14,10},{7,3},{... | collective-permute-start | bytes 786440 | tf_op jit(solution)/shard_map/ppermute | solution.py:105
  94.2 25.1 %collective-permute-start.25 = (bf16[128,1792]{1,0:T(8,128)(2,1)S(1)}, bf16[128,1792]{1,0:T(8,128)(2,1)S(1)}, u32[]{:S(2)}, u32[]{:S(2)}) collective-permute-start(bf16[128,1792]{1,0:T(8,128)(2,1)S(1)} %get-tuple-element.33), channel_id=1, source_target_pairs={{0,8},{4,12},{8,0},{12,4},{1,9},{5,13},{9,1},{13,5},{2,10},{6,14},... | collective-permute-start | bytes 1376264 | tf_op jit(solution)/shard_map/ppermute | solution.py:109
  98.1 23.1 %collective-permute-start.21 = (bf16[128,1792]{1,0:T(8,128)(2,1)S(1)}, bf16[128,1792]{1,0:T(8,128)(2,1)S(1)}, u32[]{:S(2)}, u32[]{:S(2)}) collective-permute-start(bf16[128,1792]{1,0:T(8,128)(2,1)S(1)} %get-tuple-element.32.refs_0_), channel_id=1, source_target_pairs={{0,4},{4,8},{8,12},{1,5},{5,9},{9,13},{2,6},{6,10},{10,14},{3,7},{... | collective-permute-start | bytes 1376264 | tf_op jit(solution)/shard_map/ppermute | solution.py:104
  102.5 21.7 %collective-permute-start.22 = (bf16[128,1792]{1,0:T(8,128)(2,1)S(1)}, bf16[128,1792]{1,0:T(8,128)(2,1)S(1)}, u32[]{:S(2)}, u32[]{:S(2)}) collective-permute-start(bf16[128,1792]{1,0:T(8,128)(2,1)S(1)} %get-tuple-element.32.refs_0_), channel_id=1, source_target_pairs={{4,0},{8,4},{12,8},{5,1},{9,5},{13,9},{6,2},{10,6},{14,10},{7,3},{... | collective-permute-start | bytes 1376264 | tf_op jit(solution)/shard_map/ppermute | solution.py:105
  119.8 28.9 %collective-permute-start.29 = (bf16[128,1792]{1,0:T(8,128)(2,1)S(1)}, bf16[128,1792]{1,0:T(8,128)(2,1)S(1)}, u32[]{:S(2)}, u32[]{:S(2)}) collective-permute-start(bf16[128,1792]{1,0:T(8,128)(2,1)S(1)} %gate.22), channel_id=1, source_target_pairs={{0,8},{4,12},{8,0},{12,4},{1,9},{5,13},{9,1},{13,5},{2,10},{6,14},... | collective-permute-start | bytes 1376264 | tf_op jit(solution)/shard_map/ppermute | solution.py:109
  119.9 35.1 %collective-permute-start.26 = (bf16[128,1792]{1,0:T(8,128)(2,1)S(1)}, bf16[128,1792]{1,0:T(8,128)(2,1)S(1)}, u32[]{:S(2)}, u32[]{:S(2)}) collective-permute-start(bf16[128,1792]{1,0:T(8,128)(2,1)S(1)} %collective-permute-done.25.refs_1_.refs_3_), channel_id=1, source_target_pairs={{4,0},{8,12},{5,1},{9,13},{6,2},{10,14},{7,3},{11,15},{20,16},{24,... | collective-permute-start | bytes 1376264 | tf_op jit(solution)/shard_map/ppermute | solution.py:110
  124.8 30.3 %collective-permute-start.23 = (bf16[128,1792]{1,0:T(8,128)(2,1)S(1)}, bf16[128,1792]{1,0:T(8,128)(2,1)S(1)}, u32[]{:S(2)}, u32[]{:S(2)}) collective-permute-start(bf16[128,1792]{1,0:T(8,128)(2,1)S(1)} %gate.20.refs_0_), channel_id=1, source_target_pairs={{0,4},{4,8},{8,12},{1,5},{5,9},{9,13},{2,6},{6,10},{10,14},{3,7},{... | collective-permute-start | bytes 1376264 | tf_op jit(solution)/shard_map/ppermute | solution.py:104
  149.3 29.0 %collective-permute-start.33 = (bf16[128,1792]{1,0:T(8,128)(2,1)S(1)}, bf16[128,1792]{1,0:T(8,128)(2,1)S(1)}, u32[]{:S(2)}, u32[]{:S(2)}) collective-permute-start(bf16[128,1792]{1,0:T(8,128)(2,1)S(1)} %gate.24), channel_id=1, source_target_pairs={{0,8},{4,12},{8,0},{12,4},{1,9},{5,13},{9,1},{13,5},{2,10},{6,14},... | collective-permute-start | bytes 1376264 | tf_op jit(solution)/shard_map/ppermute | solution.py:109
  153.8 26.4 %collective-permute-start.30 = (bf16[128,1792]{1,0:T(8,128)(2,1)S(1)}, bf16[128,1792]{1,0:T(8,128)(2,1)S(1)}, u32[]{:S(2)}, u32[]{:S(2)}) collective-permute-start(bf16[128,1792]{1,0:T(8,128)(2,1)S(1)} %collective-permute-done.29.refs_1_.refs_3_), channel_id=1, source_target_pairs={{4,0},{8,12},{5,1},{9,13},{6,2},{10,14},{7,3},{11,15},{20,16},{24,... | collective-permute-start | bytes 1376264 | tf_op jit(solution)/shard_map/ppermute | solution.py:110
  158.7 24.1 %collective-permute-start.27 = (bf16[128,1792]{1,0:T(8,128)(2,1)S(1)}, bf16[128,1792]{1,0:T(8,128)(2,1)S(1)}, u32[]{:S(2)}, u32[]{:S(2)}) collective-permute-start(bf16[128,1792]{1,0:T(8,128)(2,1)S(1)} %gate.21.refs_0_), channel_id=1, source_target_pairs={{0,4},{4,8},{8,12},{1,5},{5,9},{9,13},{2,6},{6,10},{10,14},{3,7},{... | collective-permute-start | bytes 1376264 | tf_op jit(solution)/shard_map/ppermute | solution.py:104
  171.9 17.8 %collective-permute-start.28 = (bf16[128,1792]{1,0:T(8,128)(2,1)S(1)}, bf16[128,1792]{1,0:T(8,128)(2,1)S(1)}, u32[]{:S(2)}, u32[]{:S(2)}) collective-permute-start(bf16[128,1792]{1,0:T(8,128)(2,1)S(1)} %gate.21.refs_0_), channel_id=1, source_target_pairs={{4,0},{8,4},{12,8},{5,1},{9,5},{13,9},{6,2},{10,6},{14,10},{7,3},{... | collective-permute-start | bytes 1376264 | tf_op jit(solution)/shard_map/ppermute | solution.py:105
  178.8 29.0 %collective-permute-start.34 = (bf16[128,1792]{1,0:T(8,128)(2,1)S(1)}, bf16[128,1792]{1,0:T(8,128)(2,1)S(1)}, u32[]{:S(2)}, u32[]{:S(2)}) collective-permute-start(bf16[128,1792]{1,0:T(8,128)(2,1)S(1)} %gate.25), channel_id=1, source_target_pairs={{0,8},{4,12},{8,0},{12,4},{1,9},{5,13},{9,1},{13,5},{2,10},{6,14},... | collective-permute-start | bytes 1376264 | tf_op jit(solution)/shard_map/ppermute | solution.py:109
  178.9 37.2 %collective-permute-start.36 = (bf16[128,1792]{1,0:T(8,128)(2,1)S(1)}, bf16[128,1792]{1,0:T(8,128)(2,1)S(1)}, u32[]{:S(2)}, u32[]{:S(2)}) collective-permute-start(bf16[128,1792]{1,0:T(8,128)(2,1)S(1)} %collective-permute-done.33.refs_1_.refs_3_), channel_id=1, source_target_pairs={{4,0},{8,12},{5,1},{9,13},{6,2},{10,14},{7,3},{11,15},{20,16},{24,... | collective-permute-start | bytes 1376264 | tf_op jit(solution)/shard_map/ppermute | solution.py:110
  190.3 29.2 %collective-permute-start.31 = (bf16[128,1792]{1,0:T(8,128)(2,1)S(1)}, bf16[128,1792]{1,0:T(8,128)(2,1)S(1)}, u32[]{:S(2)}, u32[]{:S(2)}) collective-permute-start(bf16[128,1792]{1,0:T(8,128)(2,1)S(1)} %gate.23.refs_0_), channel_id=1, source_target_pairs={{0,4},{4,8},{8,12},{1,5},{5,9},{9,13},{2,6},{6,10},{10,14},{3,7},{... | collective-permute-start | bytes 1376264 | tf_op jit(solution)/shard_map/ppermute | solution.py:104
  201.4 18.1 %collective-permute-start.32 = (bf16[128,1792]{1,0:T(8,128)(2,1)S(1)}, bf16[128,1792]{1,0:T(8,128)(2,1)S(1)}, u32[]{:S(2)}, u32[]{:S(2)}) collective-permute-start(bf16[128,1792]{1,0:T(8,128)(2,1)S(1)} %gate.23.refs_0_), channel_id=1, source_target_pairs={{4,0},{8,4},{12,8},{5,1},{9,5},{13,9},{6,2},{10,6},{14,10},{7,3},{... | collective-permute-start | bytes 1376264 | tf_op jit(solution)/shard_map/ppermute | solution.py:105
  207.8 20.2 %collective-permute-start.35 = (bf16[128,1792]{1,0:T(8,128)(2,1)S(1)}, bf16[128,1792]{1,0:T(8,128)(2,1)S(1)}, u32[]{:S(2)}, u32[]{:S(2)}) collective-permute-start(bf16[128,1792]{1,0:T(8,128)(2,1)S(1)} %collective-permute-done.34.refs_3_), channel_id=1, source_target_pairs={{4,0},{8,12},{5,1},{9,13},{6,2},{10,14},{7,3},{11,15},{20,16},{24,... | collective-permute-start | bytes 1376264 | tf_op jit(solution)/shard_map/ppermute | solution.py:110
  (20 other events, 280.6 us)

commit v15 on v14

--- a/solution.py
+++ b/solution.py
@@ -16,7 +16,7 @@
 CHUNK = 128
 KEY_BLOCK = 512
 ATTEND_FLOPS = 16
-RAW_PART = 8
+RAW_PART = 4
 TAIL = 16
 DIGIT = 32
 ANYWHERE = pl.BlockSpec(memory_space=pl.ANY)
@@ -202,6 +202,7 @@
     ]
     if raw:
         moves.append((r_hbm.at[:, pl.ds(keep, raw)], refs[2 + count]))
+        moves.append((r_hbm.at[:, pl.ds(keep, raw)], refs[3 + count]))
     copies = [pltpu.make_async_copy(*move, sems.at[n]) for n, move in enumerate(moves)]
     for copy in copies:
         copy.start()
@@ -247,7 +248,7 @@
     width = keep + table.count * (slab - keep)
     shapes += [jax.ShapeDtypeStruct((part, width), out_weight.dtype)] * table.count
     if keep < slab:
-        shapes.append(jax.ShapeDtypeStruct((rows, slab - keep), residual.dtype))
+        shapes += [jax.ShapeDtypeStruct((rows, slab - keep), residual.dtype)] * 2
     return call(
         functools.partial(prepare_kernel, table, slab, keep),
         "prepare",
@@ -261,7 +262,7 @@
             pltpu.VMEM(queries.shape, jnp.bfloat16),
             pltpu.VMEM(span_pairs.shape, jnp.bfloat16),
             pltpu.VMEM((part, out_weight.shape[1]), out_weight.dtype),
-            pltpu.SemaphoreType.DMA((5,)),
+            pltpu.SemaphoreType.DMA((6,)),
         ],
         vmem=0,
     )
@@ -616,10 +617,18 @@
         attend(table, info, q_turned, pieces, slots, number * half, half, chunk)
         for number in range(halves)
     ]
-    residuals = line_gather(own_raw[0], count) if raw else []
-    ready = [gate(info, mixed[0], residuals[1:4] or residuals), *mixed[1:]] if raw else mixed
-    attention = [line_gather(value, count) for value in ready]
-    before = [*attention[0][1:], *mixed[1:], *residuals[4:]]
+    residuals, early = [], ()
+    if raw and count == 4:
+        early = line_far(own_raw[0])
+    attention = [
+        line_gather(gate(info, value, early[:1]) if early else value, count) for value in mixed
+    ]
+    if early:
+        near = gate(info, cuts[count + 1], attention[0][3:4])
+        residuals = [near, *line_near(near), *early]
+    elif raw:
+        residuals = line_gather(own_raw[0], count)
+    before = [*attention[0][1:], *mixed[1:], *residuals[1:3], *residuals[4:]]
     weights = plane_gather(
         own_weights,
         groups,

time: 232 us -> 239 us (1.030)
  waiting for transfers between devices: 84.2 us -> 104 us
  starting transfers between devices: 91.8 us -> 80 us
  local copies, waits for them, and re-layouts: 4.18 us -> 1.59 us
    ppermute x6, starting transfers between devices: 56.7 us -> 46 us  [line_near(): up = lax.ppermute(value, 'tensor', [(0, 1), (1, 2), (2, 3)])]
    ppermute x6, waiting for transfers between devices: 13.6 us -> 20.3 us  [line_near(): return (up, lax.ppermute(value, 'tensor', [(1, 0), (2, 1), (3, 2)]))]
    ppermute x6, waiting for transfers between devices: 17.1 us -> 21.6 us  [line_far(): return (far, lax.ppermute(far, 'tensor', [(1, 0), (2, 3)]))]
    ppermute x3, waiting for transfers between devices: 0.01 us -> 3.88 us  [plane_gather(): held[mask | bit] = lax.ppermute(held[mask], axis, pairs)]
    ppermute x3, waiting for transfers between devices: 10.4 us -> 13.6 us  [per_device(): parts.append(lax.ppermute(cuts[shift], 'tensor', pairs))]
    unnamed x14, local copies, waits for them, and re-layouts: 3.59 us -> 0.96 us
    pallas_call x22 -> x23, Pallas kernels: 46.9 us -> 47.9 us  [call(): pl.pallas_call(kernel, grid_spec=pltpu.PrefetchScalarGridSpec(num_scalar_...]
  transfers between devices with their start and end apart: 37 -> 37, of which waited for: 18 -> 20; matrix products, arithmetic and copies ran while one was open for 0% -> 0% of each run, Pallas kernels for 15% -> 15%
where the time goes in v15:
time: 239 us; the launch traced here: 238 us
  waiting for transfers between devices  104 us (44%)
  starting transfers between devices  80 us (33%)
  Pallas kernels  47.9 us (20%)
  between operations  2.45 us (1%)
    pallas_call x23, Pallas kernels, call(): pl.pallas_call(kernel, grid_spec=pltpu.PrefetchScalarGridSpec(num_scalar_...  47.9 us
    ppermute x6, starting transfers between devices, line_near(): up = lax.ppermute(value, 'tensor', [(0, 1), (1, 2), (2, 3)])  46 us
    ppermute x6, waiting for transfers between devices, line_far(): far = lax.ppermute(value, 'tensor', [(0, 2), (1, 3), (2, 0), (3, 1)])  39.9 us
    ppermute x6, waiting for transfers between devices, line_far(): return (far, lax.ppermute(far, 'tensor', [(1, 0), (2, 3)]))  21.6 us
    ppermute x6, waiting for transfers between devices, line_near(): return (up, lax.ppermute(value, 'tensor', [(1, 0), (2, 1), (3, 2)]))  20.3 us
    ppermute x3, waiting for transfers between devices, per_device(): parts.append(lax.ppermute(cuts[shift], 'tensor', pairs))  13.6 us
    ppermute x6, starting transfers between devices, line_far(): return (far, lax.ppermute(far, 'tensor', [(1, 0), (2, 3)]))  7.85 us
    ppermute x6, starting transfers between devices, line_near(): return (up, lax.ppermute(value, 'tensor', [(1, 0), (2, 1), (3, 2)]))  7.74 us
  transfers between devices with their start and end apart: 37, of which 20 were waited for; matrix products, arithmetic and copies ran while one was open for 0% of the time, Pallas kernels for 15%

profile of v15, /device:TPU:0, one launch (start us, length us, event | category | flops | bytes accessed | tf_op | source)
XLA Modules:
  0.0 238.1 jit_solution(10723361727583642052)
XLA Ops:
  4.6 5.2 %prepare.1 = (bf16[512,256]{1,0:T(8,128)(2,1)}, bf16[1552,256]{1,0:T(8,128)(2,1)}, bf16[32,3584]{1,0:T(8,128)(2,1)}, bf16[32,3584]{1,0:T(8,128)(2,1)}, bf16[32,3...) custom-call(s32[20]{0:T(128)} %stack.86.info, ...), custom_call_target="tpu_custom_call" | custom-call | flops 1 | bytes 1 | tf_op jit(solution)/shard_map/prepare/pallas_call | solution.py:167
  18.4 5.2 %collective-permute-done.2.refs_1_ = bf16[32,3584]{1,0:T(8,128)(2,1)S(1)} collective-permute-done((bf16[32,3584]{1,0:T(8,128)(2,1)}, bf16[32,3584]{1,0:T(8,128)(2,1)S(1)}, u32[]{:S(2)}, u32[]{:S(2)}) %collective-permute-start.2) | collective-permute-done | bytes 229408 | tf_op jit(solution)/shard_map/ppermute | solution.py:609
  23.5 8.4 %collective-permute-done.3.refs_2_ = bf16[32,3584]{1,0:T(8,128)(2,1)S(1)} collective-permute-done((bf16[32,3584]{1,0:T(8,128)(2,1)}, bf16[32,3584]{1,0:T(8,128)(2,1)S(1)}, u32[]{:S(2)}, u32[]{:S(2)}) %collective-permute-start.3) | collective-permute-done | bytes 229408 | tf_op jit(solution)/shard_map/ppermute | solution.py:609
  35.3 4.5 %collective-permute-start.6 = (bf16[512,512]{1,0:T(8,128)(2,1)}, bf16[512,512]{1,0:T(8,128)(2,1)S(1)}, u32[]{:S(2)}, u32[]{:S(2)}) collective-permute-start(bf16[512,512]{1,0:T(8,128)(2,1)} %gate.14.refs_2_), channel_id=1, source_target_pairs={{0,8},{4,12},{8,0},{12,4},{1,9},{5,13},{9,1},{13,5},{2,10},{6,14},... | collective-permute-start | bytes 1572872 | tf_op jit(solution)/shard_map/ppermute | solution.py:109
  41.4 12.2 %attend.1.refs_0_.refs_1_ = bf16[512,256]{1,0:T(8,128)(2,1)S(1)} custom-call(s32[20]{0:T(128)S(1)} %copy-done.3, bf16[512,256]{1,0:T(8,128)(2,1)S(1)} %copy-done.6, bf16[1552,256]{1,0:T(8,128)(2,1)S(1)} %copy-done.5, bf16[1552,256]{1,0:T(8,128)(2,1)S(1)} %collective-permute-done.refs_1_, bf16[1552,256]{1,0:T(8,128)(2,1)S(1)} %gate.15.refs_2_, ...), custom_call_target="tpu_custom_call" | custom-call | flops 12884901888 | bytes 1 | tf_op jit(solution)/shard_map/attend/pallas_call | solution.py:167
  53.6 3.9 %collective-permute-done.15.refs_0_ = bf16[4,32,3584]{2,1,0:T(8,128)(2,1)S(1)} collective-permute-done((bf16[4,32,3584]{2,1,0:T(8,128)(2,1)S(1)}, bf16[4,32,3584]{2,1,0:T(8,128)(2,1)S(1)}, u32[]{:S(2)}, u32[]{:S(2)}) %collective-permute-start.15) | collective-permute-done | bytes 917536 | tf_op jit(solution)/shard_map/ppermute | solution.py:78
  59.6 3.9 %collective-permute-done.6.refs_1_.refs_8_ = bf16[512,512]{1,0:T(8,128)(2,1)S(1)} collective-permute-done((bf16[512,512]{1,0:T(8,128)(2,1)}, bf16[512,512]{1,0:T(8,128)(2,1)S(1)}, u32[]{:S(2)}, u32[]{:S(2)}) %collective-permute-start.6) | collective-permute-done | bytes 524320 | tf_op jit(solution)/shard_map/ppermute | solution.py:109
  64.6 5.5 %collective-permute-start.7 = (bf16[512,256]{1,0:T(8,128)(2,1)S(1)}, bf16[512,256]{1,0:T(8,128)(2,1)S(1)}, u32[]{:S(2)}, u32[]{:S(2)}) collective-permute-start(bf16[512,256]{1,0:T(8,128)(2,1)S(1)} %gate.16.refs_0_), channel_id=1, source_target_pairs={{0,4},{4,8},{8,12},{1,5},{5,9},{9,13},{2,6},{6,10},{10,14},{3,7},{... | collective-permute-start | bytes 786440 | tf_op jit(solution)/shard_map/ppermute | solution.py:104
  71.4 7.2 %collective-permute-done.9.refs_1_.refs_3_ = bf16[512,256]{1,0:T(8,128)(2,1)S(1)} collective-permute-done((bf16[512,256]{1,0:T(8,128)(2,1)S(1)}, bf16[512,256]{1,0:T(8,128)(2,1)S(1)}, u32[]{:S(2)}, u32[]{:S(2)}) %collective-permute-start.9) | collective-permute-done | bytes 262176 | tf_op jit(solution)/shard_map/ppermute | solution.py:109
  80.4 4.7 %collective-permute-start.11 = (bf16[512,512]{1,0:T(8,128)(2,1)S(1)}, bf16[512,512]{1,0:T(8,128)(2,1)S(1)}, u32[]{:S(2)}, u32[]{:S(2)}) collective-permute-start(bf16[512,512]{1,0:T(8,128)(2,1)S(1)} %gate.17.refs_5_), channel_id=1, source_target_pairs={{0,4},{4,8},{8,12},{1,5},{5,9},{9,13},{2,6},{6,10},{10,14},{3,7},{... | collective-permute-start | bytes 1572872 | tf_op jit(solution)/shard_map/ppermute | solution.py:104
  86.5 8.9 %collective-permute-done.8.refs_2_ = bf16[512,256]{1,0:T(8,128)(2,1)S(1)} collective-permute-done((bf16[512,256]{1,0:T(8,128)(2,1)S(1)}, bf16[512,256]{1,0:T(8,128)(2,1)S(1)}, u32[]{:S(2)}, u32[]{:S(2)}) %collective-permute-start.8) | collective-permute-done | bytes 262176 | tf_op jit(solution)/shard_map/ppermute | solution.py:105
  97.3 14.7 %collective-permute-done.10.refs_4_ = bf16[512,256]{1,0:T(8,128)(2,1)S(1)} collective-permute-done((bf16[512,256]{1,0:T(8,128)(2,1)S(1)}, bf16[512,256]{1,0:T(8,128)(2,1)S(1)}, u32[]{:S(2)}, u32[]{:S(2)}) %collective-permute-start.10) | collective-permute-done | bytes 262176 | tf_op jit(solution)/shard_map/ppermute | solution.py:110
  117.1 3.9 %project.1 = (bf16[128,1536]{1,0:T(8,128)(2,1)S(1)}, bf16[128,1536]{1,0:T(8,128)(2,1)S(1)}, bf16[128,1536]{1,0:T(8,128)(2,1)S(1)}, bf16[128,1536]{1,0:T(8,128)(2...) custom-call(s32[20]{0:T(128)S(1)} %copy-done.3, ...), custom_call_target="tpu_custom_call" | custom-call | flops 1 | bytes 1 | tf_op jit(solution)/shard_map/project/pallas_call | solution.py:167
  124.2 16.4 %collective-permute-done.25.refs_1_.refs_3_ = bf16[128,1536]{1,0:T(8,128)(2,1)S(1)} collective-permute-done((bf16[128,1536]{1,0:T(8,128)(2,1)S(1)}, bf16[128,1536]{1,0:T(8,128)(2,1)S(1)}, u32[]{:S(2)}, u32[]{:S(2)}) %collective-permute-start.25) | collective-permute-done | bytes 393248 | tf_op jit(solution)/shard_map/ppermute | solution.py:109
  146.1 14.5 %collective-permute-start.23 = (bf16[128,1536]{1,0:T(8,128)(2,1)S(1)}, bf16[128,1536]{1,0:T(8,128)(2,1)S(1)}, u32[]{:S(2)}, u32[]{:S(2)}) collective-permute-start(bf16[128,1536]{1,0:T(8,128)(2,1)S(1)} %gate.22.refs_0_), channel_id=1, source_target_pairs={{0,4},{4,8},{8,12},{1,5},{5,9},{9,13},{2,6},{6,10},{10,14},{3,7},{... | collective-permute-start | bytes 1179656 | tf_op jit(solution)/shard_map/ppermute | solution.py:104
  161.8 4.1 %collective-permute-done.29.refs_1_.refs_3_ = bf16[128,1536]{1,0:T(8,128)(2,1)S(1)} collective-permute-done((bf16[128,1536]{1,0:T(8,128)(2,1)S(1)}, bf16[128,1536]{1,0:T(8,128)(2,1)S(1)}, u32[]{:S(2)}, u32[]{:S(2)}) %collective-permute-start.29) | collective-permute-done | bytes 393248 | tf_op jit(solution)/shard_map/ppermute | solution.py:109
  166.6 4.6 %project_raw.1 = (bf16[512,2048]{1,0:T(8,128)(2,1)S(1)}, bf16[512,2048]{1,0:T(8,128)(2,1)}) custom-call(s32[20]{0:T(128)S(1)} %copy-done.3, bf16[512,256]{1,0:T(8,128)(2,1)S(1)} %gate.16.refs_0_, bf16[512,256]{1,0:T(8,128)(2,1)S(1)} %collective-permute-done.7.refs_1_, ...), custom_call_target="tpu_custom_call", output_to_operand_aliasing={{1}: (19, {})} | custom-call | flops 1 | bytes 1 | tf_op jit(solution)/shard_map/project_raw/pallas_call | solution.py:167
  174.8 11.0 %collective-permute-start.27 = (bf16[128,1536]{1,0:T(8,128)(2,1)S(1)}, bf16[128,1536]{1,0:T(8,128)(2,1)S(1)}, u32[]{:S(2)}, u32[]{:S(2)}) collective-permute-start(bf16[128,1536]{1,0:T(8,128)(2,1)S(1)} %gate.23.refs_0_), channel_id=1, source_target_pairs={{0,4},{4,8},{8,12},{1,5},{5,9},{9,13},{2,6},{6,10},{10,14},{3,7},{... | collective-permute-start | bytes 1179656 | tf_op jit(solution)/shard_map/ppermute | solution.py:104
  187.1 4.1 %collective-permute-done.33.refs_1_.refs_3_ = bf16[128,1536]{1,0:T(8,128)(2,1)S(1)} collective-permute-done((bf16[128,1536]{1,0:T(8,128)(2,1)S(1)}, bf16[128,1536]{1,0:T(8,128)(2,1)S(1)}, u32[]{:S(2)}, u32[]{:S(2)}) %collective-permute-start.33) | collective-permute-done | bytes 393248 | tf_op jit(solution)/shard_map/ppermute | solution.py:109
  195.3 6.7 %collective-permute-done.28.refs_2_ = bf16[128,1536]{1,0:T(8,128)(2,1)S(1)} collective-permute-done((bf16[128,1536]{1,0:T(8,128)(2,1)S(1)}, bf16[128,1536]{1,0:T(8,128)(2,1)S(1)}, u32[]{:S(2)}, u32[]{:S(2)}) %collective-permute-start.28) | collective-permute-done | bytes 393248 | tf_op jit(solution)/shard_map/ppermute | solution.py:105
  202.6 8.6 %collective-permute-start.31 = (bf16[128,1536]{1,0:T(8,128)(2,1)S(1)}, bf16[128,1536]{1,0:T(8,128)(2,1)S(1)}, u32[]{:S(2)}, u32[]{:S(2)}) collective-permute-start(bf16[128,1536]{1,0:T(8,128)(2,1)S(1)} %gate.25.refs_0_), channel_id=1, source_target_pairs={{0,4},{4,8},{8,12},{1,5},{5,9},{9,13},{2,6},{6,10},{10,14},{3,7},{... | collective-permute-start | bytes 1179656 | tf_op jit(solution)/shard_map/ppermute | solution.py:104
  212.4 4.1 %collective-permute-done.34.refs_3_ = bf16[128,1536]{1,0:T(8,128)(2,1)S(1)} collective-permute-done((bf16[128,1536]{1,0:T(8,128)(2,1)S(1)}, bf16[128,1536]{1,0:T(8,128)(2,1)S(1)}, u32[]{:S(2)}, u32[]{:S(2)}) %collective-permute-start.34) | collective-permute-done | bytes 393248 | tf_op jit(solution)/shard_map/ppermute | solution.py:109
  217.8 3.4 %norm.4.refs_6_ = bf16[512,8192]{1,0:T(8,128)(2,1)} custom-call(s32[20]{0:T(128)S(1)} %copy-done.3, f32[1,8192]{1,0:T(1,128)S(1)} %bitcast.23, bf16[128,1536]{1,0:T(8,128)(2,1)S(1)} %get-tuple-element.34.refs_0_, bf16[128,1536]{1,0:T(8,128)(2,1)S(1)} %collective-permute-done.21.refs_1_, bf16[128,1536]{1,0:T(8,128)(2,1)S(1)} %collective-permute-done.22.refs_2_, ...), custom_call_target="tpu_custom_call" | custom-call | flops 1 | bytes 1 | tf_op jit(solution)/shard_map/norm/pallas_call | solution.py:167
  228.2 6.5 %collective-permute-done.35.refs_4_ = bf16[128,1536]{1,0:T(8,128)(2,1)S(1)} collective-permute-done((bf16[128,1536]{1,0:T(8,128)(2,1)S(1)}, bf16[128,1536]{1,0:T(8,128)(2,1)S(1)}, u32[]{:S(2)}, u32[]{:S(2)}) %collective-permute-start.35) | collective-permute-done | bytes 393248 | tf_op jit(solution)/shard_map/ppermute | solution.py:110
  (92 shorter events, 63.4 us)
Async XLA Ops:
  9.8 24.2 %collective-permute-start.1 = (bf16[1552,256]{1,0:T(8,128)(2,1)}, bf16[1552,256]{1,0:T(8,128)(2,1)S(1)}, u32[]{:S(2)}, u32[]{:S(2)}) collective-permute-start(bf16[1552,256]{1,0:T(8,128)(2,1)} %get-tuple-element.22.refs_0_), channel_id=1, source_target_pairs={{0,2},{1,3},{2,0},{3,1},{4,6},{5,7},{6,4},{7,5},{8,10},{9,11},{10,... | collective-permute-start | bytes 2383880 | tf_op jit(solution)/shard_map/ppermute | solution.py:43
  14.5 17.5 %collective-permute-start.3 = (bf16[32,3584]{1,0:T(8,128)(2,1)}, bf16[32,3584]{1,0:T(8,128)(2,1)S(1)}, u32[]{:S(2)}, u32[]{:S(2)}) collective-permute-start(bf16[32,3584]{1,0:T(8,128)(2,1)} %get-tuple-element.25), channel_id=1, source_target_pairs={{0,8},{4,12},{8,0},{12,4},{1,9},{5,13},{9,1},{13,5},{2,10},{6,14},... | collective-permute-start | bytes 688136 | tf_op jit(solution)/shard_map/ppermute | solution.py:609
  18.4 23.0 %collective-permute-start = (bf16[1552,256]{1,0:T(8,128)(2,1)}, bf16[1552,256]{1,0:T(8,128)(2,1)S(1)}, u32[]{:S(2)}, u32[]{:S(2)}) collective-permute-start(bf16[1552,256]{1,0:T(8,128)(2,1)} %get-tuple-element.22.refs_0_), channel_id=1, source_target_pairs={{0,1},{1,0},{2,3},{3,2},{4,5},{5,4},{6,7},{7,6},{8,9},{9,8},{10,11... | collective-permute-start | bytes 2383880 | tf_op jit(solution)/shard_map/ppermute | solution.py:43
  34.7 22.8 %collective-permute-start.15 = (bf16[4,32,3584]{2,1,0:T(8,128)(2,1)S(1)}, bf16[4,32,3584]{2,1,0:T(8,128)(2,1)S(1)}, u32[]{:S(2)}, u32[]{:S(2)}) collective-permute-start(bf16[4,32,3584]{2,1,0:T(8,128)(2,1)S(1)} %stack.89.refs_1_.refs_5_.refs_10_), channel_id=1, source_target_pairs={{0,2},{1,3},{2,0},{3,1},{4,6},{5,7},{6,4},{7,5},{8,10},{9,11},{10,... | collective-permute-start | bytes 2752520 | tf_op jit(solution)/shard_map/ppermute | solution.py:78
  35.3 28.2 %collective-permute-start.6 = (bf16[512,512]{1,0:T(8,128)(2,1)}, bf16[512,512]{1,0:T(8,128)(2,1)S(1)}, u32[]{:S(2)}, u32[]{:S(2)}) collective-permute-start(bf16[512,512]{1,0:T(8,128)(2,1)} %gate.14.refs_2_), channel_id=1, source_target_pairs={{0,8},{4,12},{8,0},{12,4},{1,9},{5,13},{9,1},{13,5},{2,10},{6,14},... | collective-permute-start | bytes 1572872 | tf_op jit(solution)/shard_map/ppermute | solution.py:109
  39.8 40.7 %collective-permute-start.17 = (bf16[4,32,3584]{2,1,0:T(8,128)(2,1)S(1)}, bf16[4,32,3584]{2,1,0:T(8,128)(2,1)S(1)}, u32[]{:S(2)}, u32[]{:S(2)}) collective-permute-start(bf16[4,32,3584]{2,1,0:T(8,128)(2,1)S(1)} %stack.89.refs_1_.refs_5_.refs_10_), channel_id=1, source_target_pairs={{0,16},{16,0},{1,17},{17,1},{2,18},{18,2},{3,19},{19,3},{4,20},{20... | collective-permute-start | bytes 2752520 | tf_op jit(solution)/shard_map/ppermute | solution.py:78
  58.0 54.0 %collective-permute-start.19 = (bf16[4,32,3584]{2,1,0:T(8,128)(2,1)S(1)}, bf16[4,32,3584]{2,1,0:T(8,128)(2,1)S(1)}, u32[]{:S(2)}, u32[]{:S(2)}) collective-permute-start(bf16[4,32,3584]{2,1,0:T(8,128)(2,1)S(1)} %gate.18.refs_0_), channel_id=1, source_target_pairs={{0,16},{16,0},{1,17},{17,1},{2,18},{18,2},{3,19},{19,3},{4,20},{20... | collective-permute-start | bytes 2752520 | tf_op jit(solution)/shard_map/ppermute | solution.py:78
  64.6 20.5 %collective-permute-start.7 = (bf16[512,256]{1,0:T(8,128)(2,1)S(1)}, bf16[512,256]{1,0:T(8,128)(2,1)S(1)}, u32[]{:S(2)}, u32[]{:S(2)}) collective-permute-start(bf16[512,256]{1,0:T(8,128)(2,1)S(1)} %gate.16.refs_0_), channel_id=1, source_target_pairs={{0,4},{4,8},{8,12},{1,5},{5,9},{9,13},{2,6},{6,10},{10,14},{3,7},{... | collective-permute-start | bytes 786440 | tf_op jit(solution)/shard_map/ppermute | solution.py:104
  70.1 27.2 %collective-permute-start.13 = (bf16[512,512]{1,0:T(8,128)(2,1)S(1)}, bf16[512,512]{1,0:T(8,128)(2,1)S(1)}, u32[]{:S(2)}, u32[]{:S(2)}) collective-permute-start(bf16[512,512]{1,0:T(8,128)(2,1)S(1)} %collective-permute-done.6.refs_1_.refs_8_), channel_id=1, source_target_pairs={{4,0},{8,12},{5,1},{9,13},{6,2},{10,14},{7,3},{11,15},{20,16},{24,... | collective-permute-start | bytes 1572872 | tf_op jit(solution)/shard_map/ppermute | solution.py:110
  80.4 31.6 %collective-permute-start.11 = (bf16[512,512]{1,0:T(8,128)(2,1)S(1)}, bf16[512,512]{1,0:T(8,128)(2,1)S(1)}, u32[]{:S(2)}, u32[]{:S(2)}) collective-permute-start(bf16[512,512]{1,0:T(8,128)(2,1)S(1)} %gate.17.refs_5_), channel_id=1, source_target_pairs={{0,4},{4,8},{8,12},{1,5},{5,9},{9,13},{2,6},{6,10},{10,14},{3,7},{... | collective-permute-start | bytes 1572872 | tf_op jit(solution)/shard_map/ppermute | solution.py:104
  85.2 26.8 %collective-permute-start.12 = (bf16[512,512]{1,0:T(8,128)(2,1)S(1)}, bf16[512,512]{1,0:T(8,128)(2,1)S(1)}, u32[]{:S(2)}, u32[]{:S(2)}) collective-permute-start(bf16[512,512]{1,0:T(8,128)(2,1)S(1)} %gate.17.refs_5_), channel_id=1, source_target_pairs={{4,0},{8,4},{12,8},{5,1},{9,5},{13,9},{6,2},{10,6},{14,10},{7,3},{... | collective-permute-start | bytes 1572872 | tf_op jit(solution)/shard_map/ppermute | solution.py:105
  121.0 19.6 %collective-permute-start.25 = (bf16[128,1536]{1,0:T(8,128)(2,1)S(1)}, bf16[128,1536]{1,0:T(8,128)(2,1)S(1)}, u32[]{:S(2)}, u32[]{:S(2)}) collective-permute-start(bf16[128,1536]{1,0:T(8,128)(2,1)S(1)} %get-tuple-element.35), channel_id=1, source_target_pairs={{0,8},{4,12},{8,0},{12,4},{1,9},{5,13},{9,1},{13,5},{2,10},{6,14},... | collective-permute-start | bytes 1179656 | tf_op jit(solution)/shard_map/ppermute | solution.py:109
  121.0 21.5 %collective-permute-start.21 = (bf16[128,1536]{1,0:T(8,128)(2,1)S(1)}, bf16[128,1536]{1,0:T(8,128)(2,1)S(1)}, u32[]{:S(2)}, u32[]{:S(2)}) collective-permute-start(bf16[128,1536]{1,0:T(8,128)(2,1)S(1)} %get-tuple-element.34.refs_0_), channel_id=1, source_target_pairs={{0,4},{4,8},{8,12},{1,5},{5,9},{9,13},{2,6},{6,10},{10,14},{3,7},{... | collective-permute-start | bytes 1179656 | tf_op jit(solution)/shard_map/ppermute | solution.py:104
  122.9 22.6 %collective-permute-start.22 = (bf16[128,1536]{1,0:T(8,128)(2,1)S(1)}, bf16[128,1536]{1,0:T(8,128)(2,1)S(1)}, u32[]{:S(2)}, u32[]{:S(2)}) collective-permute-start(bf16[128,1536]{1,0:T(8,128)(2,1)S(1)} %get-tuple-element.34.refs_0_), channel_id=1, source_target_pairs={{4,0},{8,4},{12,8},{5,1},{9,5},{13,9},{6,2},{10,6},{14,10},{7,3},{... | collective-permute-start | bytes 1179656 | tf_op jit(solution)/shard_map/ppermute | solution.py:105
  141.2 24.8 %collective-permute-start.29 = (bf16[128,1536]{1,0:T(8,128)(2,1)S(1)}, bf16[128,1536]{1,0:T(8,128)(2,1)S(1)}, u32[]{:S(2)}, u32[]{:S(2)}) collective-permute-start(bf16[128,1536]{1,0:T(8,128)(2,1)S(1)} %gate.24), channel_id=1, source_target_pairs={{0,8},{4,12},{8,0},{12,4},{1,9},{5,13},{9,1},{13,5},{2,10},{6,14},... | collective-permute-start | bytes 1179656 | tf_op jit(solution)/shard_map/ppermute | solution.py:109
  141.3 31.3 %collective-permute-start.26 = (bf16[128,1536]{1,0:T(8,128)(2,1)S(1)}, bf16[128,1536]{1,0:T(8,128)(2,1)S(1)}, u32[]{:S(2)}, u32[]{:S(2)}) collective-permute-start(bf16[128,1536]{1,0:T(8,128)(2,1)S(1)} %collective-permute-done.25.refs_1_.refs_3_), channel_id=1, source_target_pairs={{4,0},{8,12},{5,1},{9,13},{6,2},{10,14},{7,3},{11,15},{20,16},{24,... | collective-permute-start | bytes 1179656 | tf_op jit(solution)/shard_map/ppermute | solution.py:110
  146.1 26.5 %collective-permute-start.23 = (bf16[128,1536]{1,0:T(8,128)(2,1)S(1)}, bf16[128,1536]{1,0:T(8,128)(2,1)S(1)}, u32[]{:S(2)}, u32[]{:S(2)}) collective-permute-start(bf16[128,1536]{1,0:T(8,128)(2,1)S(1)} %gate.22.refs_0_), channel_id=1, source_target_pairs={{0,4},{4,8},{8,12},{1,5},{5,9},{9,13},{2,6},{6,10},{10,14},{3,7},{... | collective-permute-start | bytes 1179656 | tf_op jit(solution)/shard_map/ppermute | solution.py:104
  166.5 24.7 %collective-permute-start.33 = (bf16[128,1536]{1,0:T(8,128)(2,1)S(1)}, bf16[128,1536]{1,0:T(8,128)(2,1)S(1)}, u32[]{:S(2)}, u32[]{:S(2)}) collective-permute-start(bf16[128,1536]{1,0:T(8,128)(2,1)S(1)} %gate.26), channel_id=1, source_target_pairs={{0,8},{4,12},{8,0},{12,4},{1,9},{5,13},{9,1},{13,5},{2,10},{6,14},... | collective-permute-start | bytes 1179656 | tf_op jit(solution)/shard_map/ppermute | solution.py:109
  171.2 22.4 %collective-permute-start.30 = (bf16[128,1536]{1,0:T(8,128)(2,1)S(1)}, bf16[128,1536]{1,0:T(8,128)(2,1)S(1)}, u32[]{:S(2)}, u32[]{:S(2)}) collective-permute-start(bf16[128,1536]{1,0:T(8,128)(2,1)S(1)} %collective-permute-done.29.refs_1_.refs_3_), channel_id=1, source_target_pairs={{4,0},{8,12},{5,1},{9,13},{6,2},{10,14},{7,3},{11,15},{20,16},{24,... | collective-permute-start | bytes 1179656 | tf_op jit(solution)/shard_map/ppermute | solution.py:110
  174.8 20.5 %collective-permute-start.27 = (bf16[128,1536]{1,0:T(8,128)(2,1)S(1)}, bf16[128,1536]{1,0:T(8,128)(2,1)S(1)}, u32[]{:S(2)}, u32[]{:S(2)}) collective-permute-start(bf16[128,1536]{1,0:T(8,128)(2,1)S(1)} %gate.23.refs_0_), channel_id=1, source_target_pairs={{0,4},{4,8},{8,12},{1,5},{5,9},{9,13},{2,6},{6,10},{10,14},{3,7},{... | collective-permute-start | bytes 1179656 | tf_op jit(solution)/shard_map/ppermute | solution.py:104
  191.8 24.8 %collective-permute-start.34 = (bf16[128,1536]{1,0:T(8,128)(2,1)S(1)}, bf16[128,1536]{1,0:T(8,128)(2,1)S(1)}, u32[]{:S(2)}, u32[]{:S(2)}) collective-permute-start(bf16[128,1536]{1,0:T(8,128)(2,1)S(1)} %gate.27), channel_id=1, source_target_pairs={{0,8},{4,12},{8,0},{12,4},{1,9},{5,13},{9,1},{13,5},{2,10},{6,14},... | collective-permute-start | bytes 1179656 | tf_op jit(solution)/shard_map/ppermute | solution.py:109
  191.9 32.9 %collective-permute-start.36 = (bf16[128,1536]{1,0:T(8,128)(2,1)S(1)}, bf16[128,1536]{1,0:T(8,128)(2,1)S(1)}, u32[]{:S(2)}, u32[]{:S(2)}) collective-permute-start(bf16[128,1536]{1,0:T(8,128)(2,1)S(1)} %collective-permute-done.33.refs_1_.refs_3_), channel_id=1, source_target_pairs={{4,0},{8,12},{5,1},{9,13},{6,2},{10,14},{7,3},{11,15},{20,16},{24,... | collective-permute-start | bytes 1179656 | tf_op jit(solution)/shard_map/ppermute | solution.py:110
  202.6 25.6 %collective-permute-start.31 = (bf16[128,1536]{1,0:T(8,128)(2,1)S(1)}, bf16[128,1536]{1,0:T(8,128)(2,1)S(1)}, u32[]{:S(2)}, u32[]{:S(2)}) collective-permute-start(bf16[128,1536]{1,0:T(8,128)(2,1)S(1)} %gate.25.refs_0_), channel_id=1, source_target_pairs={{0,4},{4,8},{8,12},{1,5},{5,9},{9,13},{2,6},{6,10},{10,14},{3,7},{... | collective-permute-start | bytes 1179656 | tf_op jit(solution)/shard_map/ppermute | solution.py:104
  216.6 18.1 %collective-permute-start.35 = (bf16[128,1536]{1,0:T(8,128)(2,1)S(1)}, bf16[128,1536]{1,0:T(8,128)(2,1)S(1)}, u32[]{:S(2)}, u32[]{:S(2)}) collective-permute-start(bf16[128,1536]{1,0:T(8,128)(2,1)S(1)} %collective-permute-done.34.refs_3_), channel_id=1, source_target_pairs={{4,0},{8,12},{5,1},{9,13},{6,2},{10,14},{7,3},{11,15},{20,16},{24,... | collective-permute-start | bytes 1179656 | tf_op jit(solution)/shard_map/ppermute | solution.py:110
  (20 other events, 366.2 us)

commit v16 on v15

--- a/solution.py
+++ b/solution.py
@@ -619,13 +619,14 @@
     ]
     residuals, early = [], ()
     if raw and count == 4:
-        early = line_far(own_raw[0])
+        early = [lax.ppermute(own_raw[0], "tensor", [(0, 2), (1, 3), (2, 0), (3, 1)])]
     attention = [
         line_gather(gate(info, value, early[:1]) if early else value, count) for value in mixed
     ]
     if early:
-        near = gate(info, cuts[count + 1], attention[0][3:4])
-        residuals = [near, *line_near(near), *early]
+        near = gate(info, cuts[count + 1], attention[0][1:])
+        far = gate(info, early[0], attention[0][1:])
+        residuals = [near, *line_near(near), far, lax.ppermute(far, "tensor", [(1, 0), (2, 3)])]
     elif raw:
         residuals = line_gather(own_raw[0], count)
     before = [*attention[0][1:], *mixed[1:], *residuals[1:3], *residuals[4:]]

time: 239 us -> 241 us (level)
    ppermute x6 -> x5, waiting for transfers between devices: 21.6 us -> 11.5 us  [line_far(): return (far, lax.ppermute(far, 'tensor', [(1, 0), (2, 3)]))]
    ppermute x3, waiting for transfers between devices: 3.88 us -> 12.4 us  [plane_gather(): held[mask | bit] = lax.ppermute(held[mask], axis, pairs)]
    ppermute x6 -> x5, waiting for transfers between devices: 39.9 us -> 32 us  [line_far(): far = lax.ppermute(value, 'tensor', [(0, 2), (1, 3), (2, 0), (3, 1)])]
    ppermute x0 -> x2, waiting for transfers between devices: none -> 6.17 us  [the longest x1 5.46 us: per_device(): lax.ppermute(own_raw[0], 'tensor', [(0, 2), (1, 3), (2, 0), (3, 1)])]
    ppermute x0 -> x2, starting transfers between devices: none -> 5.76 us  [the longest x1 4.47 us: per_device(): lax.ppermute(own_raw[0], 'tensor', [(0, 2), (1, 3), (2, 0), (3, 1)])]
    ppermute x6 -> x5, starting transfers between devices: 5.31 us -> 0.29 us  [line_far(): far = lax.ppermute(value, 'tensor', [(0, 2), (1, 3), (2, 0), (3, 1)])]
    ppermute x6, waiting for transfers between devices: 20.3 us -> 24.4 us  [line_near(): return (up, lax.ppermute(value, 'tensor', [(1, 0), (2, 1), (3, 2)]))]
    ppermute x6, starting transfers between devices: 46 us -> 50 us  [line_near(): up = lax.ppermute(value, 'tensor', [(0, 1), (1, 2), (2, 3)])]
where the time goes in v16:
time: 241 us; the launch traced here: 240 us
  waiting for transfers between devices  104 us (43%)
  starting transfers between devices  81.8 us (34%)
  Pallas kernels  48.4 us (20%)
  between operations  2.48 us (1%)
    ppermute x6, starting transfers between devices, line_near(): up = lax.ppermute(value, 'tensor', [(0, 1), (1, 2), (2, 3)])  50 us
    pallas_call x24, Pallas kernels, call(): pl.pallas_call(kernel, grid_spec=pltpu.PrefetchScalarGridSpec(num_scalar_...  48.4 us
    ppermute x5, waiting for transfers between devices, line_far(): far = lax.ppermute(value, 'tensor', [(0, 2), (1, 3), (2, 0), (3, 1)])  32 us
    ppermute x6, waiting for transfers between devices, line_near(): return (up, lax.ppermute(value, 'tensor', [(1, 0), (2, 1), (3, 2)]))  24.4 us
    ppermute x3, waiting for transfers between devices, per_device(): parts.append(lax.ppermute(cuts[shift], 'tensor', pairs))  13.6 us
    ppermute x3, waiting for transfers between devices, plane_gather(): held[mask | bit] = lax.ppermute(held[mask], axis, pairs)  12.4 us
    ppermute x5, waiting for transfers between devices, line_far(): return (far, lax.ppermute(far, 'tensor', [(1, 0), (2, 3)]))  11.5 us
    ppermute x6, starting transfers between devices, line_near(): return (up, lax.ppermute(value, 'tensor', [(1, 0), (2, 1), (3, 2)]))  7.75 us
  transfers between devices with their start and end apart: 37, of which 20 were waited for; matrix products, arithmetic and copies ran while one was open for 0% of the time, Pallas kernels for 15%

profile of v16, /device:TPU:0, one launch (start us, length us, event | category | flops | bytes accessed | tf_op | source)
XLA Modules:
  0.0 240.1 jit_solution(5424473327702772836)
XLA Ops:
  4.6 5.2 %prepare.1 = (bf16[512,256]{1,0:T(8,128)(2,1)}, bf16[1552,256]{1,0:T(8,128)(2,1)}, bf16[32,3584]{1,0:T(8,128)(2,1)}, bf16[32,3584]{1,0:T(8,128)(2,1)}, bf16[32,3...) custom-call(s32[20]{0:T(128)} %stack.86.info, ...), custom_call_target="tpu_custom_call" | custom-call | flops 1 | bytes 1 | tf_op jit(solution)/shard_map/prepare/pallas_call | solution.py:167
  18.4 5.2 %collective-permute-done.2.refs_1_ = bf16[32,3584]{1,0:T(8,128)(2,1)S(1)} collective-permute-done((bf16[32,3584]{1,0:T(8,128)(2,1)}, bf16[32,3584]{1,0:T(8,128)(2,1)S(1)}, u32[]{:S(2)}, u32[]{:S(2)}) %collective-permute-start.2) | collective-permute-done | bytes 229408 | tf_op jit(solution)/shard_map/ppermute | solution.py:609
  23.5 8.4 %collective-permute-done.3.refs_2_ = bf16[32,3584]{1,0:T(8,128)(2,1)S(1)} collective-permute-done((bf16[32,3584]{1,0:T(8,128)(2,1)}, bf16[32,3584]{1,0:T(8,128)(2,1)S(1)}, u32[]{:S(2)}, u32[]{:S(2)}) %collective-permute-start.3) | collective-permute-done | bytes 229408 | tf_op jit(solution)/shard_map/ppermute | solution.py:609
  35.3 4.5 %collective-permute-start.6 = (bf16[512,512]{1,0:T(8,128)(2,1)}, bf16[512,512]{1,0:T(8,128)(2,1)S(1)}, u32[]{:S(2)}, u32[]{:S(2)}) collective-permute-start(bf16[512,512]{1,0:T(8,128)(2,1)} %gate.15.refs_2_), channel_id=1, source_target_pairs={{0,8},{4,12},{8,0},{12,4},{1,9},{5,13},{9,1},{13,5},{2,10},{6,14},... | collective-permute-start | bytes 1572872 | tf_op jit(solution)/shard_map/ppermute | solution.py:622
  39.8 12.2 %attend.1.refs_0_.refs_1_ = bf16[512,256]{1,0:T(8,128)(2,1)S(1)} custom-call(s32[20]{0:T(128)S(1)} %copy-done.3, bf16[512,256]{1,0:T(8,128)(2,1)S(1)} %copy-done.6, bf16[1552,256]{1,0:T(8,128)(2,1)S(1)} %copy-done.5, bf16[1552,256]{1,0:T(8,128)(2,1)S(1)} %collective-permute-done.refs_1_, bf16[1552,256]{1,0:T(8,128)(2,1)S(1)} %gate.16.refs_2_, ...), custom_call_target="tpu_custom_call" | custom-call | flops 12884901888 | bytes 1 | tf_op jit(solution)/shard_map/attend/pallas_call | solution.py:167
  52.0 5.4 %collective-permute-done.15.refs_0_ = bf16[4,32,3584]{2,1,0:T(8,128)(2,1)S(1)} collective-permute-done((bf16[4,32,3584]{2,1,0:T(8,128)(2,1)S(1)}, bf16[4,32,3584]{2,1,0:T(8,128)(2,1)S(1)}, u32[]{:S(2)}, u32[]{:S(2)}) %collective-permute-start.15) | collective-permute-done | bytes 917536 | tf_op jit(solution)/shard_map/ppermute | solution.py:78
  58.0 5.5 %collective-permute-done.6.refs_1_.refs_0_ = bf16[512,512]{1,0:T(8,128)(2,1)S(1)} collective-permute-done((bf16[512,512]{1,0:T(8,128)(2,1)}, bf16[512,512]{1,0:T(8,128)(2,1)S(1)}, u32[]{:S(2)}, u32[]{:S(2)}) %collective-permute-start.6) | collective-permute-done | bytes 524320 | tf_op jit(solution)/shard_map/ppermute | solution.py:622
  66.2 5.9 %collective-permute-start.7 = (bf16[512,256]{1,0:T(8,128)(2,1)S(1)}, bf16[512,256]{1,0:T(8,128)(2,1)S(1)}, u32[]{:S(2)}, u32[]{:S(2)}) collective-permute-start(bf16[512,256]{1,0:T(8,128)(2,1)S(1)} %gate.17.refs_0_), channel_id=1, source_target_pairs={{0,4},{4,8},{8,12},{1,5},{5,9},{9,13},{2,6},{6,10},{10,14},{3,7},{... | collective-permute-start | bytes 786440 | tf_op jit(solution)/shard_map/ppermute | solution.py:104
  73.4 6.4 %collective-permute-done.9.refs_3_ = bf16[512,256]{1,0:T(8,128)(2,1)S(1)} collective-permute-done((bf16[512,256]{1,0:T(8,128)(2,1)S(1)}, bf16[512,256]{1,0:T(8,128)(2,1)S(1)}, u32[]{:S(2)}, u32[]{:S(2)}) %collective-permute-start.9) | collective-permute-done | bytes 262176 | tf_op jit(solution)/shard_map/ppermute | solution.py:109
  84.3 5.4 %collective-permute-done.10.refs_4_ = bf16[512,256]{1,0:T(8,128)(2,1)S(1)} collective-permute-done((bf16[512,256]{1,0:T(8,128)(2,1)S(1)}, bf16[512,256]{1,0:T(8,128)(2,1)S(1)}, u32[]{:S(2)}, u32[]{:S(2)}) %collective-permute-start.10) | collective-permute-done | bytes 262176 | tf_op jit(solution)/shard_map/ppermute | solution.py:110
  92.1 4.7 %collective-permute-start.11 = (bf16[512,512]{1,0:T(8,128)(2,1)S(1)}, bf16[512,512]{1,0:T(8,128)(2,1)S(1)}, u32[]{:S(2)}, u32[]{:S(2)}) collective-permute-start(bf16[512,512]{1,0:T(8,128)(2,1)S(1)} %gate.18.refs_5_), channel_id=1, source_target_pairs={{0,4},{4,8},{8,12},{1,5},{5,9},{9,13},{2,6},{6,10},{10,14},{3,7},{... | collective-permute-start | bytes 1572872 | tf_op jit(solution)/shard_map/ppermute | solution.py:104
  98.8 6.9 %collective-permute-done.19.refs_0_ = bf16[4,32,3584]{2,1,0:T(8,128)(2,1)S(1)} collective-permute-done((bf16[4,32,3584]{2,1,0:T(8,128)(2,1)S(1)}, bf16[4,32,3584]{2,1,0:T(8,128)(2,1)S(1)}, u32[]{:S(2)}, u32[]{:S(2)}) %collective-permute-start.19) | collective-permute-done | bytes 917536 | tf_op jit(solution)/shard_map/ppermute | solution.py:78
  107.0 9.1 %collective-permute-done.12.refs_6_.refs_7_ = bf16[512,512]{1,0:T(8,128)(2,1)S(1)} collective-permute-done((bf16[512,512]{1,0:T(8,128)(2,1)S(1)}, bf16[512,512]{1,0:T(8,128)(2,1)S(1)}, u32[]{:S(2)}, u32[]{:S(2)}) %collective-permute-start.12) | collective-permute-done | bytes 524320 | tf_op jit(solution)/shard_map/ppermute | solution.py:105
  119.2 3.9 %project.1 = (bf16[128,1536]{1,0:T(8,128)(2,1)S(1)}, bf16[128,1536]{1,0:T(8,128)(2,1)S(1)}, bf16[128,1536]{1,0:T(8,128)(2,1)S(1)}, bf16[128,1536]{1,0:T(8,128)(2...) custom-call(s32[20]{0:T(128)S(1)} %copy-done.3, ...), custom_call_target="tpu_custom_call" | custom-call | flops 1 | bytes 1 | tf_op jit(solution)/shard_map/project/pallas_call | solution.py:167
  123.1 3.9 %collective-permute-start.21 = (bf16[128,1536]{1,0:T(8,128)(2,1)S(1)}, bf16[128,1536]{1,0:T(8,128)(2,1)S(1)}, u32[]{:S(2)}, u32[]{:S(2)}) collective-permute-start(bf16[128,1536]{1,0:T(8,128)(2,1)S(1)} %get-tuple-element.34.refs_0_), channel_id=1, source_target_pairs={{0,4},{4,8},{8,12},{1,5},{5,9},{9,13},{2,6},{6,10},{10,14},{3,7},{... | collective-permute-start | bytes 1179656 | tf_op jit(solution)/shard_map/ppermute | solution.py:104
  128.3 14.4 %collective-permute-done.25.refs_1_.refs_3_ = bf16[128,1536]{1,0:T(8,128)(2,1)S(1)} collective-permute-done((bf16[128,1536]{1,0:T(8,128)(2,1)S(1)}, bf16[128,1536]{1,0:T(8,128)(2,1)S(1)}, u32[]{:S(2)}, u32[]{:S(2)}) %collective-permute-start.25) | collective-permute-done | bytes 393248 | tf_op jit(solution)/shard_map/ppermute | solution.py:109
  148.4 14.2 %collective-permute-start.23 = (bf16[128,1536]{1,0:T(8,128)(2,1)S(1)}, bf16[128,1536]{1,0:T(8,128)(2,1)S(1)}, u32[]{:S(2)}, u32[]{:S(2)}) collective-permute-start(bf16[128,1536]{1,0:T(8,128)(2,1)S(1)} %gate.24.refs_0_), channel_id=1, source_target_pairs={{0,4},{4,8},{8,12},{1,5},{5,9},{9,13},{2,6},{6,10},{10,14},{3,7},{... | collective-permute-start | bytes 1179656 | tf_op jit(solution)/shard_map/ppermute | solution.py:104
  163.9 4.1 %collective-permute-done.29.refs_1_.refs_3_ = bf16[128,1536]{1,0:T(8,128)(2,1)S(1)} collective-permute-done((bf16[128,1536]{1,0:T(8,128)(2,1)S(1)}, bf16[128,1536]{1,0:T(8,128)(2,1)S(1)}, u32[]{:S(2)}, u32[]{:S(2)}) %collective-permute-start.29) | collective-permute-done | bytes 393248 | tf_op jit(solution)/shard_map/ppermute | solution.py:109
  168.6 4.6 %project_raw.1 = (bf16[512,2048]{1,0:T(8,128)(2,1)S(1)}, bf16[512,2048]{1,0:T(8,128)(2,1)}) custom-call(s32[20]{0:T(128)S(1)} %copy-done.3, bf16[512,256]{1,0:T(8,128)(2,1)S(1)} %gate.17.refs_0_, bf16[512,256]{1,0:T(8,128)(2,1)S(1)} %collective-permute-done.7.refs_1_, ...), custom_call_target="tpu_custom_call", output_to_operand_aliasing={{1}: (19, {})} | custom-call | flops 1 | bytes 1 | tf_op jit(solution)/shard_map/project_raw/pallas_call | solution.py:167
  176.9 11.8 %collective-permute-start.27 = (bf16[128,1536]{1,0:T(8,128)(2,1)S(1)}, bf16[128,1536]{1,0:T(8,128)(2,1)S(1)}, u32[]{:S(2)}, u32[]{:S(2)}) collective-permute-start(bf16[128,1536]{1,0:T(8,128)(2,1)S(1)} %gate.25.refs_0_), channel_id=1, source_target_pairs={{0,4},{4,8},{8,12},{1,5},{5,9},{9,13},{2,6},{6,10},{10,14},{3,7},{... | collective-permute-start | bytes 1179656 | tf_op jit(solution)/shard_map/ppermute | solution.py:104
  196.9 7.2 %collective-permute-done.28.refs_2_ = bf16[128,1536]{1,0:T(8,128)(2,1)S(1)} collective-permute-done((bf16[128,1536]{1,0:T(8,128)(2,1)S(1)}, bf16[128,1536]{1,0:T(8,128)(2,1)S(1)}, u32[]{:S(2)}, u32[]{:S(2)}) %collective-permute-start.28) | collective-permute-done | bytes 393248 | tf_op jit(solution)/shard_map/ppermute | solution.py:105
  204.6 9.4 %collective-permute-start.31 = (bf16[128,1536]{1,0:T(8,128)(2,1)S(1)}, bf16[128,1536]{1,0:T(8,128)(2,1)S(1)}, u32[]{:S(2)}, u32[]{:S(2)}) collective-permute-start(bf16[128,1536]{1,0:T(8,128)(2,1)S(1)} %gate.27.refs_0_), channel_id=1, source_target_pairs={{0,4},{4,8},{8,12},{1,5},{5,9},{9,13},{2,6},{6,10},{10,14},{3,7},{... | collective-permute-start | bytes 1179656 | tf_op jit(solution)/shard_map/ppermute | solution.py:104
  215.3 3.6 %collective-permute-done.34.refs_3_ = bf16[128,1536]{1,0:T(8,128)(2,1)S(1)} collective-permute-done((bf16[128,1536]{1,0:T(8,128)(2,1)S(1)}, bf16[128,1536]{1,0:T(8,128)(2,1)S(1)}, u32[]{:S(2)}, u32[]{:S(2)}) %collective-permute-start.34) | collective-permute-done | bytes 393248 | tf_op jit(solution)/shard_map/ppermute | solution.py:109
  230.5 6.1 %collective-permute-done.35.refs_4_ = bf16[128,1536]{1,0:T(8,128)(2,1)S(1)} collective-permute-done((bf16[128,1536]{1,0:T(8,128)(2,1)S(1)}, bf16[128,1536]{1,0:T(8,128)(2,1)S(1)}, u32[]{:S(2)}, u32[]{:S(2)}) %collective-permute-start.35) | collective-permute-done | bytes 393248 | tf_op jit(solution)/shard_map/ppermute | solution.py:110
  (93 shorter events, 69.6 us)
Async XLA Ops:
  9.8 24.2 %collective-permute-start.1 = (bf16[1552,256]{1,0:T(8,128)(2,1)}, bf16[1552,256]{1,0:T(8,128)(2,1)S(1)}, u32[]{:S(2)}, u32[]{:S(2)}) collective-permute-start(bf16[1552,256]{1,0:T(8,128)(2,1)} %get-tuple-element.22.refs_0_), channel_id=1, source_target_pairs={{0,2},{1,3},{2,0},{3,1},{4,6},{5,7},{6,4},{7,5},{8,10},{9,11},{10,... | collective-permute-start | bytes 2383880 | tf_op jit(solution)/shard_map/ppermute | solution.py:43
  14.5 17.5 %collective-permute-start.3 = (bf16[32,3584]{1,0:T(8,128)(2,1)}, bf16[32,3584]{1,0:T(8,128)(2,1)S(1)}, u32[]{:S(2)}, u32[]{:S(2)}) collective-permute-start(bf16[32,3584]{1,0:T(8,128)(2,1)} %get-tuple-element.25), channel_id=1, source_target_pairs={{0,8},{4,12},{8,0},{12,4},{1,9},{5,13},{9,1},{13,5},{2,10},{6,14},... | collective-permute-start | bytes 688136 | tf_op jit(solution)/shard_map/ppermute | solution.py:609
  18.4 21.4 %collective-permute-start = (bf16[1552,256]{1,0:T(8,128)(2,1)}, bf16[1552,256]{1,0:T(8,128)(2,1)S(1)}, u32[]{:S(2)}, u32[]{:S(2)}) collective-permute-start(bf16[1552,256]{1,0:T(8,128)(2,1)} %get-tuple-element.22.refs_0_), channel_id=1, source_target_pairs={{0,1},{1,0},{2,3},{3,2},{4,5},{5,4},{6,7},{7,6},{8,9},{9,8},{10,11... | collective-permute-start | bytes 2383880 | tf_op jit(solution)/shard_map/ppermute | solution.py:43
  34.7 22.8 %collective-permute-start.15 = (bf16[4,32,3584]{2,1,0:T(8,128)(2,1)S(1)}, bf16[4,32,3584]{2,1,0:T(8,128)(2,1)S(1)}, u32[]{:S(2)}, u32[]{:S(2)}) collective-permute-start(bf16[4,32,3584]{2,1,0:T(8,128)(2,1)S(1)} %stack.89.refs_1_.refs_5_.refs_10_), channel_id=1, source_target_pairs={{0,2},{1,3},{2,0},{3,1},{4,6},{5,7},{6,4},{7,5},{8,10},{9,11},{10,... | collective-permute-start | bytes 2752520 | tf_op jit(solution)/shard_map/ppermute | solution.py:78
  35.3 28.2 %collective-permute-start.6 = (bf16[512,512]{1,0:T(8,128)(2,1)}, bf16[512,512]{1,0:T(8,128)(2,1)S(1)}, u32[]{:S(2)}, u32[]{:S(2)}) collective-permute-start(bf16[512,512]{1,0:T(8,128)(2,1)} %gate.15.refs_2_), channel_id=1, source_target_pairs={{0,8},{4,12},{8,0},{12,4},{1,9},{5,13},{9,1},{13,5},{2,10},{6,14},... | collective-permute-start | bytes 1572872 | tf_op jit(solution)/shard_map/ppermute | solution.py:622
  64.1 34.1 %collective-permute-start.17 = (bf16[4,32,3584]{2,1,0:T(8,128)(2,1)S(1)}, bf16[4,32,3584]{2,1,0:T(8,128)(2,1)S(1)}, u32[]{:S(2)}, u32[]{:S(2)}) collective-permute-start(bf16[4,32,3584]{2,1,0:T(8,128)(2,1)S(1)} %stack.89.refs_1_.refs_5_.refs_10_), channel_id=1, source_target_pairs={{0,16},{16,0},{1,17},{17,1},{2,18},{18,2},{3,19},{19,3},{4,20},{20... | collective-permute-start | bytes 2752520 | tf_op jit(solution)/shard_map/ppermute | solution.py:78
  65.7 40.0 %collective-permute-start.19 = (bf16[4,32,3584]{2,1,0:T(8,128)(2,1)S(1)}, bf16[4,32,3584]{2,1,0:T(8,128)(2,1)S(1)}, u32[]{:S(2)}, u32[]{:S(2)}) collective-permute-start(bf16[4,32,3584]{2,1,0:T(8,128)(2,1)S(1)} %gate.20.refs_0_), channel_id=1, source_target_pairs={{0,16},{16,0},{1,17},{17,1},{2,18},{18,2},{3,19},{19,3},{4,20},{20... | collective-permute-start | bytes 2752520 | tf_op jit(solution)/shard_map/ppermute | solution.py:78
  90.2 16.8 %collective-permute-start.13 = (bf16[512,512]{1,0:T(8,128)(2,1)S(1)}, bf16[512,512]{1,0:T(8,128)(2,1)S(1)}, u32[]{:S(2)}, u32[]{:S(2)}) collective-permute-start(bf16[512,512]{1,0:T(8,128)(2,1)S(1)} %gate.19.refs_8_), channel_id=1, source_target_pairs={{4,0},{8,12},{5,1},{9,13},{6,2},{10,14},{7,3},{11,15},{20,16},{24,... | collective-permute-start | bytes 1572872 | tf_op jit(solution)/shard_map/ppermute | solution.py:629
  96.9 19.2 %collective-permute-start.12 = (bf16[512,512]{1,0:T(8,128)(2,1)S(1)}, bf16[512,512]{1,0:T(8,128)(2,1)S(1)}, u32[]{:S(2)}, u32[]{:S(2)}) collective-permute-start(bf16[512,512]{1,0:T(8,128)(2,1)S(1)} %gate.18.refs_5_), channel_id=1, source_target_pairs={{4,0},{8,4},{12,8},{5,1},{9,5},{13,9},{6,2},{10,6},{14,10},{7,3},{... | collective-permute-start | bytes 1572872 | tf_op jit(solution)/shard_map/ppermute | solution.py:105
  98.2 18.5 %collective-permute-start.14 = (bf16[4,32,3584]{2,1,0:T(8,128)(2,1)S(1)}, bf16[4,32,3584]{2,1,0:T(8,128)(2,1)S(1)}, u32[]{:S(2)}, u32[]{:S(2)}) collective-permute-start(bf16[4,32,3584]{2,1,0:T(8,128)(2,1)S(1)} %stack.89.refs_1_.refs_5_.refs_10_), channel_id=1, source_target_pairs={{0,1},{1,0},{2,3},{3,2},{4,5},{5,4},{6,7},{7,6},{8,9},{9,8},{10,11... | collective-permute-start | bytes 2752520 | tf_op jit(solution)/shard_map/ppermute | solution.py:87
  123.1 19.6 %collective-permute-start.25 = (bf16[128,1536]{1,0:T(8,128)(2,1)S(1)}, bf16[128,1536]{1,0:T(8,128)(2,1)S(1)}, u32[]{:S(2)}, u32[]{:S(2)}) collective-permute-start(bf16[128,1536]{1,0:T(8,128)(2,1)S(1)} %get-tuple-element.35), channel_id=1, source_target_pairs={{0,8},{4,12},{8,0},{12,4},{1,9},{5,13},{9,1},{13,5},{2,10},{6,14},... | collective-permute-start | bytes 1179656 | tf_op jit(solution)/shard_map/ppermute | solution.py:109
  123.1 21.5 %collective-permute-start.21 = (bf16[128,1536]{1,0:T(8,128)(2,1)S(1)}, bf16[128,1536]{1,0:T(8,128)(2,1)S(1)}, u32[]{:S(2)}, u32[]{:S(2)}) collective-permute-start(bf16[128,1536]{1,0:T(8,128)(2,1)S(1)} %get-tuple-element.34.refs_0_), channel_id=1, source_target_pairs={{0,4},{4,8},{8,12},{1,5},{5,9},{9,13},{2,6},{6,10},{10,14},{3,7},{... | collective-permute-start | bytes 1179656 | tf_op jit(solution)/shard_map/ppermute | solution.py:104
  127.0 20.8 %collective-permute-start.22 = (bf16[128,1536]{1,0:T(8,128)(2,1)S(1)}, bf16[128,1536]{1,0:T(8,128)(2,1)S(1)}, u32[]{:S(2)}, u32[]{:S(2)}) collective-permute-start(bf16[128,1536]{1,0:T(8,128)(2,1)S(1)} %get-tuple-element.34.refs_0_), channel_id=1, source_target_pairs={{4,0},{8,4},{12,8},{5,1},{9,5},{13,9},{6,2},{10,6},{14,10},{7,3},{... | collective-permute-start | bytes 1179656 | tf_op jit(solution)/shard_map/ppermute | solution.py:105
  143.2 24.8 %collective-permute-start.29 = (bf16[128,1536]{1,0:T(8,128)(2,1)S(1)}, bf16[128,1536]{1,0:T(8,128)(2,1)S(1)}, u32[]{:S(2)}, u32[]{:S(2)}) collective-permute-start(bf16[128,1536]{1,0:T(8,128)(2,1)S(1)} %gate.26), channel_id=1, source_target_pairs={{0,8},{4,12},{8,0},{12,4},{1,9},{5,13},{9,1},{13,5},{2,10},{6,14},... | collective-permute-start | bytes 1179656 | tf_op jit(solution)/shard_map/ppermute | solution.py:109
  143.3 31.3 %collective-permute-start.26 = (bf16[128,1536]{1,0:T(8,128)(2,1)S(1)}, bf16[128,1536]{1,0:T(8,128)(2,1)S(1)}, u32[]{:S(2)}, u32[]{:S(2)}) collective-permute-start(bf16[128,1536]{1,0:T(8,128)(2,1)S(1)} %collective-permute-done.25.refs_1_.refs_3_), channel_id=1, source_target_pairs={{4,0},{8,12},{5,1},{9,13},{6,2},{10,14},{7,3},{11,15},{20,16},{24,... | collective-permute-start | bytes 1179656 | tf_op jit(solution)/shard_map/ppermute | solution.py:110
  148.4 26.3 %collective-permute-start.23 = (bf16[128,1536]{1,0:T(8,128)(2,1)S(1)}, bf16[128,1536]{1,0:T(8,128)(2,1)S(1)}, u32[]{:S(2)}, u32[]{:S(2)}) collective-permute-start(bf16[128,1536]{1,0:T(8,128)(2,1)S(1)} %gate.24.refs_0_), channel_id=1, source_target_pairs={{0,4},{4,8},{8,12},{1,5},{5,9},{9,13},{2,6},{6,10},{10,14},{3,7},{... | collective-permute-start | bytes 1179656 | tf_op jit(solution)/shard_map/ppermute | solution.py:104
  168.5 25.0 %collective-permute-start.33 = (bf16[128,1536]{1,0:T(8,128)(2,1)S(1)}, bf16[128,1536]{1,0:T(8,128)(2,1)S(1)}, u32[]{:S(2)}, u32[]{:S(2)}) collective-permute-start(bf16[128,1536]{1,0:T(8,128)(2,1)S(1)} %gate.28), channel_id=1, source_target_pairs={{0,8},{4,12},{8,0},{12,4},{1,9},{5,13},{9,1},{13,5},{2,10},{6,14},... | collective-permute-start | bytes 1179656 | tf_op jit(solution)/shard_map/ppermute | solution.py:109
  173.2 22.3 %collective-permute-start.30 = (bf16[128,1536]{1,0:T(8,128)(2,1)S(1)}, bf16[128,1536]{1,0:T(8,128)(2,1)S(1)}, u32[]{:S(2)}, u32[]{:S(2)}) collective-permute-start(bf16[128,1536]{1,0:T(8,128)(2,1)S(1)} %collective-permute-done.29.refs_1_.refs_3_), channel_id=1, source_target_pairs={{4,0},{8,12},{5,1},{9,13},{6,2},{10,14},{7,3},{11,15},{20,16},{24,... | collective-permute-start | bytes 1179656 | tf_op jit(solution)/shard_map/ppermute | solution.py:110
  176.9 20.0 %collective-permute-start.27 = (bf16[128,1536]{1,0:T(8,128)(2,1)S(1)}, bf16[128,1536]{1,0:T(8,128)(2,1)S(1)}, u32[]{:S(2)}, u32[]{:S(2)}) collective-permute-start(bf16[128,1536]{1,0:T(8,128)(2,1)S(1)} %gate.25.refs_0_), channel_id=1, source_target_pairs={{0,4},{4,8},{8,12},{1,5},{5,9},{9,13},{2,6},{6,10},{10,14},{3,7},{... | collective-permute-start | bytes 1179656 | tf_op jit(solution)/shard_map/ppermute | solution.py:104
  194.1 24.8 %collective-permute-start.34 = (bf16[128,1536]{1,0:T(8,128)(2,1)S(1)}, bf16[128,1536]{1,0:T(8,128)(2,1)S(1)}, u32[]{:S(2)}, u32[]{:S(2)}) collective-permute-start(bf16[128,1536]{1,0:T(8,128)(2,1)S(1)} %gate.29), channel_id=1, source_target_pairs={{0,8},{4,12},{8,0},{12,4},{1,9},{5,13},{9,1},{13,5},{2,10},{6,14},... | collective-permute-start | bytes 1179656 | tf_op jit(solution)/shard_map/ppermute | solution.py:109
  194.2 32.9 %collective-permute-start.36 = (bf16[128,1536]{1,0:T(8,128)(2,1)S(1)}, bf16[128,1536]{1,0:T(8,128)(2,1)S(1)}, u32[]{:S(2)}, u32[]{:S(2)}) collective-permute-start(bf16[128,1536]{1,0:T(8,128)(2,1)S(1)} %collective-permute-done.33.refs_1_.refs_3_), channel_id=1, source_target_pairs={{4,0},{8,12},{5,1},{9,13},{6,2},{10,14},{7,3},{11,15},{20,16},{24,... | collective-permute-start | bytes 1179656 | tf_op jit(solution)/shard_map/ppermute | solution.py:110
  204.6 25.9 %collective-permute-start.31 = (bf16[128,1536]{1,0:T(8,128)(2,1)S(1)}, bf16[128,1536]{1,0:T(8,128)(2,1)S(1)}, u32[]{:S(2)}, u32[]{:S(2)}) collective-permute-start(bf16[128,1536]{1,0:T(8,128)(2,1)S(1)} %gate.27.refs_0_), channel_id=1, source_target_pairs={{0,4},{4,8},{8,12},{1,5},{5,9},{9,13},{2,6},{6,10},{10,14},{3,7},{... | collective-permute-start | bytes 1179656 | tf_op jit(solution)/shard_map/ppermute | solution.py:104
  214.0 16.5 %collective-permute-start.32 = (bf16[128,1536]{1,0:T(8,128)(2,1)S(1)}, bf16[128,1536]{1,0:T(8,128)(2,1)S(1)}, u32[]{:S(2)}, u32[]{:S(2)}) collective-permute-start(bf16[128,1536]{1,0:T(8,128)(2,1)S(1)} %gate.27.refs_0_), channel_id=1, source_target_pairs={{4,0},{8,4},{12,8},{5,1},{9,5},{13,9},{6,2},{10,6},{14,10},{7,3},{... | collective-permute-start | bytes 1179656 | tf_op jit(solution)/shard_map/ppermute | solution.py:105
  218.9 17.7 %collective-permute-start.35 = (bf16[128,1536]{1,0:T(8,128)(2,1)S(1)}, bf16[128,1536]{1,0:T(8,128)(2,1)S(1)}, u32[]{:S(2)}, u32[]{:S(2)}) collective-permute-start(bf16[128,1536]{1,0:T(8,128)(2,1)S(1)} %collective-permute-done.34.refs_3_), channel_id=1, source_target_pairs={{4,0},{8,12},{5,1},{9,13},{6,2},{10,14},{7,3},{11,15},{20,16},{24,... | collective-permute-start | bytes 1179656 | tf_op jit(solution)/shard_map/ppermute | solution.py:110
  (20 other events, 352.6 us)

commit v17 on v14

--- a/solution.py
+++ b/solution.py
@@ -117,14 +117,12 @@
     for number, value in enumerate(values):
         after = [fars[-1][0]] if number else []
         if number == 1:
-            after += second
+            after += second + made
         fars.append(line_far(gate(info, value, after) if after else value))
     for number, value in enumerate(copies):
         after = list(lines[number - 1][1:3]) if number else []
         if number > 1:
             after.append(fars[number - 2][1])
-        if number == len(copies) // 2:
-            after += made
         value = gate(info, value, after) if after else value
         lines.append([value, *line_near(value), *fars[number]])
     return lines
@@ -583,7 +581,11 @@
     chunk = min(CHUNK, rows)
     halves = 1
     half = rows // halves
-    splits = [[(begin, chunk) for begin in range(0, half, chunk)]] * halves
+    sizes = [chunk] * (half // chunk)
+    if len(sizes) > 1 and chunk % 128 == 0:
+        sizes[0] += 32
+        sizes[-1] -= 32
+    splits = [[(sum(sizes[:n]), size) for n, size in enumerate(sizes)]] * halves
 
     table = Table(contexts, count)
     steering = [context_index, *owners_of(contexts, context_index)]

time: 232 us -> 231 us (level)
  waiting for transfers between devices: 84.2 us -> 80.6 us
    ppermute x6, waiting for transfers between devices: 17.1 us -> 13.2 us  [line_far(): return (far, lax.ppermute(far, 'tensor', [(1, 0), (2, 3)]))]
    ppermute x6, waiting for transfers between devices: 2.62 us -> 5.04 us  [line_near(): up = lax.ppermute(value, 'tensor', [(0, 1), (1, 2), (2, 3)])]
    ppermute x6, waiting for transfers between devices: 38.4 us -> 36 us  [line_far(): far = lax.ppermute(value, 'tensor', [(0, 2), (1, 3), (2, 0), (3, 1)])]
  transfers between devices with their start and end apart: 37 -> 37, of which waited for: 18 -> 19; matrix products, arithmetic and copies ran while one was open for 0% -> 0% of each run, Pallas kernels for 15% -> 15%
where the time goes in v17:
time: 231 us; the launch traced here: 230 us
  starting transfers between devices  93.6 us (41%)
  waiting for transfers between devices  80.6 us (35%)
  Pallas kernels  47.4 us (21%)
  local copies, waits for them, and re-layouts  4.17 us (2%)
  between operations  2.38 us (1%)
    ppermute x6, starting transfers between devices, line_near(): up = lax.ppermute(value, 'tensor', [(0, 1), (1, 2), (2, 3)])  58.5 us
    pallas_call x22, Pallas kernels, call(): pl.pallas_call(kernel, grid_spec=pltpu.PrefetchScalarGridSpec(num_scalar_...  47.4 us
    ppermute x6, waiting for transfers between devices, line_far(): far = lax.ppermute(value, 'tensor', [(0, 2), (1, 3), (2, 0), (3, 1)])  36 us
    ppermute x6, waiting for transfers between devices, line_near(): return (up, lax.ppermute(value, 'tensor', [(1, 0), (2, 1), (3, 2)]))  13.9 us
    ppermute x6, waiting for transfers between devices, line_far(): return (far, lax.ppermute(far, 'tensor', [(1, 0), (2, 3)]))  13.2 us
    ppermute x3, waiting for transfers between devices, per_device(): parts.append(lax.ppermute(cuts[shift], 'tensor', pairs))  10.4 us
    ppermute x6, starting transfers between devices, line_near(): return (up, lax.ppermute(value, 'tensor', [(1, 0), (2, 1), (3, 2)]))  7.75 us
    ppermute x6, starting transfers between devices, line_far(): return (far, lax.ppermute(far, 'tensor', [(1, 0), (2, 3)]))  7.73 us
  transfers between devices with their start and end apart: 37, of which 19 were waited for; matrix products, arithmetic and copies ran while one was open for 0% of the time, Pallas kernels for 15%

profile of v17, /device:TPU:0, one launch (start us, length us, event | category | flops | bytes accessed | tf_op | source)
XLA Modules:
  0.0 230.1 jit_solution(5707165152928016870)
XLA Ops:
  4.5 4.6 %prepare.1 = (bf16[512,256]{1,0:T(8,128)(2,1)}, bf16[1552,256]{1,0:T(8,128)(2,1)}, bf16[32,2816]{1,0:T(8,128)(2,1)}, bf16[32,2816]{1,0:T(8,128)(2,1)}, bf16[32,2...) custom-call(s32[20]{0:T(128)} %stack.86.info, bf16[512,256]{1,0:T(8,128)(2,1)} %q_hbm.1, ...), custom_call_target="tpu_custom_call" | custom-call | flops 1 | bytes 1 | tf_op jit(solution)/shard_map/prepare/pallas_call | solution.py:165
  17.6 4.1 %collective-permute-done.2.refs_1_ = bf16[32,2816]{1,0:T(8,128)(2,1)S(1)} collective-permute-done((bf16[32,2816]{1,0:T(8,128)(2,1)}, bf16[32,2816]{1,0:T(8,128)(2,1)S(1)}, u32[]{:S(2)}, u32[]{:S(2)}) %collective-permute-start.2) | collective-permute-done | bytes 180256 | tf_op jit(solution)/shard_map/ppermute | solution.py:610
  21.7 6.3 %collective-permute-done.3.refs_2_ = bf16[32,2816]{1,0:T(8,128)(2,1)S(1)} collective-permute-done((bf16[32,2816]{1,0:T(8,128)(2,1)}, bf16[32,2816]{1,0:T(8,128)(2,1)S(1)}, u32[]{:S(2)}, u32[]{:S(2)}) %collective-permute-start.3) | collective-permute-done | bytes 180256 | tf_op jit(solution)/shard_map/ppermute | solution.py:610
  32.4 5.7 %collective-permute-start.6 = (bf16[512,256]{1,0:T(8,128)(2,1)}, bf16[512,256]{1,0:T(8,128)(2,1)S(1)}, u32[]{:S(2)}, u32[]{:S(2)}) collective-permute-start(bf16[512,256]{1,0:T(8,128)(2,1)} %gate.13.refs_2_.refs_5_), channel_id=1, source_target_pairs={{0,4},{4,8},{8,12},{1,5},{5,9},{9,13},{2,6},{6,10},{10,14},{3,7},{... | collective-permute-start | bytes 786440 | tf_op jit(solution)/shard_map/ppermute | solution.py:104
  45.4 12.2 %attend.1.refs_0_.refs_1_ = bf16[512,256]{1,0:T(8,128)(2,1)S(1)} custom-call(s32[20]{0:T(128)S(1)} %copy-done.3, bf16[512,256]{1,0:T(8,128)(2,1)S(1)} %copy-done.6, bf16[1552,256]{1,0:T(8,128)(2,1)S(1)} %copy-done.5, bf16[1552,256]{1,0:T(8,128)(2,1)S(1)} %collective-permute-done.refs_1_, bf16[1552,256]{1,0:T(8,128)(2,1)S(1)} %gate.14.refs_2_, ...), custom_call_target="tpu_custom_call" | custom-call | flops 12884901888 | bytes 1 | tf_op jit(solution)/shard_map/attend/pallas_call | solution.py:165
  61.4 5.1 %collective-permute-start.9 = (bf16[512,256]{1,0:T(8,128)(2,1)S(1)}, bf16[512,256]{1,0:T(8,128)(2,1)S(1)}, u32[]{:S(2)}, u32[]{:S(2)}) collective-permute-start(bf16[512,256]{1,0:T(8,128)(2,1)S(1)} %gate.15.refs_0_), channel_id=1, source_target_pairs={{0,4},{4,8},{8,12},{1,5},{5,9},{9,13},{2,6},{6,10},{10,14},{3,7},{... | collective-permute-start | bytes 786440 | tf_op jit(solution)/shard_map/ppermute | solution.py:104
  67.8 6.6 %collective-permute-done.11.refs_3_ = bf16[512,256]{1,0:T(8,128)(2,1)S(1)} collective-permute-done((bf16[512,256]{1,0:T(8,128)(2,1)S(1)}, bf16[512,256]{1,0:T(8,128)(2,1)S(1)}, u32[]{:S(2)}, u32[]{:S(2)}) %collective-permute-start.11) | collective-permute-done | bytes 262176 | tf_op jit(solution)/shard_map/ppermute | solution.py:109
  77.5 4.5 %collective-permute-done.13.refs_5_.refs_9_ = bf16[512,256]{1,0:T(8,128)(2,1)S(1)} collective-permute-done((bf16[512,256]{1,0:T(8,128)(2,1)S(1)}, bf16[512,256]{1,0:T(8,128)(2,1)S(1)}, u32[]{:S(2)}, u32[]{:S(2)}) %collective-permute-start.13) | collective-permute-done | bytes 262176 | tf_op jit(solution)/shard_map/ppermute | solution.py:110
  82.0 4.1 %collective-permute-done.12.refs_4_ = bf16[512,256]{1,0:T(8,128)(2,1)S(1)} collective-permute-done((bf16[512,256]{1,0:T(8,128)(2,1)S(1)}, bf16[512,256]{1,0:T(8,128)(2,1)S(1)}, u32[]{:S(2)}, u32[]{:S(2)}) %collective-permute-start.12) | collective-permute-done | bytes 262176 | tf_op jit(solution)/shard_map/ppermute | solution.py:110
  89.9 4.4 %project.1 = (bf16[160,1792]{1,0:T(8,128)(2,1)S(1)}, bf16[128,1792]{1,0:T(8,128)(2,1)S(1)}, bf16[128,1792]{1,0:T(8,128)(2,1)S(1)}, bf16[96,1792]{1,0:T(8,128)(2,...) custom-call(s32[20]{0:T(128)S(1)} %copy-done.3, ...), custom_call_target="tpu_custom_call" | custom-call | flops 1 | bytes 1 | tf_op jit(solution)/shard_map/project/pallas_call | solution.py:165
  94.4 4.0 %collective-permute-start.25 = (bf16[160,1792]{1,0:T(8,128)(2,1)S(1)}, bf16[160,1792]{1,0:T(8,128)(2,1)S(1)}, u32[]{:S(2)}, u32[]{:S(2)}) collective-permute-start(bf16[160,1792]{1,0:T(8,128)(2,1)S(1)} %get-tuple-element.33), channel_id=1, source_target_pairs={{0,8},{4,12},{8,0},{12,4},{1,9},{5,13},{9,1},{13,5},{2,10},{6,14},... | collective-permute-start | bytes 1720328 | tf_op jit(solution)/shard_map/ppermute | solution.py:109
  98.3 4.4 %collective-permute-start.21 = (bf16[160,1792]{1,0:T(8,128)(2,1)S(1)}, bf16[160,1792]{1,0:T(8,128)(2,1)S(1)}, u32[]{:S(2)}, u32[]{:S(2)}) collective-permute-start(bf16[160,1792]{1,0:T(8,128)(2,1)S(1)} %get-tuple-element.32.refs_0_), channel_id=1, source_target_pairs={{0,4},{4,8},{8,12},{1,5},{5,9},{9,13},{2,6},{6,10},{10,14},{3,7},{... | collective-permute-start | bytes 1720328 | tf_op jit(solution)/shard_map/ppermute | solution.py:104
  104.0 4.4 %project_raw.1 = (bf16[512,1024]{1,0:T(8,128)(2,1)S(1)}, bf16[512,2048]{1,0:T(8,128)(2,1)}) custom-call(s32[20]{0:T(128)S(1)} %copy-done.3, bf16[512,256]{1,0:T(8,128)(2,1)S(1)} %gate.15.refs_0_, bf16[512,256]{1,0:T(8,128)(2,1)S(1)} %collective-permute-done.9.refs_1_, ...), custom_call_target="tpu_custom_call", output_to_operand_aliasing={{1}: (19, {})} | custom-call | flops 1 | bytes 1 | tf_op jit(solution)/shard_map/project_raw/pallas_call | solution.py:165
  108.4 16.0 %collective-permute-done.25.refs_1_.refs_3_ = bf16[160,1792]{1,0:T(8,128)(2,1)S(1)} collective-permute-done((bf16[160,1792]{1,0:T(8,128)(2,1)S(1)}, bf16[160,1792]{1,0:T(8,128)(2,1)S(1)}, u32[]{:S(2)}, u32[]{:S(2)}) %collective-permute-start.25) | collective-permute-done | bytes 573472 | tf_op jit(solution)/shard_map/ppermute | solution.py:109
  129.9 19.7 %collective-permute-start.23 = (bf16[128,1792]{1,0:T(8,128)(2,1)S(1)}, bf16[128,1792]{1,0:T(8,128)(2,1)S(1)}, u32[]{:S(2)}, u32[]{:S(2)}) collective-permute-start(bf16[128,1792]{1,0:T(8,128)(2,1)S(1)} %gate.20.refs_0_), channel_id=1, source_target_pairs={{0,4},{4,8},{8,12},{1,5},{5,9},{9,13},{2,6},{6,10},{10,14},{3,7},{... | collective-permute-start | bytes 1376264 | tf_op jit(solution)/shard_map/ppermute | solution.py:104
  150.9 5.4 %collective-permute-done.29.refs_1_.refs_3_ = bf16[128,1792]{1,0:T(8,128)(2,1)S(1)} collective-permute-done((bf16[128,1792]{1,0:T(8,128)(2,1)S(1)}, bf16[128,1792]{1,0:T(8,128)(2,1)S(1)}, u32[]{:S(2)}, u32[]{:S(2)}) %collective-permute-start.29) | collective-permute-done | bytes 458784 | tf_op jit(solution)/shard_map/ppermute | solution.py:109
  160.5 5.3 %collective-permute-done.24.refs_2_ = bf16[128,1792]{1,0:T(8,128)(2,1)S(1)} collective-permute-done((bf16[128,1792]{1,0:T(8,128)(2,1)S(1)}, bf16[128,1792]{1,0:T(8,128)(2,1)S(1)}, u32[]{:S(2)}, u32[]{:S(2)}) %collective-permute-start.24) | collective-permute-done | bytes 458784 | tf_op jit(solution)/shard_map/ppermute | solution.py:105
  166.3 13.1 %collective-permute-start.27 = (bf16[128,1792]{1,0:T(8,128)(2,1)S(1)}, bf16[128,1792]{1,0:T(8,128)(2,1)S(1)}, u32[]{:S(2)}, u32[]{:S(2)}) collective-permute-start(bf16[128,1792]{1,0:T(8,128)(2,1)S(1)} %gate.21.refs_0_), channel_id=1, source_target_pairs={{0,4},{4,8},{8,12},{1,5},{5,9},{9,13},{2,6},{6,10},{10,14},{3,7},{... | collective-permute-start | bytes 1376264 | tf_op jit(solution)/shard_map/ppermute | solution.py:104
  180.7 5.0 %collective-permute-done.33.refs_1_.refs_3_ = bf16[128,1792]{1,0:T(8,128)(2,1)S(1)} collective-permute-done((bf16[128,1792]{1,0:T(8,128)(2,1)S(1)}, bf16[128,1792]{1,0:T(8,128)(2,1)S(1)}, u32[]{:S(2)}, u32[]{:S(2)}) %collective-permute-start.33) | collective-permute-done | bytes 458784 | tf_op jit(solution)/shard_map/ppermute | solution.py:109
  190.3 5.0 %collective-permute-done.28.refs_2_ = bf16[128,1792]{1,0:T(8,128)(2,1)S(1)} collective-permute-done((bf16[128,1792]{1,0:T(8,128)(2,1)S(1)}, bf16[128,1792]{1,0:T(8,128)(2,1)S(1)}, u32[]{:S(2)}, u32[]{:S(2)}) %collective-permute-start.28) | collective-permute-done | bytes 458784 | tf_op jit(solution)/shard_map/ppermute | solution.py:105
  195.9 10.6 %collective-permute-start.31 = (bf16[96,1792]{1,0:T(8,128)(2,1)S(1)}, bf16[96,1792]{1,0:T(8,128)(2,1)S(1)}, u32[]{:S(2)}, u32[]{:S(2)}) collective-permute-start(bf16[96,1792]{1,0:T(8,128)(2,1)S(1)} %gate.23.refs_0_), channel_id=1, source_target_pairs={{0,4},{4,8},{8,12},{1,5},{5,9},{9,13},{2,6},{6,10},{10,14},{3,7},{... | collective-permute-start | bytes 1032200 | tf_op jit(solution)/shard_map/ppermute | solution.py:104
  211.3 4.2 %norm.4.refs_6_ = bf16[512,8192]{1,0:T(8,128)(2,1)} custom-call(s32[20]{0:T(128)S(1)} %copy-done.3, f32[1,8192]{1,0:T(1,128)S(1)} %bitcast.23, bf16[160,1792]{1,0:T(8,128)(2,1)S(1)} %get-tuple-element.32.refs_0_, bf16[160,1792]{1,0:T(8,128)(2,1)S(1)} %collective-permute-done.21.refs_1_, bf16[160,1792]{1,0:T(8,128)(2,1)S(1)} %collective-permute-done.22.refs_2_, ...), custom_call_target="tpu_custom_call" | custom-call | flops 1 | bytes 1 | tf_op jit(solution)/shard_map/norm/pallas_call | solution.py:165
  219.0 3.5 %norm.6.refs_6_ = bf16[512,8192]{1,0:T(8,128)(2,1)} custom-call(s32[20]{0:T(128)S(1)} %copy-done.3, f32[1,8192]{1,0:T(1,128)S(1)} %bitcast.25, bf16[128,1792]{1,0:T(8,128)(2,1)S(1)} %gate.21.refs_0_, bf16[128,1792]{1,0:T(8,128)(2,1)S(1)} %collective-permute-done.27.refs_1_, ...), custom_call_target="tpu_custom_call", output_to_operand_aliasing={{}: (8, {})} | custom-call | flops 1 | bytes 1 | tf_op jit(solution)/shard_map/norm/pallas_call | solution.py:165
  222.5 4.6 %collective-permute-done.35.refs_4_ = bf16[96,1792]{1,0:T(8,128)(2,1)S(1)} collective-permute-done((bf16[96,1792]{1,0:T(8,128)(2,1)S(1)}, bf16[96,1792]{1,0:T(8,128)(2,1)S(1)}, u32[]{:S(2)}, u32[]{:S(2)}) %collective-permute-start.35) | collective-permute-done | bytes 344096 | tf_op jit(solution)/shard_map/ppermute | solution.py:110
  (91 shorter events, 65.2 us)
Async XLA Ops:
  9.1 21.5 %collective-permute-start.1 = (bf16[1552,256]{1,0:T(8,128)(2,1)}, bf16[1552,256]{1,0:T(8,128)(2,1)S(1)}, u32[]{:S(2)}, u32[]{:S(2)}) collective-permute-start(bf16[1552,256]{1,0:T(8,128)(2,1)} %get-tuple-element.21.refs_0_), channel_id=1, source_target_pairs={{0,2},{1,3},{2,0},{3,1},{4,6},{5,7},{6,4},{7,5},{8,10},{9,11},{10,... | collective-permute-start | bytes 2383880 | tf_op jit(solution)/shard_map/ppermute | solution.py:43
  17.6 21.8 %collective-permute-start = (bf16[1552,256]{1,0:T(8,128)(2,1)}, bf16[1552,256]{1,0:T(8,128)(2,1)S(1)}, u32[]{:S(2)}, u32[]{:S(2)}) collective-permute-start(bf16[1552,256]{1,0:T(8,128)(2,1)} %get-tuple-element.21.refs_0_), channel_id=1, source_target_pairs={{0,1},{1,0},{2,3},{3,2},{4,5},{5,4},{6,7},{7,6},{8,9},{9,8},{10,11... | collective-permute-start | bytes 2383880 | tf_op jit(solution)/shard_map/ppermute | solution.py:43
  31.3 26.3 %collective-permute-start.15 = (bf16[4,32,2816]{2,1,0:T(8,128)(2,1)S(1)}, bf16[4,32,2816]{2,1,0:T(8,128)(2,1)S(1)}, u32[]{:S(2)}, u32[]{:S(2)}) collective-permute-start(bf16[4,32,2816]{2,1,0:T(8,128)(2,1)S(1)} %stack.89.refs_1_.refs_5_.refs_10_), channel_id=1, source_target_pairs={{0,2},{1,3},{2,0},{3,1},{4,6},{5,7},{6,4},{7,5},{8,10},{9,11},{10,... | collective-permute-start | bytes 2162696 | tf_op jit(solution)/shard_map/ppermute | solution.py:78
  32.4 26.2 %collective-permute-start.6 = (bf16[512,256]{1,0:T(8,128)(2,1)}, bf16[512,256]{1,0:T(8,128)(2,1)S(1)}, u32[]{:S(2)}, u32[]{:S(2)}) collective-permute-start(bf16[512,256]{1,0:T(8,128)(2,1)} %gate.13.refs_2_.refs_5_), channel_id=1, source_target_pairs={{0,4},{4,8},{8,12},{1,5},{5,9},{9,13},{2,6},{6,10},{10,14},{3,7},{... | collective-permute-start | bytes 786440 | tf_op jit(solution)/shard_map/ppermute | solution.py:104
  38.1 20.6 %collective-permute-start.7 = (bf16[512,256]{1,0:T(8,128)(2,1)}, bf16[512,256]{1,0:T(8,128)(2,1)S(1)}, u32[]{:S(2)}, u32[]{:S(2)}) collective-permute-start(bf16[512,256]{1,0:T(8,128)(2,1)} %gate.13.refs_2_.refs_5_), channel_id=1, source_target_pairs={{4,0},{8,4},{12,8},{5,1},{9,5},{13,9},{6,2},{10,6},{14,10},{7,3},{... | collective-permute-start | bytes 786440 | tf_op jit(solution)/shard_map/ppermute | solution.py:105
  39.4 20.0 %collective-permute-start.8 = (bf16[512,256]{1,0:T(8,128)(2,1)}, bf16[512,256]{1,0:T(8,128)(2,1)S(1)}, u32[]{:S(2)}, u32[]{:S(2)}) collective-permute-start(bf16[512,256]{1,0:T(8,128)(2,1)} %gate.13.refs_2_.refs_5_), channel_id=1, source_target_pairs={{0,8},{4,12},{8,0},{12,4},{1,9},{5,13},{9,1},{13,5},{2,10},{6,14},... | collective-permute-start | bytes 786440 | tf_op jit(solution)/shard_map/ppermute | solution.py:109
  41.7 24.7 %collective-permute-start.17 = (bf16[4,32,2816]{2,1,0:T(8,128)(2,1)S(1)}, bf16[4,32,2816]{2,1,0:T(8,128)(2,1)S(1)}, u32[]{:S(2)}, u32[]{:S(2)}) collective-permute-start(bf16[4,32,2816]{2,1,0:T(8,128)(2,1)S(1)} %stack.89.refs_1_.refs_5_.refs_10_), channel_id=1, source_target_pairs={{0,16},{16,0},{1,17},{17,1},{2,18},{18,2},{3,19},{19,3},{4,20},{20... | collective-permute-start | bytes 2162696 | tf_op jit(solution)/shard_map/ppermute | solution.py:78
  58.1 28.0 %collective-permute-start.19 = (bf16[4,32,2816]{2,1,0:T(8,128)(2,1)S(1)}, bf16[4,32,2816]{2,1,0:T(8,128)(2,1)S(1)}, u32[]{:S(2)}, u32[]{:S(2)}) collective-permute-start(bf16[4,32,2816]{2,1,0:T(8,128)(2,1)S(1)} %gate.16.refs_0_), channel_id=1, source_target_pairs={{0,16},{16,0},{1,17},{17,1},{2,18},{18,2},{3,19},{19,3},{4,20},{20... | collective-permute-start | bytes 2162696 | tf_op jit(solution)/shard_map/ppermute | solution.py:78
  60.1 16.3 %collective-permute-start.10 = (bf16[512,256]{1,0:T(8,128)(2,1)S(1)}, bf16[512,256]{1,0:T(8,128)(2,1)S(1)}, u32[]{:S(2)}, u32[]{:S(2)}) collective-permute-start(bf16[512,256]{1,0:T(8,128)(2,1)S(1)} %gate.15.refs_0_), channel_id=1, source_target_pairs={{4,0},{8,4},{12,8},{5,1},{9,5},{13,9},{6,2},{10,6},{14,10},{7,3},{... | collective-permute-start | bytes 786440 | tf_op jit(solution)/shard_map/ppermute | solution.py:105
  94.4 30.1 %collective-permute-start.25 = (bf16[160,1792]{1,0:T(8,128)(2,1)S(1)}, bf16[160,1792]{1,0:T(8,128)(2,1)S(1)}, u32[]{:S(2)}, u32[]{:S(2)}) collective-permute-start(bf16[160,1792]{1,0:T(8,128)(2,1)S(1)} %get-tuple-element.33), channel_id=1, source_target_pairs={{0,8},{4,12},{8,0},{12,4},{1,9},{5,13},{9,1},{13,5},{2,10},{6,14},... | collective-permute-start | bytes 1720328 | tf_op jit(solution)/shard_map/ppermute | solution.py:109
  98.3 28.0 %collective-permute-start.21 = (bf16[160,1792]{1,0:T(8,128)(2,1)S(1)}, bf16[160,1792]{1,0:T(8,128)(2,1)S(1)}, u32[]{:S(2)}, u32[]{:S(2)}) collective-permute-start(bf16[160,1792]{1,0:T(8,128)(2,1)S(1)} %get-tuple-element.32.refs_0_), channel_id=1, source_target_pairs={{0,4},{4,8},{8,12},{1,5},{5,9},{9,13},{2,6},{6,10},{10,14},{3,7},{... | collective-permute-start | bytes 1720328 | tf_op jit(solution)/shard_map/ppermute | solution.py:104
  102.7 26.6 %collective-permute-start.22 = (bf16[160,1792]{1,0:T(8,128)(2,1)S(1)}, bf16[160,1792]{1,0:T(8,128)(2,1)S(1)}, u32[]{:S(2)}, u32[]{:S(2)}) collective-permute-start(bf16[160,1792]{1,0:T(8,128)(2,1)S(1)} %get-tuple-element.32.refs_0_), channel_id=1, source_target_pairs={{4,0},{8,4},{12,8},{5,1},{9,5},{13,9},{6,2},{10,6},{14,10},{7,3},{... | collective-permute-start | bytes 1720328 | tf_op jit(solution)/shard_map/ppermute | solution.py:105
  125.0 31.3 %collective-permute-start.29 = (bf16[128,1792]{1,0:T(8,128)(2,1)S(1)}, bf16[128,1792]{1,0:T(8,128)(2,1)S(1)}, u32[]{:S(2)}, u32[]{:S(2)}) collective-permute-start(bf16[128,1792]{1,0:T(8,128)(2,1)S(1)} %gate.22), channel_id=1, source_target_pairs={{0,8},{4,12},{8,0},{12,4},{1,9},{5,13},{9,1},{13,5},{2,10},{6,14},... | collective-permute-start | bytes 1376264 | tf_op jit(solution)/shard_map/ppermute | solution.py:109
  125.1 40.7 %collective-permute-start.26 = (bf16[160,1792]{1,0:T(8,128)(2,1)S(1)}, bf16[160,1792]{1,0:T(8,128)(2,1)S(1)}, u32[]{:S(2)}, u32[]{:S(2)}) collective-permute-start(bf16[160,1792]{1,0:T(8,128)(2,1)S(1)} %collective-permute-done.25.refs_1_.refs_3_), channel_id=1, source_target_pairs={{4,0},{8,12},{5,1},{9,13},{6,2},{10,14},{7,3},{11,15},{20,16},{24,... | collective-permute-start | bytes 1720328 | tf_op jit(solution)/shard_map/ppermute | solution.py:110
  129.9 30.6 %collective-permute-start.23 = (bf16[128,1792]{1,0:T(8,128)(2,1)S(1)}, bf16[128,1792]{1,0:T(8,128)(2,1)S(1)}, u32[]{:S(2)}, u32[]{:S(2)}) collective-permute-start(bf16[128,1792]{1,0:T(8,128)(2,1)S(1)} %gate.20.refs_0_), channel_id=1, source_target_pairs={{0,4},{4,8},{8,12},{1,5},{5,9},{9,13},{2,6},{6,10},{10,14},{3,7},{... | collective-permute-start | bytes 1376264 | tf_op jit(solution)/shard_map/ppermute | solution.py:104
  149.6 16.2 %collective-permute-start.24 = (bf16[128,1792]{1,0:T(8,128)(2,1)S(1)}, bf16[128,1792]{1,0:T(8,128)(2,1)S(1)}, u32[]{:S(2)}, u32[]{:S(2)}) collective-permute-start(bf16[128,1792]{1,0:T(8,128)(2,1)S(1)} %gate.20.refs_0_), channel_id=1, source_target_pairs={{4,0},{8,4},{12,8},{5,1},{9,5},{13,9},{6,2},{10,6},{14,10},{7,3},{... | collective-permute-start | bytes 1376264 | tf_op jit(solution)/shard_map/ppermute | solution.py:105
  156.8 28.9 %collective-permute-start.33 = (bf16[128,1792]{1,0:T(8,128)(2,1)S(1)}, bf16[128,1792]{1,0:T(8,128)(2,1)S(1)}, u32[]{:S(2)}, u32[]{:S(2)}) collective-permute-start(bf16[128,1792]{1,0:T(8,128)(2,1)S(1)} %gate.24), channel_id=1, source_target_pairs={{0,8},{4,12},{8,0},{12,4},{1,9},{5,13},{9,1},{13,5},{2,10},{6,14},... | collective-permute-start | bytes 1376264 | tf_op jit(solution)/shard_map/ppermute | solution.py:109
  156.9 30.7 %collective-permute-start.30 = (bf16[128,1792]{1,0:T(8,128)(2,1)S(1)}, bf16[128,1792]{1,0:T(8,128)(2,1)S(1)}, u32[]{:S(2)}, u32[]{:S(2)}) collective-permute-start(bf16[128,1792]{1,0:T(8,128)(2,1)S(1)} %collective-permute-done.29.refs_1_.refs_3_), channel_id=1, source_target_pairs={{4,0},{8,12},{5,1},{9,13},{6,2},{10,14},{7,3},{11,15},{20,16},{24,... | collective-permute-start | bytes 1376264 | tf_op jit(solution)/shard_map/ppermute | solution.py:110
  166.3 24.0 %collective-permute-start.27 = (bf16[128,1792]{1,0:T(8,128)(2,1)S(1)}, bf16[128,1792]{1,0:T(8,128)(2,1)S(1)}, u32[]{:S(2)}, u32[]{:S(2)}) collective-permute-start(bf16[128,1792]{1,0:T(8,128)(2,1)S(1)} %gate.21.refs_0_), channel_id=1, source_target_pairs={{0,4},{4,8},{8,12},{1,5},{5,9},{9,13},{2,6},{6,10},{10,14},{3,7},{... | collective-permute-start | bytes 1376264 | tf_op jit(solution)/shard_map/ppermute | solution.py:104
  186.2 23.8 %collective-permute-start.34 = (bf16[96,1792]{1,0:T(8,128)(2,1)S(1)}, bf16[96,1792]{1,0:T(8,128)(2,1)S(1)}, u32[]{:S(2)}, u32[]{:S(2)}) collective-permute-start(bf16[96,1792]{1,0:T(8,128)(2,1)S(1)} %gate.25), channel_id=1, source_target_pairs={{0,8},{4,12},{8,0},{12,4},{1,9},{5,13},{9,1},{13,5},{2,10},{6,14},... | collective-permute-start | bytes 1032200 | tf_op jit(solution)/shard_map/ppermute | solution.py:109
  186.3 32.7 %collective-permute-start.36 = (bf16[128,1792]{1,0:T(8,128)(2,1)S(1)}, bf16[128,1792]{1,0:T(8,128)(2,1)S(1)}, u32[]{:S(2)}, u32[]{:S(2)}) collective-permute-start(bf16[128,1792]{1,0:T(8,128)(2,1)S(1)} %collective-permute-done.33.refs_1_.refs_3_), channel_id=1, source_target_pairs={{4,0},{8,12},{5,1},{9,13},{6,2},{10,14},{7,3},{11,15},{20,16},{24,... | collective-permute-start | bytes 1376264 | tf_op jit(solution)/shard_map/ppermute | solution.py:110
  195.9 26.6 %collective-permute-start.31 = (bf16[96,1792]{1,0:T(8,128)(2,1)S(1)}, bf16[96,1792]{1,0:T(8,128)(2,1)S(1)}, u32[]{:S(2)}, u32[]{:S(2)}) collective-permute-start(bf16[96,1792]{1,0:T(8,128)(2,1)S(1)} %gate.23.refs_0_), channel_id=1, source_target_pairs={{0,4},{4,8},{8,12},{1,5},{5,9},{9,13},{2,6},{6,10},{10,14},{3,7},{... | collective-permute-start | bytes 1032200 | tf_op jit(solution)/shard_map/ppermute | solution.py:104
  206.5 16.0 %collective-permute-start.32 = (bf16[96,1792]{1,0:T(8,128)(2,1)S(1)}, bf16[96,1792]{1,0:T(8,128)(2,1)S(1)}, u32[]{:S(2)}, u32[]{:S(2)}) collective-permute-start(bf16[96,1792]{1,0:T(8,128)(2,1)S(1)} %gate.23.refs_0_), channel_id=1, source_target_pairs={{4,0},{8,4},{12,8},{5,1},{9,5},{13,9},{6,2},{10,6},{14,10},{7,3},{... | collective-permute-start | bytes 1032200 | tf_op jit(solution)/shard_map/ppermute | solution.py:105
  210.0 17.1 %collective-permute-start.35 = (bf16[96,1792]{1,0:T(8,128)(2,1)S(1)}, bf16[96,1792]{1,0:T(8,128)(2,1)S(1)}, u32[]{:S(2)}, u32[]{:S(2)}) collective-permute-start(bf16[96,1792]{1,0:T(8,128)(2,1)S(1)} %collective-permute-done.34.refs_3_), channel_id=1, source_target_pairs={{4,0},{8,12},{5,1},{9,13},{6,2},{10,14},{7,3},{11,15},{20,16},{24,... | collective-permute-start | bytes 1032200 | tf_op jit(solution)/shard_map/ppermute | solution.py:110
  (20 other events, 323.7 us)

commit v18 on v17

--- a/solution.py
+++ b/solution.py
@@ -582,9 +582,6 @@
     halves = 1
     half = rows // halves
     sizes = [chunk] * (half // chunk)
-    if len(sizes) > 1 and chunk % 128 == 0:
-        sizes[0] += 32
-        sizes[-1] -= 32
     splits = [[(sum(sizes[:n]), size) for n, size in enumerate(sizes)]] * halves
 
     table = Table(contexts, count)

time: 231 us -> 231 us (level)
    ppermute x6, waiting for transfers between devices: 13.2 us -> 16.2 us  [line_far(): return (far, lax.ppermute(far, 'tensor', [(1, 0), (2, 3)]))]
where the time goes in v18:
time: 231 us; the launch traced here: 230 us
  starting transfers between devices  93.7 us (41%)
  waiting for transfers between devices  81.3 us (35%)
  Pallas kernels  46.9 us (20%)
  local copies, waits for them, and re-layouts  4.17 us (2%)
  between operations  2.39 us (1%)
    ppermute x6, starting transfers between devices, line_near(): up = lax.ppermute(value, 'tensor', [(0, 1), (1, 2), (2, 3)])  58.6 us
    pallas_call x22, Pallas kernels, call(): pl.pallas_call(kernel, grid_spec=pltpu.PrefetchScalarGridSpec(num_scalar_...  46.9 us
    ppermute x6, waiting for transfers between devices, line_far(): far = lax.ppermute(value, 'tensor', [(0, 2), (1, 3), (2, 0), (3, 1)])  33.7 us
    ppermute x6, waiting for transfers between devices, line_far(): return (far, lax.ppermute(far, 'tensor', [(1, 0), (2, 3)]))  16.2 us
    ppermute x6, waiting for transfers between devices, line_near(): return (up, lax.ppermute(value, 'tensor', [(1, 0), (2, 1), (3, 2)]))  14 us
    ppermute x3, waiting for transfers between devices, per_device(): parts.append(lax.ppermute(cuts[shift], 'tensor', pairs))  10.4 us
    ppermute x6, starting transfers between devices, line_near(): return (up, lax.ppermute(value, 'tensor', [(1, 0), (2, 1), (3, 2)]))  7.75 us
    ppermute x6, starting transfers between devices, line_far(): return (far, lax.ppermute(far, 'tensor', [(1, 0), (2, 3)]))  7.73 us
  transfers between devices with their start and end apart: 37, of which 19 were waited for; matrix products, arithmetic and copies ran while one was open for 0% of the time, Pallas kernels for 15%

profile of v18, /device:TPU:0, one launch (start us, length us, event | category | flops | bytes accessed | tf_op | source)
XLA Modules:
  0.0 230.4 jit_solution(12520602738896983872)
XLA Ops:
  4.5 4.6 %prepare.1 = (bf16[512,256]{1,0:T(8,128)(2,1)}, bf16[1552,256]{1,0:T(8,128)(2,1)}, bf16[32,2816]{1,0:T(8,128)(2,1)}, bf16[32,2816]{1,0:T(8,128)(2,1)}, bf16[32,2...) custom-call(s32[20]{0:T(128)} %stack.86.info, bf16[512,256]{1,0:T(8,128)(2,1)} %q_hbm.1, ...), custom_call_target="tpu_custom_call" | custom-call | flops 1 | bytes 1 | tf_op jit(solution)/shard_map/prepare/pallas_call | solution.py:165
  17.6 4.1 %collective-permute-done.2.refs_1_ = bf16[32,2816]{1,0:T(8,128)(2,1)S(1)} collective-permute-done((bf16[32,2816]{1,0:T(8,128)(2,1)}, bf16[32,2816]{1,0:T(8,128)(2,1)S(1)}, u32[]{:S(2)}, u32[]{:S(2)}) %collective-permute-start.2) | collective-permute-done | bytes 180256 | tf_op jit(solution)/shard_map/ppermute | solution.py:607
  21.7 6.3 %collective-permute-done.3.refs_2_ = bf16[32,2816]{1,0:T(8,128)(2,1)S(1)} collective-permute-done((bf16[32,2816]{1,0:T(8,128)(2,1)}, bf16[32,2816]{1,0:T(8,128)(2,1)S(1)}, u32[]{:S(2)}, u32[]{:S(2)}) %collective-permute-start.3) | collective-permute-done | bytes 180256 | tf_op jit(solution)/shard_map/ppermute | solution.py:607
  32.4 5.7 %collective-permute-start.6 = (bf16[512,256]{1,0:T(8,128)(2,1)}, bf16[512,256]{1,0:T(8,128)(2,1)S(1)}, u32[]{:S(2)}, u32[]{:S(2)}) collective-permute-start(bf16[512,256]{1,0:T(8,128)(2,1)} %gate.13.refs_2_.refs_5_), channel_id=1, source_target_pairs={{0,4},{4,8},{8,12},{1,5},{5,9},{9,13},{2,6},{6,10},{10,14},{3,7},{... | collective-permute-start | bytes 786440 | tf_op jit(solution)/shard_map/ppermute | solution.py:104
  45.4 12.2 %attend.1.refs_0_.refs_1_ = bf16[512,256]{1,0:T(8,128)(2,1)S(1)} custom-call(s32[20]{0:T(128)S(1)} %copy-done.3, bf16[512,256]{1,0:T(8,128)(2,1)S(1)} %copy-done.6, bf16[1552,256]{1,0:T(8,128)(2,1)S(1)} %copy-done.5, bf16[1552,256]{1,0:T(8,128)(2,1)S(1)} %collective-permute-done.refs_1_, bf16[1552,256]{1,0:T(8,128)(2,1)S(1)} %gate.14.refs_2_, ...), custom_call_target="tpu_custom_call" | custom-call | flops 12884901888 | bytes 1 | tf_op jit(solution)/shard_map/attend/pallas_call | solution.py:165
  61.4 5.1 %collective-permute-start.9 = (bf16[512,256]{1,0:T(8,128)(2,1)S(1)}, bf16[512,256]{1,0:T(8,128)(2,1)S(1)}, u32[]{:S(2)}, u32[]{:S(2)}) collective-permute-start(bf16[512,256]{1,0:T(8,128)(2,1)S(1)} %gate.15.refs_0_), channel_id=1, source_target_pairs={{0,4},{4,8},{8,12},{1,5},{5,9},{9,13},{2,6},{6,10},{10,14},{3,7},{... | collective-permute-start | bytes 786440 | tf_op jit(solution)/shard_map/ppermute | solution.py:104
  67.8 6.6 %collective-permute-done.11.refs_3_ = bf16[512,256]{1,0:T(8,128)(2,1)S(1)} collective-permute-done((bf16[512,256]{1,0:T(8,128)(2,1)S(1)}, bf16[512,256]{1,0:T(8,128)(2,1)S(1)}, u32[]{:S(2)}, u32[]{:S(2)}) %collective-permute-start.11) | collective-permute-done | bytes 262176 | tf_op jit(solution)/shard_map/ppermute | solution.py:109
  77.5 4.5 %collective-permute-done.13.refs_5_.refs_9_ = bf16[512,256]{1,0:T(8,128)(2,1)S(1)} collective-permute-done((bf16[512,256]{1,0:T(8,128)(2,1)S(1)}, bf16[512,256]{1,0:T(8,128)(2,1)S(1)}, u32[]{:S(2)}, u32[]{:S(2)}) %collective-permute-start.13) | collective-permute-done | bytes 262176 | tf_op jit(solution)/shard_map/ppermute | solution.py:110
  82.0 4.1 %collective-permute-done.12.refs_4_ = bf16[512,256]{1,0:T(8,128)(2,1)S(1)} collective-permute-done((bf16[512,256]{1,0:T(8,128)(2,1)S(1)}, bf16[512,256]{1,0:T(8,128)(2,1)S(1)}, u32[]{:S(2)}, u32[]{:S(2)}) %collective-permute-start.12) | collective-permute-done | bytes 262176 | tf_op jit(solution)/shard_map/ppermute | solution.py:110
  89.9 4.2 %project.1 = (bf16[128,1792]{1,0:T(8,128)(2,1)S(1)}, bf16[128,1792]{1,0:T(8,128)(2,1)S(1)}, bf16[128,1792]{1,0:T(8,128)(2,1)S(1)}, bf16[128,1792]{1,0:T(8,128)(2...) custom-call(s32[20]{0:T(128)S(1)} %copy-done.3, ...), custom_call_target="tpu_custom_call" | custom-call | flops 1 | bytes 1 | tf_op jit(solution)/shard_map/project/pallas_call | solution.py:165
  94.2 4.0 %collective-permute-start.25 = (bf16[128,1792]{1,0:T(8,128)(2,1)S(1)}, bf16[128,1792]{1,0:T(8,128)(2,1)S(1)}, u32[]{:S(2)}, u32[]{:S(2)}) collective-permute-start(bf16[128,1792]{1,0:T(8,128)(2,1)S(1)} %get-tuple-element.33), channel_id=1, source_target_pairs={{0,8},{4,12},{8,0},{12,4},{1,9},{5,13},{9,1},{13,5},{2,10},{6,14},... | collective-permute-start | bytes 1376264 | tf_op jit(solution)/shard_map/ppermute | solution.py:109
  98.1 4.4 %collective-permute-start.21 = (bf16[128,1792]{1,0:T(8,128)(2,1)S(1)}, bf16[128,1792]{1,0:T(8,128)(2,1)S(1)}, u32[]{:S(2)}, u32[]{:S(2)}) collective-permute-start(bf16[128,1792]{1,0:T(8,128)(2,1)S(1)} %get-tuple-element.32.refs_0_), channel_id=1, source_target_pairs={{0,4},{4,8},{8,12},{1,5},{5,9},{9,13},{2,6},{6,10},{10,14},{3,7},{... | collective-permute-start | bytes 1376264 | tf_op jit(solution)/shard_map/ppermute | solution.py:104
  103.8 4.4 %project_raw.1 = (bf16[512,1024]{1,0:T(8,128)(2,1)S(1)}, bf16[512,2048]{1,0:T(8,128)(2,1)}) custom-call(s32[20]{0:T(128)S(1)} %copy-done.3, bf16[512,256]{1,0:T(8,128)(2,1)S(1)} %gate.15.refs_0_, bf16[512,256]{1,0:T(8,128)(2,1)S(1)} %collective-permute-done.9.refs_1_, ...), custom_call_target="tpu_custom_call", output_to_operand_aliasing={{1}: (19, {})} | custom-call | flops 1 | bytes 1 | tf_op jit(solution)/shard_map/project_raw/pallas_call | solution.py:165
  108.2 11.1 %collective-permute-done.25.refs_1_.refs_3_ = bf16[128,1792]{1,0:T(8,128)(2,1)S(1)} collective-permute-done((bf16[128,1792]{1,0:T(8,128)(2,1)S(1)}, bf16[128,1792]{1,0:T(8,128)(2,1)S(1)}, u32[]{:S(2)}, u32[]{:S(2)}) %collective-permute-start.25) | collective-permute-done | bytes 458784 | tf_op jit(solution)/shard_map/ppermute | solution.py:109
  124.8 17.2 %collective-permute-start.23 = (bf16[128,1792]{1,0:T(8,128)(2,1)S(1)}, bf16[128,1792]{1,0:T(8,128)(2,1)S(1)}, u32[]{:S(2)}, u32[]{:S(2)}) collective-permute-start(bf16[128,1792]{1,0:T(8,128)(2,1)S(1)} %gate.20.refs_0_), channel_id=1, source_target_pairs={{0,4},{4,8},{8,12},{1,5},{5,9},{9,13},{2,6},{6,10},{10,14},{3,7},{... | collective-permute-start | bytes 1376264 | tf_op jit(solution)/shard_map/ppermute | solution.py:104
  143.3 5.4 %collective-permute-done.29.refs_1_.refs_3_ = bf16[128,1792]{1,0:T(8,128)(2,1)S(1)} collective-permute-done((bf16[128,1792]{1,0:T(8,128)(2,1)S(1)}, bf16[128,1792]{1,0:T(8,128)(2,1)S(1)}, u32[]{:S(2)}, u32[]{:S(2)}) %collective-permute-start.29) | collective-permute-done | bytes 458784 | tf_op jit(solution)/shard_map/ppermute | solution.py:109
  152.9 5.3 %collective-permute-done.24.refs_2_ = bf16[128,1792]{1,0:T(8,128)(2,1)S(1)} collective-permute-done((bf16[128,1792]{1,0:T(8,128)(2,1)S(1)}, bf16[128,1792]{1,0:T(8,128)(2,1)S(1)}, u32[]{:S(2)}, u32[]{:S(2)}) %collective-permute-start.24) | collective-permute-done | bytes 458784 | tf_op jit(solution)/shard_map/ppermute | solution.py:105
  158.8 13.1 %collective-permute-start.27 = (bf16[128,1792]{1,0:T(8,128)(2,1)S(1)}, bf16[128,1792]{1,0:T(8,128)(2,1)S(1)}, u32[]{:S(2)}, u32[]{:S(2)}) collective-permute-start(bf16[128,1792]{1,0:T(8,128)(2,1)S(1)} %gate.21.refs_0_), channel_id=1, source_target_pairs={{0,4},{4,8},{8,12},{1,5},{5,9},{9,13},{2,6},{6,10},{10,14},{3,7},{... | collective-permute-start | bytes 1376264 | tf_op jit(solution)/shard_map/ppermute | solution.py:104
  173.2 5.0 %collective-permute-done.33.refs_1_.refs_3_ = bf16[128,1792]{1,0:T(8,128)(2,1)S(1)} collective-permute-done((bf16[128,1792]{1,0:T(8,128)(2,1)S(1)}, bf16[128,1792]{1,0:T(8,128)(2,1)S(1)}, u32[]{:S(2)}, u32[]{:S(2)}) %collective-permute-start.33) | collective-permute-done | bytes 458784 | tf_op jit(solution)/shard_map/ppermute | solution.py:109
  182.8 5.0 %collective-permute-done.28.refs_2_ = bf16[128,1792]{1,0:T(8,128)(2,1)S(1)} collective-permute-done((bf16[128,1792]{1,0:T(8,128)(2,1)S(1)}, bf16[128,1792]{1,0:T(8,128)(2,1)S(1)}, u32[]{:S(2)}, u32[]{:S(2)}) %collective-permute-start.28) | collective-permute-done | bytes 458784 | tf_op jit(solution)/shard_map/ppermute | solution.py:105
  188.3 13.1 %collective-permute-start.31 = (bf16[128,1792]{1,0:T(8,128)(2,1)S(1)}, bf16[128,1792]{1,0:T(8,128)(2,1)S(1)}, u32[]{:S(2)}, u32[]{:S(2)}) collective-permute-start(bf16[128,1792]{1,0:T(8,128)(2,1)S(1)} %gate.23.refs_0_), channel_id=1, source_target_pairs={{0,4},{4,8},{8,12},{1,5},{5,9},{9,13},{2,6},{6,10},{10,14},{3,7},{... | collective-permute-start | bytes 1376264 | tf_op jit(solution)/shard_map/ppermute | solution.py:104
  202.7 4.9 %collective-permute-done.34.refs_3_ = bf16[128,1792]{1,0:T(8,128)(2,1)S(1)} collective-permute-done((bf16[128,1792]{1,0:T(8,128)(2,1)S(1)}, bf16[128,1792]{1,0:T(8,128)(2,1)S(1)}, u32[]{:S(2)}, u32[]{:S(2)}) %collective-permute-start.34) | collective-permute-done | bytes 458784 | tf_op jit(solution)/shard_map/ppermute | solution.py:109
  208.9 3.5 %norm.4.refs_6_ = bf16[512,8192]{1,0:T(8,128)(2,1)} custom-call(s32[20]{0:T(128)S(1)} %copy-done.3, f32[1,8192]{1,0:T(1,128)S(1)} %bitcast.23, bf16[128,1792]{1,0:T(8,128)(2,1)S(1)} %get-tuple-element.32.refs_0_, bf16[128,1792]{1,0:T(8,128)(2,1)S(1)} %collective-permute-done.21.refs_1_, bf16[128,1792]{1,0:T(8,128)(2,1)S(1)} %collective-permute-done.22.refs_2_, ...), custom_call_target="tpu_custom_call" | custom-call | flops 1 | bytes 1 | tf_op jit(solution)/shard_map/norm/pallas_call | solution.py:165
  219.3 7.6 %collective-permute-done.35.refs_4_ = bf16[128,1792]{1,0:T(8,128)(2,1)S(1)} collective-permute-done((bf16[128,1792]{1,0:T(8,128)(2,1)S(1)}, bf16[128,1792]{1,0:T(8,128)(2,1)S(1)}, u32[]{:S(2)}, u32[]{:S(2)}) %collective-permute-start.35) | collective-permute-done | bytes 458784 | tf_op jit(solution)/shard_map/ppermute | solution.py:110
  (91 shorter events, 66.7 us)
Async XLA Ops:
  9.1 21.5 %collective-permute-start.1 = (bf16[1552,256]{1,0:T(8,128)(2,1)}, bf16[1552,256]{1,0:T(8,128)(2,1)S(1)}, u32[]{:S(2)}, u32[]{:S(2)}) collective-permute-start(bf16[1552,256]{1,0:T(8,128)(2,1)} %get-tuple-element.21.refs_0_), channel_id=1, source_target_pairs={{0,2},{1,3},{2,0},{3,1},{4,6},{5,7},{6,4},{7,5},{8,10},{9,11},{10,... | collective-permute-start | bytes 2383880 | tf_op jit(solution)/shard_map/ppermute | solution.py:43
  17.6 21.8 %collective-permute-start = (bf16[1552,256]{1,0:T(8,128)(2,1)}, bf16[1552,256]{1,0:T(8,128)(2,1)S(1)}, u32[]{:S(2)}, u32[]{:S(2)}) collective-permute-start(bf16[1552,256]{1,0:T(8,128)(2,1)} %get-tuple-element.21.refs_0_), channel_id=1, source_target_pairs={{0,1},{1,0},{2,3},{3,2},{4,5},{5,4},{6,7},{7,6},{8,9},{9,8},{10,11... | collective-permute-start | bytes 2383880 | tf_op jit(solution)/shard_map/ppermute | solution.py:43
  31.3 26.3 %collective-permute-start.15 = (bf16[4,32,2816]{2,1,0:T(8,128)(2,1)S(1)}, bf16[4,32,2816]{2,1,0:T(8,128)(2,1)S(1)}, u32[]{:S(2)}, u32[]{:S(2)}) collective-permute-start(bf16[4,32,2816]{2,1,0:T(8,128)(2,1)S(1)} %stack.89.refs_1_.refs_5_.refs_10_), channel_id=1, source_target_pairs={{0,2},{1,3},{2,0},{3,1},{4,6},{5,7},{6,4},{7,5},{8,10},{9,11},{10,... | collective-permute-start | bytes 2162696 | tf_op jit(solution)/shard_map/ppermute | solution.py:78
  32.4 26.3 %collective-permute-start.6 = (bf16[512,256]{1,0:T(8,128)(2,1)}, bf16[512,256]{1,0:T(8,128)(2,1)S(1)}, u32[]{:S(2)}, u32[]{:S(2)}) collective-permute-start(bf16[512,256]{1,0:T(8,128)(2,1)} %gate.13.refs_2_.refs_5_), channel_id=1, source_target_pairs={{0,4},{4,8},{8,12},{1,5},{5,9},{9,13},{2,6},{6,10},{10,14},{3,7},{... | collective-permute-start | bytes 786440 | tf_op jit(solution)/shard_map/ppermute | solution.py:104
  38.1 20.6 %collective-permute-start.7 = (bf16[512,256]{1,0:T(8,128)(2,1)}, bf16[512,256]{1,0:T(8,128)(2,1)S(1)}, u32[]{:S(2)}, u32[]{:S(2)}) collective-permute-start(bf16[512,256]{1,0:T(8,128)(2,1)} %gate.13.refs_2_.refs_5_), channel_id=1, source_target_pairs={{4,0},{8,4},{12,8},{5,1},{9,5},{13,9},{6,2},{10,6},{14,10},{7,3},{... | collective-permute-start | bytes 786440 | tf_op jit(solution)/shard_map/ppermute | solution.py:105
  39.4 20.0 %collective-permute-start.8 = (bf16[512,256]{1,0:T(8,128)(2,1)}, bf16[512,256]{1,0:T(8,128)(2,1)S(1)}, u32[]{:S(2)}, u32[]{:S(2)}) collective-permute-start(bf16[512,256]{1,0:T(8,128)(2,1)} %gate.13.refs_2_.refs_5_), channel_id=1, source_target_pairs={{0,8},{4,12},{8,0},{12,4},{1,9},{5,13},{9,1},{13,5},{2,10},{6,14},... | collective-permute-start | bytes 786440 | tf_op jit(solution)/shard_map/ppermute | solution.py:109
  41.7 24.8 %collective-permute-start.17 = (bf16[4,32,2816]{2,1,0:T(8,128)(2,1)S(1)}, bf16[4,32,2816]{2,1,0:T(8,128)(2,1)S(1)}, u32[]{:S(2)}, u32[]{:S(2)}) collective-permute-start(bf16[4,32,2816]{2,1,0:T(8,128)(2,1)S(1)} %stack.89.refs_1_.refs_5_.refs_10_), channel_id=1, source_target_pairs={{0,16},{16,0},{1,17},{17,1},{2,18},{18,2},{3,19},{19,3},{4,20},{20... | collective-permute-start | bytes 2162696 | tf_op jit(solution)/shard_map/ppermute | solution.py:78
  58.1 27.9 %collective-permute-start.19 = (bf16[4,32,2816]{2,1,0:T(8,128)(2,1)S(1)}, bf16[4,32,2816]{2,1,0:T(8,128)(2,1)S(1)}, u32[]{:S(2)}, u32[]{:S(2)}) collective-permute-start(bf16[4,32,2816]{2,1,0:T(8,128)(2,1)S(1)} %gate.16.refs_0_), channel_id=1, source_target_pairs={{0,16},{16,0},{1,17},{17,1},{2,18},{18,2},{3,19},{19,3},{4,20},{20... | collective-permute-start | bytes 2162696 | tf_op jit(solution)/shard_map/ppermute | solution.py:78
  60.1 16.3 %collective-permute-start.10 = (bf16[512,256]{1,0:T(8,128)(2,1)S(1)}, bf16[512,256]{1,0:T(8,128)(2,1)S(1)}, u32[]{:S(2)}, u32[]{:S(2)}) collective-permute-start(bf16[512,256]{1,0:T(8,128)(2,1)S(1)} %gate.15.refs_0_), channel_id=1, source_target_pairs={{4,0},{8,4},{12,8},{5,1},{9,5},{13,9},{6,2},{10,6},{14,10},{7,3},{... | collective-permute-start | bytes 786440 | tf_op jit(solution)/shard_map/ppermute | solution.py:105
  94.2 25.1 %collective-permute-start.25 = (bf16[128,1792]{1,0:T(8,128)(2,1)S(1)}, bf16[128,1792]{1,0:T(8,128)(2,1)S(1)}, u32[]{:S(2)}, u32[]{:S(2)}) collective-permute-start(bf16[128,1792]{1,0:T(8,128)(2,1)S(1)} %get-tuple-element.33), channel_id=1, source_target_pairs={{0,8},{4,12},{8,0},{12,4},{1,9},{5,13},{9,1},{13,5},{2,10},{6,14},... | collective-permute-start | bytes 1376264 | tf_op jit(solution)/shard_map/ppermute | solution.py:109
  98.1 23.1 %collective-permute-start.21 = (bf16[128,1792]{1,0:T(8,128)(2,1)S(1)}, bf16[128,1792]{1,0:T(8,128)(2,1)S(1)}, u32[]{:S(2)}, u32[]{:S(2)}) collective-permute-start(bf16[128,1792]{1,0:T(8,128)(2,1)S(1)} %get-tuple-element.32.refs_0_), channel_id=1, source_target_pairs={{0,4},{4,8},{8,12},{1,5},{5,9},{9,13},{2,6},{6,10},{10,14},{3,7},{... | collective-permute-start | bytes 1376264 | tf_op jit(solution)/shard_map/ppermute | solution.py:104
  102.5 21.7 %collective-permute-start.22 = (bf16[128,1792]{1,0:T(8,128)(2,1)S(1)}, bf16[128,1792]{1,0:T(8,128)(2,1)S(1)}, u32[]{:S(2)}, u32[]{:S(2)}) collective-permute-start(bf16[128,1792]{1,0:T(8,128)(2,1)S(1)} %get-tuple-element.32.refs_0_), channel_id=1, source_target_pairs={{4,0},{8,4},{12,8},{5,1},{9,5},{13,9},{6,2},{10,6},{14,10},{7,3},{... | collective-permute-start | bytes 1376264 | tf_op jit(solution)/shard_map/ppermute | solution.py:105
  119.8 28.9 %collective-permute-start.29 = (bf16[128,1792]{1,0:T(8,128)(2,1)S(1)}, bf16[128,1792]{1,0:T(8,128)(2,1)S(1)}, u32[]{:S(2)}, u32[]{:S(2)}) collective-permute-start(bf16[128,1792]{1,0:T(8,128)(2,1)S(1)} %gate.22), channel_id=1, source_target_pairs={{0,8},{4,12},{8,0},{12,4},{1,9},{5,13},{9,1},{13,5},{2,10},{6,14},... | collective-permute-start | bytes 1376264 | tf_op jit(solution)/shard_map/ppermute | solution.py:109
  119.9 30.7 %collective-permute-start.26 = (bf16[128,1792]{1,0:T(8,128)(2,1)S(1)}, bf16[128,1792]{1,0:T(8,128)(2,1)S(1)}, u32[]{:S(2)}, u32[]{:S(2)}) collective-permute-start(bf16[128,1792]{1,0:T(8,128)(2,1)S(1)} %collective-permute-done.25.refs_1_.refs_3_), channel_id=1, source_target_pairs={{4,0},{8,12},{5,1},{9,13},{6,2},{10,14},{7,3},{11,15},{20,16},{24,... | collective-permute-start | bytes 1376264 | tf_op jit(solution)/shard_map/ppermute | solution.py:110
  124.8 28.1 %collective-permute-start.23 = (bf16[128,1792]{1,0:T(8,128)(2,1)S(1)}, bf16[128,1792]{1,0:T(8,128)(2,1)S(1)}, u32[]{:S(2)}, u32[]{:S(2)}) collective-permute-start(bf16[128,1792]{1,0:T(8,128)(2,1)S(1)} %gate.20.refs_0_), channel_id=1, source_target_pairs={{0,4},{4,8},{8,12},{1,5},{5,9},{9,13},{2,6},{6,10},{10,14},{3,7},{... | collective-permute-start | bytes 1376264 | tf_op jit(solution)/shard_map/ppermute | solution.py:104
  142.0 16.2 %collective-permute-start.24 = (bf16[128,1792]{1,0:T(8,128)(2,1)S(1)}, bf16[128,1792]{1,0:T(8,128)(2,1)S(1)}, u32[]{:S(2)}, u32[]{:S(2)}) collective-permute-start(bf16[128,1792]{1,0:T(8,128)(2,1)S(1)} %gate.20.refs_0_), channel_id=1, source_target_pairs={{4,0},{8,4},{12,8},{5,1},{9,5},{13,9},{6,2},{10,6},{14,10},{7,3},{... | collective-permute-start | bytes 1376264 | tf_op jit(solution)/shard_map/ppermute | solution.py:105
  149.3 28.9 %collective-permute-start.33 = (bf16[128,1792]{1,0:T(8,128)(2,1)S(1)}, bf16[128,1792]{1,0:T(8,128)(2,1)S(1)}, u32[]{:S(2)}, u32[]{:S(2)}) collective-permute-start(bf16[128,1792]{1,0:T(8,128)(2,1)S(1)} %gate.24), channel_id=1, source_target_pairs={{0,8},{4,12},{8,0},{12,4},{1,9},{5,13},{9,1},{13,5},{2,10},{6,14},... | collective-permute-start | bytes 1376264 | tf_op jit(solution)/shard_map/ppermute | solution.py:109
  149.3 30.8 %collective-permute-start.30 = (bf16[128,1792]{1,0:T(8,128)(2,1)S(1)}, bf16[128,1792]{1,0:T(8,128)(2,1)S(1)}, u32[]{:S(2)}, u32[]{:S(2)}) collective-permute-start(bf16[128,1792]{1,0:T(8,128)(2,1)S(1)} %collective-permute-done.29.refs_1_.refs_3_), channel_id=1, source_target_pairs={{4,0},{8,12},{5,1},{9,13},{6,2},{10,14},{7,3},{11,15},{20,16},{24,... | collective-permute-start | bytes 1376264 | tf_op jit(solution)/shard_map/ppermute | solution.py:110
  158.8 24.0 %collective-permute-start.27 = (bf16[128,1792]{1,0:T(8,128)(2,1)S(1)}, bf16[128,1792]{1,0:T(8,128)(2,1)S(1)}, u32[]{:S(2)}, u32[]{:S(2)}) collective-permute-start(bf16[128,1792]{1,0:T(8,128)(2,1)S(1)} %gate.21.refs_0_), channel_id=1, source_target_pairs={{0,4},{4,8},{8,12},{1,5},{5,9},{9,13},{2,6},{6,10},{10,14},{3,7},{... | collective-permute-start | bytes 1376264 | tf_op jit(solution)/shard_map/ppermute | solution.py:104
  178.7 28.9 %collective-permute-start.34 = (bf16[128,1792]{1,0:T(8,128)(2,1)S(1)}, bf16[128,1792]{1,0:T(8,128)(2,1)S(1)}, u32[]{:S(2)}, u32[]{:S(2)}) collective-permute-start(bf16[128,1792]{1,0:T(8,128)(2,1)S(1)} %gate.25), channel_id=1, source_target_pairs={{0,8},{4,12},{8,0},{12,4},{1,9},{5,13},{9,1},{13,5},{2,10},{6,14},... | collective-permute-start | bytes 1376264 | tf_op jit(solution)/shard_map/ppermute | solution.py:109
  178.8 37.1 %collective-permute-start.36 = (bf16[128,1792]{1,0:T(8,128)(2,1)S(1)}, bf16[128,1792]{1,0:T(8,128)(2,1)S(1)}, u32[]{:S(2)}, u32[]{:S(2)}) collective-permute-start(bf16[128,1792]{1,0:T(8,128)(2,1)S(1)} %collective-permute-done.33.refs_1_.refs_3_), channel_id=1, source_target_pairs={{4,0},{8,12},{5,1},{9,13},{6,2},{10,14},{7,3},{11,15},{20,16},{24,... | collective-permute-start | bytes 1376264 | tf_op jit(solution)/shard_map/ppermute | solution.py:110
  188.3 31.0 %collective-permute-start.31 = (bf16[128,1792]{1,0:T(8,128)(2,1)S(1)}, bf16[128,1792]{1,0:T(8,128)(2,1)S(1)}, u32[]{:S(2)}, u32[]{:S(2)}) collective-permute-start(bf16[128,1792]{1,0:T(8,128)(2,1)S(1)} %gate.23.refs_0_), channel_id=1, source_target_pairs={{0,4},{4,8},{8,12},{1,5},{5,9},{9,13},{2,6},{6,10},{10,14},{3,7},{... | collective-permute-start | bytes 1376264 | tf_op jit(solution)/shard_map/ppermute | solution.py:104
  201.4 17.9 %collective-permute-start.32 = (bf16[128,1792]{1,0:T(8,128)(2,1)S(1)}, bf16[128,1792]{1,0:T(8,128)(2,1)S(1)}, u32[]{:S(2)}, u32[]{:S(2)}) collective-permute-start(bf16[128,1792]{1,0:T(8,128)(2,1)S(1)} %gate.23.refs_0_), channel_id=1, source_target_pairs={{4,0},{8,4},{12,8},{5,1},{9,5},{13,9},{6,2},{10,6},{14,10},{7,3},{... | collective-permute-start | bytes 1376264 | tf_op jit(solution)/shard_map/ppermute | solution.py:105
  207.6 19.3 %collective-permute-start.35 = (bf16[128,1792]{1,0:T(8,128)(2,1)S(1)}, bf16[128,1792]{1,0:T(8,128)(2,1)S(1)}, u32[]{:S(2)}, u32[]{:S(2)}) collective-permute-start(bf16[128,1792]{1,0:T(8,128)(2,1)S(1)} %collective-permute-done.34.refs_3_), channel_id=1, source_target_pairs={{4,0},{8,12},{5,1},{9,13},{6,2},{10,14},{7,3},{11,15},{20,16},{24,... | collective-permute-start | bytes 1376264 | tf_op jit(solution)/shard_map/ppermute | solution.py:110
  (20 other events, 321.3 us)
